TPU v7x, 256 devices: a whole 4x4x8 slice. The times are simulated.
256 devices in a mesh: gx: 16 (over x, z_hi), gy: 8 (over z_lo, y), gz: 2 (over core).
Axes of the slice: x: 4, y: 4, z: 8 (z_hi: 4, z_lo: 2; z = z_hi * 2 + z_lo), core: 2. Of those that a mesh axis runs over, the one named last changes fastest.
Arguments:
- efield: float32 [3, 128, 192, 256], P(None, 'gx', 'gy', 'gz'), may hold values from -6 to 6
- hfield: float32 [3, 128, 192, 256], P(None, 'gx', 'gy', 'gz'), may hold values from -6 to 6
- inv_eps: float32 [128, 192, 256], P('gx', 'gy', 'gz'), may hold values from 0.15 to 1
- gain_state: float32 [16, 8, 2, 32, 10, 128], P('gx', 'gy', 'gz'), as said below
- pump: float32 [16, 8, 2, 32, 128], P('gx', 'gy', 'gz'), may hold values from 0.01 to 0.3
- gain_offsets: int32 [16, 8, 2, 32, 128], P('gx', 'gy', 'gz'), may hold values from 0 to 24575, as said below
- gain_count: int32 [16, 8, 2], P('gx', 'gy', 'gz'), may hold values from 1 to 32, as said below
- block_owner: int32 [16, 8, 2, 32], P('gx', 'gy', 'gz'), may hold values from 0 to 31, each once within a row
- surf_offsets: int32 [16, 8, 2, 128], P('gx', 'gy', 'gz'), may hold values from 0 to 24575, as said below
- far_acc: float32 [64, 12, 128], P('gz'), may hold values from -6 to 6
Outputs:
- efield_out: float32 [3, 128, 192, 256], P(None, 'gx', 'gy', 'gz')
- hfield_out: float32 [3, 128, 192, 256], P(None, 'gx', 'gy', 'gz')
- state_out: float32 [16, 8, 2, 32, 10, 128], P('gx', 'gy', 'gz')
- far_out: float32 [64, 12, 128], P('gz')
Inputs may be any that keep to these rules, and one draw needn't show every extreme that they name: `gain_offsets`: within one brick all offsets are distinct. `gain_count`: some brick holds 32 live blocks in every draw. `block_owner`: each brick's codes are a permutation of 0 to 31. `surf_offsets`: within one brick all offsets are distinct. `gain_state`: populations lie in 0.05 to 1.
All inputs are finite; a program needn't handle non-finite values.
Results may differ from a plain program's by a relative error of at most 0.00022.
Values sent between devices are 32-bit elements; how exact they have to be, the bound alone decides.
No kernel may reach another device: no remote copies, remote signals or barrier semaphores. Data moves between devices by JAX's collectives and lax.ppermute only.
A program may use at most 64 MiB of HBM per device.

v0:
```python
import math

import jax
import jax.numpy as jnp
from jax import lax
from jax.sharding import PartitionSpec as P

FREQ = 64
STEPS = 2


time_step = 0.5
damping = 0.1
omega_rest = 1.0
coupling = 0.5
cross_rate = 0.3
upper_life = 2.0
lasing_life = 20.0
lower_life = 2.0
freq_low = 0.3
freq_pitch = 0.01
golden = 2.399963229728653


def with_halo(value, sides, width):
    for axis, dim in sides:
        peers, length = (lax.axis_size(axis), value.shape[dim])
        up = [(i, (i + 1) % peers) for i in range(peers - 1)]
        down = [(j, i) for i, j in up]
        last = lax.slice_in_dim(value, length - width, length, axis=dim)
        first = lax.slice_in_dim(value, 0, width, axis=dim)
        before = lax.ppermute(last, axis, up)
        after = lax.ppermute(first, axis, down)
        value = jnp.concatenate([before, value, after], axis=dim)
    return value


def bloch_update(state, drive, pump):
    polar = state[:, 0:3]
    rate = state[:, 3:6]
    ground = state[:, 6]
    lower = state[:, 7]
    lasing = state[:, 8]
    upper = state[:, 9]
    inversion = (lasing - lower)[:, None]
    half = 0.5 * damping * time_step
    rate_new = (
        (1.0 - half) * rate
        + time_step * (coupling * inversion * drive - omega_rest * omega_rest * polar)
    ) / (1.0 + half)
    polar_new = polar + time_step * rate_new
    power = jnp.sum(drive * rate_new, axis=1)
    upper_new = upper + time_step * (pump * ground - upper / upper_life)
    lasing_new = lasing + time_step * (
        upper / upper_life - lasing / lasing_life + cross_rate * power
    )
    lower_new = lower + time_step * (lasing / lasing_life - lower / lower_life - cross_rate * power)
    ground_new = ground + time_step * (lower / lower_life - pump * ground)
    levels = jnp.stack([ground_new, lower_new, lasing_new, upper_new], axis=1)
    return (jnp.concatenate([polar_new, rate_new, levels], axis=1), rate_new)


def directions(count):
    index = jnp.arange(count, dtype=jnp.float32)
    cosine = 1.0 - 2.0 * (index + 0.5) / count
    sine = jnp.sqrt(1.0 - cosine * cosine)
    azimuth = golden * index
    return (sine * jnp.cos(azimuth), sine * jnp.sin(azimuth), cosine)


def window(padded, comp, start_x, start_y, start_z, size_x, size_y, size_z):
    return padded[
        comp,
        start_x : start_x + size_x + 1,
        start_y : start_y + size_y + 1,
        start_z : start_z + size_z + 1,
    ]


def magnetic(padded, size_x, size_y, size_z):

    def forward(comp, axis):
        starts = [0, 0, 0]
        starts[axis] = 1
        moved = window(padded, comp, starts[0], starts[1], starts[2], size_x, size_y, size_z)
        return moved - window(padded, comp, 0, 0, 0, size_x, size_y, size_z)

    first = forward(2, 1) - forward(1, 2)
    second = forward(0, 2) - forward(2, 0)
    third = forward(1, 0) - forward(0, 1)
    rotation = jnp.stack([first, second, third])
    old = jnp.stack([window(padded, comp, 0, 0, 0, size_x, size_y, size_z) for comp in (3, 4, 5)])
    return old - time_step * rotation


def electric_curl(h_rim):

    def backward(comp, axis):
        here = h_rim[comp, 1:, 1:, 1:]
        if axis == 0:
            return here - h_rim[comp, :-1, 1:, 1:]
        if axis == 1:
            return here - h_rim[comp, 1:, :-1, 1:]
        return here - h_rim[comp, 1:, 1:, :-1]

    first = backward(2, 1) - backward(1, 2)
    second = backward(0, 2) - backward(2, 0)
    third = backward(1, 0) - backward(0, 1)
    return jnp.stack([first, second, third])


def mixing(left, right):
    return jnp.einsum("gcs,gsd->gcd", left, right, precision=lax.Precision.HIGHEST)


def local(
    efield,
    hfield,
    inv_eps,
    gain_state,
    pump,
    gain_offsets,
    gain_count,
    block_owner,
    surf_offsets,
    far_acc,
):
    comps, size_x, size_y, size_z = efield.shape
    slots = block_owner.shape[3]
    block = gain_offsets.shape[4]
    owners = lax.axis_size("gx")
    capacity = slots // owners
    surf = surf_offsets.shape[3]
    dirs = far_acc.shape[2]
    index_x = lax.axis_index("gx")
    index_y = lax.axis_index("gy")
    index_z = lax.axis_index("gz")
    mask_x = ((jnp.arange(size_x + 1) > 0) | (index_x > 0)).astype(jnp.float32)
    mask_y = ((jnp.arange(size_y + 1) > 0) | (index_y > 0)).astype(jnp.float32)
    mask_z = ((jnp.arange(size_z + 1) > 0) | (index_z > 0)).astype(jnp.float32)
    rim_mask = mask_x[:, None, None] * mask_y[None, :, None] * mask_z[None, None, :]
    offsets = gain_offsets.reshape(slots * block)
    owner_code = block_owner.reshape(slots)
    live = (jnp.arange(slots, dtype=jnp.int32) < gain_count.reshape(())).astype(jnp.float32)[
        :, None, None
    ]
    state = gain_state.reshape(slots, 10, block)
    pumps = pump.reshape(slots, block)
    surf_cells = surf_offsets.reshape(surf)
    pos_x = (index_x * size_x + surf_cells // (size_y * size_z)).astype(jnp.float32) - 0.5 * (
        size_x * lax.axis_size("gx") - 1
    )
    pos_y = (index_y * size_y + surf_cells // size_z % size_y).astype(jnp.float32) - 0.5 * (
        size_y * lax.axis_size("gy") - 1
    )
    pos_z = (index_z * size_z + surf_cells % size_z).astype(jnp.float32) - 0.5 * (
        size_z * lax.axis_size("gz") - 1
    )
    omega = freq_low + freq_pitch * jnp.arange(FREQ, dtype=jnp.float32)
    spec_re = jnp.zeros((FREQ, 6, surf), jnp.float32)
    spec_im = jnp.zeros((FREQ, 6, surf), jnp.float32)
    scaled_eps = time_step * inv_eps[None]
    for step in range(STEPS):
        both = jnp.concatenate([efield, hfield], axis=0)
        padded = with_halo(both, (("gx", 1), ("gy", 2), ("gz", 3)), 1)
        h_rim = magnetic(padded, size_x, size_y, size_z) * rim_mask[None]
        hnew = h_rim[:, 1:, 1:, 1:]
        rotation = electric_curl(h_rim)
        samples = (
            efield.reshape(3, -1)[:, offsets].reshape(3, slots, block).transpose(1, 0, 2) * live
        )
        outgoing = jnp.zeros_like(samples).at[owner_code].set(samples)
        drive = lax.all_to_all(
            outgoing.reshape(owners, capacity, 3, block),
            "gx",
            split_axis=0,
            concat_axis=0,
            tiled=True,
        ).reshape(slots, 3, block)
        state, rate = bloch_update(state, drive, pumps)
        returned = lax.all_to_all(
            rate.reshape(owners, capacity, 3, block), "gx", split_axis=0, concat_axis=0, tiled=True
        ).reshape(slots, 3, block)
        current = returned[owner_code] * live
        source = (
            jnp.zeros((3, size_x * size_y * size_z), jnp.float32)
            .at[:, offsets]
            .add(current.transpose(1, 0, 2).reshape(3, -1))
        )
        source = source.reshape(3, size_x, size_y, size_z)
        efield = efield + scaled_eps * (rotation - source)
        hfield = hnew
        sampled = jnp.concatenate([efield, hfield], axis=0).reshape(6, -1)[:, surf_cells]
        moment = omega * ((step + 1) * time_step)
        spec_re = spec_re + jnp.cos(moment)[:, None, None] * sampled[None]
        spec_im = spec_im - jnp.sin(moment)[:, None, None] * sampled[None]
    unit_x, unit_y, unit_z = directions(dirs)
    along = (
        pos_x[:, None] * unit_x[None]
        + pos_y[:, None] * unit_y[None]
        + pos_z[:, None] * unit_z[None]
    )

    def far_group(pieces):
        part_re, part_im, freqs = pieces
        phase = freqs[:, None, None] * along[None]
        table_re = jnp.cos(phase)
        table_im = jnp.sin(phase)
        real = mixing(part_re, table_re) - mixing(part_im, table_im)
        imag = mixing(part_re, table_im) + mixing(part_im, table_re)
        return jnp.concatenate([real, imag], axis=1)

    groups = FREQ // 8
    grouped = lax.map(
        far_group,
        (
            spec_re.reshape(groups, 8, 6, surf),
            spec_im.reshape(groups, 8, 6, surf),
            omega.reshape(groups, 8),
        ),
    )
    devices = lax.axis_size("gx") * lax.axis_size("gy") * lax.axis_size("gz")
    scale = 1.0 / math.sqrt(STEPS * surf * devices)
    partial_value = grouped.reshape(FREQ, 12, dirs) * scale
    summed = lax.psum(partial_value, ("gx", "gy"))
    owned = lax.psum_scatter(summed, "gz", scatter_dimension=0, tiled=True)
    far_out = far_acc + owned
    return (efield, hfield, state.reshape(1, 1, 1, slots, 10, block), far_out)


def solution(mesh):
    placed = (
        P(None, "gx", "gy", "gz"),
        P(None, "gx", "gy", "gz"),
        P("gx", "gy", "gz"),
        P("gx", "gy", "gz", None, None, None),
        P("gx", "gy", "gz", None, None),
        P("gx", "gy", "gz", None, None),
        P("gx", "gy", "gz"),
        P("gx", "gy", "gz", None),
        P("gx", "gy", "gz", None),
        P("gz", None, None),
    )
    return jax.shard_map(
        local,
        mesh=mesh,
        in_specs=placed,
        out_specs=(
            P(None, "gx", "gy", "gz"),
            P(None, "gx", "gy", "gz"),
            P("gx", "gy", "gz", None, None, None),
            P("gz", None, None),
        ),
        check_vma=False,
    )
```

profile of v0, /device:TPU:8, one launch (start us, length us, event | category | flops | bytes accessed | tf_op | source)
XLA Modules:
  0.0 626.1 jit_solution(16798058520438655139)
XLA Ops:
  9.8 5.2 collective-permute-start
  16.4 7.7 %copy.194 = f32[3,8,24,128]{0,3,2,1:T(8,128)} copy(f32[3,8,24,128]{3,2,1,0:T(8,128)} %param.12) | data formatting | bytes 589824 | tf_op args[0]
  24.2 15.3 %gather_fusion = f32[4096,3]{1,0:T(8,128)S(1)} fusion(f32[3,24576]{0,1:T(8,128)} %bitcast.164, s32[4096]{0:T(1024)S(1)} %broadcast_clamp_fusion), kind=kCustom, calls=%fused_computation | custom fusion | bytes 114688 | tf_op jit(solution)/shard_map/gather | solution.py:170
  43.2 12.5 %all-to-all-start = ((f32[16,2,3,128]{3,1,2,0:T(2,128)}), f32[16,2,3,128]{3,1,2,0:T(2,128)S(1)}, u32[]{:S(2)}, u32[]{:S(2)}) async-start(f32[16,2,3,128]{3,1,2,0:T(2,128)} %copy.197), calls=%async_computation | async-start | bytes 98304 | tf_op jit(solution)/shard_map/all_to_all | solution.py:173
  61.7 3.2 copy.188
  64.8 3.5 collective-permute-start.2
  71.4 9.7 %all-to-all-start.1 = ((f32[16,2,3,128]{3,1,2,0:T(2,128)}), f32[16,2,3,128]{3,1,2,0:T(2,128)}, u32[]{:S(2)}, u32[]{:S(2)}) async-start(f32[16,2,3,128]{3,1,2,0:T(2,128)} %copy.199), calls=%async_computation.1 | async-start | bytes 98304 | tf_op jit(solution)/shard_map/all_to_all | solution.py:181
  84.2 3.2 copy.189
  87.4 8.3 %pad_maximum_fusion = f32[6,10,26,128]{2,0,3,1:T(8,128)S(1)} fusion(f32[6,10,1,128]{2,0,3,1:T(8,128)} %copy.189, f32[6,10,24,128]{2,0,3,1:T(8,128)} %copy.188, f32[6,10,1,128]{2,0,3,1:T(8,128)} %copy.187), kind=kLoop, calls=%fused_computation.46 | loop fusion | flops 399360 | bytes 1597440 | tf_op jit(solution)/shard_map/concatenate | solution.py:34
  101.8 3.1 copy.191
  110.4 27.8 %scatter_custom_fusion.1 = f32[3,24576]{0,1:T(8,128)} fusion(s32[4096]{0:T(1024)} %bitcast.189, f32[4096,3]{1,0:T(8,128)S(1)} %copy.201, f32[]{:T(128)} %constant.122.clone.1), kind=kCustom, calls=%fused_computation.44 | custom fusion | flops 12288 | bytes 295424 | tf_op jit(solution)/shard_map/scatter-add | solution.py:188
  138.2 7.7 %copy.202 = f32[3,8,24,128]{3,2,1,0:T(8,128)S(1)} copy(f32[3,8,24,128]{0,3,2,1:T(8,128)} %bitcast.162) | data formatting | bytes 589824 | tf_op jit(solution)/shard_map/reshape | solution.py:190
  146.0 6.7 %copy.212 = f32[3,8,24,128]{0,3,2,1:T(8,128)} copy(f32[3,8,24,128]{3,2,1,0:T(8,128)S(1)} %fusion.65) | data formatting | bytes 589824 | tf_op jit(solution)/shard_map/add | solution.py:191
  152.7 4.7 collective-permute-start.6
  158.7 15.3 %gather_fusion.2 = f32[4096,3]{1,0:T(8,128)S(1)} fusion(f32[3,24576]{0,1:T(8,128)} %bitcast.163, s32[4096]{0:T(1024)S(1)} %broadcast_clamp_fusion), kind=kCustom, calls=%fused_computation.2 | custom fusion | bytes 114688 | tf_op jit(solution)/shard_map/gather | solution.py:170
  176.9 11.5 %all-to-all-start.2 = ((f32[16,2,3,128]{3,1,2,0:T(2,128)}), f32[16,2,3,128]{3,1,2,0:T(2,128)S(1)}, u32[]{:S(2)}, u32[]{:S(2)}) async-start(f32[16,2,3,128]{3,1,2,0:T(2,128)} %copy.215), calls=%async_computation.2 | async-start | bytes 98304 | tf_op jit(solution)/shard_map/all_to_all | solution.py:173
  188.5 6.8 %copy.221 = f32[6,8,24,128]{0,3,2,1:T(8,128)} copy(f32[6,8,24,128]{3,2,1,0:T(8,128)S(1)} %pad_maximum_fusion.2) | data formatting | bytes 1179648 | tf_op jit(solution)/shard_map/concatenate | solution.py:164
  195.4 5.4 gather_fusion.4
  201.5 3.2 copy.206
  204.8 3.5 collective-permute-start.8
  214.2 3.1 copy.207
  217.3 8.3 %pad_maximum_fusion.1 = f32[6,10,26,128]{2,0,3,1:T(8,128)S(1)} fusion(f32[6,10,1,128]{2,0,3,1:T(8,128)} %copy.207, f32[6,10,24,128]{2,0,3,1:T(8,128)} %copy.206, f32[6,10,1,128]{2,0,3,1:T(8,128)} %copy.205), kind=kLoop, calls=%fused_computation.47 | loop fusion | flops 399360 | bytes 1597440 | tf_op jit(solution)/shard_map/concatenate | solution.py:34
  231.4 9.5 %all-to-all-start.3 = ((f32[16,2,3,128]{3,1,2,0:T(2,128)}), f32[16,2,3,128]{3,1,2,0:T(2,128)}, u32[]{:S(2)}, u32[]{:S(2)}) async-start(f32[16,2,3,128]{3,1,2,0:T(2,128)} %copy.217), calls=%async_computation.3 | async-start | bytes 98304 | tf_op jit(solution)/shard_map/all_to_all | solution.py:181
  240.9 3.1 copy.209
  247.5 3.7 all-to-all-done.3
  253.5 28.0 %scatter_custom_fusion.3 = f32[3,24576]{0,1:T(8,128)} fusion(s32[4096]{0:T(1024)} %bitcast.190, f32[4096,3]{1,0:T(8,128)S(1)} %copy.219, f32[]{:T(128)} %constant.122.clone.1), kind=kCustom, calls=%fused_computation.42 | custom fusion | flops 12288 | bytes 295424 | tf_op jit(solution)/shard_map/scatter-add | solution.py:188
  281.5 7.6 %copy.220 = f32[3,8,24,128]{3,2,1,0:T(8,128)S(1)} copy(f32[3,8,24,128]{0,3,2,1:T(8,128)} %bitcast.161) | data formatting | bytes 589824 | tf_op jit(solution)/shard_map/reshape | solution.py:190
  289.4 6.8 %copy.223 = f32[6,8,24,128]{0,3,2,1:T(8,128)} copy(f32[6,8,24,128]{3,2,1,0:T(8,128)S(1)} %pad_maximum_fusion.5) | data formatting | bytes 1179648 | tf_op jit(solution)/shard_map/concatenate | solution.py:193
  296.2 5.4 gather_fusion.5
  302.2 79.8 %while.11 = (s32[]{:T(128)}, f32[8,8,12,128]{3,2,1,0:T(8,128)S(1)}, f32[8,8,6,128]{3,2,1,0:T(8,128)S(1)}, f32[8,8]{1,0:T(8,128)}, f32[8,8,6,128]{3,2,1,0:T(8,128...) while((s32[]{:T(128)}, f32[8,8,12,128]{3,2,1,0:T(8,128)S(1)}, ...), condition=%wide.region_7.8_spmd.clone, body=%wide.region_6.7_spmd.clone.sunk | while | flops 38379520 | bytes 758989 | solution.py:214
  384.8 13.0 %reduce-scatter.2.cloned.1.call-done = f32[32,12,128]{2,0,1:T(8,128)} async-done(((f32[64,12,128]{2,0,1:T(8,128)}), f32[32,12,128]{2,0,1:T(8,128)}) %reduce-scatter.2.cloned.1.call-update) | async-done | bytes 196624 | tf_op jit(solution)/shard_map/reduce_scatter | solution.py:226
  398.5 218.8 %all-reduce.2.cloned.1.call-done = f32[32,12,128]{2,0,1:T(8,128)} async-done(((f32[32,12,128]{2,0,1:T(8,128)}), f32[32,12,128]{2,0,1:T(8,128)}) %all-reduce.2.cloned.1.call-update) | async-done | bytes 196624 | tf_op jit(solution)/shard_map/psum | solution.py:225
  (255 shorter events, 138.0 us)
Async XLA Ops:
  9.8 51.8 %collective-permute-start = (f32[6,1,24,128]{3,2,1,0:T(8,128)}, f32[6,1,24,128]{3,2,1,0:T(8,128)S(1)}, u32[]{:S(2)}, u32[]{:S(2)}) collective-permute-start(f32[6,1,24,128]{3,2,1,0:T(8,128)} %get-tuple-element.126), channel_id=1, source_target_pairs={{0,16},{16,32},{32,48},{48,64},{64,80},{80,96},{96,112},{112,128},... | collective-permute-start | bytes 221192 | tf_op jit(solution)/shard_map/ppermute | solution.py:32
  15.0 26.0 %copy-start.39 = (s32[1,1,1,32]{3,2,1,0:T(1,128)S(1)}, s32[1,1,1,32]{3,2,1,0:T(1,128)}, u32[]{:S(2)}) copy-start(s32[1,1,1,32]{3,2,1,0:T(1,128)} %param.19) | copy-start | bytes 388
  15.0 43.2 %copy-start.5 = (f32[1,1,1,32,10,128]{5,3,4,2,1,0:T(8,128)S(1)}, f32[1,1,1,32,10,128]{5,3,4,2,1,0:T(8,128)}, u32[]{:S(2)}) copy-start(f32[1,1,1,32,10,128]{5,3,4,2,1,0:T(8,128)} %param.15) | copy-start | bytes 491524
  15.0 43.2 %copy-start.17 = (f32[8,24,128]{2,1,0:T(8,128)S(1)}, f32[8,24,128]{2,1,0:T(8,128)}, u32[]{:S(2)}) copy-start(f32[8,24,128]{2,1,0:T(8,128)} %param.14) | copy-start | bytes 294916
  15.0 43.9 %copy-start.38 = (s32[1,1,1,128]{3,2,1,0:T(1,128)S(1)}, s32[1,1,1,128]{3,2,1,0:T(1,128)}, u32[]{:S(2)}) copy-start(s32[1,1,1,128]{3,2,1,0:T(1,128)} %param.20) | copy-start | bytes 1540
  15.0 46.6 %collective-permute-start.1 = (f32[6,1,24,128]{3,2,1,0:T(8,128)S(1)}, f32[6,1,24,128]{3,2,1,0:T(8,128)S(1)}, u32[]{:S(2)}, u32[]{:S(2)}) collective-permute-start(f32[6,1,24,128]{3,2,1,0:T(8,128)S(1)} %get-tuple-element.127), channel_id=1, source_target_pairs={{16,0},{32,16},{48,32},{64,48},{80,64},{96,80},{112,96},{128,112},... | collective-permute-start | bytes 221192 | tf_op jit(solution)/shard_map/ppermute | solution.py:33
  40.8 17.4 %copy-start.33 = (f32[32]{0:T(128)}, f32[32]{0:T(128)S(1)}, u32[]{:S(2)}) copy-start(f32[32]{0:T(128)S(1)} %compare_convert_fusion) | copy-start | bytes 388
  41.0 17.2 %copy-start.36 = (s32[32]{0:T(128)}, s32[32]{0:T(128)S(1)}, u32[]{:S(2)}) copy-start(s32[32]{0:T(128)S(1)} %fusion.99) | copy-start | bytes 388
  43.2 27.6 %all-to-all-start = ((f32[16,2,3,128]{3,1,2,0:T(2,128)}), f32[16,2,3,128]{3,1,2,0:T(2,128)S(1)}, u32[]{:S(2)}, u32[]{:S(2)}) async-start(f32[16,2,3,128]{3,1,2,0:T(2,128)} %copy.197), calls=%async_computation | async-start | bytes 98304 | tf_op jit(solution)/shard_map/all_to_all | solution.py:173
  64.8 16.3 %collective-permute-start.2 = (f32[6,10,1,128]{3,0,2,1:T(8,128)S(1)}, f32[6,10,1,128]{3,0,2,1:T(8,128)S(1)}, u32[]{:S(2)}, u32[]{:S(2)}) collective-permute-start(f32[6,10,1,128]{3,0,2,1:T(8,128)S(1)} %copy.228), channel_id=1, source_target_pairs={{0,2},{2,4},{4,6},{6,8},{8,10},{10,12},{12,14},{1,3},{3,5},{5,7},{... | collective-permute-start | bytes 92168 | tf_op jit(solution)/shard_map/ppermute | solution.py:32
  68.3 15.9 %collective-permute-start.3 = (f32[6,10,1,128]{3,0,2,1:T(8,128)S(1)}, f32[6,10,1,128]{3,0,2,1:T(8,128)S(1)}, u32[]{:S(2)}, u32[]{:S(2)}) collective-permute-start(f32[6,10,1,128]{3,0,2,1:T(8,128)S(1)} %copy.229), channel_id=1, source_target_pairs={{2,0},{4,2},{6,4},{8,6},{10,8},{12,10},{14,12},{3,1},{5,3},{7,5},{... | collective-permute-start | bytes 92168 | tf_op jit(solution)/shard_map/ppermute | solution.py:33
  71.4 36.0 %all-to-all-start.1 = ((f32[16,2,3,128]{3,1,2,0:T(2,128)}), f32[16,2,3,128]{3,1,2,0:T(2,128)}, u32[]{:S(2)}, u32[]{:S(2)}) async-start(f32[16,2,3,128]{3,1,2,0:T(2,128)} %copy.199), calls=%async_computation.1 | async-start | bytes 98304 | tf_op jit(solution)/shard_map/all_to_all | solution.py:181
  98.1 6.8 %collective-permute-start.4 = (f32[6,10,26,1]{2,0,3,1:T(8,128)S(1)}, f32[6,10,26,1]{2,0,3,1:T(8,128)S(1)}, u32[]{:S(2)}, u32[]{:S(2)}) collective-permute-start(f32[6,10,26,1]{2,0,3,1:T(8,128)S(1)} %get-tuple-element.107), channel_id=1, source_target_pairs={{0,1},{2,3},{4,5},{6,7},{8,9},{10,11},{12,13},{14,15},{16,17},{18,... | collective-permute-start | bytes 18728 | tf_op jit(solution)/shard_map/ppermute | solution.py:32
  99.4 6.0 collective-permute-start.5
  145.9 28.7 %copy-start.34 = (f32[32]{0:T(128)S(1)}, f32[32]{0:T(128)}, u32[]{:S(2)}) copy-start(f32[32]{0:T(128)} %copy-done.33) | copy-start | bytes 388
  145.9 28.8 %copy-start.37 = (s32[32]{0:T(128)S(1)}, s32[32]{0:T(128)}, u32[]{:S(2)}) copy-start(s32[32]{0:T(128)} %copy-done.36) | copy-start | bytes 388
  152.7 48.7 %collective-permute-start.6 = (f32[6,1,24,128]{3,2,1,0:T(8,128)S(1)}, f32[6,1,24,128]{3,2,1,0:T(8,128)S(1)}, u32[]{:S(2)}, u32[]{:S(2)}) collective-permute-start(f32[6,1,24,128]{3,2,1,0:T(8,128)S(1)} %get-tuple-element.124), channel_id=1, source_target_pairs={{0,16},{16,32},{32,48},{48,64},{64,80},{80,96},{96,112},{112,128},... | collective-permute-start | bytes 221192 | tf_op jit(solution)/shard_map/ppermute | solution.py:32
  157.4 44.0 %collective-permute-start.7 = (f32[6,1,24,128]{3,2,1,0:T(8,128)S(1)}, f32[6,1,24,128]{3,2,1,0:T(8,128)S(1)}, u32[]{:S(2)}, u32[]{:S(2)}) collective-permute-start(f32[6,1,24,128]{3,2,1,0:T(8,128)S(1)} %get-tuple-element.125), channel_id=1, source_target_pairs={{16,0},{32,16},{48,32},{64,48},{80,64},{96,80},{112,96},{128,112},... | collective-permute-start | bytes 221192 | tf_op jit(solution)/shard_map/ppermute | solution.py:33
  176.9 33.9 %all-to-all-start.2 = ((f32[16,2,3,128]{3,1,2,0:T(2,128)}), f32[16,2,3,128]{3,1,2,0:T(2,128)S(1)}, u32[]{:S(2)}, u32[]{:S(2)}) async-start(f32[16,2,3,128]{3,1,2,0:T(2,128)} %copy.215), calls=%async_computation.2 | async-start | bytes 98304 | tf_op jit(solution)/shard_map/all_to_all | solution.py:173
  204.8 6.2 collective-permute-start.8
  208.3 5.9 collective-permute-start.9
  228.0 16.1 %collective-permute-start.10 = (f32[6,10,26,1]{2,0,3,1:T(8,128)S(1)}, f32[6,10,26,1]{2,0,3,1:T(8,128)S(1)}, u32[]{:S(2)}, u32[]{:S(2)}) collective-permute-start(f32[6,10,26,1]{2,0,3,1:T(8,128)S(1)} %get-tuple-element.105), channel_id=1, source_target_pairs={{0,1},{2,3},{4,5},{6,7},{8,9},{10,11},{12,13},{14,15},{16,17},{18,... | collective-permute-start | bytes 18728 | tf_op jit(solution)/shard_map/ppermute | solution.py:32
  229.4 15.2 %collective-permute-start.11 = (f32[6,10,26,1]{2,0,3,1:T(8,128)S(1)}, f32[6,10,26,1]{2,0,3,1:T(8,128)}, u32[]{:S(2)}, u32[]{:S(2)}) collective-permute-start(f32[6,10,26,1]{2,0,3,1:T(8,128)S(1)} %get-tuple-element.104), channel_id=1, source_target_pairs={{1,0},{3,2},{5,4},{7,6},{9,8},{11,10},{13,12},{15,14},{17,16},{19,... | collective-permute-start | bytes 18728 | tf_op jit(solution)/shard_map/ppermute | solution.py:33
  231.4 19.7 %all-to-all-start.3 = ((f32[16,2,3,128]{3,1,2,0:T(2,128)}), f32[16,2,3,128]{3,1,2,0:T(2,128)}, u32[]{:S(2)}, u32[]{:S(2)}) async-start(f32[16,2,3,128]{3,1,2,0:T(2,128)} %copy.217), calls=%async_computation.3 | async-start | bytes 98304 | tf_op jit(solution)/shard_map/all_to_all | solution.py:181
  240.9 157.0 %reduce-scatter.2.cloned.1.call-start = ((), (), s32[]{:S(2)}) async-start(), calls=%async_computation.5 | async-start | bytes 589824 | tf_op jit(solution)/shard_map/reduce_scatter | solution.py:226
  247.4 41.8 %copy-start.4 = (f32[3,8,24,128]{3,2,1,0:T(8,128)}, f32[3,8,24,128]{3,2,1,0:T(8,128)S(1)}, u32[]{:S(2)}) copy-start(f32[3,8,24,128]{3,2,1,0:T(8,128)S(1)} %slice.352) | copy-start | bytes 884740
  296.2 86.7 %copy-start.7 = (f32[1,1,1,32,10,128]{5,3,4,2,1,0:T(8,128)S(1)}, f32[1,1,1,32,10,128]{5,3,4,2,1,0:T(8,128)}, u32[]{:S(2)}) copy-start(f32[1,1,1,32,10,128]{5,3,4,2,1,0:T(8,128)} %param.15) | copy-start | bytes 491524
  296.2 86.7 %copy-start.14 = (f32[1,1,1,32,128]{4,3,2,1,0:T(8,128)S(1)}, f32[1,1,1,32,128]{4,3,2,1,0:T(8,128)}, u32[]{:S(2)}) copy-start(f32[1,1,1,32,128]{4,3,2,1,0:T(8,128)} %param.16) | copy-start | bytes 49156
  296.2 86.8 %copy-start.15 = (f32[32,1,128]{2,0,1:T(8,128)S(1)}, f32[32,1,128]{2,0,1:T(8,128)}, u32[]{:S(2)}) copy-start(f32[32,1,128]{2,0,1:T(8,128)} %get-tuple-element.100) | copy-start | bytes 49156
  296.2 87.4 %copy-start.16 = (f32[32,1,128]{2,0,1:T(8,128)S(1)}, f32[32,1,128]{2,0,1:T(8,128)}, u32[]{:S(2)}) copy-start(f32[32,1,128]{2,0,1:T(8,128)} %get-tuple-element.101) | copy-start | bytes 49156
  296.2 321.1 %copy-start.13 = (f32[32,12,128]{2,0,1:T(8,128)S(1)}, f32[32,12,128]{2,0,1:T(8,128)}, u32[]{:S(2)}) copy-start(f32[32,12,128]{2,0,1:T(8,128)} %param.21) | copy-start | bytes 589828
  382.9 234.4 %all-reduce.2.cloned.1.call-start = ((), (), s32[]{:S(2)}) async-start(), calls=%async_computation.6 | async-start | bytes 393216 | tf_op jit(solution)/shard_map/psum | solution.py:225
  (26 other events, 293.5 us)
Sparse Core Ops, SparseCore 0:
  383.0 14.8 reduce-scatter.1
  404.2 213.0 all-reduce.1
where the time goes:
time: 634 us; the launch traced here: 626 us
  waiting for transfers between devices  236 us (37%)
  local copies, waits for them, and re-layouts  139 us (22%)
  other arithmetic  88.5 us (14%)
  starting transfers between devices  73.5 us (12%)
  matrix products  73 us (12%)
  between operations  16 us (3%)
    psum x1, waiting for transfers between devices, local(): summed = lax.psum(partial_value, ('gx', 'gy'))  219 us
    dot_general x32, matrix products, mixing(): jnp.einsum('gcs,gsd->gcd', left, right, precision=lax.Precision.HIGHEST)  73 us
    scatter-add x2, other arithmetic, local(): source = jnp.zeros((3, size_x * size_y * size_z), jnp.float32).at[:, offs...  55.8 us
    gather x2, local copies, waits for them, and re-layouts, local(): efield.reshape(3, -1)[:, offsets].reshape(3, slots, block)  30.7 us
    all_to_all x2, starting transfers between devices, local(): lax.all_to_all(outgoing.reshape(owners, capacity, 3, block), 'gx', split_...  24.1 us
    ppermute x6, starting transfers between devices, with_halo(): before = lax.ppermute(last, axis, up)  19.6 us
    all_to_all x2, starting transfers between devices, local(): lax.all_to_all(rate.reshape(owners, capacity, 3, block), 'gx', split_axis...  19.1 us
    concatenate x4, other arithmetic, with_halo(): value = jnp.concatenate([before, value, after], axis=dim)  16.7 us
  transfers between devices with their start and end apart: 18, of which 4 were waited for; matrix products, arithmetic and copies ran while one was open for 17% of the time, Pallas kernels for 0%

commit v1 on v0

v1 whole, which is shorter than its diff:
```python
import math

import jax
import jax.numpy as jnp
import numpy as np
from jax import lax
from jax.experimental import pallas as pl
from jax.experimental.pallas import tpu as pltpu
from jax.sharding import PartitionSpec as P

FREQ = 64
STEPS = 2
CX = 8
CY = 24
CZ = 128
ROWS = CX * CY
SLOTS = 32
DIRS = 128

time_step = 0.5
damping = 0.1
omega_rest = 1.0
coupling = 0.5
cross_rate = 0.3
upper_life = 2.0
lasing_life = 20.0
lower_life = 2.0
freq_low = 0.3
freq_pitch = 0.01
golden = 2.399963229728653

half = 0.5 * damping * time_step
keep_rate = (1.0 - half) / (1.0 + half)
spring = time_step * omega_rest * omega_rest / (1.0 + half)
gain_push = time_step * coupling / (1.0 + half)

F32 = jnp.float32
BF16 = jnp.bfloat16
MIB = 1 << 20


def shape(*dims, dtype=F32):
    return jax.ShapeDtypeStruct(dims, dtype)


def call(kernel, outs, args, in_specs=None, scratch=(), vmem=16, flops=0, moved=2 * MIB, name=None):
    return pl.pallas_call(
        kernel,
        out_shape=outs,
        in_specs=in_specs or [pl.BlockSpec(memory_space=pltpu.VMEM)] * len(args),
        scratch_shapes=scratch,
        compiler_params=pltpu.CompilerParams(vmem_limit_bytes=vmem * MIB),
        cost_estimate=pl.CostEstimate(flops=flops, bytes_accessed=moved, transcendentals=0),
        name=name,
    )(*args)


def split_parts(value):
    high = value.astype(BF16)
    low = (value - high.astype(F32)).astype(BF16)
    return high, low


def row_index(count, width):
    return lax.broadcasted_iota(jnp.int32, (count, width), 0)


def lane_index(count):
    return lax.broadcasted_iota(jnp.int32, (count, CZ), 1)


def ahead_x(field, face):
    return jnp.concatenate([field[CY:], face], axis=0)


def behind_x(field, face):
    return jnp.concatenate([face, field[:-CY]], axis=0)


def spread(face):
    return jnp.broadcast_to(face[:, None, :], (CX, CY, CZ)).reshape(ROWS, CZ)


def ahead_y(field, face, last):
    return jnp.where(last, spread(face), pltpu.roll(field, ROWS - 1, 0))


def behind_y(field, face, first):
    return jnp.where(first, spread(face), pltpu.roll(field, 1, 0))


def ahead_z(field, other, lane):
    return pltpu.roll(jnp.where(lane == 0, other, field), CZ - 1, 1)


def behind_z(field, other, lane):
    return pltpu.roll(jnp.where(lane == CZ - 1, other, field), 1, 1)


def row_in_brick():
    rows = row_index(ROWS, CZ)
    return rows - CY * ((rows * 2731) >> 16)


def first_layers(field_ref, out_x, out_y, out_z):
    out_x[0] = field_ref[1, 0:CY]
    out_x[1] = field_ref[2, 0:CY]
    for place, comp in ((0, 0), (1, 2)):
        for layer in range(CX):
            out_y[place, layer : layer + 1] = field_ref[comp, layer * CY : layer * CY + 1]
    if out_z is not None:
        out_z[0] = field_ref[0]
        out_z[1] = field_ref[1]


def last_layers(field_ref, out_x, out_y, out_z):
    out_x[0] = field_ref[1, ROWS - CY : ROWS]
    out_x[1] = field_ref[2, ROWS - CY : ROWS]
    for place, comp in ((0, 0), (1, 2)):
        for layer in range(CX):
            row = layer * CY + CY - 1
            out_y[place, layer : layer + 1] = field_ref[comp, row : row + 1]
    out_z[0] = field_ref[0]
    out_z[1] = field_ref[1]


def prepare_kernel(e_ref, state_ref, out_x, out_y, out_z, packed):
    first_layers(e_ref, out_x, out_y, out_z)
    lower = state_ref[:, 7]
    lasing = state_ref[:, 8]
    upper = state_ref[:, 9]
    for comp in range(3):
        polar = state_ref[:, comp]
        packed[:, comp] = keep_rate * state_ref[:, 3 + comp] - spring * polar
        packed[:, 3 + comp] = polar
    packed[:, 6] = lasing - lower
    lasing_free = lasing + time_step * (upper / upper_life - lasing / lasing_life)
    lower_free = lower + time_step * (lasing / lasing_life - lower / lower_life)
    packed[:, 7] = lasing_free - lower_free


def magnetic_kernel(e_ref, h_ref, face_x, face_y, face_z, h_out, out_x, out_y, out_z):
    lane = lane_index(ROWS)
    last = row_in_brick() == CY - 1
    ex, ey, ez = e_ref[0], e_ref[1], e_ref[2]
    first = (ahead_y(ez, face_y[1], last) - ez) - (ahead_z(ey, face_z[1], lane) - ey)
    second = (ahead_z(ex, face_z[0], lane) - ex) - (ahead_x(ez, face_x[1]) - ez)
    third = (ahead_x(ey, face_x[0]) - ey) - (ahead_y(ex, face_y[0], last) - ex)
    h_out[0] = h_ref[0] - time_step * first
    h_out[1] = h_ref[1] - time_step * second
    h_out[2] = h_ref[2] - time_step * third
    last_layers(h_out, out_x, out_y, out_z)


def electric_curl(h_ref, face_x, face_y, face_z):
    lane = lane_index(ROWS)
    start = row_in_brick() == 0
    hx, hy, hz = h_ref[0], h_ref[1], h_ref[2]
    first = (hz - behind_y(hz, face_y[1], start)) - (hy - behind_z(hy, face_z[1], lane))
    second = (hx - behind_z(hx, face_z[0], lane)) - (hz - behind_x(hz, face_x[1]))
    third = (hy - behind_x(hy, face_x[0])) - (hx - behind_y(hx, face_y[0], start))
    return first, second, third


def row_hits(offsets, width):
    return (row_index(ROWS, width) == (offsets >> 7)).astype(F32).astype(BF16)


def lane_hits(offsets, width):
    return row_index(CZ, width) == (offsets & (CZ - 1))


def scatter_kernel(count_ref, owner_ref, offsets_ref, fields_ref, dense, placed, total):
    count = count_ref[0]
    for slot in range(SLOTS):
        line = offsets_ref[slot : slot + 1]
        placed[pl.ds(owner_ref[slot], 1)] = jnp.where(slot < count, line, -1)
    total[...] = jnp.zeros_like(total)

    def pair(index, carry):
        lines = placed[pl.ds(2 * index, 2)]
        offsets = jnp.concatenate([lines[0:1], lines[1:2]], axis=1)
        rows = row_hits(offsets, 2 * CZ)
        lanes = lane_hits(offsets, 2 * CZ)
        values = jnp.concatenate([fields_ref[2 * index], fields_ref[2 * index + 1]], axis=1)
        for part in split_parts(values):
            part = part.astype(F32)
            spots = jnp.concatenate(
                [
                    jnp.where(lanes, part[field : field + 1], 0.0).astype(BF16)
                    for field in range(8)
                ],
                axis=0,
            )
            total[...] += lax.dot_general(
                rows, spots, (((1,), (1,)), ((), ())), preferred_element_type=F32
            )
        return carry

    lax.fori_loop(0, SLOTS // 2, pair, 0)
    for field in range(8):
        dense[field] = total[:, field * CZ : (field + 1) * CZ]


def electric_kernel(
    e_ref, h_ref, face_x, face_y, face_z, eps_ref, dense, e_out, out_x, out_y, out_z, source_out
):
    curls = electric_curl(h_ref, face_x, face_y, face_z)
    scaled = time_step * eps_ref[...]
    inversion = dense[6]
    power = jnp.zeros_like(inversion)
    rates = []
    for comp in range(3):
        field = e_ref[comp]
        rate = dense[comp] + gain_push * inversion * field
        power = power + field * rate
        rates.append(rate)
        e_out[comp] = field + scaled * (curls[comp] - rate)
    later = dense[7] + (2.0 * time_step * cross_rate) * power
    for comp in range(3):
        polar = dense[3 + comp] + time_step * rates[comp]
        free = keep_rate * rates[comp] - spring * polar
        source_out[comp] = free + gain_push * later * e_out[comp]
    first_layers(e_out, out_x, out_y, out_z)


def gather_lines(high, low, offsets, width, fields):
    rows = row_hits(offsets, width)
    lanes = lane_hits(offsets, width)
    picked = jnp.dot(high, rows, preferred_element_type=F32)
    picked = picked + jnp.dot(low, rows, preferred_element_type=F32)
    return [
        jnp.sum(jnp.where(lanes, picked[field * CZ : (field + 1) * CZ], 0.0), axis=0, keepdims=True)
        for field in range(fields)
    ]


def turned(fields):
    return split_parts(jnp.concatenate([jnp.transpose(field) for field in fields], axis=0))


def drive_kernel(e_old, e_new, h_new, placed, surf_ref, drives, sampled):
    high, low = turned([e_old[c] for c in range(3)] + [e_new[c] for c in range(3)])
    drives[...] = jnp.zeros_like(drives)

    def pair(index, carry):
        lines = placed[pl.ds(2 * index, 2)]
        offsets = jnp.concatenate([lines[0:1], lines[1:2]], axis=1)
        got = gather_lines(high, low, offsets, 2 * CZ, 6)
        for field in range(6):
            drives[2 * index, field : field + 1] = got[field][:, :CZ]
            drives[2 * index + 1, field : field + 1] = got[field][:, CZ:]
        return carry

    lax.fori_loop(0, SLOTS // 2, pair, 0)
    sample_rows(e_new, h_new, surf_ref, sampled)


def sample_rows(e_ref, h_ref, surf_ref, sampled):
    high, low = turned([e_ref[c] for c in range(3)] + [h_ref[c] for c in range(3)])
    got = gather_lines(high, low, surf_ref[...], CZ, 6)
    sampled[...] = jnp.zeros_like(sampled)
    for field in range(6):
        sampled[field : field + 1] = got[field]


def table_kernel(surf_ref, units_ref, table):
    cells = surf_ref[...]
    rows = cells >> 7
    layer = (rows * 2731) >> 16
    cell_x = lax.axis_index("gx") * CX + layer
    cell_y = lax.axis_index("gy") * CY + (rows - CY * layer)
    cell_z = lax.axis_index("gz") * CZ + (cells & (CZ - 1))
    along = jnp.zeros((CZ, DIRS), F32)
    for axis, (cell, size) in enumerate(((cell_x, 128), (cell_y, 192), (cell_z, 256))):
        place = cell.astype(F32) - 0.5 * (size - 1)
        column = jnp.transpose(jnp.broadcast_to(place, (CZ, CZ)))
        along = along + column * units_ref[axis : axis + 1]
    tall = 32
    for block in range(CZ // tall):
        part = along[block * tall : (block + 1) * tall]
        turn_re = jnp.cos(freq_pitch * part)
        turn_im = jnp.sin(freq_pitch * part)
        now_re = jnp.cos(freq_low * part)
        now_im = jnp.sin(freq_low * part)

        def step(freq, now, block=block, turn_re=turn_re, turn_im=turn_im):
            now_re, now_im = now
            for place, value in ((0, now_re), (1, now_im)):
                high, low = split_parts(value)
                across = pl.ds(place * DIRS, DIRS)
                table[freq, pl.ds(block * tall, tall), across] = high
                table[freq, pl.ds(CZ + block * tall, tall), across] = low
            return (
                now_re * turn_re - now_im * turn_im,
                now_im * turn_re + now_re * turn_im,
            )

        lax.fori_loop(0, FREQ, step, (now_re, now_im))


def final_kernel(
    e_ref,
    h_ref,
    face_x,
    face_y,
    face_z,
    eps_ref,
    source,
    surf_ref,
    early_ref,
    table,
    e_out,
    keep_out,
    send_out,
    late,
):
    curls = electric_curl(h_ref, face_x, face_y, face_z)
    scaled = time_step * eps_ref[...]
    for comp in range(3):
        e_out[comp] = e_ref[comp] + scaled * (curls[comp] - source[comp])
    sample_rows(e_out, h_ref, surf_ref, late)
    high, low = split_parts(jnp.concatenate([early_ref[...], late[...]], axis=0))
    left = jnp.concatenate(
        [
            jnp.concatenate([high, high], axis=1),
            jnp.concatenate([low, jnp.zeros_like(low)], axis=1),
        ],
        axis=0,
    )
    own = lax.axis_index("gz")
    scale = 1.0 / math.sqrt(STEPS * CZ * 256)
    for freq in range(FREQ // 2):
        for side, out in ((0, keep_out), (1, send_out)):
            target = lax.rem(own + side, 2)
            omega = freq_low + freq_pitch * (target * (FREQ // 2) + freq).astype(F32)
            both = jnp.dot(
                left, table[target * (FREQ // 2) + freq], preferred_element_type=F32
            )
            both = both[0:16] + both[16:32]
            real = jnp.zeros((8, DIRS), F32)
            imag = jnp.zeros((8, DIRS), F32)
            for step in range(STEPS):
                moment = jnp.full((8, DIRS), (step + 1) * time_step, F32) * omega
                cosine = jnp.cos(moment)
                sine = jnp.sin(moment)
                upper = both[8 * step : 8 * step + 8, 0:DIRS]
                under = both[8 * step : 8 * step + 8, DIRS:]
                real = real + cosine * upper + sine * under
                imag = imag + cosine * under - sine * upper
            out[freq, 0:8] = scale * real
            out[freq, 8:16] = scale * imag


def atoms_kernel(state_ref, pump_ref, drives, out):
    polar = [state_ref[:, c] for c in range(3)]
    rate = [state_ref[:, 3 + c] for c in range(3)]
    ground, lower, lasing, upper = [state_ref[:, 6 + level] for level in range(4)]
    pump = pump_ref[...]
    for step in range(STEPS):
        drive = [drives[:, 3 * step + c] for c in range(3)]
        inversion = lasing - lower
        power = jnp.zeros_like(pump)
        for c in range(3):
            rate[c] = (
                (1.0 - half) * rate[c]
                + time_step
                * (coupling * inversion * drive[c] - omega_rest * omega_rest * polar[c])
            ) / (1.0 + half)
            polar[c] = polar[c] + time_step * rate[c]
            power = power + drive[c] * rate[c]
        upper_new = upper + time_step * (pump * ground - upper / upper_life)
        lasing_new = lasing + time_step * (
            upper / upper_life - lasing / lasing_life + cross_rate * power
        )
        lower_new = lower + time_step * (
            lasing / lasing_life - lower / lower_life - cross_rate * power
        )
        ground = ground + time_step * (lower / lower_life - pump * ground)
        lower, lasing, upper = lower_new, lasing_new, upper_new
    for place, value in enumerate(polar + rate + [ground, lower, lasing, upper]):
        out[:, place] = value


def directions(count):
    index = np.arange(count, dtype=np.float32)
    cosine = np.float32(1.0) - np.float32(2.0) * (index + np.float32(0.5)) / np.float32(count)
    sine = np.sqrt(np.float32(1.0) - cosine * cosine)
    azimuth = (np.float32(golden) * index).astype(np.float64)
    rows = np.zeros((8, count), np.float32)
    rows[0] = sine * np.cos(azimuth).astype(np.float32)
    rows[1] = sine * np.sin(azimuth).astype(np.float32)
    rows[2] = cosine
    return rows


def all_reduce(value, axis, peers):
    one, two, three = [lax.ppermute(value, axis, peers(k)) for k in (1, 2, 3)]
    return (value + one) + (two + three)


def local(
    efield,
    hfield,
    inv_eps,
    gain_state,
    pump,
    gain_offsets,
    gain_count,
    block_owner,
    surf_offsets,
    far_acc,
):
    e_old = efield.reshape(3, ROWS, CZ)
    h_old = hfield.reshape(3, ROWS, CZ)
    eps = inv_eps.reshape(ROWS, CZ)
    state = gain_state.reshape(SLOTS, 10, CZ)
    surf = surf_offsets.reshape(1, CZ)
    faces = (shape(2, CY, CZ), shape(2, CX, CZ), shape(2, ROWS, CZ))
    dense = shape(3, ROWS, CZ)
    down = [[(i + 1, i) for i in range(n - 1)] for n in (16, 8, 2)]
    up = [[(i, i + 1) for i in range(n - 1)] for n in (16, 8, 2)]

    def shifted(parts, perms):
        return [
            lax.ppermute(part, axis, perm)
            for part, axis, perm in zip(parts, ("gx", "gy", "gz"), perms)
        ]

    def whole(count):
        return [pl.BlockSpec(memory_space=pltpu.VMEM)] * count

    scalars = [pl.BlockSpec(memory_space=pltpu.SMEM)]

    *near, packed = call(
        prepare_kernel, faces + (shape(SLOTS, 8, CZ),), (e_old, state), name="prepare"
    )
    near = shifted(near, down)
    fields = lax.all_to_all(packed, "gx", 0, 0, tiled=True)
    h_one, *edge = call(magnetic_kernel, (dense,) + faces, (e_old, h_old, *near), name="magnetic")
    edge = shifted(edge, up)
    spread_fields, placed = call(
        scatter_kernel,
        (shape(8, ROWS, CZ), shape(SLOTS, CZ, dtype=jnp.int32)),
        (
            gain_count.reshape(1),
            block_owner.reshape(SLOTS),
            gain_offsets.reshape(SLOTS, CZ),
            fields,
        ),
        in_specs=scalars * 2 + whole(2),
        scratch=[pltpu.VMEM((ROWS, 8 * CZ), F32)],
        flops=4 * 10**9,
        name="scatter",
    )
    e_one, *near_rest = call(
        electric_kernel,
        (dense,) + faces + (dense,),
        (e_old, h_one, *edge, eps, spread_fields),
        name="electric",
    )
    *near, source = near_rest
    near = shifted(near, down)
    drives, early = call(
        drive_kernel,
        (shape(SLOTS, 8, CZ), shape(8, CZ)),
        (e_old, e_one, h_one, placed, surf),
        flops=4 * 10**9,
        name="drive",
    )
    h_two, *edge = call(magnetic_kernel, (dense,) + faces, (e_one, h_one, *near), name="magnetic2")
    edge = shifted(edge, up)
    table = call(
        table_kernel,
        shape(FREQ, 2 * CZ, 2 * DIRS, dtype=BF16),
        (surf, jnp.asarray(directions(DIRS))),
        flops=4 * 10**9,
        vmem=24,
        moved=8 * MIB,
        name="table",
    )
    part = shape(FREQ // 2, 16, DIRS)
    e_two, keep, send = call(
        final_kernel,
        (dense, part, part),
        (e_one, h_two, *edge, eps, source, surf, early, table),
        scratch=[pltpu.VMEM((8, CZ), F32)],
        vmem=28,
        flops=4 * 10**9,
        moved=10 * MIB,
        name="final",
    )
    back = lax.all_to_all(drives, "gx", 0, 0, tiled=True)
    state_out = call(
        atoms_kernel, shape(SLOTS, 10, CZ), (state, pump.reshape(SLOTS, CZ), back), name="atoms"
    )
    chip = keep + lax.ppermute(send, "gz", [(0, 1), (1, 0)])
    pieces = lax.all_to_all(chip.reshape(8, 4, 16, DIRS), "gy", 0, 0, tiled=True)
    total = jnp.sum(pieces, axis=0)
    total = all_reduce(
        total, "gx", lambda k: [(a * 4 + z, (a ^ k) * 4 + z) for a in range(4) for z in range(4)]
    )
    total = all_reduce(
        total, "gx", lambda k: [(a * 4 + z, a * 4 + (z ^ k)) for a in range(4) for z in range(4)]
    )
    gathered = lax.all_to_all(
        jnp.broadcast_to(total[None], (8, 4, 16, DIRS)), "gy", 0, 0, tiled=True
    ).reshape(FREQ // 2, 16, DIRS)
    far_out = far_acc + jnp.concatenate([gathered[:, 0:6], gathered[:, 8:14]], axis=1)
    return (
        e_two.reshape(efield.shape),
        h_two.reshape(hfield.shape),
        state_out.reshape(gain_state.shape),
        far_out,
    )


def solution(mesh):
    placed = (
        P(None, "gx", "gy", "gz"),
        P(None, "gx", "gy", "gz"),
        P("gx", "gy", "gz"),
        P("gx", "gy", "gz", None, None, None),
        P("gx", "gy", "gz", None, None),
        P("gx", "gy", "gz", None, None),
        P("gx", "gy", "gz"),
        P("gx", "gy", "gz", None),
        P("gx", "gy", "gz", None),
        P("gz", None, None),
    )
    return jax.shard_map(
        local,
        mesh=mesh,
        in_specs=placed,
        out_specs=(
            P(None, "gx", "gy", "gz"),
            P(None, "gx", "gy", "gz"),
            P("gx", "gy", "gz", None, None, None),
            P("gz", None, None),
        ),
        check_vma=False,
    )
```

time: 634 us -> 140 us (0.22); the launches traced: 626 us -> 139 us
  waiting for transfers between devices: 236 us -> 24.7 us
  local copies, waits for them, and re-layouts: 139 us -> 7.59 us
  other arithmetic: 88.5 us -> 0.22 us
  matrix products: 73 us -> 0 us
  Pallas kernels: 0 us -> 24.8 us
  between operations: 16 us -> 1.66 us
  blocking collectives: 0 us -> 11.6 us
    psum x1 -> x0, waiting for transfers between devices: 219 us -> none  [local(): summed = lax.psum(partial_value, ('gx', 'gy'))]
    dot_general x32 -> x0, matrix products: 73 us -> none  [mixing(): jnp.einsum('gcs,gsd->gcd', left, right, precision=lax.Precision.HIGHEST)]
    scatter-add x2 -> x0, other arithmetic: 55.8 us -> none  [local(): source = jnp.zeros((3, size_x * size_y * size_z), jnp.float32).at[:, offs...]
    gather x8 -> x0, local copies, waits for them, and re-layouts: 43.6 us -> none  [the longest x2 30.7 us: local(): efield.reshape(3, -1)[:, offsets].reshape(3, slots, block)]
    concatenate x7 -> x0, local copies, waits for them, and re-layouts: 27.3 us -> none  [the longest x4 12.7 us: with_halo(): value = jnp.concatenate([before, value, after], axis=dim)]
    pallas_call x0 -> x9, Pallas kernels: none -> 24.8 us  [call(): pl.pallas_call(kernel, out_shape=outs, in_specs=in_specs or [pl.BlockSpec...]
    all_to_all x4 -> x3, starting transfers between devices: 43.2 us -> 22.7 us  [the longest x1 11 us: local(): fields = lax.all_to_all(packed, 'gx', 0, 0, tiled=True)]
    reshape x10 -> x0, local copies, waits for them, and re-layouts: 20.4 us -> none  [the longest x2 15.3 us: local(): source = source.reshape(3, size_x, size_y, size_z)]
  transfers between devices with their start and end apart: 18 -> 22, of which waited for: 4 -> 7; matrix products, arithmetic and copies ran while one was open for 17% -> 1% of each run, Pallas kernels for 0% -> 14%
where the time goes in v1:
time: 140 us; the launch traced here: 139 us
  starting transfers between devices  68.7 us (49%)
  Pallas kernels  24.8 us (18%)
  waiting for transfers between devices  24.7 us (18%)
  blocking collectives  11.6 us (8%)
  local copies, waits for them, and re-layouts  7.59 us (5%)
  between operations  1.66 us (1%)
    ppermute x12, starting transfers between devices, shifted(): lax.ppermute(part, axis, perm)  33 us
    pallas_call x9, Pallas kernels, call(): pl.pallas_call(kernel, out_shape=outs, in_specs=in_specs or [pl.BlockSpec...  24.8 us
    ppermute x6, starting transfers between devices, all_reduce(): one, two, three = [lax.ppermute(value, axis, peers(k)) for k in (1, 2, 3)]  13 us
    all_to_all x1, blocking collectives, local(): lax.all_to_all(chip.reshape(8, 4, 16, DIRS), 'gy', 0, 0, tiled=True)  11.6 us
    all_to_all x1, starting transfers between devices, local(): fields = lax.all_to_all(packed, 'gx', 0, 0, tiled=True)  11 us
    all_to_all x1, waiting for transfers between devices, local(): back = lax.all_to_all(drives, 'gx', 0, 0, tiled=True)  10.7 us
    unnamed x27, local copies, waits for them, and re-layouts  6.81 us
    all_to_all x1, starting transfers between devices, local(): back = lax.all_to_all(drives, 'gx', 0, 0, tiled=True)  6.68 us
  transfers between devices with their start and end apart: 22, of which 7 were waited for; matrix products, arithmetic and copies ran while one was open for 1% of the time, Pallas kernels for 14%

profile of v1, /device:TPU:8, one launch (start us, length us, event | category | flops | bytes accessed | tf_op | source)
XLA Modules:
  0.0 139.2 jit_solution(14073797710683937749)
XLA Ops:
  0.7 1.1 copy.28
  3.5 11.0 %all-to-all-start = ((f32[32,8,128]{2,1,0:T(8,128)}), f32[32,8,128]{2,1,0:T(8,128)S(1)}, u32[]{:S(2)}, u32[]{:S(2)}) async-start(f32[32,8,128]{2,1,0:T(8,128)} %get-tuple-element.35), calls=%async_computation | async-start | bytes 262144 | tf_op jit(solution)/shard_map/all_to_all | solution.py:439
  14.6 1.3 collective-permute-start.2
  15.9 1.3 collective-permute-start
  17.2 2.4 %collective-permute-start.1 = (f32[2,8,128]{2,1,0:T(8,128)S(1)}, f32[2,8,128]{2,1,0:T(8,128)S(1)}, u32[]{:S(2)}, u32[]{:S(2)}) collective-permute-start(f32[2,8,128]{2,1,0:T(8,128)S(1)} %get-tuple-element.29), channel_id=1, source_target_pairs={{2,0},{4,2},{6,4},{8,6},{10,8},{12,10},{14,12},{3,1},{5,3},{7,5},{... | collective-permute-start | bytes 24584 | tf_op jit(solution)/shard_map/ppermute | solution.py:426
  20.2 2.5 %collective-permute-done.1.face_y = f32[2,8,128]{2,1,0:T(8,128)S(1)} collective-permute-done((f32[2,8,128]{2,1,0:T(8,128)S(1)}, f32[2,8,128]{2,1,0:T(8,128)S(1)}, u32[]{:S(2)}, u32[]{:S(2)}) %collective-permute-start.1) | collective-permute-done | bytes 8224 | tf_op jit(solution)/shard_map/ppermute | solution.py:426
  22.7 1.0 copy-done.1
  24.8 3.5 %collective-permute-start.4 = (f32[2,8,128]{2,1,0:T(8,128)S(1)}, f32[2,8,128]{2,1,0:T(8,128)S(1)}, u32[]{:S(2)}, u32[]{:S(2)}) collective-permute-start(f32[2,8,128]{2,1,0:T(8,128)S(1)} %get-tuple-element.33), channel_id=1, source_target_pairs={{0,2},{2,4},{4,6},{6,8},{8,10},{10,12},{12,14},{1,3},{3,5},{5,7},{... | collective-permute-start | bytes 24584 | tf_op jit(solution)/shard_map/ppermute | solution.py:426
  28.3 5.8 %collective-permute-start.3 = (f32[2,24,128]{2,1,0:T(8,128)S(1)}, f32[2,24,128]{2,1,0:T(8,128)S(1)}, u32[]{:S(2)}, u32[]{:S(2)}) collective-permute-start(f32[2,24,128]{2,1,0:T(8,128)S(1)} %get-tuple-element.32), channel_id=1, source_target_pairs={{0,16},{16,32},{32,48},{48,64},{64,80},{80,96},{96,112},{112,128},... | collective-permute-start | bytes 73736 | tf_op jit(solution)/shard_map/ppermute | solution.py:426
  34.1 1.5 %collective-permute-start.5 = (f32[2,192,128]{2,1,0:T(8,128)S(1)}, f32[2,192,128]{2,1,0:T(8,128)S(1)}, u32[]{:S(2)}, u32[]{:S(2)}) collective-permute-start(f32[2,192,128]{2,1,0:T(8,128)S(1)} %get-tuple-element.34), channel_id=1, source_target_pairs={{0,1},{2,3},{4,5},{6,7},{8,9},{10,11},{12,13},{14,15},{16,17},{18,... | collective-permute-start | bytes 589832 | tf_op jit(solution)/shard_map/ppermute | solution.py:426
  37.0 8.7 %scatter.1 = (f32[8,192,128]{2,1,0:T(8,128)S(1)}, s32[32,128]{1,0:T(8,128)S(1)}) custom-call(s32[1]{0:T(128)} %bitcast.16.count_ref, s32[32]{0:T(128)S(1)} %bitcast.30, s32[32,128]{1,0:T(8,128)S(1)} %bitcast.29, f32[32,8,128]{2,1,0:T(8,128)S(1)} %all-to-all-done.fields_ref), custom_call_target="tpu_custom_call" | custom-call | flops 4000000000 | bytes 2097152 | tf_op jit(solution)/shard_map/scatter/pallas_call | solution.py:47
  46.0 2.3 %collective-permute-start.7 = (f32[2,8,128]{2,1,0:T(8,128)S(1)}, f32[2,8,128]{2,1,0:T(8,128)S(1)}, u32[]{:S(2)}, u32[]{:S(2)}) collective-permute-start(f32[2,8,128]{2,1,0:T(8,128)S(1)} %get-tuple-element.39), channel_id=1, source_target_pairs={{2,0},{4,2},{6,4},{8,6},{10,8},{12,10},{14,12},{3,1},{5,3},{7,5},{... | collective-permute-start | bytes 24584 | tf_op jit(solution)/shard_map/ppermute | solution.py:426
  48.4 1.3 collective-permute-start.6
  49.7 1.3 collective-permute-start.8
  51.0 3.4 %table.1 = bf16[64,256,256]{2,1,0:T(8,128)(2,1)S(1)} custom-call(s32[1,128]{1,0:T(1,128)S(1)} %bitcast.31, f32[8,128]{1,0:T(8,128)S(1)} %copy-done.10), custom_call_target="tpu_custom_call" | custom-call | flops 4000000000 | bytes 8388608 | tf_op jit(solution)/shard_map/table/pallas_call | solution.py:47
  54.4 1.2 collective-permute-done.6.face_x
  56.4 5.0 %collective-permute-start.10 = (f32[2,8,128]{2,1,0:T(8,128)S(1)}, f32[2,8,128]{2,1,0:T(8,128)S(1)}, u32[]{:S(2)}, u32[]{:S(2)}) collective-permute-start(f32[2,8,128]{2,1,0:T(8,128)S(1)} %get-tuple-element.43), channel_id=1, source_target_pairs={{0,2},{2,4},{4,6},{6,8},{8,10},{10,12},{12,14},{1,3},{3,5},{5,7},{... | collective-permute-start | bytes 24584 | tf_op jit(solution)/shard_map/ppermute | solution.py:426
  61.4 6.0 %collective-permute-start.9 = (f32[2,24,128]{2,1,0:T(8,128)S(1)}, f32[2,24,128]{2,1,0:T(8,128)S(1)}, u32[]{:S(2)}, u32[]{:S(2)}) collective-permute-start(f32[2,24,128]{2,1,0:T(8,128)S(1)} %get-tuple-element.42), channel_id=1, source_target_pairs={{0,16},{16,32},{32,48},{48,64},{64,80},{80,96},{96,112},{112,128},... | collective-permute-start | bytes 73736 | tf_op jit(solution)/shard_map/ppermute | solution.py:426
  67.5 1.4 collective-permute-start.11
  68.8 6.9 %drive.1 = (f32[32,8,128]{2,1,0:T(8,128)}, f32[8,128]{1,0:T(8,128)S(1)}) custom-call(f32[3,192,128]{2,1,0:T(8,128)S(1)} %bitcast.20, f32[3,192,128]{2,1,0:T(8,128)S(1)} %get-tuple-element.37.e_ref.e_new, f32[3,192,128]{2,1,0:T(8,128)S(1)} %get-tuple-element.31.h_ref.h_new, s32[32,128]{1,0:T(8,128)S(1)} %get-tuple-element.46.placed, s32[1,128]{1,0:T(1,128)S(1)} %bitcast.32), custom_call_target="tpu_custom_call" | custom-call | flops 4000000000 | bytes 2097152 | tf_op jit(solution)/shard_map/drive/pallas_call | solution.py:47
  75.8 3.2 %final.1 = (f32[3,192,128]{2,1,0:T(8,128)}, f32[32,16,128]{2,1,0:T(8,128)S(1)}, f32[32,16,128]{2,1,0:T(8,128)S(1)}) custom-call(f32[3,192,128]{2,1,0:T(8,128)S(1)} %get-tuple-element.37.e_ref.e_new, f32[3,192,128]{2,1,0:T(8,128)S(1)} %copy-done.6, f32[2,24,128]{2,1,0:T(8,128)S(1)} %collective-permute-done.9.face_x, ...), custom_call_target="tpu_custom_call" | custom-call | flops 4000000000 | bytes 10485760 | tf_op jit(solution)/shard_map/final/pallas_call | solution.py:47
  79.0 1.5 %collective-permute-done.12 = f32[32,16,128]{2,1,0:T(8,128)S(1)} collective-permute-done((f32[32,16,128]{2,1,0:T(8,128)S(1)}, f32[32,16,128]{2,1,0:T(8,128)S(1)}, u32[]{:S(2)}, u32[]{:S(2)}) %collective-permute-start.12) | collective-permute-done | bytes 262176 | tf_op jit(solution)/shard_map/ppermute | solution.py:497
  80.6 11.6 %all_to_all.20 = f32[8,4,16,128]{3,2,1,0:T(8,128)S(1)} all-to-all(f32[8,4,16,128]{3,2,1,0:T(8,128)S(1)} %bitcast.34), channel_id=1, replica_groups=mesh['gx'=16,'gy'=8,'gz'=2] {'gy'}, dimensions={0} | all-to-all | bytes 524288 | tf_op jit(solution)/shard_map/all_to_all | solution.py:498
  92.1 5.4 %collective-permute-start.15 = (f32[4,16,128]{2,1,0:T(8,128)S(1)}, f32[4,16,128]{2,1,0:T(8,128)S(1)}, u32[]{:S(2)}, u32[]{:S(2)}) collective-permute-start(f32[4,16,128]{2,1,0:T(8,128)S(1)} %reduce_sum.9), channel_id=1, source_target_pairs={{0,192},{16,208},{32,224},{48,240},{64,128},{80,144},{96,160},{112... | collective-permute-start | bytes 98312 | tf_op jit(solution)/shard_map/ppermute | solution.py:398
  99.5 3.5 %collective-permute-done.14 = f32[4,16,128]{2,1,0:T(8,128)S(1)} collective-permute-done((f32[4,16,128]{2,1,0:T(8,128)S(1)}, f32[4,16,128]{2,1,0:T(8,128)S(1)}, u32[]{:S(2)}, u32[]{:S(2)}) %collective-permute-start.14) | collective-permute-done | bytes 32800 | tf_op jit(solution)/shard_map/ppermute | solution.py:398
  103.0 3.9 %collective-permute-start.18 = (f32[4,16,128]{2,1,0:T(8,128)S(1)}, f32[4,16,128]{2,1,0:T(8,128)S(1)}, u32[]{:S(2)}, u32[]{:S(2)}) collective-permute-start(f32[4,16,128]{2,1,0:T(8,128)S(1)} %add_add_fusion.1), channel_id=1, source_target_pairs={{0,48},{16,32},{32,16},{48,0},{64,112},{80,96},{96,80},{112,64},{1... | collective-permute-start | bytes 98312 | tf_op jit(solution)/shard_map/ppermute | solution.py:398
  106.9 1.2 collective-permute-start.17
  108.1 1.5 %collective-permute-start.16 = (f32[4,16,128]{2,1,0:T(8,128)S(1)}, f32[4,16,128]{2,1,0:T(8,128)S(1)}, u32[]{:S(2)}, u32[]{:S(2)}) collective-permute-start(f32[4,16,128]{2,1,0:T(8,128)S(1)} %add_add_fusion.1), channel_id=1, source_target_pairs={{0,16},{16,0},{32,48},{48,32},{64,80},{80,64},{96,112},{112,96},{1... | collective-permute-start | bytes 98312 | tf_op jit(solution)/shard_map/ppermute | solution.py:398
  109.6 6.7 %all-to-all-start.1 = ((f32[32,8,128]{2,1,0:T(8,128)}), f32[32,8,128]{2,1,0:T(8,128)S(1)}, u32[]{:S(2)}, u32[]{:S(2)}) async-start(f32[32,8,128]{2,1,0:T(8,128)} %get-tuple-element.49), calls=%async_computation.1 | async-start | bytes 262144 | tf_op jit(solution)/shard_map/all_to_all | solution.py:493
  116.4 10.7 %all-to-all-done.1.drives = f32[32,8,128]{2,1,0:T(8,128)S(1)} async-done(((f32[32,8,128]{2,1,0:T(8,128)}), f32[32,8,128]{2,1,0:T(8,128)S(1)}, u32[]{:S(2)}, u32[]{:S(2)}) %all-to-all-start.1) | async-done | bytes 131104 | tf_op jit(solution)/shard_map/all_to_all | solution.py:493
  127.8 5.0 %all-to-all-start.3 = ((f32[8,4,16,128]{3,1,2,0:T(4,128)}), f32[8,4,16,128]{3,1,2,0:T(4,128)S(1)}, u32[]{:S(2)}, u32[]{:S(2)}) async-start(f32[8,4,16,128]{3,1,2,0:T(4,128)} %broadcast_in_dim.2), calls=%async_computation.3 | async-start | bytes 524288 | tf_op jit(solution)/shard_map/all_to_all | solution.py:506
  134.0 4.2 %all-to-all-done.3 = f32[8,4,16,128]{3,1,2,0:T(4,128)S(1)} async-done(((f32[8,4,16,128]{3,1,2,0:T(4,128)}), f32[8,4,16,128]{3,1,2,0:T(4,128)S(1)}, u32[]{:S(2)}, u32[]{:S(2)}) %all-to-all-start.3) | async-done | bytes 262176 | tf_op jit(solution)/shard_map/all_to_all | solution.py:506
  (58 shorter events, 10.4 us)
Async XLA Ops:
  0.6 45.0 %copy-start.2 = (f32[3,8,24,128]{3,2,1,0:T(8,128)S(1)}, f32[3,8,24,128]{3,2,1,0:T(8,128)}, u32[]{:S(2)}) copy-start(f32[3,8,24,128]{3,2,1,0:T(8,128)} %param.11) | copy-start | bytes 884740
  0.6 45.0 %copy-start.4 = (f32[8,24,128]{2,1,0:T(8,128)S(1)}, f32[8,24,128]{2,1,0:T(8,128)}, u32[]{:S(2)}) copy-start(f32[8,24,128]{2,1,0:T(8,128)} %param.13) | copy-start | bytes 294916
  1.7 1.0 copy-start
  3.5 32.1 %all-to-all-start = ((f32[32,8,128]{2,1,0:T(8,128)}), f32[32,8,128]{2,1,0:T(8,128)S(1)}, u32[]{:S(2)}, u32[]{:S(2)}) async-start(f32[32,8,128]{2,1,0:T(8,128)} %get-tuple-element.35), calls=%async_computation | async-start | bytes 262144 | tf_op jit(solution)/shard_map/all_to_all | solution.py:439
  14.6 8.2 %collective-permute-start.2 = (f32[2,192,128]{2,1,0:T(8,128)S(1)}, f32[2,192,128]{2,1,0:T(8,128)S(1)}, u32[]{:S(2)}, u32[]{:S(2)}) collective-permute-start(f32[2,192,128]{2,1,0:T(8,128)S(1)} %get-tuple-element.30), channel_id=1, source_target_pairs={{1,0},{3,2},{5,4},{7,6},{9,8},{11,10},{13,12},{15,14},{17,16},{19,... | collective-permute-start | bytes 589832 | tf_op jit(solution)/shard_map/ppermute | solution.py:426
  15.9 6.8 %collective-permute-start = (f32[2,24,128]{2,1,0:T(8,128)S(1)}, f32[2,24,128]{2,1,0:T(8,128)S(1)}, u32[]{:S(2)}, u32[]{:S(2)}) collective-permute-start(f32[2,24,128]{2,1,0:T(8,128)S(1)} %get-tuple-element.28), channel_id=1, source_target_pairs={{16,0},{32,16},{48,32},{64,48},{80,64},{96,80},{112,96},{128,112},... | collective-permute-start | bytes 73736 | tf_op jit(solution)/shard_map/ppermute | solution.py:426
  17.2 5.5 %collective-permute-start.1 = (f32[2,8,128]{2,1,0:T(8,128)S(1)}, f32[2,8,128]{2,1,0:T(8,128)S(1)}, u32[]{:S(2)}, u32[]{:S(2)}) collective-permute-start(f32[2,8,128]{2,1,0:T(8,128)S(1)} %get-tuple-element.29), channel_id=1, source_target_pairs={{2,0},{4,2},{6,4},{8,6},{10,8},{12,10},{14,12},{3,1},{5,3},{7,5},{... | collective-permute-start | bytes 24584 | tf_op jit(solution)/shard_map/ppermute | solution.py:426
  22.7 1.0 copy-start.1
  23.7 1.0 copy-start.3
  24.8 26.2 %copy-start.9 = (s32[1,1,1,128]{3,2,1,0:T(1,128)S(1)}, s32[1,1,1,128]{3,2,1,0:T(1,128)}, u32[]{:S(2)}) copy-start(s32[1,1,1,128]{3,2,1,0:T(1,128)} %param.19) | copy-start | bytes 1540
  24.8 26.2 %copy-start.10 = (f32[8,128]{1,0:T(8,128)S(1)}, f32[8,128]{1,0:T(8,128)}, u32[]{:S(2)}) copy-start(f32[8,128]{1,0:T(8,128)} %constant.4.clone.units_ref) | copy-start | bytes 12292
  24.8 20.8 %collective-permute-start.4 = (f32[2,8,128]{2,1,0:T(8,128)S(1)}, f32[2,8,128]{2,1,0:T(8,128)S(1)}, u32[]{:S(2)}, u32[]{:S(2)}) collective-permute-start(f32[2,8,128]{2,1,0:T(8,128)S(1)} %get-tuple-element.33), channel_id=1, source_target_pairs={{0,2},{2,4},{4,6},{6,8},{8,10},{10,12},{12,14},{1,3},{3,5},{5,7},{... | collective-permute-start | bytes 24584 | tf_op jit(solution)/shard_map/ppermute | solution.py:426
  28.3 17.4 %collective-permute-start.3 = (f32[2,24,128]{2,1,0:T(8,128)S(1)}, f32[2,24,128]{2,1,0:T(8,128)S(1)}, u32[]{:S(2)}, u32[]{:S(2)}) collective-permute-start(f32[2,24,128]{2,1,0:T(8,128)S(1)} %get-tuple-element.32), channel_id=1, source_target_pairs={{0,16},{16,32},{32,48},{48,64},{64,80},{80,96},{96,112},{112,128},... | collective-permute-start | bytes 73736 | tf_op jit(solution)/shard_map/ppermute | solution.py:426
  34.1 11.6 %collective-permute-start.5 = (f32[2,192,128]{2,1,0:T(8,128)S(1)}, f32[2,192,128]{2,1,0:T(8,128)S(1)}, u32[]{:S(2)}, u32[]{:S(2)}) collective-permute-start(f32[2,192,128]{2,1,0:T(8,128)S(1)} %get-tuple-element.34), channel_id=1, source_target_pairs={{0,1},{2,3},{4,5},{6,7},{8,9},{10,11},{12,13},{14,15},{16,17},{18,... | collective-permute-start | bytes 589832 | tf_op jit(solution)/shard_map/ppermute | solution.py:426
  46.0 8.4 %collective-permute-start.7 = (f32[2,8,128]{2,1,0:T(8,128)S(1)}, f32[2,8,128]{2,1,0:T(8,128)S(1)}, u32[]{:S(2)}, u32[]{:S(2)}) collective-permute-start(f32[2,8,128]{2,1,0:T(8,128)S(1)} %get-tuple-element.39), channel_id=1, source_target_pairs={{2,0},{4,2},{6,4},{8,6},{10,8},{12,10},{14,12},{3,1},{5,3},{7,5},{... | collective-permute-start | bytes 24584 | tf_op jit(solution)/shard_map/ppermute | solution.py:426
  48.4 7.2 %collective-permute-start.6 = (f32[2,24,128]{2,1,0:T(8,128)S(1)}, f32[2,24,128]{2,1,0:T(8,128)S(1)}, u32[]{:S(2)}, u32[]{:S(2)}) collective-permute-start(f32[2,24,128]{2,1,0:T(8,128)S(1)} %get-tuple-element.38), channel_id=1, source_target_pairs={{16,0},{32,16},{48,32},{64,48},{80,64},{96,80},{112,96},{128,112},... | collective-permute-start | bytes 73736 | tf_op jit(solution)/shard_map/ppermute | solution.py:426
  49.7 5.9 %collective-permute-start.8 = (f32[2,192,128]{2,1,0:T(8,128)S(1)}, f32[2,192,128]{2,1,0:T(8,128)S(1)}, u32[]{:S(2)}, u32[]{:S(2)}) collective-permute-start(f32[2,192,128]{2,1,0:T(8,128)S(1)} %get-tuple-element.40), channel_id=1, source_target_pairs={{1,0},{3,2},{5,4},{7,6},{9,8},{11,10},{13,12},{15,14},{17,16},{19,... | collective-permute-start | bytes 589832 | tf_op jit(solution)/shard_map/ppermute | solution.py:426
  56.4 19.3 %copy-start.6 = (f32[3,192,128]{2,1,0:T(8,128)S(1)}, f32[3,192,128]{2,1,0:T(8,128)}, u32[]{:S(2)}) copy-start(f32[3,192,128]{2,1,0:T(8,128)} %get-tuple-element.41.h_ref) | copy-start | bytes 884740
  56.4 19.3 %collective-permute-start.10 = (f32[2,8,128]{2,1,0:T(8,128)S(1)}, f32[2,8,128]{2,1,0:T(8,128)S(1)}, u32[]{:S(2)}, u32[]{:S(2)}) collective-permute-start(f32[2,8,128]{2,1,0:T(8,128)S(1)} %get-tuple-element.43), channel_id=1, source_target_pairs={{0,2},{2,4},{4,6},{6,8},{8,10},{10,12},{12,14},{1,3},{3,5},{5,7},{... | collective-permute-start | bytes 24584 | tf_op jit(solution)/shard_map/ppermute | solution.py:426
  61.4 14.3 %collective-permute-start.9 = (f32[2,24,128]{2,1,0:T(8,128)S(1)}, f32[2,24,128]{2,1,0:T(8,128)S(1)}, u32[]{:S(2)}, u32[]{:S(2)}) collective-permute-start(f32[2,24,128]{2,1,0:T(8,128)S(1)} %get-tuple-element.42), channel_id=1, source_target_pairs={{0,16},{16,32},{32,48},{48,64},{64,80},{80,96},{96,112},{112,128},... | collective-permute-start | bytes 73736 | tf_op jit(solution)/shard_map/ppermute | solution.py:426
  67.5 8.2 %collective-permute-start.11 = (f32[2,192,128]{2,1,0:T(8,128)S(1)}, f32[2,192,128]{2,1,0:T(8,128)S(1)}, u32[]{:S(2)}, u32[]{:S(2)}) collective-permute-start(f32[2,192,128]{2,1,0:T(8,128)S(1)} %get-tuple-element.44), channel_id=1, source_target_pairs={{0,1},{2,3},{4,5},{6,7},{8,9},{10,11},{12,13},{14,15},{16,17},{18,... | collective-permute-start | bytes 589832 | tf_op jit(solution)/shard_map/ppermute | solution.py:426
  75.7 57.1 %copy-start.5 = (f32[1,1,1,32,128]{4,3,2,1,0:T(8,128)S(1)}, f32[1,1,1,32,128]{4,3,2,1,0:T(8,128)}, u32[]{:S(2)}) copy-start(f32[1,1,1,32,128]{4,3,2,1,0:T(8,128)} %param.15) | copy-start | bytes 49156
  75.8 62.6 %copy-start.11 = (f32[32,12,128]{2,0,1:T(8,128)S(1)}, f32[32,12,128]{2,0,1:T(8,128)}, u32[]{:S(2)}) copy-start(f32[32,12,128]{2,0,1:T(8,128)} %param.20) | copy-start | bytes 589828
  79.0 1.5 %collective-permute-start.12 = (f32[32,16,128]{2,1,0:T(8,128)S(1)}, f32[32,16,128]{2,1,0:T(8,128)S(1)}, u32[]{:S(2)}, u32[]{:S(2)}) collective-permute-start(f32[32,16,128]{2,1,0:T(8,128)S(1)} %get-tuple-element.51), channel_id=1, source_target_pairs={{0,1},{1,0},{2,3},{3,2},{4,5},{5,4},{6,7},{7,6},{8,9},{9,8},{10,11... | collective-permute-start | bytes 786440 | tf_op jit(solution)/shard_map/ppermute | solution.py:497
  92.1 7.3 %collective-permute-start.15 = (f32[4,16,128]{2,1,0:T(8,128)S(1)}, f32[4,16,128]{2,1,0:T(8,128)S(1)}, u32[]{:S(2)}, u32[]{:S(2)}) collective-permute-start(f32[4,16,128]{2,1,0:T(8,128)S(1)} %reduce_sum.9), channel_id=1, source_target_pairs={{0,192},{16,208},{32,224},{48,240},{64,128},{80,144},{96,160},{112... | collective-permute-start | bytes 98312 | tf_op jit(solution)/shard_map/ppermute | solution.py:398
  97.6 5.4 %collective-permute-start.14 = (f32[4,16,128]{2,1,0:T(8,128)S(1)}, f32[4,16,128]{2,1,0:T(8,128)S(1)}, u32[]{:S(2)}, u32[]{:S(2)}) collective-permute-start(f32[4,16,128]{2,1,0:T(8,128)S(1)} %reduce_sum.9), channel_id=1, source_target_pairs={{0,128},{16,144},{32,160},{48,176},{64,192},{80,208},{96,224},{112... | collective-permute-start | bytes 98312 | tf_op jit(solution)/shard_map/ppermute | solution.py:398
  98.1 4.9 %collective-permute-start.13 = (f32[4,16,128]{2,1,0:T(8,128)S(1)}, f32[4,16,128]{2,1,0:T(8,128)S(1)}, u32[]{:S(2)}, u32[]{:S(2)}) collective-permute-start(f32[4,16,128]{2,1,0:T(8,128)S(1)} %reduce_sum.9), channel_id=1, source_target_pairs={{0,64},{16,80},{32,96},{48,112},{64,0},{80,16},{96,32},{112,48},{1... | collective-permute-start | bytes 98312 | tf_op jit(solution)/shard_map/ppermute | solution.py:398
  103.0 13.3 %collective-permute-start.18 = (f32[4,16,128]{2,1,0:T(8,128)S(1)}, f32[4,16,128]{2,1,0:T(8,128)S(1)}, u32[]{:S(2)}, u32[]{:S(2)}) collective-permute-start(f32[4,16,128]{2,1,0:T(8,128)S(1)} %add_add_fusion.1), channel_id=1, source_target_pairs={{0,48},{16,32},{32,16},{48,0},{64,112},{80,96},{96,80},{112,64},{1... | collective-permute-start | bytes 98312 | tf_op jit(solution)/shard_map/ppermute | solution.py:398
  106.9 9.4 %collective-permute-start.17 = (f32[4,16,128]{2,1,0:T(8,128)S(1)}, f32[4,16,128]{2,1,0:T(8,128)S(1)}, u32[]{:S(2)}, u32[]{:S(2)}) collective-permute-start(f32[4,16,128]{2,1,0:T(8,128)S(1)} %add_add_fusion.1), channel_id=1, source_target_pairs={{0,32},{16,48},{32,0},{48,16},{64,96},{80,112},{96,64},{112,80},{1... | collective-permute-start | bytes 98312 | tf_op jit(solution)/shard_map/ppermute | solution.py:398
  108.1 8.2 %collective-permute-start.16 = (f32[4,16,128]{2,1,0:T(8,128)S(1)}, f32[4,16,128]{2,1,0:T(8,128)S(1)}, u32[]{:S(2)}, u32[]{:S(2)}) collective-permute-start(f32[4,16,128]{2,1,0:T(8,128)S(1)} %add_add_fusion.1), channel_id=1, source_target_pairs={{0,16},{16,0},{32,48},{48,32},{64,80},{80,64},{96,112},{112,96},{1... | collective-permute-start | bytes 98312 | tf_op jit(solution)/shard_map/ppermute | solution.py:398
  109.6 17.5 %all-to-all-start.1 = ((f32[32,8,128]{2,1,0:T(8,128)}), f32[32,8,128]{2,1,0:T(8,128)S(1)}, u32[]{:S(2)}, u32[]{:S(2)}) async-start(f32[32,8,128]{2,1,0:T(8,128)} %get-tuple-element.49), calls=%async_computation.1 | async-start | bytes 262144 | tf_op jit(solution)/shard_map/all_to_all | solution.py:493
  127.8 10.4 %all-to-all-start.3 = ((f32[8,4,16,128]{3,1,2,0:T(4,128)}), f32[8,4,16,128]{3,1,2,0:T(4,128)S(1)}, u32[]{:S(2)}, u32[]{:S(2)}) async-start(f32[8,4,16,128]{3,1,2,0:T(4,128)} %broadcast_in_dim.2), calls=%async_computation.3 | async-start | bytes 524288 | tf_op jit(solution)/shard_map/all_to_all | solution.py:506
  (2 other events, 1.4 us)

commit v2 on v1

--- a/solution.py
+++ b/solution.py
@@ -55,6 +55,10 @@
     )(*args)
 
 
+def stay(*values):
+    return [pltpu.with_memory_space_constraint(value, pltpu.HBM) for value in values]
+
+
 def split_parts(value):
     high = value.astype(BF16)
     low = (value - high.astype(F32)).astype(BF16)
@@ -108,9 +112,8 @@
     for place, comp in ((0, 0), (1, 2)):
         for layer in range(CX):
             out_y[place, layer : layer + 1] = field_ref[comp, layer * CY : layer * CY + 1]
-    if out_z is not None:
-        out_z[0] = field_ref[0]
-        out_z[1] = field_ref[1]
+    out_z[0] = field_ref[0]
+    out_z[1] = field_ref[1]
 
 
 def last_layers(field_ref, out_x, out_y, out_z):
@@ -124,24 +127,46 @@
     out_z[1] = field_ref[1]
 
 
-def prepare_kernel(e_ref, state_ref, out_x, out_y, out_z, packed):
-    first_layers(e_ref, out_x, out_y, out_z)
-    lower = state_ref[:, 7]
-    lasing = state_ref[:, 8]
-    upper = state_ref[:, 9]
+def inside(faces, ahead):
+    kept = []
+    for face, axis in zip(faces, ("gx", "gy", "gz")):
+        index = lax.axis_index(axis)
+        real = index < lax.axis_size(axis) - 1 if ahead else index > 0
+        kept.append([jnp.where(real, face[place], 0.0) for place in range(2)])
+    return kept
+
+
+def prepare_kernel(
+    e_hbm, state_hbm, h_hbm, eps_hbm, out_x, out_y, out_z, packed, e_out, h_out, eps_out, state, sems
+):
+    copies = [
+        pltpu.make_async_copy(source, target, sems.at[place])
+        for place, (source, target) in enumerate(
+            ((e_hbm, e_out), (state_hbm, state), (h_hbm, h_out), (eps_hbm, eps_out))
+        )
+    ]
+    for copy in copies:
+        copy.start()
+    copies[0].wait()
+    first_layers(e_out, out_x, out_y, out_z)
+    copies[1].wait()
+    lower, lasing, upper = state[7], state[8], state[9]
     for comp in range(3):
-        polar = state_ref[:, comp]
-        packed[:, comp] = keep_rate * state_ref[:, 3 + comp] - spring * polar
+        polar = state[comp]
+        packed[:, comp] = keep_rate * state[3 + comp] - spring * polar
         packed[:, 3 + comp] = polar
     packed[:, 6] = lasing - lower
     lasing_free = lasing + time_step * (upper / upper_life - lasing / lasing_life)
     lower_free = lower + time_step * (lasing / lasing_life - lower / lower_life)
     packed[:, 7] = lasing_free - lower_free
+    copies[2].wait()
+    copies[3].wait()
 
 
 def magnetic_kernel(e_ref, h_ref, face_x, face_y, face_z, h_out, out_x, out_y, out_z):
     lane = lane_index(ROWS)
     last = row_in_brick() == CY - 1
+    face_x, face_y, face_z = inside((face_x, face_y, face_z), True)
     ex, ey, ez = e_ref[0], e_ref[1], e_ref[2]
     first = (ahead_y(ez, face_y[1], last) - ez) - (ahead_z(ey, face_z[1], lane) - ey)
     second = (ahead_z(ex, face_z[0], lane) - ex) - (ahead_x(ez, face_x[1]) - ez)
@@ -155,6 +180,7 @@
 def electric_curl(h_ref, face_x, face_y, face_z):
     lane = lane_index(ROWS)
     start = row_in_brick() == 0
+    face_x, face_y, face_z = inside((face_x, face_y, face_z), False)
     hx, hy, hz = h_ref[0], h_ref[1], h_ref[2]
     first = (hz - behind_y(hz, face_y[1], start)) - (hy - behind_z(hy, face_z[1], lane))
     second = (hx - behind_z(hx, face_z[0], lane)) - (hz - behind_x(hz, face_x[1]))
@@ -163,43 +189,43 @@
 
 
 def row_hits(offsets, width):
-    return (row_index(ROWS, width) == (offsets >> 7)).astype(F32).astype(BF16)
+    return row_index(ROWS, width) == (offsets >> 7)
 
 
 def lane_hits(offsets, width):
-    return row_index(CZ, width) == (offsets & (CZ - 1))
-
-
-def scatter_kernel(count_ref, owner_ref, offsets_ref, fields_ref, dense, placed, total):
-    count = count_ref[0]
-    for slot in range(SLOTS):
-        line = offsets_ref[slot : slot + 1]
-        placed[pl.ds(owner_ref[slot], 1)] = jnp.where(slot < count, line, -1)
+    hits = row_index(CZ, width) == (offsets & (CZ - 1))
+    return hits.astype(F32).astype(BF16)
+
+
+GROUP = 4
+
+
+def scatter_kernel(placed, fields_ref, dense, total, spots, rows):
     total[...] = jnp.zeros_like(total)
 
-    def pair(index, carry):
-        lines = placed[pl.ds(2 * index, 2)]
-        offsets = jnp.concatenate([lines[0:1], lines[1:2]], axis=1)
-        rows = row_hits(offsets, 2 * CZ)
-        lanes = lane_hits(offsets, 2 * CZ)
-        values = jnp.concatenate([fields_ref[2 * index], fields_ref[2 * index + 1]], axis=1)
-        for part in split_parts(values):
-            part = part.astype(F32)
-            spots = jnp.concatenate(
-                [
-                    jnp.where(lanes, part[field : field + 1], 0.0).astype(BF16)
-                    for field in range(8)
-                ],
-                axis=0,
-            )
-            total[...] += lax.dot_general(
-                rows, spots, (((1,), (1,)), ((), ())), preferred_element_type=F32
-            )
+    def group(index, carry):
+        lines = placed[pl.ds(GROUP * index, GROUP)]
+        for slot in range(GROUP):
+            line = lines[slot : slot + 1]
+            hits = row_hits(line, CZ).astype(F32).astype(BF16)
+            lanes = lane_hits(line, CZ).reshape(8, 16, CZ)
+            for place, part in enumerate(split_parts(fields_ref[GROUP * index + slot])):
+                across = (place * GROUP + slot) * CZ
+                rows[:, across : across + CZ] = hits
+                part = part.astype(F32)
+                for field in range(8):
+                    line = jnp.broadcast_to(part[field : field + 1], (16, CZ)).astype(BF16)
+                    spots[field * CZ : (field + 1) * CZ, across : across + CZ] = (
+                        lanes * line[None]
+                    ).reshape(CZ, CZ)
+        total[...] += lax.dot_general(
+            spots[...], rows[...], (((1,), (1,)), ((), ())), preferred_element_type=F32
+        )
         return carry
 
-    lax.fori_loop(0, SLOTS // 2, pair, 0)
+    lax.fori_loop(0, SLOTS // GROUP, group, 0)
     for field in range(8):
-        dense[field] = total[:, field * CZ : (field + 1) * CZ]
+        dense[field] = jnp.transpose(total[field * CZ : (field + 1) * CZ])
 
 
 def electric_kernel(
@@ -224,29 +250,33 @@
     first_layers(e_out, out_x, out_y, out_z)
 
 
-def gather_lines(high, low, offsets, width, fields):
+def stacked(fields):
+    high, low = split_parts(jnp.concatenate(fields, axis=0))
+    return jnp.concatenate([high, low], axis=1)
+
+
+def gather_lines(values, offsets, width):
+    lanes = lane_hits(offsets, width)
     rows = row_hits(offsets, width)
-    lanes = lane_hits(offsets, width)
-    picked = jnp.dot(high, rows, preferred_element_type=F32)
-    picked = picked + jnp.dot(low, rows, preferred_element_type=F32)
+    picked = jnp.dot(
+        values, jnp.concatenate([lanes, lanes], axis=0), preferred_element_type=F32
+    )
     return [
-        jnp.sum(jnp.where(lanes, picked[field * CZ : (field + 1) * CZ], 0.0), axis=0, keepdims=True)
-        for field in range(fields)
+        jnp.sum(
+            jnp.where(rows, picked[field * ROWS : (field + 1) * ROWS], 0.0), axis=0, keepdims=True
+        )
+        for field in range(6)
     ]
 
 
-def turned(fields):
-    return split_parts(jnp.concatenate([jnp.transpose(field) for field in fields], axis=0))
-
-
-def drive_kernel(e_old, e_new, h_new, placed, surf_ref, drives, sampled):
-    high, low = turned([e_old[c] for c in range(3)] + [e_new[c] for c in range(3)])
+def drive_kernel(e_old, e_new, h_new, placed, surf_ref, drives, sampled, values):
+    values[...] = stacked([e_old[c] for c in range(3)] + [e_new[c] for c in range(3)])
     drives[...] = jnp.zeros_like(drives)
 
     def pair(index, carry):
         lines = placed[pl.ds(2 * index, 2)]
         offsets = jnp.concatenate([lines[0:1], lines[1:2]], axis=1)
-        got = gather_lines(high, low, offsets, 2 * CZ, 6)
+        got = gather_lines(values[...], offsets, 2 * CZ)
         for field in range(6):
             drives[2 * index, field : field + 1] = got[field][:, :CZ]
             drives[2 * index + 1, field : field + 1] = got[field][:, CZ:]
@@ -257,15 +287,40 @@
 
 
 def sample_rows(e_ref, h_ref, surf_ref, sampled):
-    high, low = turned([e_ref[c] for c in range(3)] + [h_ref[c] for c in range(3)])
-    got = gather_lines(high, low, surf_ref[...], CZ, 6)
+    values = stacked([e_ref[c] for c in range(3)] + [h_ref[c] for c in range(3)])
+    got = gather_lines(values, surf_ref[...], CZ)
     sampled[...] = jnp.zeros_like(sampled)
     for field in range(6):
         sampled[field : field + 1] = got[field]
 
 
-def table_kernel(surf_ref, units_ref, table):
+def table_kernel(
+    count_ref,
+    owner_hbm,
+    offsets_ref,
+    surf_ref,
+    units_ref,
+    table,
+    factors,
+    placed,
+    surf_out,
+    owner_ref,
+    sem,
+):
+    copy = pltpu.make_async_copy(owner_hbm, owner_ref, sem)
+    copy.start()
+    copy.wait()
+    count = count_ref[0]
+    for slot in range(SLOTS):
+        line = offsets_ref[slot : slot + 1]
+        placed[pl.ds(owner_ref[0, slot], 1)] = jnp.where(slot < count, line, -1)
+    omega = freq_low + freq_pitch * row_index(FREQ, DIRS).astype(F32)
+    for step in range(STEPS):
+        moment = omega * ((step + 1) * time_step)
+        factors[2 * step] = jnp.cos(moment)
+        factors[2 * step + 1] = jnp.sin(moment)
     cells = surf_ref[...]
+    surf_out[...] = cells
     rows = cells >> 7
     layer = (rows * 2731) >> 16
     cell_x = lax.axis_index("gx") * CX + layer
@@ -310,6 +365,7 @@
     surf_ref,
     early_ref,
     table,
+    factors,
     e_out,
     keep_out,
     send_out,
@@ -320,7 +376,8 @@
     for comp in range(3):
         e_out[comp] = e_ref[comp] + scaled * (curls[comp] - source[comp])
     sample_rows(e_out, h_ref, surf_ref, late)
-    high, low = split_parts(jnp.concatenate([early_ref[...], late[...]], axis=0))
+    scale = 1.0 / math.sqrt(STEPS * CZ * 256)
+    high, low = split_parts(scale * jnp.concatenate([early_ref[...], late[...]], axis=0))
     left = jnp.concatenate(
         [
             jnp.concatenate([high, high], axis=1),
@@ -329,33 +386,31 @@
         axis=0,
     )
     own = lax.axis_index("gz")
-    scale = 1.0 / math.sqrt(STEPS * CZ * 256)
-    for freq in range(FREQ // 2):
-        for side, out in ((0, keep_out), (1, send_out)):
-            target = lax.rem(own + side, 2)
-            omega = freq_low + freq_pitch * (target * (FREQ // 2) + freq).astype(F32)
-            both = jnp.dot(
-                left, table[target * (FREQ // 2) + freq], preferred_element_type=F32
-            )
+    for side, out in ((1, send_out), (0, keep_out)):
+        base = lax.rem(own + side, 2) * (FREQ // 2)
+        for freq in range(FREQ // 2):
+            both = jnp.dot(left, table[base + freq], preferred_element_type=F32)
             both = both[0:16] + both[16:32]
             real = jnp.zeros((8, DIRS), F32)
             imag = jnp.zeros((8, DIRS), F32)
             for step in range(STEPS):
-                moment = jnp.full((8, DIRS), (step + 1) * time_step, F32) * omega
-                cosine = jnp.cos(moment)
-                sine = jnp.sin(moment)
+                cosine = factors[2 * step, pl.ds(base + freq, 1)]
+                sine = factors[2 * step + 1, pl.ds(base + freq, 1)]
                 upper = both[8 * step : 8 * step + 8, 0:DIRS]
                 under = both[8 * step : 8 * step + 8, DIRS:]
-                real = real + cosine * upper + sine * under
-                imag = imag + cosine * under - sine * upper
-            out[freq, 0:8] = scale * real
-            out[freq, 8:16] = scale * imag
-
-
-def atoms_kernel(state_ref, pump_ref, drives, out):
-    polar = [state_ref[:, c] for c in range(3)]
-    rate = [state_ref[:, 3 + c] for c in range(3)]
-    ground, lower, lasing, upper = [state_ref[:, 6 + level] for level in range(4)]
+                real = real + (cosine * upper + sine * under)
+                imag = imag + (cosine * under - sine * upper)
+            for comp in range(6):
+                row = comp * (FREQ // 2) + freq
+                out[row : row + 1] = real[comp : comp + 1]
+                row = (comp + 6) * (FREQ // 2) + freq
+                out[row : row + 1] = imag[comp : comp + 1]
+
+
+def atoms_kernel(state_ref, pump_ref, drives, e_ref, h_ref, out, e_out, h_out):
+    polar = [state_ref[c] for c in range(3)]
+    rate = [state_ref[3 + c] for c in range(3)]
+    ground, lower, lasing, upper = [state_ref[6 + level] for level in range(4)]
     pump = pump_ref[...]
     for step in range(STEPS):
         drive = [drives[:, 3 * step + c] for c in range(3)]
@@ -379,7 +434,9 @@
         ground = ground + time_step * (lower / lower_life - pump * ground)
         lower, lasing, upper = lower_new, lasing_new, upper_new
     for place, value in enumerate(polar + rate + [ground, lower, lasing, upper]):
-        out[:, place] = value
+        out[place] = value
+    e_out[...] = e_ref[...]
+    h_out[...] = h_ref[...]
 
 
 def directions(count):
@@ -411,15 +468,14 @@
     surf_offsets,
     far_acc,
 ):
-    e_old = efield.reshape(3, ROWS, CZ)
-    h_old = hfield.reshape(3, ROWS, CZ)
-    eps = inv_eps.reshape(ROWS, CZ)
-    state = gain_state.reshape(SLOTS, 10, CZ)
-    surf = surf_offsets.reshape(1, CZ)
+    state = jnp.transpose(gain_state.reshape(SLOTS, 10, CZ), (1, 0, 2))
+    dense = shape(3, ROWS, CZ)
     faces = (shape(2, CY, CZ), shape(2, CX, CZ), shape(2, ROWS, CZ))
-    dense = shape(3, ROWS, CZ)
-    down = [[(i + 1, i) for i in range(n - 1)] for n in (16, 8, 2)]
-    up = [[(i, i + 1) for i in range(n - 1)] for n in (16, 8, 2)]
+    down = [[((i + 1) % n, i) for i in range(n)] for n in (16, 8, 2)]
+    up = [[(i, (i + 1) % n) for i in range(n)] for n in (16, 8, 2)]
+    vmem = pl.BlockSpec(memory_space=pltpu.VMEM)
+
+    hbm = pl.BlockSpec(memory_space=pltpu.HBM)
 
     def shifted(parts, perms):
         return [
@@ -427,75 +483,87 @@
             for part, axis, perm in zip(parts, ("gx", "gy", "gz"), perms)
         ]
 
-    def whole(count):
-        return [pl.BlockSpec(memory_space=pltpu.VMEM)] * count
-
-    scalars = [pl.BlockSpec(memory_space=pltpu.SMEM)]
-
-    *near, packed = call(
-        prepare_kernel, faces + (shape(SLOTS, 8, CZ),), (e_old, state), name="prepare"
+    *near, packed, e_old, h_old, eps = call(
+        prepare_kernel,
+        faces + (shape(SLOTS, 8, CZ), dense, dense, shape(ROWS, CZ)),
+        stay(
+            efield.reshape(3, ROWS, CZ),
+            state,
+            hfield.reshape(3, ROWS, CZ),
+            inv_eps.reshape(ROWS, CZ),
+        ),
+        in_specs=[hbm] * 4,
+        scratch=[pltpu.VMEM((10, SLOTS, CZ), F32), pltpu.SemaphoreType.DMA((4,))],
+        name="prepare",
     )
     near = shifted(near, down)
     fields = lax.all_to_all(packed, "gx", 0, 0, tiled=True)
+    table, factors, placed, surf = call(
+        table_kernel,
+        (
+            shape(FREQ, 2 * CZ, 2 * DIRS, dtype=BF16),
+            shape(2 * STEPS, FREQ, DIRS),
+            shape(SLOTS, CZ, dtype=jnp.int32),
+            shape(1, CZ, dtype=jnp.int32),
+        ),
+        [gain_count.reshape(1)]
+        + stay(
+            block_owner.reshape(1, SLOTS),
+            gain_offsets.reshape(SLOTS, CZ),
+            surf_offsets.reshape(1, CZ),
+            jnp.asarray(directions(DIRS)),
+        ),
+        in_specs=[pl.BlockSpec(memory_space=pltpu.SMEM), hbm, vmem, vmem, vmem],
+        scratch=[pltpu.SMEM((1, SLOTS), jnp.int32), pltpu.SemaphoreType.DMA],
+        vmem=24,
+        moved=8 * MIB,
+        name="table",
+    )
+    *near, placed = lax.optimization_barrier((*near, placed))
     h_one, *edge = call(magnetic_kernel, (dense,) + faces, (e_old, h_old, *near), name="magnetic")
     edge = shifted(edge, up)
-    spread_fields, placed = call(
+    spread_fields = call(
         scatter_kernel,
-        (shape(8, ROWS, CZ), shape(SLOTS, CZ, dtype=jnp.int32)),
-        (
-            gain_count.reshape(1),
-            block_owner.reshape(SLOTS),
-            gain_offsets.reshape(SLOTS, CZ),
-            fields,
-        ),
-        in_specs=scalars * 2 + whole(2),
-        scratch=[pltpu.VMEM((ROWS, 8 * CZ), F32)],
-        flops=4 * 10**9,
+        shape(8, ROWS, CZ),
+        (placed, fields),
+        scratch=[
+            pltpu.VMEM((8 * CZ, ROWS), F32),
+            pltpu.VMEM((8 * CZ, 2 * GROUP * CZ), BF16),
+            pltpu.VMEM((ROWS, 2 * GROUP * CZ), BF16),
+        ],
         name="scatter",
     )
-    e_one, *near_rest = call(
+    e_one, *near, source = call(
         electric_kernel,
         (dense,) + faces + (dense,),
         (e_old, h_one, *edge, eps, spread_fields),
         name="electric",
     )
-    *near, source = near_rest
     near = shifted(near, down)
     drives, early = call(
         drive_kernel,
         (shape(SLOTS, 8, CZ), shape(8, CZ)),
         (e_old, e_one, h_one, placed, surf),
-        flops=4 * 10**9,
+        scratch=[pltpu.VMEM((6 * ROWS, 2 * CZ), BF16)],
         name="drive",
     )
+    *near, early = lax.optimization_barrier((*near, early))
     h_two, *edge = call(magnetic_kernel, (dense,) + faces, (e_one, h_one, *near), name="magnetic2")
     edge = shifted(edge, up)
-    table = call(
-        table_kernel,
-        shape(FREQ, 2 * CZ, 2 * DIRS, dtype=BF16),
-        (surf, jnp.asarray(directions(DIRS))),
-        flops=4 * 10**9,
-        vmem=24,
-        moved=8 * MIB,
-        name="table",
-    )
-    part = shape(FREQ // 2, 16, DIRS)
+    back = lax.all_to_all(drives, "gx", 0, 0, tiled=True)
+    part = shape(12 * FREQ // 2, DIRS)
     e_two, keep, send = call(
         final_kernel,
         (dense, part, part),
-        (e_one, h_two, *edge, eps, source, surf, early, table),
+        (e_one, h_two, *edge, eps, source, surf, early, table, factors),
         scratch=[pltpu.VMEM((8, CZ), F32)],
-        vmem=28,
-        flops=4 * 10**9,
-        moved=10 * MIB,
+        vmem=24,
+        moved=8 * MIB,
         name="final",
     )
-    back = lax.all_to_all(drives, "gx", 0, 0, tiled=True)
-    state_out = call(
-        atoms_kernel, shape(SLOTS, 10, CZ), (state, pump.reshape(SLOTS, CZ), back), name="atoms"
-    )
-    chip = keep + lax.ppermute(send, "gz", [(0, 1), (1, 0)])
-    pieces = lax.all_to_all(chip.reshape(8, 4, 16, DIRS), "gy", 0, 0, tiled=True)
+    chip = keep + lax.ppermute(send, "gz", down[2])
+    chip, back = lax.optimization_barrier((chip, back))
+    pieces = lax.all_to_all(chip.reshape(8, 48, DIRS), "gy", 0, 0, tiled=True)
     total = jnp.sum(pieces, axis=0)
     total = all_reduce(
         total, "gx", lambda k: [(a * 4 + z, (a ^ k) * 4 + z) for a in range(4) for z in range(4)]
@@ -504,13 +572,19 @@
         total, "gx", lambda k: [(a * 4 + z, a * 4 + (z ^ k)) for a in range(4) for z in range(4)]
     )
     gathered = lax.all_to_all(
-        jnp.broadcast_to(total[None], (8, 4, 16, DIRS)), "gy", 0, 0, tiled=True
-    ).reshape(FREQ // 2, 16, DIRS)
-    far_out = far_acc + jnp.concatenate([gathered[:, 0:6], gathered[:, 8:14]], axis=1)
+        jnp.broadcast_to(total[None], (8, 48, DIRS)), "gy", 0, 0, tiled=True
+    )
+    far_out = far_acc + jnp.transpose(gathered.reshape(12, FREQ // 2, DIRS), (1, 0, 2))
+    state_out, e_out, h_out = call(
+        atoms_kernel,
+        (shape(10, SLOTS, CZ), dense, dense),
+        (state, pump.reshape(SLOTS, CZ), back, e_two, h_two),
+        name="atoms",
+    )
     return (
-        e_two.reshape(efield.shape),
-        h_two.reshape(hfield.shape),
-        state_out.reshape(gain_state.shape),
+        e_out.reshape(efield.shape),
+        h_out.reshape(hfield.shape),
+        jnp.transpose(state_out, (1, 0, 2)).reshape(gain_state.shape),
         far_out,
     )
 

time: 140 us -> 117 us (0.84)
  starting transfers between devices: 68.7 us -> 50.7 us
  waiting for transfers between devices: 24.7 us -> 20.4 us
    ppermute x12, starting transfers between devices: 33 us -> 19.7 us  [shifted(): lax.ppermute(part, axis, perm)]
    all_to_all x1, waiting for transfers between devices: 10.7 us -> 0.01 us  [local(): back = lax.all_to_all(drives, 'gx', 0, 0, tiled=True)]
    ppermute x12, waiting for transfers between devices: 3.71 us -> 7.65 us  [shifted(): lax.ppermute(part, axis, perm)]
    all_to_all x1, starting transfers between devices: 6.68 us -> 3.52 us  [local(): back = lax.all_to_all(drives, 'gx', 0, 0, tiled=True)]
    ppermute x6, waiting for transfers between devices: 4.47 us -> 6.98 us  [all_reduce(): one, two, three = [lax.ppermute(value, axis, peers(k)) for k in (1, 2, 3)]]
    ppermute x6, starting transfers between devices: 13 us -> 11.1 us  [all_reduce(): one, two, three = [lax.ppermute(value, axis, peers(k)) for k in (1, 2, 3)]]
    unnamed x27 -> x10, local copies, waits for them, and re-layouts: 6.81 us -> 6.66 us
  transfers between devices with their start and end apart: 22 -> 22, of which waited for: 7 -> 8; matrix products, arithmetic and copies ran while one was open for 1% -> 0% of each run, Pallas kernels for 14% -> 18%
where the time goes in v2:
time: 117 us; the launch traced here: 116 us
  starting transfers between devices  50.7 us (43%)
  Pallas kernels  23.6 us (20%)
  waiting for transfers between devices  20.4 us (17%)
  blocking collectives  12.1 us (10%)
  local copies, waits for them, and re-layouts  7.35 us (6%)
  between operations  1.47 us (1%)
    pallas_call x9, Pallas kernels, call(): pl.pallas_call(kernel, out_shape=outs, in_specs=in_specs or [pl.BlockSpec...  23.6 us
    ppermute x12, starting transfers between devices, shifted(): lax.ppermute(part, axis, perm)  19.7 us
    all_to_all x1, blocking collectives, local(): pieces = lax.all_to_all(chip.reshape(8, 48, DIRS), 'gy', 0, 0, tiled=True)  12.1 us
    ppermute x6, starting transfers between devices, all_reduce(): one, two, three = [lax.ppermute(value, axis, peers(k)) for k in (1, 2, 3)]  11.1 us
    all_to_all x1, starting transfers between devices, local(): fields = lax.all_to_all(packed, 'gx', 0, 0, tiled=True)  11 us
    ppermute x12, waiting for transfers between devices, shifted(): lax.ppermute(part, axis, perm)  7.65 us
    ppermute x6, waiting for transfers between devices, all_reduce(): one, two, three = [lax.ppermute(value, axis, peers(k)) for k in (1, 2, 3)]  6.98 us
    unnamed x10, local copies, waits for them, and re-layouts  6.66 us
  transfers between devices with their start and end apart: 22, of which 8 were waited for; matrix products, arithmetic and copies ran while one was open for 0% of the time, Pallas kernels for 18%

profile of v2, /device:TPU:8, one launch (start us, length us, event | category | flops | bytes accessed | tf_op | source)
XLA Modules:
  0.0 116.3 jit_solution(8180786309293611159)
XLA Ops:
  0.6 1.8 %prepare.1 = (f32[2,24,128]{2,1,0:T(8,128)S(1)}, f32[2,8,128]{2,1,0:T(8,128)S(1)}, f32[2,192,128]{2,1,0:T(8,128)S(1)}, f32[32,8,128]{2,1,0:T(8,128)}, f32[3,192,...) custom-call(f32[3,192,128]{2,1,0:T(8,128)} %bitcast.26, f32[10,32,128]{2,1,0:T(8,128)} %bitcast.21, ...), custom_call_target="tpu_custom_call" | custom-call | bytes 2097152 | tf_op jit(solution)/shard_map/prepare/pallas_call | solution.py:47
  2.6 11.0 %all-to-all-start = ((f32[32,8,128]{2,1,0:T(8,128)}), f32[32,8,128]{2,1,0:T(8,128)S(1)}, u32[]{:S(2)}, u32[]{:S(2)}) async-start(f32[32,8,128]{2,1,0:T(8,128)} %get-tuple-element.61), calls=%async_computation | async-start | bytes 262144 | tf_op jit(solution)/shard_map/all_to_all | solution.py:500
  13.6 6.2 %collective-permute-start = (f32[2,24,128]{2,1,0:T(8,128)S(1)}, f32[2,24,128]{2,1,0:T(8,128)S(1)}, u32[]{:S(2)}, u32[]{:S(2)}) collective-permute-start(f32[2,24,128]{2,1,0:T(8,128)S(1)} %get-tuple-element.48), channel_id=1, source_target_pairs={{16,0},{32,16},{48,32},{64,48},{80,64},{96,80},{112,96},{128,112},... | collective-permute-start | bytes 73736 | tf_op jit(solution)/shard_map/ppermute | solution.py:482
  20.9 5.2 %table.1 = (bf16[64,256,256]{2,1,0:T(8,128)(2,1)S(1)}, f32[4,64,128]{2,1,0:T(8,128)S(1)}, s32[32,128]{1,0:T(8,128)S(1)}, s32[1,128]{1,0:T(1,128)S(1)}) custom-call(s32[1]{0:T(128)} %bitcast.20.count_ref, s32[1,32]{1,0:T(1,128)} %bitcast.30, s32[32,128]{1,0:T(8,128)} %bitcast.29, s32[1,128]{1,0:T(1,128)} %bitcast.31, f32[8,128]{1,0:T(8,128)} %constant.4.clone.units_ref), custom_call_target="tpu_custom_call" | custom-call | bytes 8388608 | tf_op jit(solution)/shard_map/table/pallas_call | solution.py:47
  26.1 3.3 %copy-done = bf16[64,256,256]{2,1,0:T(8,128)(2,1)} copy-done((bf16[64,256,256]{2,1,0:T(8,128)(2,1)}, bf16[64,256,256]{2,1,0:T(8,128)(2,1)S(1)}, u32[]{:S(2)}) %copy-start) | copy-done | bytes 8388632
  29.8 1.7 %collective-permute-start.4 = (f32[2,8,128]{2,1,0:T(8,128)S(1)}, f32[2,8,128]{2,1,0:T(8,128)S(1)}, u32[]{:S(2)}, u32[]{:S(2)}) collective-permute-start(f32[2,8,128]{2,1,0:T(8,128)S(1)} %get-tuple-element.57), channel_id=1, source_target_pairs={{0,2},{2,4},{4,6},{6,8},{8,10},{10,12},{12,14},{14,0},{1,3},{3,5},... | collective-permute-start | bytes 24584 | tf_op jit(solution)/shard_map/ppermute | solution.py:482
  31.4 6.7 %scatter.1.dense = f32[8,192,128]{2,1,0:T(8,128)S(1)} custom-call(s32[32,128]{1,0:T(8,128)S(1)} %get-tuple-element.60.placed, f32[32,8,128]{2,1,0:T(8,128)S(1)} %all-to-all-done.fields_ref), custom_call_target="tpu_custom_call" | custom-call | bytes 2097152 | tf_op jit(solution)/shard_map/scatter/pallas_call | solution.py:47
  38.6 6.2 %collective-permute-start.6 = (f32[2,24,128]{2,1,0:T(8,128)S(1)}, f32[2,24,128]{2,1,0:T(8,128)S(1)}, u32[]{:S(2)}, u32[]{:S(2)}) collective-permute-start(f32[2,24,128]{2,1,0:T(8,128)S(1)} %get-tuple-element.63), channel_id=1, source_target_pairs={{16,0},{32,16},{48,32},{64,48},{80,64},{96,80},{112,96},{128,112},... | collective-permute-start | bytes 73736 | tf_op jit(solution)/shard_map/ppermute | solution.py:482
  44.8 2.0 %collective-permute-start.7 = (f32[2,8,128]{2,1,0:T(8,128)S(1)}, f32[2,8,128]{2,1,0:T(8,128)S(1)}, u32[]{:S(2)}, u32[]{:S(2)}) collective-permute-start(f32[2,8,128]{2,1,0:T(8,128)S(1)} %get-tuple-element.64), channel_id=1, source_target_pairs={{2,0},{4,2},{6,4},{8,6},{10,8},{12,10},{14,12},{0,14},{3,1},{5,3},... | collective-permute-start | bytes 24584 | tf_op jit(solution)/shard_map/ppermute | solution.py:482
  46.8 6.0 %drive.1 = (f32[32,8,128]{2,1,0:T(8,128)}, f32[8,128]{1,0:T(8,128)S(1)}) custom-call(f32[3,192,128]{2,1,0:T(8,128)S(1)} %get-tuple-element.46.e_ref.e_old, f32[3,192,128]{2,1,0:T(8,128)S(1)} %get-tuple-element.62.e_new.e_ref, f32[3,192,128]{2,1,0:T(8,128)S(1)} %get-tuple-element.55.h_ref.h_new, s32[32,128]{1,0:T(8,128)S(1)} %get-tuple-element.60.placed, ...), custom_call_target="tpu_custom_call" | custom-call | bytes 2097152 | tf_op jit(solution)/shard_map/drive/pallas_call | solution.py:47
  53.1 3.5 %all-to-all-start.1 = ((f32[32,8,128]{2,1,0:T(8,128)}), f32[32,8,128]{2,1,0:T(8,128)S(1)}, u32[]{:S(2)}, u32[]{:S(2)}) async-start(f32[32,8,128]{2,1,0:T(8,128)} %get-tuple-element.81), calls=%async_computation.1 | async-start | bytes 262144 | tf_op jit(solution)/shard_map/all_to_all | solution.py:553
  56.6 2.7 %collective-permute-start.9 = (f32[2,24,128]{2,1,0:T(8,128)S(1)}, f32[2,24,128]{2,1,0:T(8,128)S(1)}, u32[]{:S(2)}, u32[]{:S(2)}) collective-permute-start(f32[2,24,128]{2,1,0:T(8,128)S(1)} %get-tuple-element.72), channel_id=1, source_target_pairs={{0,16},{16,32},{32,48},{48,64},{64,80},{80,96},{96,112},{112,128},... | collective-permute-start | bytes 73736 | tf_op jit(solution)/shard_map/ppermute | solution.py:482
  59.4 5.7 %collective-permute-done.10.face_y = f32[2,8,128]{2,1,0:T(8,128)S(1)} collective-permute-done((f32[2,8,128]{2,1,0:T(8,128)S(1)}, f32[2,8,128]{2,1,0:T(8,128)S(1)}, u32[]{:S(2)}, u32[]{:S(2)}) %collective-permute-start.10) | collective-permute-done | bytes 8224 | tf_op jit(solution)/shard_map/ppermute | solution.py:482
  65.0 2.0 %collective-permute-done.9.face_x = f32[2,24,128]{2,1,0:T(8,128)S(1)} collective-permute-done((f32[2,24,128]{2,1,0:T(8,128)S(1)}, f32[2,24,128]{2,1,0:T(8,128)S(1)}, u32[]{:S(2)}, u32[]{:S(2)}) %collective-permute-start.9) | collective-permute-done | bytes 24608 | tf_op jit(solution)/shard_map/ppermute | solution.py:482
  67.0 3.4 %copy-done.1 = bf16[64,256,256]{2,1,0:T(8,128)(2,1)S(1)} copy-done((bf16[64,256,256]{2,1,0:T(8,128)(2,1)S(1)}, bf16[64,256,256]{2,1,0:T(8,128)(2,1)}, u32[]{:S(2)}) %copy-start.1) | copy-done | bytes 8388632
  70.4 2.3 %final.1 = (f32[3,192,128]{2,1,0:T(8,128)S(1)}, f32[384,128]{1,0:T(8,128)S(1)}, f32[384,128]{1,0:T(8,128)S(1)}) custom-call(f32[3,192,128]{2,1,0:T(8,128)S(1)} %get-tuple-element.62.e_new.e_ref, f32[3,192,128]{2,1,0:T(8,128)S(1)} %get-tuple-element.71.h_ref, f32[2,24,128]{2,1,0:T(8,128)S(1)} %collective-permute-done.9.face_x, ...), custom_call_target="tpu_custom_call" | custom-call | bytes 8388608 | tf_op jit(solution)/shard_map/final/pallas_call | solution.py:47
  72.7 1.4 %collective-permute-done.12 = f32[384,128]{1,0:T(8,128)S(1)} collective-permute-done((f32[384,128]{1,0:T(8,128)S(1)}, f32[384,128]{1,0:T(8,128)S(1)}, u32[]{:S(2)}, u32[]{:S(2)}) %collective-permute-start.12) | collective-permute-done | bytes 196640 | tf_op jit(solution)/shard_map/ppermute | solution.py:564
  74.2 12.1 %all_to_all.20 = f32[8,48,128]{2,1,0:T(8,128)S(1)} all-to-all(f32[8,48,128]{2,1,0:T(8,128)S(1)} %bitcast.25), channel_id=1, replica_groups=mesh['gx'=16,'gy'=8,'gz'=2] {'gy'}, dimensions={0} | all-to-all | bytes 393216 | tf_op jit(solution)/shard_map/all_to_all | solution.py:566
  86.3 1.1 collective-permute-start.15
  87.4 0.5 collective-permute-start.14
  87.9 2.6 %collective-permute-start.13 = (f32[48,128]{1,0:T(8,128)S(1)}, f32[48,128]{1,0:T(8,128)S(1)}, u32[]{:S(2)}, u32[]{:S(2)}) collective-permute-start(f32[48,128]{1,0:T(8,128)S(1)} %reduce_sum.9), channel_id=1, source_target_pairs={{0,64},{16,80},{32,96},{48,112},{64,0},{80,16},{96,32},{112,48},{1... | collective-permute-start | bytes 73736 | tf_op jit(solution)/shard_map/ppermute | solution.py:455
  90.4 0.9 collective-permute-done.15
  91.4 1.3 %collective-permute-done.14 = f32[48,128]{1,0:T(8,128)S(1)} collective-permute-done((f32[48,128]{1,0:T(8,128)S(1)}, f32[48,128]{1,0:T(8,128)S(1)}, u32[]{:S(2)}, u32[]{:S(2)}) %collective-permute-start.14) | collective-permute-done | bytes 24608 | tf_op jit(solution)/shard_map/ppermute | solution.py:455
  92.7 2.2 %collective-permute-start.18 = (f32[48,128]{1,0:T(8,128)S(1)}, f32[48,128]{1,0:T(8,128)S(1)}, u32[]{:S(2)}, u32[]{:S(2)}) collective-permute-start(f32[48,128]{1,0:T(8,128)S(1)} %add_add_fusion.1), channel_id=1, source_target_pairs={{0,48},{16,32},{32,16},{48,0},{64,112},{80,96},{96,80},{112,64},{1... | collective-permute-start | bytes 73736 | tf_op jit(solution)/shard_map/ppermute | solution.py:455
  94.9 4.8 %collective-permute-start.17 = (f32[48,128]{1,0:T(8,128)S(1)}, f32[48,128]{1,0:T(8,128)S(1)}, u32[]{:S(2)}, u32[]{:S(2)}) collective-permute-start(f32[48,128]{1,0:T(8,128)S(1)} %add_add_fusion.1), channel_id=1, source_target_pairs={{0,32},{16,48},{32,0},{48,16},{64,96},{80,112},{96,64},{112,80},{1... | collective-permute-start | bytes 73736 | tf_op jit(solution)/shard_map/ppermute | solution.py:455
  99.7 3.0 %collective-permute-done.17 = f32[48,128]{1,0:T(8,128)S(1)} collective-permute-done((f32[48,128]{1,0:T(8,128)S(1)}, f32[48,128]{1,0:T(8,128)S(1)}, u32[]{:S(2)}, u32[]{:S(2)}) %collective-permute-start.17) | collective-permute-done | bytes 24608 | tf_op jit(solution)/shard_map/ppermute | solution.py:455
  102.6 1.8 %collective-permute-done.16 = f32[48,128]{1,0:T(8,128)S(1)} collective-permute-done((f32[48,128]{1,0:T(8,128)S(1)}, f32[48,128]{1,0:T(8,128)S(1)}, u32[]{:S(2)}, u32[]{:S(2)}) %collective-permute-start.16) | collective-permute-done | bytes 24608 | tf_op jit(solution)/shard_map/ppermute | solution.py:455
  104.4 0.7 broadcast_in_dim.2
  105.1 5.3 %all-to-all-start.3 = ((f32[8,48,128]{2,1,0:T(8,128)}), f32[8,48,128]{2,1,0:T(8,128)S(1)}, u32[]{:S(2)}, u32[]{:S(2)}) async-start(f32[8,48,128]{2,1,0:T(8,128)} %broadcast_in_dim.2), calls=%async_computation.3 | async-start | bytes 393216 | tf_op jit(solution)/shard_map/all_to_all | solution.py:574
  110.3 1.0 atoms.1
  111.3 4.3 %all-to-all-done.3 = f32[8,48,128]{2,1,0:T(8,128)S(1)} async-done(((f32[8,48,128]{2,1,0:T(8,128)}), f32[8,48,128]{2,1,0:T(8,128)S(1)}, u32[]{:S(2)}, u32[]{:S(2)}) %all-to-all-start.3) | async-done | bytes 196640 | tf_op jit(solution)/shard_map/all_to_all | solution.py:574
  115.6 0.7 add.31
  (38 shorter events, 1.8 us)
Async XLA Ops:
  2.5 26.9 %collective-permute-start.2 = (f32[2,192,128]{2,1,0:T(8,128)S(1)}, f32[2,192,128]{2,1,0:T(8,128)S(1)}, u32[]{:S(2)}, u32[]{:S(2)}) collective-permute-start(f32[2,192,128]{2,1,0:T(8,128)S(1)} %get-tuple-element.50), channel_id=1, source_target_pairs={{1,0},{0,1},{3,2},{2,3},{5,4},{4,5},{7,6},{6,7},{9,8},{8,9},{11,10... | collective-permute-start | bytes 589832 | tf_op jit(solution)/shard_map/ppermute | solution.py:482
  2.6 28.8 %all-to-all-start = ((f32[32,8,128]{2,1,0:T(8,128)}), f32[32,8,128]{2,1,0:T(8,128)S(1)}, u32[]{:S(2)}, u32[]{:S(2)}) async-start(f32[32,8,128]{2,1,0:T(8,128)} %get-tuple-element.61), calls=%async_computation | async-start | bytes 262144 | tf_op jit(solution)/shard_map/all_to_all | solution.py:500
  13.6 15.7 %collective-permute-start = (f32[2,24,128]{2,1,0:T(8,128)S(1)}, f32[2,24,128]{2,1,0:T(8,128)S(1)}, u32[]{:S(2)}, u32[]{:S(2)}) collective-permute-start(f32[2,24,128]{2,1,0:T(8,128)S(1)} %get-tuple-element.48), channel_id=1, source_target_pairs={{16,0},{32,16},{48,32},{64,48},{80,64},{96,80},{112,96},{128,112},... | collective-permute-start | bytes 73736 | tf_op jit(solution)/shard_map/ppermute | solution.py:482
  19.8 9.6 %collective-permute-start.1 = (f32[2,8,128]{2,1,0:T(8,128)S(1)}, f32[2,8,128]{2,1,0:T(8,128)S(1)}, u32[]{:S(2)}, u32[]{:S(2)}) collective-permute-start(f32[2,8,128]{2,1,0:T(8,128)S(1)} %get-tuple-element.49), channel_id=1, source_target_pairs={{2,0},{4,2},{6,4},{8,6},{10,8},{12,10},{14,12},{0,14},{3,1},{5,3},... | collective-permute-start | bytes 24584 | tf_op jit(solution)/shard_map/ppermute | solution.py:482
  26.1 3.3 %copy-start = (bf16[64,256,256]{2,1,0:T(8,128)(2,1)}, bf16[64,256,256]{2,1,0:T(8,128)(2,1)S(1)}, u32[]{:S(2)}) copy-start(bf16[64,256,256]{2,1,0:T(8,128)(2,1)S(1)} %get-tuple-element.77.table) | copy-start | bytes 25165828
  29.5 80.8 %copy-start.2 = (f32[1,1,1,32,10,128]{5,3,4,2,1,0:T(8,128)S(1)}, f32[1,1,1,32,10,128]{5,3,4,2,1,0:T(8,128)}, u32[]{:S(2)}) copy-start(f32[1,1,1,32,10,128]{5,3,4,2,1,0:T(8,128)} %param.14) | copy-start | bytes 491524
  29.6 80.8 %copy-start.3 = (f32[1,1,1,32,128]{4,3,2,1,0:T(8,128)S(1)}, f32[1,1,1,32,128]{4,3,2,1,0:T(8,128)}, u32[]{:S(2)}) copy-start(f32[1,1,1,32,128]{4,3,2,1,0:T(8,128)} %param.15) | copy-start | bytes 49156
  29.6 8.6 %collective-permute-start.5 = (f32[2,192,128]{2,1,0:T(8,128)S(1)}, f32[2,192,128]{2,1,0:T(8,128)S(1)}, u32[]{:S(2)}, u32[]{:S(2)}) collective-permute-start(f32[2,192,128]{2,1,0:T(8,128)S(1)} %get-tuple-element.58), channel_id=1, source_target_pairs={{0,1},{1,0},{2,3},{3,2},{4,5},{5,4},{6,7},{7,6},{8,9},{9,8},{10,11... | collective-permute-start | bytes 589832 | tf_op jit(solution)/shard_map/ppermute | solution.py:482
  29.7 8.5 %collective-permute-start.3 = (f32[2,24,128]{2,1,0:T(8,128)S(1)}, f32[2,24,128]{2,1,0:T(8,128)S(1)}, u32[]{:S(2)}, u32[]{:S(2)}) collective-permute-start(f32[2,24,128]{2,1,0:T(8,128)S(1)} %get-tuple-element.56), channel_id=1, source_target_pairs={{0,16},{16,32},{32,48},{48,64},{64,80},{80,96},{96,112},{112,128},... | collective-permute-start | bytes 73736 | tf_op jit(solution)/shard_map/ppermute | solution.py:482
  29.8 8.4 %collective-permute-start.4 = (f32[2,8,128]{2,1,0:T(8,128)S(1)}, f32[2,8,128]{2,1,0:T(8,128)S(1)}, u32[]{:S(2)}, u32[]{:S(2)}) collective-permute-start(f32[2,8,128]{2,1,0:T(8,128)S(1)} %get-tuple-element.57), channel_id=1, source_target_pairs={{0,2},{2,4},{4,6},{6,8},{8,10},{10,12},{12,14},{14,0},{1,3},{3,5},... | collective-permute-start | bytes 24584 | tf_op jit(solution)/shard_map/ppermute | solution.py:482
  38.1 77.5 %copy-start.4 = (f32[32,12,128]{2,0,1:T(8,128)S(1)}, f32[32,12,128]{2,0,1:T(8,128)}, u32[]{:S(2)}) copy-start(f32[32,12,128]{2,0,1:T(8,128)} %param.20) | copy-start | bytes 589828
  38.5 14.3 %collective-permute-start.8 = (f32[2,192,128]{2,1,0:T(8,128)S(1)}, f32[2,192,128]{2,1,0:T(8,128)S(1)}, u32[]{:S(2)}, u32[]{:S(2)}) collective-permute-start(f32[2,192,128]{2,1,0:T(8,128)S(1)} %get-tuple-element.65), channel_id=1, source_target_pairs={{1,0},{0,1},{3,2},{2,3},{5,4},{4,5},{7,6},{6,7},{9,8},{8,9},{11,10... | collective-permute-start | bytes 589832 | tf_op jit(solution)/shard_map/ppermute | solution.py:482
  38.6 14.2 %collective-permute-start.6 = (f32[2,24,128]{2,1,0:T(8,128)S(1)}, f32[2,24,128]{2,1,0:T(8,128)S(1)}, u32[]{:S(2)}, u32[]{:S(2)}) collective-permute-start(f32[2,24,128]{2,1,0:T(8,128)S(1)} %get-tuple-element.63), channel_id=1, source_target_pairs={{16,0},{32,16},{48,32},{64,48},{80,64},{96,80},{112,96},{128,112},... | collective-permute-start | bytes 73736 | tf_op jit(solution)/shard_map/ppermute | solution.py:482
  44.8 8.0 %collective-permute-start.7 = (f32[2,8,128]{2,1,0:T(8,128)S(1)}, f32[2,8,128]{2,1,0:T(8,128)S(1)}, u32[]{:S(2)}, u32[]{:S(2)}) collective-permute-start(f32[2,8,128]{2,1,0:T(8,128)S(1)} %get-tuple-element.64), channel_id=1, source_target_pairs={{2,0},{4,2},{6,4},{8,6},{10,8},{12,10},{14,12},{0,14},{3,1},{5,3},... | collective-permute-start | bytes 24584 | tf_op jit(solution)/shard_map/ppermute | solution.py:482
  53.0 14.0 %collective-permute-start.11 = (f32[2,192,128]{2,1,0:T(8,128)S(1)}, f32[2,192,128]{2,1,0:T(8,128)S(1)}, u32[]{:S(2)}, u32[]{:S(2)}) collective-permute-start(f32[2,192,128]{2,1,0:T(8,128)S(1)} %get-tuple-element.74), channel_id=1, source_target_pairs={{0,1},{1,0},{2,3},{3,2},{4,5},{5,4},{6,7},{7,6},{8,9},{9,8},{10,11... | collective-permute-start | bytes 589832 | tf_op jit(solution)/shard_map/ppermute | solution.py:482
  53.1 21.1 %all-to-all-start.1 = ((f32[32,8,128]{2,1,0:T(8,128)}), f32[32,8,128]{2,1,0:T(8,128)S(1)}, u32[]{:S(2)}, u32[]{:S(2)}) async-start(f32[32,8,128]{2,1,0:T(8,128)} %get-tuple-element.81), calls=%async_computation.1 | async-start | bytes 262144 | tf_op jit(solution)/shard_map/all_to_all | solution.py:553
  56.6 10.4 %collective-permute-start.9 = (f32[2,24,128]{2,1,0:T(8,128)S(1)}, f32[2,24,128]{2,1,0:T(8,128)S(1)}, u32[]{:S(2)}, u32[]{:S(2)}) collective-permute-start(f32[2,24,128]{2,1,0:T(8,128)S(1)} %get-tuple-element.72), channel_id=1, source_target_pairs={{0,16},{16,32},{32,48},{48,64},{64,80},{80,96},{96,112},{112,128},... | collective-permute-start | bytes 73736 | tf_op jit(solution)/shard_map/ppermute | solution.py:482
  59.3 5.7 %collective-permute-start.10 = (f32[2,8,128]{2,1,0:T(8,128)S(1)}, f32[2,8,128]{2,1,0:T(8,128)S(1)}, u32[]{:S(2)}, u32[]{:S(2)}) collective-permute-start(f32[2,8,128]{2,1,0:T(8,128)S(1)} %get-tuple-element.73), channel_id=1, source_target_pairs={{0,2},{2,4},{4,6},{6,8},{8,10},{10,12},{12,14},{14,0},{1,3},{3,5},... | collective-permute-start | bytes 24584 | tf_op jit(solution)/shard_map/ppermute | solution.py:482
  67.0 3.4 %copy-start.1 = (bf16[64,256,256]{2,1,0:T(8,128)(2,1)S(1)}, bf16[64,256,256]{2,1,0:T(8,128)(2,1)}, u32[]{:S(2)}) copy-start(bf16[64,256,256]{2,1,0:T(8,128)(2,1)} %copy-done) | copy-start | bytes 25165828
  72.6 1.5 %collective-permute-start.12 = (f32[384,128]{1,0:T(8,128)S(1)}, f32[384,128]{1,0:T(8,128)S(1)}, u32[]{:S(2)}, u32[]{:S(2)}) collective-permute-start(f32[384,128]{1,0:T(8,128)S(1)} %get-tuple-element.80), channel_id=1, source_target_pairs={{1,0},{0,1},{3,2},{2,3},{5,4},{4,5},{7,6},{6,7},{9,8},{8,9},{11,10... | collective-permute-start | bytes 589832 | tf_op jit(solution)/shard_map/ppermute | solution.py:564
  86.3 5.1 %collective-permute-start.15 = (f32[48,128]{1,0:T(8,128)S(1)}, f32[48,128]{1,0:T(8,128)S(1)}, u32[]{:S(2)}, u32[]{:S(2)}) collective-permute-start(f32[48,128]{1,0:T(8,128)S(1)} %reduce_sum.9), channel_id=1, source_target_pairs={{0,192},{16,208},{32,224},{48,240},{64,128},{80,144},{96,160},{112... | collective-permute-start | bytes 73736 | tf_op jit(solution)/shard_map/ppermute | solution.py:455
  87.4 5.3 %collective-permute-start.14 = (f32[48,128]{1,0:T(8,128)S(1)}, f32[48,128]{1,0:T(8,128)S(1)}, u32[]{:S(2)}, u32[]{:S(2)}) collective-permute-start(f32[48,128]{1,0:T(8,128)S(1)} %reduce_sum.9), channel_id=1, source_target_pairs={{0,128},{16,144},{32,160},{48,176},{64,192},{80,208},{96,224},{112... | collective-permute-start | bytes 73736 | tf_op jit(solution)/shard_map/ppermute | solution.py:455
  87.9 4.8 %collective-permute-start.13 = (f32[48,128]{1,0:T(8,128)S(1)}, f32[48,128]{1,0:T(8,128)S(1)}, u32[]{:S(2)}, u32[]{:S(2)}) collective-permute-start(f32[48,128]{1,0:T(8,128)S(1)} %reduce_sum.9), channel_id=1, source_target_pairs={{0,64},{16,80},{32,96},{48,112},{64,0},{80,16},{96,32},{112,48},{1... | collective-permute-start | bytes 73736 | tf_op jit(solution)/shard_map/ppermute | solution.py:455
  92.7 6.9 %collective-permute-start.18 = (f32[48,128]{1,0:T(8,128)S(1)}, f32[48,128]{1,0:T(8,128)S(1)}, u32[]{:S(2)}, u32[]{:S(2)}) collective-permute-start(f32[48,128]{1,0:T(8,128)S(1)} %add_add_fusion.1), channel_id=1, source_target_pairs={{0,48},{16,32},{32,16},{48,0},{64,112},{80,96},{96,80},{112,64},{1... | collective-permute-start | bytes 73736 | tf_op jit(solution)/shard_map/ppermute | solution.py:455
  94.9 7.7 %collective-permute-start.17 = (f32[48,128]{1,0:T(8,128)S(1)}, f32[48,128]{1,0:T(8,128)S(1)}, u32[]{:S(2)}, u32[]{:S(2)}) collective-permute-start(f32[48,128]{1,0:T(8,128)S(1)} %add_add_fusion.1), channel_id=1, source_target_pairs={{0,32},{16,48},{32,0},{48,16},{64,96},{80,112},{96,64},{112,80},{1... | collective-permute-start | bytes 73736 | tf_op jit(solution)/shard_map/ppermute | solution.py:455
  99.7 4.7 %collective-permute-start.16 = (f32[48,128]{1,0:T(8,128)S(1)}, f32[48,128]{1,0:T(8,128)S(1)}, u32[]{:S(2)}, u32[]{:S(2)}) collective-permute-start(f32[48,128]{1,0:T(8,128)S(1)} %add_add_fusion.1), channel_id=1, source_target_pairs={{0,16},{16,0},{32,48},{48,32},{64,80},{80,64},{96,112},{112,96},{1... | collective-permute-start | bytes 73736 | tf_op jit(solution)/shard_map/ppermute | solution.py:455
  105.1 10.5 %all-to-all-start.3 = ((f32[8,48,128]{2,1,0:T(8,128)}), f32[8,48,128]{2,1,0:T(8,128)S(1)}, u32[]{:S(2)}, u32[]{:S(2)}) async-start(f32[8,48,128]{2,1,0:T(8,128)} %broadcast_in_dim.2), calls=%async_computation.3 | async-start | bytes 393216 | tf_op jit(solution)/shard_map/all_to_all | solution.py:574

commit v3 on v2

--- a/solution.py
+++ b/solution.py
@@ -1,3 +1,4 @@
+import functools
 import math
 
 import jax
@@ -151,14 +152,13 @@
     first_layers(e_out, out_x, out_y, out_z)
     copies[1].wait()
     lower, lasing, upper = state[7], state[8], state[9]
-    for comp in range(3):
-        polar = state[comp]
-        packed[:, comp] = keep_rate * state[3 + comp] - spring * polar
-        packed[:, 3 + comp] = polar
-    packed[:, 6] = lasing - lower
     lasing_free = lasing + time_step * (upper / upper_life - lasing / lasing_life)
     lower_free = lower + time_step * (lasing / lasing_life - lower / lower_life)
-    packed[:, 7] = lasing_free - lower_free
+    polar = [state[comp] for comp in range(3)]
+    free = [keep_rate * state[3 + comp] - spring * polar[comp] for comp in range(3)]
+    for field, value in enumerate(free + [lasing - lower] + polar + [lasing_free - lower_free]):
+        for owner in range(SLOTS // 2):
+            packed[owner, 2 * field : 2 * field + 2] = value[2 * owner : 2 * owner + 2]
     copies[2].wait()
     copies[3].wait()
 
@@ -188,137 +188,179 @@
     return first, second, third
 
 
-def row_hits(offsets, width):
-    return row_index(ROWS, width) == (offsets >> 7)
-
-
-def lane_hits(offsets, width):
-    hits = row_index(CZ, width) == (offsets & (CZ - 1))
+HALF = ROWS // 2
+WIDE = 2 * CZ
+
+
+def wide_hits(offsets, width):
+    hits = row_index(WIDE, width) == (offsets & (WIDE - 1))
     return hits.astype(F32).astype(BF16)
 
 
-GROUP = 4
-
-
-def scatter_kernel(placed, fields_ref, dense, total, spots, rows):
-    total[...] = jnp.zeros_like(total)
-
+def tall_hits(offsets, width):
+    return row_index(HALF, width) == (offsets >> 8)
+
+
+GROUP = 8
+
+
+def scatter_kernel(first, placed, fields_ref, dense, total, spots, columns):
     def group(index, carry):
         lines = placed[pl.ds(GROUP * index, GROUP)]
         for slot in range(GROUP):
             line = lines[slot : slot + 1]
-            hits = row_hits(line, CZ).astype(F32).astype(BF16)
-            lanes = lane_hits(line, CZ).reshape(8, 16, CZ)
-            for place, part in enumerate(split_parts(fields_ref[GROUP * index + slot])):
+            hits = wide_hits(line, CZ)
+            tall = tall_hits(line, CZ).astype(F32).astype(BF16).reshape(6, 16, CZ)
+            values = fields_ref[
+                (GROUP // 2) * index + slot // 2, pl.ds(2 * first + slot % 2, 4, 2), :
+            ]
+            for place, part in enumerate(split_parts(values)):
                 across = (place * GROUP + slot) * CZ
-                rows[:, across : across + CZ] = hits
+                columns[:, across : across + CZ] = hits
                 part = part.astype(F32)
-                for field in range(8):
-                    line = jnp.broadcast_to(part[field : field + 1], (16, CZ)).astype(BF16)
-                    spots[field * CZ : (field + 1) * CZ, across : across + CZ] = (
-                        lanes * line[None]
-                    ).reshape(CZ, CZ)
-        total[...] += lax.dot_general(
-            spots[...], rows[...], (((1,), (1,)), ((), ())), preferred_element_type=F32
+                for field in range(4):
+                    row = jnp.broadcast_to(part[field : field + 1], (16, CZ)).astype(BF16)
+                    spots[field * HALF : (field + 1) * HALF, across : across + CZ] = (
+                        tall * row[None]
+                    ).reshape(HALF, CZ)
+        got = lax.dot_general(
+            spots[...], columns[...], (((1,), (1,)), ((), ())), preferred_element_type=F32
         )
+
+        @pl.when(index == 0)
+        def _():
+            total[...] = got
+
+        @pl.when(index > 0)
+        def _():
+            total[...] += got
+
         return carry
 
     lax.fori_loop(0, SLOTS // GROUP, group, 0)
-    for field in range(8):
-        dense[field] = jnp.transpose(total[field * CZ : (field + 1) * CZ])
+    for field in range(4):
+        got = total[field * HALF : (field + 1) * HALF]
+        dense[field, pl.ds(0, HALF, 2), :] = got[:, :CZ]
+        dense[field, pl.ds(1, HALF, 2), :] = got[:, CZ:]
+
+
+def scattered(first, placed, fields, name):
+    return call(
+        functools.partial(scatter_kernel, first),
+        shape(4, ROWS, CZ),
+        (placed, fields),
+        scratch=[
+            pltpu.VMEM((4 * HALF, WIDE), F32),
+            pltpu.VMEM((4 * HALF, 2 * GROUP * CZ), BF16),
+            pltpu.VMEM((WIDE, 2 * GROUP * CZ), BF16),
+        ],
+        name=name,
+    )
 
 
 def electric_kernel(
-    e_ref, h_ref, face_x, face_y, face_z, eps_ref, dense, e_out, out_x, out_y, out_z, source_out
+    e_ref, h_ref, face_x, face_y, face_z, eps_ref, dense, e_out, out_x, out_y, out_z, rates
 ):
     curls = electric_curl(h_ref, face_x, face_y, face_z)
     scaled = time_step * eps_ref[...]
-    inversion = dense[6]
+    inversion = dense[3]
     power = jnp.zeros_like(inversion)
-    rates = []
     for comp in range(3):
         field = e_ref[comp]
         rate = dense[comp] + gain_push * inversion * field
         power = power + field * rate
-        rates.append(rate)
+        rates[comp] = rate
         e_out[comp] = field + scaled * (curls[comp] - rate)
-    later = dense[7] + (2.0 * time_step * cross_rate) * power
-    for comp in range(3):
-        polar = dense[3 + comp] + time_step * rates[comp]
-        free = keep_rate * rates[comp] - spring * polar
-        source_out[comp] = free + gain_push * later * e_out[comp]
+    rates[3] = power
     first_layers(e_out, out_x, out_y, out_z)
 
 
+def paired(ref, comp):
+    return jnp.concatenate(
+        [ref[comp, pl.ds(0, HALF, 2), :], ref[comp, pl.ds(1, HALF, 2), :]], axis=1
+    )
+
+
 def stacked(fields):
-    high, low = split_parts(jnp.concatenate(fields, axis=0))
-    return jnp.concatenate([high, low], axis=1)
-
-
-def gather_lines(values, offsets, width):
-    lanes = lane_hits(offsets, width)
-    rows = row_hits(offsets, width)
-    picked = jnp.dot(
-        values, jnp.concatenate([lanes, lanes], axis=0), preferred_element_type=F32
-    )
+    return split_parts(jnp.concatenate([paired(ref, comp) for ref, comp in fields], axis=0))
+
+
+def gather_lines(high, low, offsets, width):
+    hits = wide_hits(offsets, width)
+    tall = tall_hits(offsets, width)
+    picked = jnp.dot(high, hits, preferred_element_type=F32)
+    picked = picked + jnp.dot(low, hits, preferred_element_type=F32)
     return [
         jnp.sum(
-            jnp.where(rows, picked[field * ROWS : (field + 1) * ROWS], 0.0), axis=0, keepdims=True
+            jnp.where(tall, picked[field * HALF : (field + 1) * HALF], 0.0), axis=0, keepdims=True
         )
-        for field in range(6)
+        for field in range(picked.shape[0] // HALF)
     ]
 
 
-def drive_kernel(e_old, e_new, h_new, placed, surf_ref, drives, sampled, values):
-    values[...] = stacked([e_old[c] for c in range(3)] + [e_new[c] for c in range(3)])
-    drives[...] = jnp.zeros_like(drives)
-
-    def pair(index, carry):
-        lines = placed[pl.ds(2 * index, 2)]
-        offsets = jnp.concatenate([lines[0:1], lines[1:2]], axis=1)
-        got = gather_lines(values[...], offsets, 2 * CZ)
-        for field in range(6):
-            drives[2 * index, field : field + 1] = got[field][:, :CZ]
-            drives[2 * index + 1, field : field + 1] = got[field][:, CZ:]
+TAKE = 4
+
+
+def gather_drive(field_ref, placed, drives, first, high, low):
+    high[...], low[...] = stacked([(field_ref, comp) for comp in range(3)])
+
+    def group(index, carry):
+        lines = placed[pl.ds(TAKE * index, TAKE)]
+        offsets = jnp.concatenate([lines[slot : slot + 1] for slot in range(TAKE)], axis=1)
+        got = gather_lines(high[...], low[...], offsets, TAKE * CZ)
+        for comp in range(3):
+            for slot in range(TAKE):
+                drives[TAKE * index + slot, first + comp : first + comp + 1] = got[comp][
+                    :, slot * CZ : (slot + 1) * CZ
+                ]
         return carry
 
-    lax.fori_loop(0, SLOTS // 2, pair, 0)
-    sample_rows(e_new, h_new, surf_ref, sampled)
+    lax.fori_loop(0, SLOTS // TAKE, group, 0)
 
 
 def sample_rows(e_ref, h_ref, surf_ref, sampled):
-    values = stacked([e_ref[c] for c in range(3)] + [h_ref[c] for c in range(3)])
-    got = gather_lines(values, surf_ref[...], CZ)
+    high, low = stacked([(ref, comp) for ref in (e_ref, h_ref) for comp in range(3)])
+    got = gather_lines(high, low, surf_ref[...], CZ)
     sampled[...] = jnp.zeros_like(sampled)
     for field in range(6):
         sampled[field : field + 1] = got[field]
 
 
-def table_kernel(
+def drive_kernel(e_ref, h_ref, placed, surf_ref, before, drives, sampled, high, low):
+    drives[...] = before[...]
+    gather_drive(e_ref, placed, drives, 3, high, low)
+    sample_rows(e_ref, h_ref, surf_ref, sampled)
+
+
+def times(left, right):
+    return (left[0] * right[0] - left[1] * right[1], left[1] * right[0] + left[0] * right[1])
+
+
+def early_kernel(
     count_ref,
     owner_hbm,
     offsets_ref,
     surf_ref,
     units_ref,
-    table,
+    e_ref,
+    placed,
+    drives,
+    surf_out,
+    starts,
+    turn,
     factors,
-    placed,
-    surf_out,
     owner_ref,
     sem,
+    high,
+    low,
 ):
     copy = pltpu.make_async_copy(owner_hbm, owner_ref, sem)
     copy.start()
-    copy.wait()
-    count = count_ref[0]
-    for slot in range(SLOTS):
-        line = offsets_ref[slot : slot + 1]
-        placed[pl.ds(owner_ref[0, slot], 1)] = jnp.where(slot < count, line, -1)
-    omega = freq_low + freq_pitch * row_index(FREQ, DIRS).astype(F32)
-    for step in range(STEPS):
-        moment = omega * ((step + 1) * time_step)
-        factors[2 * step] = jnp.cos(moment)
-        factors[2 * step + 1] = jnp.sin(moment)
+    lanes = lax.broadcasted_iota(jnp.int32, (8, DIRS), 1)
+    omega = freq_low + freq_pitch * (lanes & (FREQ - 1)).astype(F32)
+    moment = omega * jnp.where(lanes < FREQ, time_step, 2.0 * time_step)
+    for place, value in enumerate((jnp.cos(moment), jnp.sin(moment))):
+        factors[place] = jnp.transpose(jnp.broadcast_to(value[0:1], (DIRS, DIRS)))
     cells = surf_ref[...]
     surf_out[...] = cells
     rows = cells >> 7
@@ -331,27 +373,30 @@
         place = cell.astype(F32) - 0.5 * (size - 1)
         column = jnp.transpose(jnp.broadcast_to(place, (CZ, CZ)))
         along = along + column * units_ref[axis : axis + 1]
-    tall = 32
-    for block in range(CZ // tall):
-        part = along[block * tall : (block + 1) * tall]
-        turn_re = jnp.cos(freq_pitch * part)
-        turn_im = jnp.sin(freq_pitch * part)
-        now_re = jnp.cos(freq_low * part)
-        now_im = jnp.sin(freq_low * part)
-
-        def step(freq, now, block=block, turn_re=turn_re, turn_im=turn_im):
-            now_re, now_im = now
-            for place, value in ((0, now_re), (1, now_im)):
-                high, low = split_parts(value)
-                across = pl.ds(place * DIRS, DIRS)
-                table[freq, pl.ds(block * tall, tall), across] = high
-                table[freq, pl.ds(CZ + block * tall, tall), across] = low
-            return (
-                now_re * turn_re - now_im * turn_im,
-                now_im * turn_re + now_re * turn_im,
-            )
-
-        lax.fori_loop(0, FREQ, step, (now_re, now_im))
+    angle = (0.25 * freq_pitch) * along
+    square = angle * angle
+    cosine = 1.0 + square * (
+        -1 / 2 + square * (1 / 24 + square * (-1 / 720 + square * (1 / 40320)))
+    )
+    sine = angle * (
+        1.0 + square * (-1 / 6 + square * (1 / 120 + square * (-1 / 5040 + square * (1 / 362880))))
+    )
+    two = times((cosine, sine), (cosine, sine))
+    powers = {1: times(two, two)}
+    for power in (2, 4, 8, 16, 32):
+        powers[power] = times(powers[power // 2], powers[power // 2])
+    low_start = times(times(powers[16], powers[8]), times(powers[4], powers[2]))
+    high_start = times(low_start, powers[32])
+    turn[0], turn[1] = powers[1]
+    starts[0], starts[1] = low_start
+    starts[2], starts[3] = high_start
+    copy.wait()
+    count = count_ref[0]
+    for slot in range(SLOTS):
+        line = offsets_ref[slot : slot + 1]
+        placed[pl.ds(owner_ref[0, slot], 1)] = jnp.where(slot < count, line, -1)
+    drives[...] = jnp.zeros_like(drives)
+    gather_drive(e_ref, placed, drives, 0, high, low)
 
 
 def final_kernel(
@@ -361,20 +406,27 @@
     face_y,
     face_z,
     eps_ref,
-    source,
+    rates,
+    dense,
     surf_ref,
     early_ref,
-    table,
+    starts,
+    turn,
     factors,
     e_out,
     keep_out,
     send_out,
     late,
+    now,
 ):
     curls = electric_curl(h_ref, face_x, face_y, face_z)
     scaled = time_step * eps_ref[...]
+    later = dense[3] + (2.0 * time_step * cross_rate) * rates[3]
     for comp in range(3):
-        e_out[comp] = e_ref[comp] + scaled * (curls[comp] - source[comp])
+        field = e_ref[comp]
+        polar = dense[comp] + time_step * rates[comp]
+        rate = keep_rate * rates[comp] - spring * polar + gain_push * later * field
+        e_out[comp] = field + scaled * (curls[comp] - rate)
     sample_rows(e_out, h_ref, surf_ref, late)
     scale = 1.0 / math.sqrt(STEPS * CZ * 256)
     high, low = split_parts(scale * jnp.concatenate([early_ref[...], late[...]], axis=0))
@@ -387,15 +439,29 @@
     )
     own = lax.axis_index("gz")
     for side, out in ((1, send_out), (0, keep_out)):
-        base = lax.rem(own + side, 2) * (FREQ // 2)
+        target = lax.rem(own + side, 2)
+        now[0] = starts[2 * target]
+        now[1] = starts[2 * target + 1]
         for freq in range(FREQ // 2):
-            both = jnp.dot(left, table[base + freq], preferred_element_type=F32)
+            here = (now[0], now[1])
+            re_high, re_low = split_parts(here[0])
+            im_high, im_low = split_parts(here[1])
+            right = jnp.concatenate(
+                [
+                    jnp.concatenate([re_high, im_high], axis=1),
+                    jnp.concatenate([re_low, im_low], axis=1),
+                ],
+                axis=0,
+            )
+            now[0], now[1] = times(here, (turn[0], turn[1]))
+            both = jnp.dot(left, right, preferred_element_type=F32)
             both = both[0:16] + both[16:32]
             real = jnp.zeros((8, DIRS), F32)
             imag = jnp.zeros((8, DIRS), F32)
             for step in range(STEPS):
-                cosine = factors[2 * step, pl.ds(base + freq, 1)]
-                sine = factors[2 * step + 1, pl.ds(base + freq, 1)]
+                row = pl.ds(step * FREQ + target * (FREQ // 2) + freq, 1)
+                cosine = factors[0, row]
+                sine = factors[1, row]
                 upper = both[8 * step : 8 * step + 8, 0:DIRS]
                 under = both[8 * step : 8 * step + 8, DIRS:]
                 real = real + (cosine * upper + sine * under)
@@ -485,7 +551,7 @@
 
     *near, packed, e_old, h_old, eps = call(
         prepare_kernel,
-        faces + (shape(SLOTS, 8, CZ), dense, dense, shape(ROWS, CZ)),
+        faces + (shape(SLOTS // 2, 16, CZ), dense, dense, shape(ROWS, CZ)),
         stay(
             efield.reshape(3, ROWS, CZ),
             state,
@@ -498,13 +564,16 @@
     )
     near = shifted(near, down)
     fields = lax.all_to_all(packed, "gx", 0, 0, tiled=True)
-    table, factors, placed, surf = call(
-        table_kernel,
+    halves = [pltpu.VMEM((3 * HALF, WIDE), BF16)] * 2
+    placed, before, surf, starts, turn, factors = call(
+        early_kernel,
         (
-            shape(FREQ, 2 * CZ, 2 * DIRS, dtype=BF16),
-            shape(2 * STEPS, FREQ, DIRS),
             shape(SLOTS, CZ, dtype=jnp.int32),
+            shape(SLOTS, 8, CZ),
             shape(1, CZ, dtype=jnp.int32),
+            shape(4, CZ, DIRS),
+            shape(2, CZ, DIRS),
+            shape(2, STEPS * FREQ, DIRS),
         ),
         [gain_count.reshape(1)]
         + stay(
@@ -512,53 +581,42 @@
             gain_offsets.reshape(SLOTS, CZ),
             surf_offsets.reshape(1, CZ),
             jnp.asarray(directions(DIRS)),
-        ),
-        in_specs=[pl.BlockSpec(memory_space=pltpu.SMEM), hbm, vmem, vmem, vmem],
-        scratch=[pltpu.SMEM((1, SLOTS), jnp.int32), pltpu.SemaphoreType.DMA],
-        vmem=24,
-        moved=8 * MIB,
-        name="table",
+        )
+        + [e_old],
+        in_specs=[pl.BlockSpec(memory_space=pltpu.SMEM), hbm, vmem, vmem, vmem, vmem],
+        scratch=[pltpu.SMEM((1, SLOTS), jnp.int32), pltpu.SemaphoreType.DMA] + halves,
+        name="early",
     )
     *near, placed = lax.optimization_barrier((*near, placed))
     h_one, *edge = call(magnetic_kernel, (dense,) + faces, (e_old, h_old, *near), name="magnetic")
     edge = shifted(edge, up)
-    spread_fields = call(
-        scatter_kernel,
-        shape(8, ROWS, CZ),
-        (placed, fields),
-        scratch=[
-            pltpu.VMEM((8 * CZ, ROWS), F32),
-            pltpu.VMEM((8 * CZ, 2 * GROUP * CZ), BF16),
-            pltpu.VMEM((ROWS, 2 * GROUP * CZ), BF16),
-        ],
-        name="scatter",
-    )
-    e_one, *near, source = call(
+    spread_now = scattered(0, placed, fields, "scatter")
+    e_one, *near, rates = call(
         electric_kernel,
-        (dense,) + faces + (dense,),
-        (e_old, h_one, *edge, eps, spread_fields),
+        (dense,) + faces + (shape(4, ROWS, CZ),),
+        (e_old, h_one, *edge, eps, spread_now),
         name="electric",
     )
     near = shifted(near, down)
     drives, early = call(
         drive_kernel,
         (shape(SLOTS, 8, CZ), shape(8, CZ)),
-        (e_old, e_one, h_one, placed, surf),
-        scratch=[pltpu.VMEM((6 * ROWS, 2 * CZ), BF16)],
+        (e_one, h_one, placed, surf, before),
+        scratch=halves,
         name="drive",
     )
     *near, early = lax.optimization_barrier((*near, early))
     h_two, *edge = call(magnetic_kernel, (dense,) + faces, (e_one, h_one, *near), name="magnetic2")
     edge = shifted(edge, up)
     back = lax.all_to_all(drives, "gx", 0, 0, tiled=True)
+    placed, fields, early = lax.optimization_barrier((placed, fields, early))
+    spread_next = scattered(4, placed, fields, "scatter2")
     part = shape(12 * FREQ // 2, DIRS)
     e_two, keep, send = call(
         final_kernel,
         (dense, part, part),
-        (e_one, h_two, *edge, eps, source, surf, early, table, factors),
-        scratch=[pltpu.VMEM((8, CZ), F32)],
-        vmem=24,
-        moved=8 * MIB,
+        (e_one, h_two, *edge, eps, rates, spread_next, surf, early, starts, turn, factors),
+        scratch=[pltpu.VMEM((8, CZ), F32), pltpu.VMEM((2, CZ, DIRS), F32)],
         name="final",
     )
     chip = keep + lax.ppermute(send, "gz", down[2])
@@ -571,16 +629,17 @@
     total = all_reduce(
         total, "gx", lambda k: [(a * 4 + z, a * 4 + (z ^ k)) for a in range(4) for z in range(4)]
     )
-    gathered = lax.all_to_all(
-        jnp.broadcast_to(total[None], (8, 48, DIRS)), "gy", 0, 0, tiled=True
-    )
-    far_out = far_acc + jnp.transpose(gathered.reshape(12, FREQ // 2, DIRS), (1, 0, 2))
-    state_out, e_out, h_out = call(
+    results = call(
         atoms_kernel,
         (shape(10, SLOTS, CZ), dense, dense),
         (state, pump.reshape(SLOTS, CZ), back, e_two, h_two),
         name="atoms",
     )
+    total, state_out, e_out, h_out = lax.optimization_barrier((total, *results))
+    gathered = lax.all_to_all(
+        jnp.broadcast_to(total[None], (8, 48, DIRS)), "gy", 0, 0, tiled=True
+    )
+    far_out = far_acc + jnp.transpose(gathered.reshape(12, FREQ // 2, DIRS), (1, 0, 2))
     return (
         e_out.reshape(efield.shape),
         h_out.reshape(hfield.shape),

time: 117 us -> 104 us (0.89)
  blocking collectives: 12.1 us -> 20 us
  local copies, waits for them, and re-layouts: 7.35 us -> 0.03 us
  starting transfers between devices: 50.7 us -> 44.4 us
  waiting for transfers between devices: 20.4 us -> 15.7 us
  Pallas kernels: 23.6 us -> 20.8 us
    all_to_all x0 -> x1, blocking collectives: none -> 9.73 us  [local(): lax.all_to_all(jnp.broadcast_to(total[None], (8, 48, DIRS)), 'gy', 0, 0,...]
    unnamed x10 -> x6, local copies, waits for them, and re-layouts: 6.66 us -> 0.02 us
    all_to_all x1 -> x0, starting transfers between devices: 5.25 us -> none  [local(): lax.all_to_all(jnp.broadcast_to(total[None], (8, 48, DIRS)), 'gy', 0, 0,...]
    all_to_all x1 -> x0, waiting for transfers between devices: 4.31 us -> none  [local(): lax.all_to_all(jnp.broadcast_to(total[None], (8, 48, DIRS)), 'gy', 0, 0,...]
    pallas_call x9 -> x10, Pallas kernels: 23.6 us -> 20.8 us  [call(): pl.pallas_call(kernel, out_shape=outs, in_specs=in_specs or [pl.BlockSpec...]
    all_to_all x1, blocking collectives: 12.1 us -> 10.2 us  [local(): pieces = lax.all_to_all(chip.reshape(8, 48, DIRS), 'gy', 0, 0, tiled=True)]
  transfers between devices with their start and end apart: 22 -> 21, of which waited for: 8 -> 9; matrix products, arithmetic and copies ran while one was open for 0% -> 0% of each run, Pallas kernels for 18% -> 18%
where the time goes in v3:
time: 104 us; the launch traced here: 103 us
  starting transfers between devices  44.4 us (43%)
  Pallas kernels  20.8 us (20%)
  blocking collectives  20 us (19%)
  waiting for transfers between devices  15.7 us (15%)
  between operations  1.48 us (1%)
    pallas_call x10, Pallas kernels, call(): pl.pallas_call(kernel, out_shape=outs, in_specs=in_specs or [pl.BlockSpec...  20.8 us
    ppermute x12, starting transfers between devices, shifted(): lax.ppermute(part, axis, perm)  18.9 us
    all_to_all x1, starting transfers between devices, local(): fields = lax.all_to_all(packed, 'gx', 0, 0, tiled=True)  11 us
    ppermute x6, starting transfers between devices, all_reduce(): one, two, three = [lax.ppermute(value, axis, peers(k)) for k in (1, 2, 3)]  10.8 us
    all_to_all x1, blocking collectives, local(): pieces = lax.all_to_all(chip.reshape(8, 48, DIRS), 'gy', 0, 0, tiled=True)  10.2 us
    all_to_all x1, blocking collectives, local(): lax.all_to_all(jnp.broadcast_to(total[None], (8, 48, DIRS)), 'gy', 0, 0,...  9.73 us
    ppermute x12, waiting for transfers between devices, shifted(): lax.ppermute(part, axis, perm)  7.69 us
    ppermute x6, waiting for transfers between devices, all_reduce(): one, two, three = [lax.ppermute(value, axis, peers(k)) for k in (1, 2, 3)]  6.6 us
  transfers between devices with their start and end apart: 21, of which 9 were waited for; matrix products, arithmetic and copies ran while one was open for 0% of the time, Pallas kernels for 18%

profile of v3, /device:TPU:8, one launch (start us, length us, event | category | flops | bytes accessed | tf_op | source)
XLA Modules:
  0.0 103.2 jit_solution(13176559319663066195)
XLA Ops:
  0.6 1.8 %prepare.1 = (f32[2,24,128]{2,1,0:T(8,128)S(1)}, f32[2,8,128]{2,1,0:T(8,128)S(1)}, f32[2,192,128]{2,1,0:T(8,128)S(1)}, f32[16,16,128]{2,1,0:T(8,128)}, f32[3,192...) custom-call(f32[3,192,128]{2,1,0:T(8,128)} %bitcast.26, f32[10,32,128]{2,1,0:T(8,128)} %bitcast.21, ...), custom_call_target="tpu_custom_call" | custom-call | bytes 2097152 | tf_op jit(solution)/shard_map/prepare/pallas_call | solution.py:48
  2.6 11.0 %all-to-all-start = ((f32[16,16,128]{2,1,0:T(8,128)}), f32[16,16,128]{2,1,0:T(8,128)S(1)}, u32[]{:S(2)}, u32[]{:S(2)}) async-start(f32[16,16,128]{2,1,0:T(8,128)} %get-tuple-element.70), calls=%async_computation | async-start | bytes 262144 | tf_op jit(solution)/shard_map/all_to_all | solution.py:566
  13.6 6.2 %collective-permute-start = (f32[2,24,128]{2,1,0:T(8,128)S(1)}, f32[2,24,128]{2,1,0:T(8,128)S(1)}, u32[]{:S(2)}, u32[]{:S(2)}) collective-permute-start(f32[2,24,128]{2,1,0:T(8,128)S(1)} %get-tuple-element.57), channel_id=1, source_target_pairs={{16,0},{32,16},{48,32},{64,48},{80,64},{96,80},{112,96},{128,112},... | collective-permute-start | bytes 73736 | tf_op jit(solution)/shard_map/ppermute | solution.py:548
  19.8 0.4 collective-permute-start.1
  20.9 4.3 %early.1 = (s32[32,128]{1,0:T(8,128)S(1)}, f32[32,8,128]{2,1,0:T(8,128)S(1)}, s32[1,128]{1,0:T(1,128)S(1)}, f32[4,128,128]{2,1,0:T(8,128)S(1)}, f32[2,128,128]{2,1,0:T(8,128)S(1)}, /*index=5*/f32[2,128,128]{2,1,0:T(8,128)S(1)}) custom-call(s32[1]{0:T(128)} %bitcast.20.count_ref, s32[1,32]{1,0:T(1,128)} %bitcast.30, s32[32,128]{1,0:T(8,128)} %bitcast.29, ...), custom_call_target="tpu_custom_call" | custom-call | bytes 2097152 | tf_op jit(solution)/shard_map/early/pallas_call | solution.py:48
  25.6 1.7 %collective-permute-start.4 = (f32[2,8,128]{2,1,0:T(8,128)S(1)}, f32[2,8,128]{2,1,0:T(8,128)S(1)}, u32[]{:S(2)}, u32[]{:S(2)}) collective-permute-start(f32[2,8,128]{2,1,0:T(8,128)S(1)} %get-tuple-element.66), channel_id=1, source_target_pairs={{0,2},{2,4},{4,6},{6,8},{8,10},{10,12},{12,14},{14,0},{1,3},{3,5},... | collective-permute-start | bytes 24584 | tf_op jit(solution)/shard_map/ppermute | solution.py:548
  27.3 3.2 %scatter.1.dense = f32[4,192,128]{2,1,0:T(8,128)S(1)} custom-call(s32[32,128]{1,0:T(8,128)S(1)} %get-tuple-element.87.placed, f32[16,16,128]{2,1,0:T(8,128)S(1)} %all-to-all-done.fields_ref), custom_call_target="tpu_custom_call" | custom-call | bytes 2097152 | tf_op jit(solution)/shard_map/scatter/pallas_call | solution.py:48
  30.4 0.3 collective-permute-done.4.face_y
  30.8 2.9 %collective-permute-done.3.face_x = f32[2,24,128]{2,1,0:T(8,128)S(1)} collective-permute-done((f32[2,24,128]{2,1,0:T(8,128)S(1)}, f32[2,24,128]{2,1,0:T(8,128)S(1)}, u32[]{:S(2)}, u32[]{:S(2)}) %collective-permute-start.3) | collective-permute-done | bytes 24608 | tf_op jit(solution)/shard_map/ppermute | solution.py:548
  34.0 3.4 %collective-permute-start.6 = (f32[2,24,128]{2,1,0:T(8,128)S(1)}, f32[2,24,128]{2,1,0:T(8,128)S(1)}, u32[]{:S(2)}, u32[]{:S(2)}) collective-permute-start(f32[2,24,128]{2,1,0:T(8,128)S(1)} %get-tuple-element.72), channel_id=1, source_target_pairs={{16,0},{32,16},{48,32},{64,48},{80,64},{96,80},{112,96},{128,112},... | collective-permute-start | bytes 73736 | tf_op jit(solution)/shard_map/ppermute | solution.py:548
  37.3 4.1 %collective-permute-start.7 = (f32[2,8,128]{2,1,0:T(8,128)S(1)}, f32[2,8,128]{2,1,0:T(8,128)S(1)}, u32[]{:S(2)}, u32[]{:S(2)}) collective-permute-start(f32[2,8,128]{2,1,0:T(8,128)S(1)} %get-tuple-element.73), channel_id=1, source_target_pairs={{2,0},{4,2},{6,4},{8,6},{10,8},{12,10},{14,12},{0,14},{3,1},{5,3},... | collective-permute-start | bytes 24584 | tf_op jit(solution)/shard_map/ppermute | solution.py:548
  41.5 3.6 %drive.1 = (f32[32,8,128]{2,1,0:T(8,128)}, f32[8,128]{1,0:T(8,128)S(1)}) custom-call(f32[3,192,128]{2,1,0:T(8,128)S(1)} %get-tuple-element.71.e_ref, f32[3,192,128]{2,1,0:T(8,128)S(1)} %get-tuple-element.64.h_ref, s32[32,128]{1,0:T(8,128)S(1)} %get-tuple-element.87.placed, s32[1,128]{1,0:T(1,128)S(1)} %get-tuple-element.75.surf_ref, ...), custom_call_target="tpu_custom_call" | custom-call | bytes 2097152 | tf_op jit(solution)/shard_map/drive/pallas_call | solution.py:48
  45.3 3.5 %all-to-all-start.1 = ((f32[32,8,128]{2,1,0:T(8,128)}), f32[32,8,128]{2,1,0:T(8,128)S(1)}, u32[]{:S(2)}, u32[]{:S(2)}) async-start(f32[32,8,128]{2,1,0:T(8,128)} %get-tuple-element.95), calls=%async_computation.1 | async-start | bytes 262144 | tf_op jit(solution)/shard_map/all_to_all | solution.py:611
  48.9 2.7 %collective-permute-start.9 = (f32[2,24,128]{2,1,0:T(8,128)S(1)}, f32[2,24,128]{2,1,0:T(8,128)S(1)}, u32[]{:S(2)}, u32[]{:S(2)}) collective-permute-start(f32[2,24,128]{2,1,0:T(8,128)S(1)} %get-tuple-element.82), channel_id=1, source_target_pairs={{0,16},{16,32},{32,48},{48,64},{64,80},{80,96},{96,112},{112,128},... | collective-permute-start | bytes 73736 | tf_op jit(solution)/shard_map/ppermute | solution.py:548
  51.6 3.2 %scatter2.1.dense = f32[4,192,128]{2,1,0:T(8,128)S(1)} custom-call(s32[32,128]{1,0:T(8,128)S(1)} %get-tuple-element.87.placed, f32[16,16,128]{2,1,0:T(8,128)S(1)} %all-to-all-done.fields_ref), custom_call_target="tpu_custom_call" | custom-call | bytes 2097152 | tf_op jit(solution)/shard_map/scatter2/pallas_call | solution.py:48
  54.7 1.1 %collective-permute-done.10.face_y = f32[2,8,128]{2,1,0:T(8,128)S(1)} collective-permute-done((f32[2,8,128]{2,1,0:T(8,128)S(1)}, f32[2,8,128]{2,1,0:T(8,128)S(1)}, u32[]{:S(2)}, u32[]{:S(2)}) %collective-permute-start.10) | collective-permute-done | bytes 8224 | tf_op jit(solution)/shard_map/ppermute | solution.py:548
  55.8 3.4 %collective-permute-done.9.face_x = f32[2,24,128]{2,1,0:T(8,128)S(1)} collective-permute-done((f32[2,24,128]{2,1,0:T(8,128)S(1)}, f32[2,24,128]{2,1,0:T(8,128)S(1)}, u32[]{:S(2)}, u32[]{:S(2)}) %collective-permute-start.9) | collective-permute-done | bytes 24608 | tf_op jit(solution)/shard_map/ppermute | solution.py:548
  59.2 3.2 %final.1 = (f32[3,192,128]{2,1,0:T(8,128)S(1)}, f32[384,128]{1,0:T(8,128)S(1)}, f32[384,128]{1,0:T(8,128)S(1)}) custom-call(f32[3,192,128]{2,1,0:T(8,128)S(1)} %get-tuple-element.71.e_ref, f32[3,192,128]{2,1,0:T(8,128)S(1)} %get-tuple-element.81.h_ref, f32[2,24,128]{2,1,0:T(8,128)S(1)} %collective-permute-done.9.face_x, ...), custom_call_target="tpu_custom_call" | custom-call | bytes 2097152 | tf_op jit(solution)/shard_map/final/pallas_call | solution.py:48
  62.5 1.4 %collective-permute-done.12 = f32[384,128]{1,0:T(8,128)S(1)} collective-permute-done((f32[384,128]{1,0:T(8,128)S(1)}, f32[384,128]{1,0:T(8,128)S(1)}, u32[]{:S(2)}, u32[]{:S(2)}) %collective-permute-start.12) | collective-permute-done | bytes 196640 | tf_op jit(solution)/shard_map/ppermute | solution.py:622
  64.0 10.2 %all_to_all.20 = f32[8,48,128]{2,1,0:T(8,128)S(1)} all-to-all(f32[8,48,128]{2,1,0:T(8,128)S(1)} %bitcast.24), channel_id=1, replica_groups=mesh['gx'=16,'gy'=8,'gz'=2] {'gy'}, dimensions={0} | all-to-all | bytes 393216 | tf_op jit(solution)/shard_map/all_to_all | solution.py:624
  74.2 1.7 %collective-permute-start.15 = (f32[48,128]{1,0:T(8,128)S(1)}, f32[48,128]{1,0:T(8,128)S(1)}, u32[]{:S(2)}, u32[]{:S(2)}) collective-permute-start(f32[48,128]{1,0:T(8,128)S(1)} %reduce_sum.9), channel_id=1, source_target_pairs={{0,192},{16,208},{32,224},{48,240},{64,128},{80,144},{96,160},{112... | collective-permute-start | bytes 73736 | tf_op jit(solution)/shard_map/ppermute | solution.py:521
  75.9 0.4 collective-permute-start.14
  76.3 2.1 %collective-permute-start.13 = (f32[48,128]{1,0:T(8,128)S(1)}, f32[48,128]{1,0:T(8,128)S(1)}, u32[]{:S(2)}, u32[]{:S(2)}) collective-permute-start(f32[48,128]{1,0:T(8,128)S(1)} %reduce_sum.9), channel_id=1, source_target_pairs={{0,64},{16,80},{32,96},{48,112},{64,0},{80,16},{96,32},{112,48},{1... | collective-permute-start | bytes 73736 | tf_op jit(solution)/shard_map/ppermute | solution.py:521
  78.4 0.9 collective-permute-done.15
  79.4 1.9 %collective-permute-done.14 = f32[48,128]{1,0:T(8,128)S(1)} collective-permute-done((f32[48,128]{1,0:T(8,128)S(1)}, f32[48,128]{1,0:T(8,128)S(1)}, u32[]{:S(2)}, u32[]{:S(2)}) %collective-permute-start.14) | collective-permute-done | bytes 24608 | tf_op jit(solution)/shard_map/ppermute | solution.py:521
  81.3 2.1 %collective-permute-start.18 = (f32[48,128]{1,0:T(8,128)S(1)}, f32[48,128]{1,0:T(8,128)S(1)}, u32[]{:S(2)}, u32[]{:S(2)}) collective-permute-start(f32[48,128]{1,0:T(8,128)S(1)} %add_add_fusion.1), channel_id=1, source_target_pairs={{0,48},{16,32},{32,16},{48,0},{64,112},{80,96},{96,80},{112,64},{1... | collective-permute-start | bytes 73736 | tf_op jit(solution)/shard_map/ppermute | solution.py:521
  83.4 4.6 %collective-permute-start.17 = (f32[48,128]{1,0:T(8,128)S(1)}, f32[48,128]{1,0:T(8,128)S(1)}, u32[]{:S(2)}, u32[]{:S(2)}) collective-permute-start(f32[48,128]{1,0:T(8,128)S(1)} %add_add_fusion.1), channel_id=1, source_target_pairs={{0,32},{16,48},{32,0},{48,16},{64,96},{80,112},{96,64},{112,80},{1... | collective-permute-start | bytes 73736 | tf_op jit(solution)/shard_map/ppermute | solution.py:521
  88.0 1.0 atoms.1
  88.9 2.2 %collective-permute-done.17 = f32[48,128]{1,0:T(8,128)S(1)} collective-permute-done((f32[48,128]{1,0:T(8,128)S(1)}, f32[48,128]{1,0:T(8,128)S(1)}, u32[]{:S(2)}, u32[]{:S(2)}) %collective-permute-start.17) | collective-permute-done | bytes 24608 | tf_op jit(solution)/shard_map/ppermute | solution.py:521
  91.1 1.6 %collective-permute-done.16 = f32[48,128]{1,0:T(8,128)S(1)} collective-permute-done((f32[48,128]{1,0:T(8,128)S(1)}, f32[48,128]{1,0:T(8,128)S(1)}, u32[]{:S(2)}, u32[]{:S(2)}) %collective-permute-start.16) | collective-permute-done | bytes 24608 | tf_op jit(solution)/shard_map/ppermute | solution.py:521
  92.7 9.7 %all_to_all.21 = f32[8,48,128]{2,1,0:T(8,128)S(1)} all-to-all(f32[8,48,128]{2,1,0:T(8,128)S(1)} %broadcast_in_dim.2), channel_id=1, replica_groups=mesh['gx'=16,'gy'=8,'gz'=2] {'gy'}, dimensions={0} | all-to-all | bytes 393216 | tf_op jit(solution)/shard_map/all_to_all | solution.py:639
  102.5 0.7 add.31
  (34 shorter events, 1.2 us)
Async XLA Ops:
  2.5 22.8 %collective-permute-start.2 = (f32[2,192,128]{2,1,0:T(8,128)S(1)}, f32[2,192,128]{2,1,0:T(8,128)S(1)}, u32[]{:S(2)}, u32[]{:S(2)}) collective-permute-start(f32[2,192,128]{2,1,0:T(8,128)S(1)} %get-tuple-element.59), channel_id=1, source_target_pairs={{1,0},{0,1},{3,2},{2,3},{5,4},{4,5},{7,6},{6,7},{9,8},{8,9},{11,10... | collective-permute-start | bytes 589832 | tf_op jit(solution)/shard_map/ppermute | solution.py:548
  2.6 24.7 %all-to-all-start = ((f32[16,16,128]{2,1,0:T(8,128)}), f32[16,16,128]{2,1,0:T(8,128)S(1)}, u32[]{:S(2)}, u32[]{:S(2)}) async-start(f32[16,16,128]{2,1,0:T(8,128)} %get-tuple-element.70), calls=%async_computation | async-start | bytes 262144 | tf_op jit(solution)/shard_map/all_to_all | solution.py:566
  13.6 11.6 %collective-permute-start = (f32[2,24,128]{2,1,0:T(8,128)S(1)}, f32[2,24,128]{2,1,0:T(8,128)S(1)}, u32[]{:S(2)}, u32[]{:S(2)}) collective-permute-start(f32[2,24,128]{2,1,0:T(8,128)S(1)} %get-tuple-element.57), channel_id=1, source_target_pairs={{16,0},{32,16},{48,32},{64,48},{80,64},{96,80},{112,96},{128,112},... | collective-permute-start | bytes 73736 | tf_op jit(solution)/shard_map/ppermute | solution.py:548
  19.8 5.4 %collective-permute-start.1 = (f32[2,8,128]{2,1,0:T(8,128)S(1)}, f32[2,8,128]{2,1,0:T(8,128)S(1)}, u32[]{:S(2)}, u32[]{:S(2)}) collective-permute-start(f32[2,8,128]{2,1,0:T(8,128)S(1)} %get-tuple-element.58), channel_id=1, source_target_pairs={{2,0},{4,2},{6,4},{8,6},{10,8},{12,10},{14,12},{0,14},{3,1},{5,3},... | collective-permute-start | bytes 24584 | tf_op jit(solution)/shard_map/ppermute | solution.py:548
  25.4 8.2 %collective-permute-start.5 = (f32[2,192,128]{2,1,0:T(8,128)S(1)}, f32[2,192,128]{2,1,0:T(8,128)S(1)}, u32[]{:S(2)}, u32[]{:S(2)}) collective-permute-start(f32[2,192,128]{2,1,0:T(8,128)S(1)} %get-tuple-element.67), channel_id=1, source_target_pairs={{0,1},{1,0},{2,3},{3,2},{4,5},{5,4},{6,7},{7,6},{8,9},{9,8},{10,11... | collective-permute-start | bytes 589832 | tf_op jit(solution)/shard_map/ppermute | solution.py:548
  25.5 8.1 %collective-permute-start.3 = (f32[2,24,128]{2,1,0:T(8,128)S(1)}, f32[2,24,128]{2,1,0:T(8,128)S(1)}, u32[]{:S(2)}, u32[]{:S(2)}) collective-permute-start(f32[2,24,128]{2,1,0:T(8,128)S(1)} %get-tuple-element.65), channel_id=1, source_target_pairs={{0,16},{16,32},{32,48},{48,64},{64,80},{80,96},{96,112},{112,128},... | collective-permute-start | bytes 73736 | tf_op jit(solution)/shard_map/ppermute | solution.py:548
  25.6 5.2 %collective-permute-start.4 = (f32[2,8,128]{2,1,0:T(8,128)S(1)}, f32[2,8,128]{2,1,0:T(8,128)S(1)}, u32[]{:S(2)}, u32[]{:S(2)}) collective-permute-start(f32[2,8,128]{2,1,0:T(8,128)S(1)} %get-tuple-element.66), channel_id=1, source_target_pairs={{0,2},{2,4},{4,6},{6,8},{8,10},{10,12},{12,14},{14,0},{1,3},{3,5},... | collective-permute-start | bytes 24584 | tf_op jit(solution)/shard_map/ppermute | solution.py:548
  33.9 11.2 %collective-permute-start.8 = (f32[2,192,128]{2,1,0:T(8,128)S(1)}, f32[2,192,128]{2,1,0:T(8,128)S(1)}, u32[]{:S(2)}, u32[]{:S(2)}) collective-permute-start(f32[2,192,128]{2,1,0:T(8,128)S(1)} %get-tuple-element.74), channel_id=1, source_target_pairs={{1,0},{0,1},{3,2},{2,3},{5,4},{4,5},{7,6},{6,7},{9,8},{8,9},{11,10... | collective-permute-start | bytes 589832 | tf_op jit(solution)/shard_map/ppermute | solution.py:548
  34.0 11.1 %collective-permute-start.6 = (f32[2,24,128]{2,1,0:T(8,128)S(1)}, f32[2,24,128]{2,1,0:T(8,128)S(1)}, u32[]{:S(2)}, u32[]{:S(2)}) collective-permute-start(f32[2,24,128]{2,1,0:T(8,128)S(1)} %get-tuple-element.72), channel_id=1, source_target_pairs={{16,0},{32,16},{48,32},{64,48},{80,64},{96,80},{112,96},{128,112},... | collective-permute-start | bytes 73736 | tf_op jit(solution)/shard_map/ppermute | solution.py:548
  37.3 7.7 %collective-permute-start.7 = (f32[2,8,128]{2,1,0:T(8,128)S(1)}, f32[2,8,128]{2,1,0:T(8,128)S(1)}, u32[]{:S(2)}, u32[]{:S(2)}) collective-permute-start(f32[2,8,128]{2,1,0:T(8,128)S(1)} %get-tuple-element.73), channel_id=1, source_target_pairs={{2,0},{4,2},{6,4},{8,6},{10,8},{12,10},{14,12},{0,14},{3,1},{5,3},... | collective-permute-start | bytes 24584 | tf_op jit(solution)/shard_map/ppermute | solution.py:548
  45.2 14.0 %collective-permute-start.11 = (f32[2,192,128]{2,1,0:T(8,128)S(1)}, f32[2,192,128]{2,1,0:T(8,128)S(1)}, u32[]{:S(2)}, u32[]{:S(2)}) collective-permute-start(f32[2,192,128]{2,1,0:T(8,128)S(1)} %get-tuple-element.84), channel_id=1, source_target_pairs={{0,1},{1,0},{2,3},{3,2},{4,5},{5,4},{6,7},{7,6},{8,9},{9,8},{10,11... | collective-permute-start | bytes 589832 | tf_op jit(solution)/shard_map/ppermute | solution.py:548
  45.3 18.6 %all-to-all-start.1 = ((f32[32,8,128]{2,1,0:T(8,128)}), f32[32,8,128]{2,1,0:T(8,128)S(1)}, u32[]{:S(2)}, u32[]{:S(2)}) async-start(f32[32,8,128]{2,1,0:T(8,128)} %get-tuple-element.95), calls=%async_computation.1 | async-start | bytes 262144 | tf_op jit(solution)/shard_map/all_to_all | solution.py:611
  48.9 10.4 %collective-permute-start.9 = (f32[2,24,128]{2,1,0:T(8,128)S(1)}, f32[2,24,128]{2,1,0:T(8,128)S(1)}, u32[]{:S(2)}, u32[]{:S(2)}) collective-permute-start(f32[2,24,128]{2,1,0:T(8,128)S(1)} %get-tuple-element.82), channel_id=1, source_target_pairs={{0,16},{16,32},{32,48},{48,64},{64,80},{80,96},{96,112},{112,128},... | collective-permute-start | bytes 73736 | tf_op jit(solution)/shard_map/ppermute | solution.py:548
  51.6 4.2 %collective-permute-start.10 = (f32[2,8,128]{2,1,0:T(8,128)S(1)}, f32[2,8,128]{2,1,0:T(8,128)S(1)}, u32[]{:S(2)}, u32[]{:S(2)}) collective-permute-start(f32[2,8,128]{2,1,0:T(8,128)S(1)} %get-tuple-element.83), channel_id=1, source_target_pairs={{0,2},{2,4},{4,6},{6,8},{8,10},{10,12},{12,14},{14,0},{1,3},{3,5},... | collective-permute-start | bytes 24584 | tf_op jit(solution)/shard_map/ppermute | solution.py:548
  62.4 1.5 %collective-permute-start.12 = (f32[384,128]{1,0:T(8,128)S(1)}, f32[384,128]{1,0:T(8,128)S(1)}, u32[]{:S(2)}, u32[]{:S(2)}) collective-permute-start(f32[384,128]{1,0:T(8,128)S(1)} %get-tuple-element.94), channel_id=1, source_target_pairs={{1,0},{0,1},{3,2},{2,3},{5,4},{4,5},{7,6},{6,7},{9,8},{8,9},{11,10... | collective-permute-start | bytes 589832 | tf_op jit(solution)/shard_map/ppermute | solution.py:622
  74.2 13.7 %copy-start = (f32[1,1,1,32,10,128]{5,3,4,2,1,0:T(8,128)S(1)}, f32[1,1,1,32,10,128]{5,3,4,2,1,0:T(8,128)}, u32[]{:S(2)}) copy-start(f32[1,1,1,32,10,128]{5,3,4,2,1,0:T(8,128)} %param.14) | copy-start | bytes 491524
  74.2 13.7 %copy-start.1 = (f32[1,1,1,32,128]{4,3,2,1,0:T(8,128)S(1)}, f32[1,1,1,32,128]{4,3,2,1,0:T(8,128)}, u32[]{:S(2)}) copy-start(f32[1,1,1,32,128]{4,3,2,1,0:T(8,128)} %param.15) | copy-start | bytes 49156
  74.2 5.1 %collective-permute-start.15 = (f32[48,128]{1,0:T(8,128)S(1)}, f32[48,128]{1,0:T(8,128)S(1)}, u32[]{:S(2)}, u32[]{:S(2)}) collective-permute-start(f32[48,128]{1,0:T(8,128)S(1)} %reduce_sum.9), channel_id=1, source_target_pairs={{0,192},{16,208},{32,224},{48,240},{64,128},{80,144},{96,160},{112... | collective-permute-start | bytes 73736 | tf_op jit(solution)/shard_map/ppermute | solution.py:521
  75.9 5.3 %collective-permute-start.14 = (f32[48,128]{1,0:T(8,128)S(1)}, f32[48,128]{1,0:T(8,128)S(1)}, u32[]{:S(2)}, u32[]{:S(2)}) collective-permute-start(f32[48,128]{1,0:T(8,128)S(1)} %reduce_sum.9), channel_id=1, source_target_pairs={{0,128},{16,144},{32,160},{48,176},{64,192},{80,208},{96,224},{112... | collective-permute-start | bytes 73736 | tf_op jit(solution)/shard_map/ppermute | solution.py:521
  76.3 4.9 %collective-permute-start.13 = (f32[48,128]{1,0:T(8,128)S(1)}, f32[48,128]{1,0:T(8,128)S(1)}, u32[]{:S(2)}, u32[]{:S(2)}) collective-permute-start(f32[48,128]{1,0:T(8,128)S(1)} %reduce_sum.9), channel_id=1, source_target_pairs={{0,64},{16,80},{32,96},{48,112},{64,0},{80,16},{96,32},{112,48},{1... | collective-permute-start | bytes 73736 | tf_op jit(solution)/shard_map/ppermute | solution.py:521
  81.3 7.6 %collective-permute-start.18 = (f32[48,128]{1,0:T(8,128)S(1)}, f32[48,128]{1,0:T(8,128)S(1)}, u32[]{:S(2)}, u32[]{:S(2)}) collective-permute-start(f32[48,128]{1,0:T(8,128)S(1)} %add_add_fusion.1), channel_id=1, source_target_pairs={{0,48},{16,32},{32,16},{48,0},{64,112},{80,96},{96,80},{112,64},{1... | collective-permute-start | bytes 73736 | tf_op jit(solution)/shard_map/ppermute | solution.py:521
  83.4 7.7 %collective-permute-start.17 = (f32[48,128]{1,0:T(8,128)S(1)}, f32[48,128]{1,0:T(8,128)S(1)}, u32[]{:S(2)}, u32[]{:S(2)}) collective-permute-start(f32[48,128]{1,0:T(8,128)S(1)} %add_add_fusion.1), channel_id=1, source_target_pairs={{0,32},{16,48},{32,0},{48,16},{64,96},{80,112},{96,64},{112,80},{1... | collective-permute-start | bytes 73736 | tf_op jit(solution)/shard_map/ppermute | solution.py:521
  87.9 4.7 %collective-permute-start.16 = (f32[48,128]{1,0:T(8,128)S(1)}, f32[48,128]{1,0:T(8,128)S(1)}, u32[]{:S(2)}, u32[]{:S(2)}) collective-permute-start(f32[48,128]{1,0:T(8,128)S(1)} %add_add_fusion.1), channel_id=1, source_target_pairs={{0,16},{16,0},{32,48},{48,32},{64,80},{80,64},{96,112},{112,96},{1... | collective-permute-start | bytes 73736 | tf_op jit(solution)/shard_map/ppermute | solution.py:521
  92.7 9.7 %copy-start.2 = (f32[32,12,128]{2,0,1:T(8,128)S(1)}, f32[32,12,128]{2,0,1:T(8,128)}, u32[]{:S(2)}) copy-start(f32[32,12,128]{2,0,1:T(8,128)} %param.20) | copy-start | bytes 589828

commit v4 on v3

--- a/solution.py
+++ b/solution.py
@@ -337,25 +337,20 @@
 
 
 def early_kernel(
-    count_ref,
-    owner_hbm,
-    offsets_ref,
-    surf_ref,
-    units_ref,
-    e_ref,
-    placed,
-    drives,
-    surf_out,
-    starts,
-    turn,
-    factors,
-    owner_ref,
-    sem,
-    high,
-    low,
+    count_ref, owner_hbm, offsets_ref, e_ref, placed, drives, owner_ref, sem, high, low
 ):
     copy = pltpu.make_async_copy(owner_hbm, owner_ref, sem)
     copy.start()
+    drives[...] = jnp.zeros_like(drives)
+    copy.wait()
+    count = count_ref[0]
+    for slot in range(SLOTS):
+        line = offsets_ref[slot : slot + 1]
+        placed[pl.ds(owner_ref[0, slot], 1)] = jnp.where(slot < count, line, -1)
+    gather_drive(e_ref, placed, drives, 0, high, low)
+
+
+def phase_kernel(surf_ref, units_ref, surf_out, starts, turn, factors):
     lanes = lax.broadcasted_iota(jnp.int32, (8, DIRS), 1)
     omega = freq_low + freq_pitch * (lanes & (FREQ - 1)).astype(F32)
     moment = omega * jnp.where(lanes < FREQ, time_step, 2.0 * time_step)
@@ -390,13 +385,54 @@
     turn[0], turn[1] = powers[1]
     starts[0], starts[1] = low_start
     starts[2], starts[3] = high_start
-    copy.wait()
-    count = count_ref[0]
-    for slot in range(SLOTS):
-        line = offsets_ref[slot : slot + 1]
-        placed[pl.ds(owner_ref[0, slot], 1)] = jnp.where(slot < count, line, -1)
-    drives[...] = jnp.zeros_like(drives)
-    gather_drive(e_ref, placed, drives, 0, high, low)
+
+
+FAR = 48
+LOAD = 64
+CELL = 16
+
+
+def partner(step):
+    index = lax.axis_index("gx")
+    return (index >> 2) ^ step, (index & 3) ^ step
+
+
+def fold_kernel(pieces, drives, total, *loads):
+    total[...] = jnp.sum(pieces[...], axis=0)
+    for step in (1, 2, 3):
+        load = loads[step - 1]
+        load[0:FAR] = total[...]
+        load[FAR:] = drives[pl.ds(partner(step)[0], 1)][0]
+
+
+def relay_kernel(total_in, drives, one, two, three, total, kept, *loads):
+    arrived = (one, two, three)
+    total[...] = (total_in[...] + one[0:FAR]) + (two[0:FAR] + three[0:FAR])
+    own = partner(0)[0]
+    for step in range(4):
+        target = partner(step)[1]
+        out, first = (kept, 0) if step == 0 else (loads[step - 1], FAR)
+        if step:
+            out[0:FAR] = total[...]
+        spot = pl.multiple_of(target * CELL, CELL)
+        for source in range(4):
+            if source == 0:
+                piece = drives[pl.ds(own, 1), pl.ds(spot, CELL)][0]
+            else:
+                piece = arrived[source - 1][pl.ds(FAR + spot, CELL)]
+            out[first + source * CELL : first + (source + 1) * CELL] = piece
+
+
+def finish_kernel(total_in, kept, one, two, three, spread_out, back):
+    total = (total_in[...] + one[0:FAR]) + (two[0:FAR] + three[0:FAR])
+    for peer in range(8):
+        spread_out[peer] = total
+    for step, arrived in enumerate((kept, one, two, three)):
+        first = FAR if step else 0
+        for source in range(4):
+            brick = partner(source)[0] * 4 + partner(step)[1]
+            start = first + source * CELL
+            back[pl.ds(brick, 1)] = arrived[start : start + CELL][None]
 
 
 def final_kernel(
@@ -473,7 +509,7 @@
                 out[row : row + 1] = imag[comp : comp + 1]
 
 
-def atoms_kernel(state_ref, pump_ref, drives, e_ref, h_ref, out, e_out, h_out):
+def atoms_kernel(state_ref, pump_ref, drives, out):
     polar = [state_ref[c] for c in range(3)]
     rate = [state_ref[3 + c] for c in range(3)]
     ground, lower, lasing, upper = [state_ref[6 + level] for level in range(4)]
@@ -501,6 +537,9 @@
         lower, lasing, upper = lower_new, lasing_new, upper_new
     for place, value in enumerate(polar + rate + [ground, lower, lasing, upper]):
         out[place] = value
+
+
+def store_kernel(e_ref, h_ref, e_out, h_out):
     e_out[...] = e_ref[...]
     h_out[...] = h_ref[...]
 
@@ -515,11 +554,6 @@
     rows[1] = sine * np.sin(azimuth).astype(np.float32)
     rows[2] = cosine
     return rows
-
-
-def all_reduce(value, axis, peers):
-    one, two, three = [lax.ppermute(value, axis, peers(k)) for k in (1, 2, 3)]
-    return (value + one) + (two + three)
 
 
 def local(
@@ -565,32 +599,32 @@
     near = shifted(near, down)
     fields = lax.all_to_all(packed, "gx", 0, 0, tiled=True)
     halves = [pltpu.VMEM((3 * HALF, WIDE), BF16)] * 2
-    placed, before, surf, starts, turn, factors = call(
+    placed, before = call(
         early_kernel,
+        (shape(SLOTS, CZ, dtype=jnp.int32), shape(SLOTS, 8, CZ)),
+        [gain_count.reshape(1)]
+        + stay(block_owner.reshape(1, SLOTS), gain_offsets.reshape(SLOTS, CZ))
+        + [e_old],
+        in_specs=[pl.BlockSpec(memory_space=pltpu.SMEM), hbm, vmem, vmem],
+        scratch=[pltpu.SMEM((1, SLOTS), jnp.int32), pltpu.SemaphoreType.DMA] + halves,
+        name="early",
+    )
+    *near, placed = lax.optimization_barrier((*near, placed))
+    h_one, *edge = call(magnetic_kernel, (dense,) + faces, (e_old, h_old, *near), name="magnetic")
+    edge = shifted(edge, up)
+    spread_now = scattered(0, placed, fields, "scatter")
+    surf, starts, turn, factors = call(
+        phase_kernel,
         (
-            shape(SLOTS, CZ, dtype=jnp.int32),
-            shape(SLOTS, 8, CZ),
             shape(1, CZ, dtype=jnp.int32),
             shape(4, CZ, DIRS),
             shape(2, CZ, DIRS),
             shape(2, STEPS * FREQ, DIRS),
         ),
-        [gain_count.reshape(1)]
-        + stay(
-            block_owner.reshape(1, SLOTS),
-            gain_offsets.reshape(SLOTS, CZ),
-            surf_offsets.reshape(1, CZ),
-            jnp.asarray(directions(DIRS)),
-        )
-        + [e_old],
-        in_specs=[pl.BlockSpec(memory_space=pltpu.SMEM), hbm, vmem, vmem, vmem, vmem],
-        scratch=[pltpu.SMEM((1, SLOTS), jnp.int32), pltpu.SemaphoreType.DMA] + halves,
-        name="early",
-    )
-    *near, placed = lax.optimization_barrier((*near, placed))
-    h_one, *edge = call(magnetic_kernel, (dense,) + faces, (e_old, h_old, *near), name="magnetic")
-    edge = shifted(edge, up)
-    spread_now = scattered(0, placed, fields, "scatter")
+        stay(surf_offsets.reshape(1, CZ), jnp.asarray(directions(DIRS))),
+        name="phase",
+    )
+    *edge, surf = lax.optimization_barrier((*edge, surf))
     e_one, *near, rates = call(
         electric_kernel,
         (dense,) + faces + (shape(4, ROWS, CZ),),
@@ -608,7 +642,6 @@
     *near, early = lax.optimization_barrier((*near, early))
     h_two, *edge = call(magnetic_kernel, (dense,) + faces, (e_one, h_one, *near), name="magnetic2")
     edge = shifted(edge, up)
-    back = lax.all_to_all(drives, "gx", 0, 0, tiled=True)
     placed, fields, early = lax.optimization_barrier((placed, fields, early))
     spread_next = scattered(4, placed, fields, "scatter2")
     part = shape(12 * FREQ // 2, DIRS)
@@ -620,25 +653,45 @@
         name="final",
     )
     chip = keep + lax.ppermute(send, "gz", down[2])
-    chip, back = lax.optimization_barrier((chip, back))
-    pieces = lax.all_to_all(chip.reshape(8, 48, DIRS), "gy", 0, 0, tiled=True)
-    total = jnp.sum(pieces, axis=0)
-    total = all_reduce(
-        total, "gx", lambda k: [(a * 4 + z, (a ^ k) * 4 + z) for a in range(4) for z in range(4)]
-    )
-    total = all_reduce(
-        total, "gx", lambda k: [(a * 4 + z, a * 4 + (z ^ k)) for a in range(4) for z in range(4)]
-    )
-    results = call(
+    pieces = lax.all_to_all(chip.reshape(8, FAR, DIRS), "gy", 0, 0, tiled=True)
+    drives = drives.reshape(4, LOAD, CZ)
+    load = shape(FAR + LOAD, CZ)
+    total, *loads = call(
+        fold_kernel, (shape(FAR, DIRS),) + (load,) * 3, (pieces, drives), name="fold"
+    )
+    loads = [
+        lax.ppermute(
+            value, "gx", [(a * 4 + z, (a ^ k) * 4 + z) for a in range(4) for z in range(4)]
+        )
+        for k, value in enumerate(loads, 1)
+    ]
+    total, kept, *loads = call(
+        relay_kernel,
+        (shape(FAR, DIRS), shape(LOAD, CZ)) + (load,) * 3,
+        (total, drives, *loads),
+        name="relay",
+    )
+    loads = [
+        lax.ppermute(
+            value, "gx", [(a * 4 + z, a * 4 + (z ^ k)) for a in range(4) for z in range(4)]
+        )
+        for k, value in enumerate(loads, 1)
+    ]
+    e_out, h_out = call(store_kernel, (dense, dense), (e_two, h_two), name="store")
+    copies, back = call(
+        finish_kernel,
+        (shape(8, FAR, DIRS), shape(SLOTS // 2, CELL, CZ)),
+        (total, kept, *loads),
+        name="finish",
+    )
+    state_out = call(
         atoms_kernel,
-        (shape(10, SLOTS, CZ), dense, dense),
-        (state, pump.reshape(SLOTS, CZ), back, e_two, h_two),
+        shape(10, SLOTS, CZ),
+        (state, pump.reshape(SLOTS, CZ), back.reshape(SLOTS, 8, CZ)),
         name="atoms",
     )
-    total, state_out, e_out, h_out = lax.optimization_barrier((total, *results))
-    gathered = lax.all_to_all(
-        jnp.broadcast_to(total[None], (8, 48, DIRS)), "gy", 0, 0, tiled=True
-    )
+    copies, state_out, e_out, h_out = lax.optimization_barrier((copies, state_out, e_out, h_out))
+    gathered = lax.all_to_all(copies, "gy", 0, 0, tiled=True)
     far_out = far_acc + jnp.transpose(gathered.reshape(12, FREQ // 2, DIRS), (1, 0, 2))
     return (
         e_out.reshape(efield.shape),

time: 104 us -> 102 us (0.981)
  starting transfers between devices: 44.4 us -> 39 us
  blocking collectives: 20 us -> 21.7 us
  Pallas kernels: 20.8 us -> 22.2 us
    all_to_all x1 -> x0, starting transfers between devices: 3.52 us -> none  [local(): back = lax.all_to_all(drives, 'gx', 0, 0, tiled=True)]
    ppermute x12, starting transfers between devices: 18.9 us -> 16.6 us  [shifted(): lax.ppermute(part, axis, perm)]
    all_to_all x2, blocking collectives: 20 us -> 21.7 us  [the longest x1 11.6 us: local(): pieces = lax.all_to_all(chip.reshape(8, FAR, DIRS), 'gy', 0, 0, tiled=True)]
    pallas_call x10 -> x15, Pallas kernels: 20.8 us -> 22.2 us  [call(): pl.pallas_call(kernel, out_shape=outs, in_specs=in_specs or [pl.BlockSpec...]
  transfers between devices with their start and end apart: 21 -> 20, of which waited for: 9 -> 8; matrix products, arithmetic and copies ran while one was open for 0% -> 0% of each run, Pallas kernels for 18% -> 16%
where the time goes in v4:
time: 102 us; the launch traced here: 101 us
  starting transfers between devices  39 us (38%)
  Pallas kernels  22.2 us (22%)
  blocking collectives  21.7 us (21%)
  waiting for transfers between devices  15.2 us (15%)
  between operations  1.53 us (2%)
    pallas_call x15, Pallas kernels, call(): pl.pallas_call(kernel, out_shape=outs, in_specs=in_specs or [pl.BlockSpec...  22.2 us
    ppermute x12, starting transfers between devices, shifted(): lax.ppermute(part, axis, perm)  16.6 us
    all_to_all x1, blocking collectives, local(): pieces = lax.all_to_all(chip.reshape(8, FAR, DIRS), 'gy', 0, 0, tiled=True)  11.6 us
    all_to_all x1, starting transfers between devices, local(): fields = lax.all_to_all(packed, 'gx', 0, 0, tiled=True)  11 us
    all_to_all x1, blocking collectives, local(): gathered = lax.all_to_all(copies, 'gy', 0, 0, tiled=True)  10.1 us
    ppermute x12, waiting for transfers between devices, shifted(): lax.ppermute(part, axis, perm)  6.76 us
    ppermute x3, starting transfers between devices, local(): lax.ppermute(value, 'gx', [(a * 4 + z, a * 4 + (z ^ k)) for a in range(4)...  6.58 us
    ppermute x3, waiting for transfers between devices, local(): lax.ppermute(value, 'gx', [(a * 4 + z, a * 4 + (z ^ k)) for a in range(4)...  4.87 us
  transfers between devices with their start and end apart: 20, of which 8 were waited for; matrix products, arithmetic and copies ran while one was open for 0% of the time, Pallas kernels for 16%

profile of v4, /device:TPU:8, one launch (start us, length us, event | category | flops | bytes accessed | tf_op | source)
XLA Modules:
  0.0 101.0 jit_solution(2165217863951367945)
XLA Ops:
  0.6 1.8 %prepare.1 = (f32[2,24,128]{2,1,0:T(8,128)S(1)}, f32[2,8,128]{2,1,0:T(8,128)S(1)}, f32[2,192,128]{2,1,0:T(8,128)S(1)}, f32[16,16,128]{2,1,0:T(8,128)}, f32[3,192...) custom-call(f32[3,192,128]{2,1,0:T(8,128)} %bitcast.31, f32[10,32,128]{2,1,0:T(8,128)} %bitcast.23, ...), custom_call_target="tpu_custom_call" | custom-call | bytes 2097152 | tf_op jit(solution)/shard_map/prepare/pallas_call | solution.py:48
  2.6 11.0 %all-to-all-start = ((f32[16,16,128]{2,1,0:T(8,128)}), f32[16,16,128]{2,1,0:T(8,128)S(1)}, u32[]{:S(2)}, u32[]{:S(2)}) async-start(f32[16,16,128]{2,1,0:T(8,128)} %get-tuple-element.86), calls=%async_computation | async-start | bytes 262144 | tf_op jit(solution)/shard_map/all_to_all | solution.py:600
  13.6 6.2 %collective-permute-start = (f32[2,24,128]{2,1,0:T(8,128)S(1)}, f32[2,24,128]{2,1,0:T(8,128)S(1)}, u32[]{:S(2)}, u32[]{:S(2)}) collective-permute-start(f32[2,24,128]{2,1,0:T(8,128)S(1)} %get-tuple-element.69), channel_id=1, source_target_pairs={{16,0},{32,16},{48,32},{64,48},{80,64},{96,80},{112,96},{128,112},... | collective-permute-start | bytes 73736 | tf_op jit(solution)/shard_map/ppermute | solution.py:582
  19.8 0.4 collective-permute-start.1
  20.9 4.3 %early.1 = (s32[32,128]{1,0:T(8,128)S(1)}, f32[32,8,128]{2,1,0:T(8,128)S(1)}) custom-call(s32[1]{0:T(128)} %bitcast.22.count_ref, s32[1,32]{1,0:T(1,128)} %bitcast.36, s32[32,128]{1,0:T(8,128)} %bitcast.35, f32[3,192,128]{2,1,0:T(8,128)S(1)} %get-tuple-element.67.e_ref), custom_call_target="tpu_custom_call" | custom-call | bytes 2097152 | tf_op jit(solution)/shard_map/early/pallas_call | solution.py:48
  25.6 1.7 %collective-permute-start.4 = (f32[2,8,128]{2,1,0:T(8,128)S(1)}, f32[2,8,128]{2,1,0:T(8,128)S(1)}, u32[]{:S(2)}, u32[]{:S(2)}) collective-permute-start(f32[2,8,128]{2,1,0:T(8,128)S(1)} %get-tuple-element.78), channel_id=1, source_target_pairs={{0,2},{2,4},{4,6},{6,8},{8,10},{10,12},{12,14},{14,0},{1,3},{3,5},... | collective-permute-start | bytes 24584 | tf_op jit(solution)/shard_map/ppermute | solution.py:582
  27.2 1.0 phase.1
  28.2 3.2 %scatter.1.dense = f32[4,192,128]{2,1,0:T(8,128)S(1)} custom-call(s32[32,128]{1,0:T(8,128)S(1)} %get-tuple-element.103.placed, f32[16,16,128]{2,1,0:T(8,128)S(1)} %all-to-all-done.fields_ref), custom_call_target="tpu_custom_call" | custom-call | bytes 2097152 | tf_op jit(solution)/shard_map/scatter/pallas_call | solution.py:48
  31.4 2.2 %collective-permute-done.3.face_x = f32[2,24,128]{2,1,0:T(8,128)S(1)} collective-permute-done((f32[2,24,128]{2,1,0:T(8,128)S(1)}, f32[2,24,128]{2,1,0:T(8,128)S(1)}, u32[]{:S(2)}, u32[]{:S(2)}) %collective-permute-start.3) | collective-permute-done | bytes 24608 | tf_op jit(solution)/shard_map/ppermute | solution.py:582
  33.6 0.2 electric.1
  33.9 4.1 %collective-permute-start.6 = (f32[2,24,128]{2,1,0:T(8,128)S(1)}, f32[2,24,128]{2,1,0:T(8,128)S(1)}, u32[]{:S(2)}, u32[]{:S(2)}) collective-permute-start(f32[2,24,128]{2,1,0:T(8,128)S(1)} %get-tuple-element.88), channel_id=1, source_target_pairs={{16,0},{32,16},{48,32},{64,48},{80,64},{96,80},{112,96},{128,112},... | collective-permute-start | bytes 73736 | tf_op jit(solution)/shard_map/ppermute | solution.py:582
  38.0 3.4 %collective-permute-start.7 = (f32[2,8,128]{2,1,0:T(8,128)S(1)}, f32[2,8,128]{2,1,0:T(8,128)S(1)}, u32[]{:S(2)}, u32[]{:S(2)}) collective-permute-start(f32[2,8,128]{2,1,0:T(8,128)S(1)} %get-tuple-element.89), channel_id=1, source_target_pairs={{2,0},{4,2},{6,4},{8,6},{10,8},{12,10},{14,12},{0,14},{3,1},{5,3},... | collective-permute-start | bytes 24584 | tf_op jit(solution)/shard_map/ppermute | solution.py:582
  41.4 3.2 %drive.1 = (f32[32,8,128]{2,1,0:T(8,128)S(1)}, f32[8,128]{1,0:T(8,128)S(1)}) custom-call(f32[3,192,128]{2,1,0:T(8,128)S(1)} %get-tuple-element.87.e_ref, f32[3,192,128]{2,1,0:T(8,128)S(1)} %get-tuple-element.76.h_ref, s32[32,128]{1,0:T(8,128)S(1)} %get-tuple-element.103.placed, s32[1,128]{1,0:T(1,128)S(1)} %get-tuple-element.91.surf_ref, ...), custom_call_target="tpu_custom_call" | custom-call | bytes 2097152 | tf_op jit(solution)/shard_map/drive/pallas_call | solution.py:48
  45.1 0.3 collective-permute-start.10
  45.4 3.2 %scatter2.1.dense = f32[4,192,128]{2,1,0:T(8,128)S(1)} custom-call(s32[32,128]{1,0:T(8,128)S(1)} %get-tuple-element.103.placed, f32[16,16,128]{2,1,0:T(8,128)S(1)} %all-to-all-done.fields_ref), custom_call_target="tpu_custom_call" | custom-call | bytes 2097152 | tf_op jit(solution)/shard_map/scatter2/pallas_call | solution.py:48
  48.5 1.0 %collective-permute-done.10.face_y = f32[2,8,128]{2,1,0:T(8,128)S(1)} collective-permute-done((f32[2,8,128]{2,1,0:T(8,128)S(1)}, f32[2,8,128]{2,1,0:T(8,128)S(1)}, u32[]{:S(2)}, u32[]{:S(2)}) %collective-permute-start.10) | collective-permute-done | bytes 8224 | tf_op jit(solution)/shard_map/ppermute | solution.py:582
  49.6 3.5 %collective-permute-done.9.face_x = f32[2,24,128]{2,1,0:T(8,128)S(1)} collective-permute-done((f32[2,24,128]{2,1,0:T(8,128)S(1)}, f32[2,24,128]{2,1,0:T(8,128)S(1)}, u32[]{:S(2)}, u32[]{:S(2)}) %collective-permute-start.9) | collective-permute-done | bytes 24608 | tf_op jit(solution)/shard_map/ppermute | solution.py:582
  53.1 3.2 %final.1 = (f32[3,192,128]{2,1,0:T(8,128)S(1)}, f32[384,128]{1,0:T(8,128)S(1)}, f32[384,128]{1,0:T(8,128)S(1)}) custom-call(f32[3,192,128]{2,1,0:T(8,128)S(1)} %get-tuple-element.87.e_ref, f32[3,192,128]{2,1,0:T(8,128)S(1)} %get-tuple-element.97.h_ref, f32[2,24,128]{2,1,0:T(8,128)S(1)} %collective-permute-done.9.face_x, ...), custom_call_target="tpu_custom_call" | custom-call | bytes 2097152 | tf_op jit(solution)/shard_map/final/pallas_call | solution.py:48
  56.4 1.4 %collective-permute-done.12 = f32[384,128]{1,0:T(8,128)S(1)} collective-permute-done((f32[384,128]{1,0:T(8,128)S(1)}, f32[384,128]{1,0:T(8,128)S(1)}, u32[]{:S(2)}, u32[]{:S(2)}) %collective-permute-start.12) | collective-permute-done | bytes 196640 | tf_op jit(solution)/shard_map/ppermute | solution.py:655
  57.9 11.6 %all_to_all.15.pieces = f32[8,48,128]{2,1,0:T(8,128)S(1)} all-to-all(f32[8,48,128]{2,1,0:T(8,128)S(1)} %bitcast.29), channel_id=1, replica_groups=mesh['gx'=16,'gy'=8,'gz'=2] {'gy'}, dimensions={0} | all-to-all | bytes 393216 | tf_op jit(solution)/shard_map/all_to_all | solution.py:656
  69.6 4.6 %collective-permute-start.15 = (f32[112,128]{1,0:T(8,128)S(1)}, f32[112,128]{1,0:T(8,128)S(1)}, u32[]{:S(2)}, u32[]{:S(2)}) collective-permute-start(f32[112,128]{1,0:T(8,128)S(1)} %get-tuple-element.115), channel_id=1, source_target_pairs={{0,192},{16,208},{32,224},{48,240},{64,128},{80,144},{96,160},{112... | collective-permute-start | bytes 172040 | tf_op jit(solution)/shard_map/ppermute | solution.py:663
  74.2 1.1 %collective-permute-done.14.two = f32[112,128]{1,0:T(8,128)S(1)} collective-permute-done((f32[112,128]{1,0:T(8,128)S(1)}, f32[112,128]{1,0:T(8,128)S(1)}, u32[]{:S(2)}, u32[]{:S(2)}) %collective-permute-start.14) | collective-permute-done | bytes 57376 | tf_op jit(solution)/shard_map/ppermute | solution.py:663
  75.3 1.1 %collective-permute-done.15.three = f32[112,128]{1,0:T(8,128)S(1)} collective-permute-done((f32[112,128]{1,0:T(8,128)S(1)}, f32[112,128]{1,0:T(8,128)S(1)}, u32[]{:S(2)}, u32[]{:S(2)}) %collective-permute-start.15) | collective-permute-done | bytes 57376 | tf_op jit(solution)/shard_map/ppermute | solution.py:663
  76.5 5.8 %collective-permute-start.17 = (f32[112,128]{1,0:T(8,128)S(1)}, f32[112,128]{1,0:T(8,128)S(1)}, u32[]{:S(2)}, u32[]{:S(2)}) collective-permute-start(f32[112,128]{1,0:T(8,128)S(1)} %get-tuple-element.119), channel_id=1, source_target_pairs={{0,32},{16,48},{32,0},{48,16},{64,96},{80,112},{96,64},{112,80},{1... | collective-permute-start | bytes 172040 | tf_op jit(solution)/shard_map/ppermute | solution.py:675
  82.3 0.7 collective-permute-start.18
  83.0 0.8 store.1
  83.9 2.2 %collective-permute-done.17.two = f32[112,128]{1,0:T(8,128)S(1)} collective-permute-done((f32[112,128]{1,0:T(8,128)S(1)}, f32[112,128]{1,0:T(8,128)S(1)}, u32[]{:S(2)}, u32[]{:S(2)}) %collective-permute-start.17) | collective-permute-done | bytes 57376 | tf_op jit(solution)/shard_map/ppermute | solution.py:675
  86.1 2.7 %collective-permute-done.18.three = f32[112,128]{1,0:T(8,128)S(1)} collective-permute-done((f32[112,128]{1,0:T(8,128)S(1)}, f32[112,128]{1,0:T(8,128)S(1)}, u32[]{:S(2)}, u32[]{:S(2)}) %collective-permute-start.18) | collective-permute-done | bytes 57376 | tf_op jit(solution)/shard_map/ppermute | solution.py:675
  88.8 0.7 copy-done.1
  89.4 0.8 atoms.1
  90.2 10.1 %all_to_all.16 = f32[8,48,128]{2,1,0:T(8,128)S(1)} all-to-all(f32[8,48,128]{2,1,0:T(8,128)S(1)} %get-tuple-element.129), channel_id=1, replica_groups=mesh['gx'=16,'gy'=8,'gz'=2] {'gy'}, dimensions={0} | all-to-all | bytes 393216 | tf_op jit(solution)/shard_map/all_to_all | solution.py:694
  100.3 0.7 add.7
  (33 shorter events, 1.4 us)
Async XLA Ops:
  2.5 22.7 %collective-permute-start.2 = (f32[2,192,128]{2,1,0:T(8,128)S(1)}, f32[2,192,128]{2,1,0:T(8,128)S(1)}, u32[]{:S(2)}, u32[]{:S(2)}) collective-permute-start(f32[2,192,128]{2,1,0:T(8,128)S(1)} %get-tuple-element.71), channel_id=1, source_target_pairs={{1,0},{0,1},{3,2},{2,3},{5,4},{4,5},{7,6},{6,7},{9,8},{8,9},{11,10... | collective-permute-start | bytes 589832 | tf_op jit(solution)/shard_map/ppermute | solution.py:582
  2.6 25.6 %all-to-all-start = ((f32[16,16,128]{2,1,0:T(8,128)}), f32[16,16,128]{2,1,0:T(8,128)S(1)}, u32[]{:S(2)}, u32[]{:S(2)}) async-start(f32[16,16,128]{2,1,0:T(8,128)} %get-tuple-element.86), calls=%async_computation | async-start | bytes 262144 | tf_op jit(solution)/shard_map/all_to_all | solution.py:600
  13.6 11.6 %collective-permute-start = (f32[2,24,128]{2,1,0:T(8,128)S(1)}, f32[2,24,128]{2,1,0:T(8,128)S(1)}, u32[]{:S(2)}, u32[]{:S(2)}) collective-permute-start(f32[2,24,128]{2,1,0:T(8,128)S(1)} %get-tuple-element.69), channel_id=1, source_target_pairs={{16,0},{32,16},{48,32},{64,48},{80,64},{96,80},{112,96},{128,112},... | collective-permute-start | bytes 73736 | tf_op jit(solution)/shard_map/ppermute | solution.py:582
  19.8 5.4 %collective-permute-start.1 = (f32[2,8,128]{2,1,0:T(8,128)S(1)}, f32[2,8,128]{2,1,0:T(8,128)S(1)}, u32[]{:S(2)}, u32[]{:S(2)}) collective-permute-start(f32[2,8,128]{2,1,0:T(8,128)S(1)} %get-tuple-element.70), channel_id=1, source_target_pairs={{2,0},{4,2},{6,4},{8,6},{10,8},{12,10},{14,12},{0,14},{3,1},{5,3},... | collective-permute-start | bytes 24584 | tf_op jit(solution)/shard_map/ppermute | solution.py:582
  25.4 8.2 %collective-permute-start.5 = (f32[2,192,128]{2,1,0:T(8,128)S(1)}, f32[2,192,128]{2,1,0:T(8,128)S(1)}, u32[]{:S(2)}, u32[]{:S(2)}) collective-permute-start(f32[2,192,128]{2,1,0:T(8,128)S(1)} %get-tuple-element.79), channel_id=1, source_target_pairs={{0,1},{1,0},{2,3},{3,2},{4,5},{5,4},{6,7},{7,6},{8,9},{9,8},{10,11... | collective-permute-start | bytes 589832 | tf_op jit(solution)/shard_map/ppermute | solution.py:582
  25.5 8.1 %collective-permute-start.3 = (f32[2,24,128]{2,1,0:T(8,128)S(1)}, f32[2,24,128]{2,1,0:T(8,128)S(1)}, u32[]{:S(2)}, u32[]{:S(2)}) collective-permute-start(f32[2,24,128]{2,1,0:T(8,128)S(1)} %get-tuple-element.77), channel_id=1, source_target_pairs={{0,16},{16,32},{32,48},{48,64},{64,80},{80,96},{96,112},{112,128},... | collective-permute-start | bytes 73736 | tf_op jit(solution)/shard_map/ppermute | solution.py:582
  25.6 5.9 %collective-permute-start.4 = (f32[2,8,128]{2,1,0:T(8,128)S(1)}, f32[2,8,128]{2,1,0:T(8,128)S(1)}, u32[]{:S(2)}, u32[]{:S(2)}) collective-permute-start(f32[2,8,128]{2,1,0:T(8,128)S(1)} %get-tuple-element.78), channel_id=1, source_target_pairs={{0,2},{2,4},{4,6},{6,8},{8,10},{10,12},{12,14},{14,0},{1,3},{3,5},... | collective-permute-start | bytes 24584 | tf_op jit(solution)/shard_map/ppermute | solution.py:582
  33.8 10.9 %collective-permute-start.8 = (f32[2,192,128]{2,1,0:T(8,128)S(1)}, f32[2,192,128]{2,1,0:T(8,128)S(1)}, u32[]{:S(2)}, u32[]{:S(2)}) collective-permute-start(f32[2,192,128]{2,1,0:T(8,128)S(1)} %get-tuple-element.90), channel_id=1, source_target_pairs={{1,0},{0,1},{3,2},{2,3},{5,4},{4,5},{7,6},{6,7},{9,8},{8,9},{11,10... | collective-permute-start | bytes 589832 | tf_op jit(solution)/shard_map/ppermute | solution.py:582
  33.9 10.8 %collective-permute-start.6 = (f32[2,24,128]{2,1,0:T(8,128)S(1)}, f32[2,24,128]{2,1,0:T(8,128)S(1)}, u32[]{:S(2)}, u32[]{:S(2)}) collective-permute-start(f32[2,24,128]{2,1,0:T(8,128)S(1)} %get-tuple-element.88), channel_id=1, source_target_pairs={{16,0},{32,16},{48,32},{64,48},{80,64},{96,80},{112,96},{128,112},... | collective-permute-start | bytes 73736 | tf_op jit(solution)/shard_map/ppermute | solution.py:582
  38.0 6.7 %collective-permute-start.7 = (f32[2,8,128]{2,1,0:T(8,128)S(1)}, f32[2,8,128]{2,1,0:T(8,128)S(1)}, u32[]{:S(2)}, u32[]{:S(2)}) collective-permute-start(f32[2,8,128]{2,1,0:T(8,128)S(1)} %get-tuple-element.89), channel_id=1, source_target_pairs={{2,0},{4,2},{6,4},{8,6},{10,8},{12,10},{14,12},{0,14},{3,1},{5,3},... | collective-permute-start | bytes 24584 | tf_op jit(solution)/shard_map/ppermute | solution.py:582
  44.9 8.2 %collective-permute-start.11 = (f32[2,192,128]{2,1,0:T(8,128)S(1)}, f32[2,192,128]{2,1,0:T(8,128)S(1)}, u32[]{:S(2)}, u32[]{:S(2)}) collective-permute-start(f32[2,192,128]{2,1,0:T(8,128)S(1)} %get-tuple-element.100), channel_id=1, source_target_pairs={{0,1},{1,0},{2,3},{3,2},{4,5},{5,4},{6,7},{7,6},{8,9},{9,8},{10,11... | collective-permute-start | bytes 589832 | tf_op jit(solution)/shard_map/ppermute | solution.py:582
  45.0 8.1 %collective-permute-start.9 = (f32[2,24,128]{2,1,0:T(8,128)S(1)}, f32[2,24,128]{2,1,0:T(8,128)S(1)}, u32[]{:S(2)}, u32[]{:S(2)}) collective-permute-start(f32[2,24,128]{2,1,0:T(8,128)S(1)} %get-tuple-element.98), channel_id=1, source_target_pairs={{0,16},{16,32},{32,48},{48,64},{64,80},{80,96},{96,112},{112,128},... | collective-permute-start | bytes 73736 | tf_op jit(solution)/shard_map/ppermute | solution.py:582
  45.1 4.5 %collective-permute-start.10 = (f32[2,8,128]{2,1,0:T(8,128)S(1)}, f32[2,8,128]{2,1,0:T(8,128)S(1)}, u32[]{:S(2)}, u32[]{:S(2)}) collective-permute-start(f32[2,8,128]{2,1,0:T(8,128)S(1)} %get-tuple-element.99), channel_id=1, source_target_pairs={{0,2},{2,4},{4,6},{6,8},{8,10},{10,12},{12,14},{14,0},{1,3},{3,5},... | collective-permute-start | bytes 24584 | tf_op jit(solution)/shard_map/ppermute | solution.py:582
  56.3 1.5 %collective-permute-start.12 = (f32[384,128]{1,0:T(8,128)S(1)}, f32[384,128]{1,0:T(8,128)S(1)}, u32[]{:S(2)}, u32[]{:S(2)}) collective-permute-start(f32[384,128]{1,0:T(8,128)S(1)} %get-tuple-element.110), channel_id=1, source_target_pairs={{1,0},{0,1},{3,2},{2,3},{5,4},{4,5},{7,6},{6,7},{9,8},{8,9},{11,10... | collective-permute-start | bytes 589832 | tf_op jit(solution)/shard_map/ppermute | solution.py:655
  69.4 4.8 %collective-permute-start.13 = (f32[112,128]{1,0:T(8,128)S(1)}, f32[112,128]{1,0:T(8,128)S(1)}, u32[]{:S(2)}, u32[]{:S(2)}) collective-permute-start(f32[112,128]{1,0:T(8,128)S(1)} %get-tuple-element.113), channel_id=1, source_target_pairs={{0,64},{16,80},{32,96},{48,112},{64,0},{80,16},{96,32},{112,48},{1... | collective-permute-start | bytes 172040 | tf_op jit(solution)/shard_map/ppermute | solution.py:663
  69.5 5.8 %collective-permute-start.14 = (f32[112,128]{1,0:T(8,128)S(1)}, f32[112,128]{1,0:T(8,128)S(1)}, u32[]{:S(2)}, u32[]{:S(2)}) collective-permute-start(f32[112,128]{1,0:T(8,128)S(1)} %get-tuple-element.114), channel_id=1, source_target_pairs={{0,128},{16,144},{32,160},{48,176},{64,192},{80,208},{96,224},{112... | collective-permute-start | bytes 172040 | tf_op jit(solution)/shard_map/ppermute | solution.py:663
  69.6 6.7 %collective-permute-start.15 = (f32[112,128]{1,0:T(8,128)S(1)}, f32[112,128]{1,0:T(8,128)S(1)}, u32[]{:S(2)}, u32[]{:S(2)}) collective-permute-start(f32[112,128]{1,0:T(8,128)S(1)} %get-tuple-element.115), channel_id=1, source_target_pairs={{0,192},{16,208},{32,224},{48,240},{64,128},{80,144},{96,160},{112... | collective-permute-start | bytes 172040 | tf_op jit(solution)/shard_map/ppermute | solution.py:663
  76.4 7.4 %collective-permute-start.16 = (f32[112,128]{1,0:T(8,128)S(1)}, f32[112,128]{1,0:T(8,128)S(1)}, u32[]{:S(2)}, u32[]{:S(2)}) collective-permute-start(f32[112,128]{1,0:T(8,128)S(1)} %get-tuple-element.118), channel_id=1, source_target_pairs={{0,16},{16,0},{32,48},{48,32},{64,80},{80,64},{96,112},{112,96},{1... | collective-permute-start | bytes 172040 | tf_op jit(solution)/shard_map/ppermute | solution.py:675
  76.5 9.5 %collective-permute-start.17 = (f32[112,128]{1,0:T(8,128)S(1)}, f32[112,128]{1,0:T(8,128)S(1)}, u32[]{:S(2)}, u32[]{:S(2)}) collective-permute-start(f32[112,128]{1,0:T(8,128)S(1)} %get-tuple-element.119), channel_id=1, source_target_pairs={{0,32},{16,48},{32,0},{48,16},{64,96},{80,112},{96,64},{112,80},{1... | collective-permute-start | bytes 172040 | tf_op jit(solution)/shard_map/ppermute | solution.py:675
  82.3 6.4 %collective-permute-start.18 = (f32[112,128]{1,0:T(8,128)S(1)}, f32[112,128]{1,0:T(8,128)S(1)}, u32[]{:S(2)}, u32[]{:S(2)}) collective-permute-start(f32[112,128]{1,0:T(8,128)S(1)} %get-tuple-element.120), channel_id=1, source_target_pairs={{0,48},{16,32},{32,16},{48,0},{64,112},{80,96},{96,80},{112,64},{1... | collective-permute-start | bytes 172040 | tf_op jit(solution)/shard_map/ppermute | solution.py:675
  83.8 4.9 %copy-start = (f32[1,1,1,32,10,128]{5,3,4,2,1,0:T(8,128)S(1)}, f32[1,1,1,32,10,128]{5,3,4,2,1,0:T(8,128)}, u32[]{:S(2)}) copy-start(f32[1,1,1,32,10,128]{5,3,4,2,1,0:T(8,128)} %param.14) | copy-start | bytes 491524
  88.7 0.7 copy-start.1
  90.2 10.1 %copy-start.2 = (f32[32,12,128]{2,0,1:T(8,128)S(1)}, f32[32,12,128]{2,0,1:T(8,128)}, u32[]{:S(2)}) copy-start(f32[32,12,128]{2,0,1:T(8,128)} %param.20) | copy-start | bytes 589828

commit v5 on v4

--- a/solution.py
+++ b/solution.py
@@ -138,12 +138,32 @@
 
 
 def prepare_kernel(
-    e_hbm, state_hbm, h_hbm, eps_hbm, out_x, out_y, out_z, packed, e_out, h_out, eps_out, state, sems
+    e_hbm,
+    state_hbm,
+    h_hbm,
+    eps_hbm,
+    pump_hbm,
+    out_x,
+    out_y,
+    out_z,
+    packed,
+    e_out,
+    state,
+    h_out,
+    eps_out,
+    pump_out,
+    sems,
 ):
     copies = [
         pltpu.make_async_copy(source, target, sems.at[place])
         for place, (source, target) in enumerate(
-            ((e_hbm, e_out), (state_hbm, state), (h_hbm, h_out), (eps_hbm, eps_out))
+            (
+                (e_hbm, e_out),
+                (state_hbm, state),
+                (h_hbm, h_out),
+                (eps_hbm, eps_out),
+                (pump_hbm, pump_out),
+            )
         )
     ]
     for copy in copies:
@@ -159,8 +179,8 @@
     for field, value in enumerate(free + [lasing - lower] + polar + [lasing_free - lower_free]):
         for owner in range(SLOTS // 2):
             packed[owner, 2 * field : 2 * field + 2] = value[2 * owner : 2 * owner + 2]
-    copies[2].wait()
-    copies[3].wait()
+    for copy in copies[2:]:
+        copy.wait()
 
 
 def magnetic_kernel(e_ref, h_ref, face_x, face_y, face_z, h_out, out_x, out_y, out_z):
@@ -201,7 +221,7 @@
     return row_index(HALF, width) == (offsets >> 8)
 
 
-GROUP = 8
+GROUP = 16
 
 
 def scatter_kernel(first, placed, fields_ref, dense, total, spots, columns):
@@ -298,19 +318,20 @@
     ]
 
 
-TAKE = 4
-
-
-def gather_drive(field_ref, placed, drives, first, high, low):
-    high[...], low[...] = stacked([(field_ref, comp) for comp in range(3)])
+TAKE = 8
+
+
+def drive_kernel(e_old, e_new, placed, drives, high, low):
+    high[...], low[...] = stacked([(ref, comp) for ref in (e_old, e_new) for comp in range(3)])
+    drives[...] = jnp.zeros_like(drives)
 
     def group(index, carry):
         lines = placed[pl.ds(TAKE * index, TAKE)]
         offsets = jnp.concatenate([lines[slot : slot + 1] for slot in range(TAKE)], axis=1)
         got = gather_lines(high[...], low[...], offsets, TAKE * CZ)
-        for comp in range(3):
+        for field in range(6):
             for slot in range(TAKE):
-                drives[TAKE * index + slot, first + comp : first + comp + 1] = got[comp][
+                drives[TAKE * index + slot, field : field + 1] = got[field][
                     :, slot * CZ : (slot + 1) * CZ
                 ]
         return carry
@@ -326,31 +347,26 @@
         sampled[field : field + 1] = got[field]
 
 
-def drive_kernel(e_ref, h_ref, placed, surf_ref, before, drives, sampled, high, low):
-    drives[...] = before[...]
-    gather_drive(e_ref, placed, drives, 3, high, low)
-    sample_rows(e_ref, h_ref, surf_ref, sampled)
-
-
 def times(left, right):
     return (left[0] * right[0] - left[1] * right[1], left[1] * right[0] + left[0] * right[1])
 
 
-def early_kernel(
-    count_ref, owner_hbm, offsets_ref, e_ref, placed, drives, owner_ref, sem, high, low
+def phase_kernel(
+    count_ref,
+    owner_hbm,
+    offsets_ref,
+    surf_ref,
+    units_ref,
+    placed,
+    surf_out,
+    starts,
+    turn,
+    factors,
+    owner_ref,
+    sem,
 ):
     copy = pltpu.make_async_copy(owner_hbm, owner_ref, sem)
     copy.start()
-    drives[...] = jnp.zeros_like(drives)
-    copy.wait()
-    count = count_ref[0]
-    for slot in range(SLOTS):
-        line = offsets_ref[slot : slot + 1]
-        placed[pl.ds(owner_ref[0, slot], 1)] = jnp.where(slot < count, line, -1)
-    gather_drive(e_ref, placed, drives, 0, high, low)
-
-
-def phase_kernel(surf_ref, units_ref, surf_out, starts, turn, factors):
     lanes = lax.broadcasted_iota(jnp.int32, (8, DIRS), 1)
     omega = freq_low + freq_pitch * (lanes & (FREQ - 1)).astype(F32)
     moment = omega * jnp.where(lanes < FREQ, time_step, 2.0 * time_step)
@@ -385,6 +401,11 @@
     turn[0], turn[1] = powers[1]
     starts[0], starts[1] = low_start
     starts[2], starts[3] = high_start
+    copy.wait()
+    count = count_ref[0]
+    for slot in range(SLOTS):
+        line = offsets_ref[slot : slot + 1]
+        placed[pl.ds(owner_ref[0, slot], 1)] = jnp.where(slot < count, line, -1)
 
 
 FAR = 48
@@ -568,7 +589,6 @@
     surf_offsets,
     far_acc,
 ):
-    state = jnp.transpose(gain_state.reshape(SLOTS, 10, CZ), (1, 0, 2))
     dense = shape(3, ROWS, CZ)
     faces = (shape(2, CY, CZ), shape(2, CX, CZ), shape(2, ROWS, CZ))
     down = [[((i + 1) % n, i) for i in range(n)] for n in (16, 8, 2)]
@@ -583,48 +603,54 @@
             for part, axis, perm in zip(parts, ("gx", "gy", "gz"), perms)
         ]
 
-    *near, packed, e_old, h_old, eps = call(
+    *near, packed, e_old, state, h_old, eps, pumps = call(
         prepare_kernel,
-        faces + (shape(SLOTS // 2, 16, CZ), dense, dense, shape(ROWS, CZ)),
+        faces
+        + (
+            shape(SLOTS // 2, 16, CZ),
+            dense,
+            shape(10, SLOTS, CZ),
+            dense,
+            shape(ROWS, CZ),
+            shape(SLOTS, CZ),
+        ),
         stay(
             efield.reshape(3, ROWS, CZ),
-            state,
+            jnp.transpose(gain_state.reshape(SLOTS, 10, CZ), (1, 0, 2)),
             hfield.reshape(3, ROWS, CZ),
             inv_eps.reshape(ROWS, CZ),
+            pump.reshape(SLOTS, CZ),
         ),
-        in_specs=[hbm] * 4,
-        scratch=[pltpu.VMEM((10, SLOTS, CZ), F32), pltpu.SemaphoreType.DMA((4,))],
+        in_specs=[hbm] * 5,
+        scratch=[pltpu.SemaphoreType.DMA((5,))],
         name="prepare",
     )
     near = shifted(near, down)
     fields = lax.all_to_all(packed, "gx", 0, 0, tiled=True)
-    halves = [pltpu.VMEM((3 * HALF, WIDE), BF16)] * 2
-    placed, before = call(
-        early_kernel,
-        (shape(SLOTS, CZ, dtype=jnp.int32), shape(SLOTS, 8, CZ)),
-        [gain_count.reshape(1)]
-        + stay(block_owner.reshape(1, SLOTS), gain_offsets.reshape(SLOTS, CZ))
-        + [e_old],
-        in_specs=[pl.BlockSpec(memory_space=pltpu.SMEM), hbm, vmem, vmem],
-        scratch=[pltpu.SMEM((1, SLOTS), jnp.int32), pltpu.SemaphoreType.DMA] + halves,
-        name="early",
-    )
-    *near, placed = lax.optimization_barrier((*near, placed))
-    h_one, *edge = call(magnetic_kernel, (dense,) + faces, (e_old, h_old, *near), name="magnetic")
-    edge = shifted(edge, up)
-    spread_now = scattered(0, placed, fields, "scatter")
-    surf, starts, turn, factors = call(
+    placed, surf, starts, turn, factors = call(
         phase_kernel,
         (
+            shape(SLOTS, CZ, dtype=jnp.int32),
             shape(1, CZ, dtype=jnp.int32),
             shape(4, CZ, DIRS),
             shape(2, CZ, DIRS),
             shape(2, STEPS * FREQ, DIRS),
         ),
-        stay(surf_offsets.reshape(1, CZ), jnp.asarray(directions(DIRS))),
+        [gain_count.reshape(1)]
+        + stay(
+            block_owner.reshape(1, SLOTS),
+            gain_offsets.reshape(SLOTS, CZ),
+            surf_offsets.reshape(1, CZ),
+            jnp.asarray(directions(DIRS)),
+        ),
+        in_specs=[pl.BlockSpec(memory_space=pltpu.SMEM), hbm, vmem, vmem, vmem],
+        scratch=[pltpu.SMEM((1, SLOTS), jnp.int32), pltpu.SemaphoreType.DMA],
         name="phase",
     )
-    *edge, surf = lax.optimization_barrier((*edge, surf))
+    *near, placed = lax.optimization_barrier((*near, placed))
+    h_one, *edge = call(magnetic_kernel, (dense,) + faces, (e_old, h_old, *near), name="magnetic")
+    edge = shifted(edge, up)
+    spread_now = scattered(0, placed, fields, "scatter")
     e_one, *near, rates = call(
         electric_kernel,
         (dense,) + faces + (shape(4, ROWS, CZ),),
@@ -632,18 +658,12 @@
         name="electric",
     )
     near = shifted(near, down)
-    drives, early = call(
-        drive_kernel,
-        (shape(SLOTS, 8, CZ), shape(8, CZ)),
-        (e_one, h_one, placed, surf, before),
-        scratch=halves,
-        name="drive",
-    )
-    *near, early = lax.optimization_barrier((*near, early))
+    spread_next = scattered(4, placed, fields, "scatter2")
+    *near, spread_next = lax.optimization_barrier((*near, spread_next))
     h_two, *edge = call(magnetic_kernel, (dense,) + faces, (e_one, h_one, *near), name="magnetic2")
     edge = shifted(edge, up)
-    placed, fields, early = lax.optimization_barrier((placed, fields, early))
-    spread_next = scattered(4, placed, fields, "scatter2")
+    e_seen, h_seen, h_two = lax.optimization_barrier((e_one, h_one, h_two))
+    early = call(sample_rows, shape(8, CZ), (e_seen, h_seen, surf), name="sample")
     part = shape(12 * FREQ // 2, DIRS)
     e_two, keep, send = call(
         final_kernel,
@@ -653,8 +673,15 @@
         name="final",
     )
     chip = keep + lax.ppermute(send, "gz", down[2])
+    chip, e_seen = lax.optimization_barrier((chip, e_one))
     pieces = lax.all_to_all(chip.reshape(8, FAR, DIRS), "gy", 0, 0, tiled=True)
-    drives = drives.reshape(4, LOAD, CZ)
+    drives = call(
+        drive_kernel,
+        shape(SLOTS, 8, CZ),
+        (e_old, e_seen, placed),
+        scratch=[pltpu.VMEM((6 * HALF, WIDE), BF16)] * 2,
+        name="drive",
+    ).reshape(4, LOAD, CZ)
     load = shape(FAR + LOAD, CZ)
     total, *loads = call(
         fold_kernel, (shape(FAR, DIRS),) + (load,) * 3, (pieces, drives), name="fold"
@@ -687,7 +714,7 @@
     state_out = call(
         atoms_kernel,
         shape(10, SLOTS, CZ),
-        (state, pump.reshape(SLOTS, CZ), back.reshape(SLOTS, 8, CZ)),
+        (state, pumps, back.reshape(SLOTS, 8, CZ)),
         name="atoms",
     )
     copies, state_out, e_out, h_out = lax.optimization_barrier((copies, state_out, e_out, h_out))

time: 102 us -> 98 us (0.961)
  blocking collectives: 21.7 us -> 10.1 us
  waiting for transfers between devices: 15.2 us -> 21.4 us
  starting transfers between devices: 39 us -> 44.8 us
  Pallas kernels: 22.2 us -> 18.4 us
    all_to_all x1 -> x0, blocking collectives: 11.6 us -> none  [local(): pieces = lax.all_to_all(chip.reshape(8, FAR, DIRS), 'gy', 0, 0, tiled=True)]
    all_to_all x0 -> x1, starting transfers between devices: none -> 5.74 us  [local(): pieces = lax.all_to_all(chip.reshape(8, FAR, DIRS), 'gy', 0, 0, tiled=True)]
    ppermute x12, waiting for transfers between devices: 6.76 us -> 10.9 us  [shifted(): lax.ppermute(part, axis, perm)]
    pallas_call x15, Pallas kernels: 22.2 us -> 18.4 us  [call(): pl.pallas_call(kernel, out_shape=outs, in_specs=in_specs or [pl.BlockSpec...]
    all_to_all x0 -> x1, waiting for transfers between devices: none -> 1.74 us  [local(): pieces = lax.all_to_all(chip.reshape(8, FAR, DIRS), 'gy', 0, 0, tiled=True)]
  transfers between devices with their start and end apart: 20 -> 21, of which waited for: 8 -> 10; matrix products, arithmetic and copies ran while one was open for 0% -> 0% of each run, Pallas kernels for 16% -> 12%
where the time goes in v5:
time: 98 us; the launch traced here: 97.6 us
  starting transfers between devices  44.8 us (46%)
  waiting for transfers between devices  21.4 us (22%)
  Pallas kernels  18.4 us (19%)
  blocking collectives  10.1 us (10%)
  between operations  1.49 us (2%)
  other arithmetic  1.41 us (1%)
    pallas_call x15, Pallas kernels, call(): pl.pallas_call(kernel, out_shape=outs, in_specs=in_specs or [pl.BlockSpec...  18.4 us
    ppermute x12, starting transfers between devices, shifted(): lax.ppermute(part, axis, perm)  16.6 us
    all_to_all x1, starting transfers between devices, local(): fields = lax.all_to_all(packed, 'gx', 0, 0, tiled=True)  11 us
    ppermute x12, waiting for transfers between devices, shifted(): lax.ppermute(part, axis, perm)  10.9 us
    all_to_all x1, blocking collectives, local(): gathered = lax.all_to_all(copies, 'gy', 0, 0, tiled=True)  10.1 us
    ppermute x3, starting transfers between devices, local(): lax.ppermute(value, 'gx', [(a * 4 + z, a * 4 + (z ^ k)) for a in range(4)...  6.58 us
    all_to_all x1, starting transfers between devices, local(): pieces = lax.all_to_all(chip.reshape(8, FAR, DIRS), 'gy', 0, 0, tiled=True)  5.74 us
    ppermute x3, waiting for transfers between devices, local(): lax.ppermute(value, 'gx', [(a * 4 + z, a * 4 + (z ^ k)) for a in range(4)...  5.24 us
  transfers between devices with their start and end apart: 21, of which 10 were waited for; matrix products, arithmetic and copies ran while one was open for 0% of the time, Pallas kernels for 12%

profile of v5, /device:TPU:8, one launch (start us, length us, event | category | flops | bytes accessed | tf_op | source)
XLA Modules:
  0.0 97.6 jit_solution(116067015345625298)
XLA Ops:
  0.6 1.8 %prepare.1 = (f32[2,24,128]{2,1,0:T(8,128)S(1)}, f32[2,8,128]{2,1,0:T(8,128)S(1)}, f32[2,192,128]{2,1,0:T(8,128)S(1)}, f32[16,16,128]{2,1,0:T(8,128)}, f32[3,192...) custom-call(f32[3,192,128]{2,1,0:T(8,128)} %bitcast.27, ...), custom_call_target="tpu_custom_call" | custom-call | bytes 2097152 | tf_op jit(solution)/shard_map/prepare/pallas_call | solution.py:48
  2.6 11.0 %all-to-all-start = ((f32[16,16,128]{2,1,0:T(8,128)}), f32[16,16,128]{2,1,0:T(8,128)S(1)}, u32[]{:S(2)}, u32[]{:S(2)}) async-start(f32[16,16,128]{2,1,0:T(8,128)} %get-tuple-element.79), calls=%async_computation | async-start | bytes 262144 | tf_op jit(solution)/shard_map/all_to_all | solution.py:629
  13.6 6.2 %collective-permute-start = (f32[2,24,128]{2,1,0:T(8,128)S(1)}, f32[2,24,128]{2,1,0:T(8,128)S(1)}, u32[]{:S(2)}, u32[]{:S(2)}) collective-permute-start(f32[2,24,128]{2,1,0:T(8,128)S(1)} %get-tuple-element.66), channel_id=1, source_target_pairs={{16,0},{32,16},{48,32},{64,48},{80,64},{96,80},{112,96},{128,112},... | collective-permute-start | bytes 73736 | tf_op jit(solution)/shard_map/ppermute | solution.py:602
  19.8 0.4 collective-permute-start.1
  20.9 1.5 %phase.1 = (s32[32,128]{1,0:T(8,128)S(1)}, s32[1,128]{1,0:T(1,128)S(1)}, f32[4,128,128]{2,1,0:T(8,128)S(1)}, f32[2,128,128]{2,1,0:T(8,128)S(1)}, f32[2,128,128]{2,1,0:T(8,128)S(1)}) custom-call(s32[1]{0:T(128)} %bitcast.22.count_ref, s32[1,32]{1,0:T(1,128)} %bitcast.34, s32[32,128]{1,0:T(8,128)} %bitcast.33, s32[1,128]{1,0:T(1,128)} %bitcast.35, ...), custom_call_target="tpu_custom_call" | custom-call | bytes 2097152 | tf_op jit(solution)/shard_map/phase/pallas_call | solution.py:48
  22.4 1.1 %collective-permute-done.1.face_y = f32[2,8,128]{2,1,0:T(8,128)S(1)} collective-permute-done((f32[2,8,128]{2,1,0:T(8,128)S(1)}, f32[2,8,128]{2,1,0:T(8,128)S(1)}, u32[]{:S(2)}, u32[]{:S(2)}) %collective-permute-start.1) | collective-permute-done | bytes 8224 | tf_op jit(solution)/shard_map/ppermute | solution.py:602
  23.7 1.1 %collective-permute-start.3 = (f32[2,24,128]{2,1,0:T(8,128)S(1)}, f32[2,24,128]{2,1,0:T(8,128)S(1)}, u32[]{:S(2)}, u32[]{:S(2)}) collective-permute-start(f32[2,24,128]{2,1,0:T(8,128)S(1)} %get-tuple-element.74), channel_id=1, source_target_pairs={{0,16},{16,32},{32,48},{48,64},{64,80},{80,96},{96,112},{112,128},... | collective-permute-start | bytes 73736 | tf_op jit(solution)/shard_map/ppermute | solution.py:602
  24.8 1.6 %collective-permute-start.4 = (f32[2,8,128]{2,1,0:T(8,128)S(1)}, f32[2,8,128]{2,1,0:T(8,128)S(1)}, u32[]{:S(2)}, u32[]{:S(2)}) collective-permute-start(f32[2,8,128]{2,1,0:T(8,128)S(1)} %get-tuple-element.75), channel_id=1, source_target_pairs={{0,2},{2,4},{4,6},{6,8},{8,10},{10,12},{12,14},{14,0},{1,3},{3,5},... | collective-permute-start | bytes 24584 | tf_op jit(solution)/shard_map/ppermute | solution.py:602
  26.4 2.9 %scatter.1.dense = f32[4,192,128]{2,1,0:T(8,128)S(1)} custom-call(s32[32,128]{1,0:T(8,128)S(1)} %get-tuple-element.78.placed, f32[16,16,128]{2,1,0:T(8,128)S(1)} %all-to-all-done.fields_ref), custom_call_target="tpu_custom_call" | custom-call | bytes 2097152 | tf_op jit(solution)/shard_map/scatter/pallas_call | solution.py:48
  29.3 2.8 %collective-permute-done.3.face_x = f32[2,24,128]{2,1,0:T(8,128)S(1)} collective-permute-done((f32[2,24,128]{2,1,0:T(8,128)S(1)}, f32[2,24,128]{2,1,0:T(8,128)S(1)}, u32[]{:S(2)}, u32[]{:S(2)}) %collective-permute-start.3) | collective-permute-done | bytes 24608 | tf_op jit(solution)/shard_map/ppermute | solution.py:602
  32.4 2.6 %collective-permute-start.6 = (f32[2,24,128]{2,1,0:T(8,128)S(1)}, f32[2,24,128]{2,1,0:T(8,128)S(1)}, u32[]{:S(2)}, u32[]{:S(2)}) collective-permute-start(f32[2,24,128]{2,1,0:T(8,128)S(1)} %get-tuple-element.81), channel_id=1, source_target_pairs={{16,0},{32,16},{48,32},{64,48},{80,64},{96,80},{112,96},{128,112},... | collective-permute-start | bytes 73736 | tf_op jit(solution)/shard_map/ppermute | solution.py:602
  35.0 3.6 %collective-permute-start.7 = (f32[2,8,128]{2,1,0:T(8,128)S(1)}, f32[2,8,128]{2,1,0:T(8,128)S(1)}, u32[]{:S(2)}, u32[]{:S(2)}) collective-permute-start(f32[2,8,128]{2,1,0:T(8,128)S(1)} %get-tuple-element.82), channel_id=1, source_target_pairs={{2,0},{4,2},{6,4},{8,6},{10,8},{12,10},{14,12},{0,14},{3,1},{5,3},... | collective-permute-start | bytes 24584 | tf_op jit(solution)/shard_map/ppermute | solution.py:602
  38.6 2.9 %scatter2.1.dense = f32[4,192,128]{2,1,0:T(8,128)S(1)} custom-call(s32[32,128]{1,0:T(8,128)S(1)} %get-tuple-element.78.placed, f32[16,16,128]{2,1,0:T(8,128)S(1)} %all-to-all-done.fields_ref), custom_call_target="tpu_custom_call" | custom-call | bytes 2097152 | tf_op jit(solution)/shard_map/scatter2/pallas_call | solution.py:48
  42.0 0.7 collective-permute-start.10
  43.0 3.3 %collective-permute-done.10.face_y = f32[2,8,128]{2,1,0:T(8,128)S(1)} collective-permute-done((f32[2,8,128]{2,1,0:T(8,128)S(1)}, f32[2,8,128]{2,1,0:T(8,128)S(1)}, u32[]{:S(2)}, u32[]{:S(2)}) %collective-permute-start.10) | collective-permute-done | bytes 8224 | tf_op jit(solution)/shard_map/ppermute | solution.py:602
  46.3 3.7 %collective-permute-done.9.face_x = f32[2,24,128]{2,1,0:T(8,128)S(1)} collective-permute-done((f32[2,24,128]{2,1,0:T(8,128)S(1)}, f32[2,24,128]{2,1,0:T(8,128)S(1)}, u32[]{:S(2)}, u32[]{:S(2)}) %collective-permute-start.9) | collective-permute-done | bytes 24608 | tf_op jit(solution)/shard_map/ppermute | solution.py:602
  50.0 3.2 %final.1 = (f32[3,192,128]{2,1,0:T(8,128)S(1)}, f32[384,128]{1,0:T(8,128)S(1)}, f32[384,128]{1,0:T(8,128)S(1)}) custom-call(f32[3,192,128]{2,1,0:T(8,128)S(1)} %get-tuple-element.103.e_ref.e_new, f32[3,192,128]{2,1,0:T(8,128)S(1)} %get-tuple-element.88.h_ref, f32[2,24,128]{2,1,0:T(8,128)S(1)} %collective-permute-done.9.face_x, ...), custom_call_target="tpu_custom_call" | custom-call | bytes 2097152 | tf_op jit(solution)/shard_map/final/pallas_call | solution.py:48
  53.3 1.4 %collective-permute-done.12 = f32[384,128]{1,0:T(8,128)S(1)} collective-permute-done((f32[384,128]{1,0:T(8,128)S(1)}, f32[384,128]{1,0:T(8,128)S(1)}, u32[]{:S(2)}, u32[]{:S(2)}) %collective-permute-start.12) | collective-permute-done | bytes 196640 | tf_op jit(solution)/shard_map/ppermute | solution.py:675
  54.7 0.7 add.6
  55.4 5.7 %all-to-all-start.1 = ((f32[8,48,128]{2,1,0:T(8,128)}), f32[8,48,128]{2,1,0:T(8,128)S(1)}, u32[]{:S(2)}, u32[]{:S(2)}) async-start(f32[8,48,128]{2,1,0:T(8,128)} %bitcast.10), calls=%async_computation.1 | async-start | bytes 393216 | tf_op jit(solution)/shard_map/all_to_all | solution.py:677
  61.1 3.5 %drive.1 = f32[32,8,128]{2,1,0:T(8,128)S(1)} custom-call(f32[3,192,128]{2,1,0:T(8,128)S(1)} %get-tuple-element.64.e_ref.e_old, f32[3,192,128]{2,1,0:T(8,128)S(1)} %get-tuple-element.103.e_ref.e_new, s32[32,128]{1,0:T(8,128)S(1)} %get-tuple-element.78.placed), custom_call_target="tpu_custom_call" | custom-call | bytes 2097152 | tf_op jit(solution)/shard_map/drive/pallas_call | solution.py:48
  64.6 1.7 %all-to-all-done.1.pieces = f32[8,48,128]{2,1,0:T(8,128)S(1)} async-done(((f32[8,48,128]{2,1,0:T(8,128)}), f32[8,48,128]{2,1,0:T(8,128)S(1)}, u32[]{:S(2)}, u32[]{:S(2)}) %all-to-all-start.1) | async-done | bytes 196640 | tf_op jit(solution)/shard_map/all_to_all | solution.py:677
  66.6 4.6 %collective-permute-start.15 = (f32[112,128]{1,0:T(8,128)S(1)}, f32[112,128]{1,0:T(8,128)S(1)}, u32[]{:S(2)}, u32[]{:S(2)}) collective-permute-start(f32[112,128]{1,0:T(8,128)S(1)} %get-tuple-element.107), channel_id=1, source_target_pairs={{0,192},{16,208},{32,224},{48,240},{64,128},{80,144},{96,160},{112... | collective-permute-start | bytes 172040 | tf_op jit(solution)/shard_map/ppermute | solution.py:690
  71.2 1.1 %collective-permute-done.14.two = f32[112,128]{1,0:T(8,128)S(1)} collective-permute-done((f32[112,128]{1,0:T(8,128)S(1)}, f32[112,128]{1,0:T(8,128)S(1)}, u32[]{:S(2)}, u32[]{:S(2)}) %collective-permute-start.14) | collective-permute-done | bytes 57376 | tf_op jit(solution)/shard_map/ppermute | solution.py:690
  72.3 1.1 %collective-permute-done.15.three = f32[112,128]{1,0:T(8,128)S(1)} collective-permute-done((f32[112,128]{1,0:T(8,128)S(1)}, f32[112,128]{1,0:T(8,128)S(1)}, u32[]{:S(2)}, u32[]{:S(2)}) %collective-permute-start.15) | collective-permute-done | bytes 57376 | tf_op jit(solution)/shard_map/ppermute | solution.py:690
  73.5 6.2 %collective-permute-start.17 = (f32[112,128]{1,0:T(8,128)S(1)}, f32[112,128]{1,0:T(8,128)S(1)}, u32[]{:S(2)}, u32[]{:S(2)}) collective-permute-start(f32[112,128]{1,0:T(8,128)S(1)} %get-tuple-element.111), channel_id=1, source_target_pairs={{0,32},{16,48},{32,0},{48,16},{64,96},{80,112},{96,64},{112,80},{1... | collective-permute-start | bytes 172040 | tf_op jit(solution)/shard_map/ppermute | solution.py:702
  80.0 0.8 store.1
  80.8 2.7 %collective-permute-done.17.two = f32[112,128]{1,0:T(8,128)S(1)} collective-permute-done((f32[112,128]{1,0:T(8,128)S(1)}, f32[112,128]{1,0:T(8,128)S(1)}, u32[]{:S(2)}, u32[]{:S(2)}) %collective-permute-start.17) | collective-permute-done | bytes 57376 | tf_op jit(solution)/shard_map/ppermute | solution.py:702
  83.5 2.6 %collective-permute-done.18.three = f32[112,128]{1,0:T(8,128)S(1)} collective-permute-done((f32[112,128]{1,0:T(8,128)S(1)}, f32[112,128]{1,0:T(8,128)S(1)}, u32[]{:S(2)}, u32[]{:S(2)}) %collective-permute-start.18) | collective-permute-done | bytes 57376 | tf_op jit(solution)/shard_map/ppermute | solution.py:702
  86.1 0.8 atoms.1
  86.9 10.1 %all_to_all.15 = f32[8,48,128]{2,1,0:T(8,128)S(1)} all-to-all(f32[8,48,128]{2,1,0:T(8,128)S(1)} %get-tuple-element.123), channel_id=1, replica_groups=mesh['gx'=16,'gy'=8,'gz'=2] {'gy'}, dimensions={0} | all-to-all | bytes 393216 | tf_op jit(solution)/shard_map/all_to_all | solution.py:721
  96.9 0.7 add.7
  (30 shorter events, 2.1 us)
Async XLA Ops:
  2.5 21.0 %collective-permute-start.2 = (f32[2,192,128]{2,1,0:T(8,128)S(1)}, f32[2,192,128]{2,1,0:T(8,128)S(1)}, u32[]{:S(2)}, u32[]{:S(2)}) collective-permute-start(f32[2,192,128]{2,1,0:T(8,128)S(1)} %get-tuple-element.68), channel_id=1, source_target_pairs={{1,0},{0,1},{3,2},{2,3},{5,4},{4,5},{7,6},{6,7},{9,8},{8,9},{11,10... | collective-permute-start | bytes 589832 | tf_op jit(solution)/shard_map/ppermute | solution.py:602
  2.6 23.8 %all-to-all-start = ((f32[16,16,128]{2,1,0:T(8,128)}), f32[16,16,128]{2,1,0:T(8,128)S(1)}, u32[]{:S(2)}, u32[]{:S(2)}) async-start(f32[16,16,128]{2,1,0:T(8,128)} %get-tuple-element.79), calls=%async_computation | async-start | bytes 262144 | tf_op jit(solution)/shard_map/all_to_all | solution.py:629
  13.6 9.8 %collective-permute-start = (f32[2,24,128]{2,1,0:T(8,128)S(1)}, f32[2,24,128]{2,1,0:T(8,128)S(1)}, u32[]{:S(2)}, u32[]{:S(2)}) collective-permute-start(f32[2,24,128]{2,1,0:T(8,128)S(1)} %get-tuple-element.66), channel_id=1, source_target_pairs={{16,0},{32,16},{48,32},{64,48},{80,64},{96,80},{112,96},{128,112},... | collective-permute-start | bytes 73736 | tf_op jit(solution)/shard_map/ppermute | solution.py:602
  19.8 3.7 %collective-permute-start.1 = (f32[2,8,128]{2,1,0:T(8,128)S(1)}, f32[2,8,128]{2,1,0:T(8,128)S(1)}, u32[]{:S(2)}, u32[]{:S(2)}) collective-permute-start(f32[2,8,128]{2,1,0:T(8,128)S(1)} %get-tuple-element.67), channel_id=1, source_target_pairs={{2,0},{4,2},{6,4},{8,6},{10,8},{12,10},{14,12},{0,14},{3,1},{5,3},... | collective-permute-start | bytes 24584 | tf_op jit(solution)/shard_map/ppermute | solution.py:602
  23.6 8.5 %collective-permute-start.5 = (f32[2,192,128]{2,1,0:T(8,128)S(1)}, f32[2,192,128]{2,1,0:T(8,128)S(1)}, u32[]{:S(2)}, u32[]{:S(2)}) collective-permute-start(f32[2,192,128]{2,1,0:T(8,128)S(1)} %get-tuple-element.76), channel_id=1, source_target_pairs={{0,1},{1,0},{2,3},{3,2},{4,5},{5,4},{6,7},{7,6},{8,9},{9,8},{10,11... | collective-permute-start | bytes 589832 | tf_op jit(solution)/shard_map/ppermute | solution.py:602
  23.7 8.4 %collective-permute-start.3 = (f32[2,24,128]{2,1,0:T(8,128)S(1)}, f32[2,24,128]{2,1,0:T(8,128)S(1)}, u32[]{:S(2)}, u32[]{:S(2)}) collective-permute-start(f32[2,24,128]{2,1,0:T(8,128)S(1)} %get-tuple-element.74), channel_id=1, source_target_pairs={{0,16},{16,32},{32,48},{48,64},{64,80},{80,96},{96,112},{112,128},... | collective-permute-start | bytes 73736 | tf_op jit(solution)/shard_map/ppermute | solution.py:602
  24.8 4.5 %collective-permute-start.4 = (f32[2,8,128]{2,1,0:T(8,128)S(1)}, f32[2,8,128]{2,1,0:T(8,128)S(1)}, u32[]{:S(2)}, u32[]{:S(2)}) collective-permute-start(f32[2,8,128]{2,1,0:T(8,128)S(1)} %get-tuple-element.75), channel_id=1, source_target_pairs={{0,2},{2,4},{4,6},{6,8},{8,10},{10,12},{12,14},{14,0},{1,3},{3,5},... | collective-permute-start | bytes 24584 | tf_op jit(solution)/shard_map/ppermute | solution.py:602
  32.3 9.3 %collective-permute-start.8 = (f32[2,192,128]{2,1,0:T(8,128)S(1)}, f32[2,192,128]{2,1,0:T(8,128)S(1)}, u32[]{:S(2)}, u32[]{:S(2)}) collective-permute-start(f32[2,192,128]{2,1,0:T(8,128)S(1)} %get-tuple-element.83), channel_id=1, source_target_pairs={{1,0},{0,1},{3,2},{2,3},{5,4},{4,5},{7,6},{6,7},{9,8},{8,9},{11,10... | collective-permute-start | bytes 589832 | tf_op jit(solution)/shard_map/ppermute | solution.py:602
  32.4 9.1 %collective-permute-start.6 = (f32[2,24,128]{2,1,0:T(8,128)S(1)}, f32[2,24,128]{2,1,0:T(8,128)S(1)}, u32[]{:S(2)}, u32[]{:S(2)}) collective-permute-start(f32[2,24,128]{2,1,0:T(8,128)S(1)} %get-tuple-element.81), channel_id=1, source_target_pairs={{16,0},{32,16},{48,32},{64,48},{80,64},{96,80},{112,96},{128,112},... | collective-permute-start | bytes 73736 | tf_op jit(solution)/shard_map/ppermute | solution.py:602
  35.0 6.6 %collective-permute-start.7 = (f32[2,8,128]{2,1,0:T(8,128)S(1)}, f32[2,8,128]{2,1,0:T(8,128)S(1)}, u32[]{:S(2)}, u32[]{:S(2)}) collective-permute-start(f32[2,8,128]{2,1,0:T(8,128)S(1)} %get-tuple-element.82), channel_id=1, source_target_pairs={{2,0},{4,2},{6,4},{8,6},{10,8},{12,10},{14,12},{0,14},{3,1},{5,3},... | collective-permute-start | bytes 24584 | tf_op jit(solution)/shard_map/ppermute | solution.py:602
  41.8 8.2 %collective-permute-start.11 = (f32[2,192,128]{2,1,0:T(8,128)S(1)}, f32[2,192,128]{2,1,0:T(8,128)S(1)}, u32[]{:S(2)}, u32[]{:S(2)}) collective-permute-start(f32[2,192,128]{2,1,0:T(8,128)S(1)} %get-tuple-element.91), channel_id=1, source_target_pairs={{0,1},{1,0},{2,3},{3,2},{4,5},{5,4},{6,7},{7,6},{8,9},{9,8},{10,11... | collective-permute-start | bytes 589832 | tf_op jit(solution)/shard_map/ppermute | solution.py:602
  41.9 8.1 %collective-permute-start.9 = (f32[2,24,128]{2,1,0:T(8,128)S(1)}, f32[2,24,128]{2,1,0:T(8,128)S(1)}, u32[]{:S(2)}, u32[]{:S(2)}) collective-permute-start(f32[2,24,128]{2,1,0:T(8,128)S(1)} %get-tuple-element.89), channel_id=1, source_target_pairs={{0,16},{16,32},{32,48},{48,64},{64,80},{80,96},{96,112},{112,128},... | collective-permute-start | bytes 73736 | tf_op jit(solution)/shard_map/ppermute | solution.py:602
  42.0 4.4 %collective-permute-start.10 = (f32[2,8,128]{2,1,0:T(8,128)S(1)}, f32[2,8,128]{2,1,0:T(8,128)S(1)}, u32[]{:S(2)}, u32[]{:S(2)}) collective-permute-start(f32[2,8,128]{2,1,0:T(8,128)S(1)} %get-tuple-element.90), channel_id=1, source_target_pairs={{0,2},{2,4},{4,6},{6,8},{8,10},{10,12},{12,14},{14,0},{1,3},{3,5},... | collective-permute-start | bytes 24584 | tf_op jit(solution)/shard_map/ppermute | solution.py:602
  53.2 1.5 %collective-permute-start.12 = (f32[384,128]{1,0:T(8,128)S(1)}, f32[384,128]{1,0:T(8,128)S(1)}, u32[]{:S(2)}, u32[]{:S(2)}) collective-permute-start(f32[384,128]{1,0:T(8,128)S(1)} %get-tuple-element.101), channel_id=1, source_target_pairs={{1,0},{0,1},{3,2},{2,3},{5,4},{4,5},{7,6},{6,7},{9,8},{8,9},{11,10... | collective-permute-start | bytes 589832 | tf_op jit(solution)/shard_map/ppermute | solution.py:675
  55.4 11.0 %all-to-all-start.1 = ((f32[8,48,128]{2,1,0:T(8,128)}), f32[8,48,128]{2,1,0:T(8,128)S(1)}, u32[]{:S(2)}, u32[]{:S(2)}) async-start(f32[8,48,128]{2,1,0:T(8,128)} %bitcast.10), calls=%async_computation.1 | async-start | bytes 393216 | tf_op jit(solution)/shard_map/all_to_all | solution.py:677
  66.4 4.8 %collective-permute-start.13 = (f32[112,128]{1,0:T(8,128)S(1)}, f32[112,128]{1,0:T(8,128)S(1)}, u32[]{:S(2)}, u32[]{:S(2)}) collective-permute-start(f32[112,128]{1,0:T(8,128)S(1)} %get-tuple-element.105), channel_id=1, source_target_pairs={{0,64},{16,80},{32,96},{48,112},{64,0},{80,16},{96,32},{112,48},{1... | collective-permute-start | bytes 172040 | tf_op jit(solution)/shard_map/ppermute | solution.py:690
  66.5 5.8 %collective-permute-start.14 = (f32[112,128]{1,0:T(8,128)S(1)}, f32[112,128]{1,0:T(8,128)S(1)}, u32[]{:S(2)}, u32[]{:S(2)}) collective-permute-start(f32[112,128]{1,0:T(8,128)S(1)} %get-tuple-element.106), channel_id=1, source_target_pairs={{0,128},{16,144},{32,160},{48,176},{64,192},{80,208},{96,224},{112... | collective-permute-start | bytes 172040 | tf_op jit(solution)/shard_map/ppermute | solution.py:690
  66.6 6.7 %collective-permute-start.15 = (f32[112,128]{1,0:T(8,128)S(1)}, f32[112,128]{1,0:T(8,128)S(1)}, u32[]{:S(2)}, u32[]{:S(2)}) collective-permute-start(f32[112,128]{1,0:T(8,128)S(1)} %get-tuple-element.107), channel_id=1, source_target_pairs={{0,192},{16,208},{32,224},{48,240},{64,128},{80,144},{96,160},{112... | collective-permute-start | bytes 172040 | tf_op jit(solution)/shard_map/ppermute | solution.py:690
  73.4 7.4 %collective-permute-start.16 = (f32[112,128]{1,0:T(8,128)S(1)}, f32[112,128]{1,0:T(8,128)S(1)}, u32[]{:S(2)}, u32[]{:S(2)}) collective-permute-start(f32[112,128]{1,0:T(8,128)S(1)} %get-tuple-element.110), channel_id=1, source_target_pairs={{0,16},{16,0},{32,48},{48,32},{64,80},{80,64},{96,112},{112,96},{1... | collective-permute-start | bytes 172040 | tf_op jit(solution)/shard_map/ppermute | solution.py:702
  73.5 10.0 %collective-permute-start.17 = (f32[112,128]{1,0:T(8,128)S(1)}, f32[112,128]{1,0:T(8,128)S(1)}, u32[]{:S(2)}, u32[]{:S(2)}) collective-permute-start(f32[112,128]{1,0:T(8,128)S(1)} %get-tuple-element.111), channel_id=1, source_target_pairs={{0,32},{16,48},{32,0},{48,16},{64,96},{80,112},{96,64},{112,80},{1... | collective-permute-start | bytes 172040 | tf_op jit(solution)/shard_map/ppermute | solution.py:702
  79.7 6.4 %collective-permute-start.18 = (f32[112,128]{1,0:T(8,128)S(1)}, f32[112,128]{1,0:T(8,128)S(1)}, u32[]{:S(2)}, u32[]{:S(2)}) collective-permute-start(f32[112,128]{1,0:T(8,128)S(1)} %get-tuple-element.112), channel_id=1, source_target_pairs={{0,48},{16,32},{32,16},{48,0},{64,112},{80,96},{96,80},{112,64},{1... | collective-permute-start | bytes 172040 | tf_op jit(solution)/shard_map/ppermute | solution.py:702
  86.9 10.1 %copy-start = (f32[32,12,128]{2,0,1:T(8,128)S(1)}, f32[32,12,128]{2,0,1:T(8,128)}, u32[]{:S(2)}) copy-start(f32[32,12,128]{2,0,1:T(8,128)} %param.20) | copy-start | bytes 589828

commit v6 on v5

--- a/solution.py
+++ b/solution.py
@@ -321,22 +321,31 @@
 TAKE = 8
 
 
-def drive_kernel(e_old, e_new, placed, drives, high, low):
-    high[...], low[...] = stacked([(ref, comp) for ref in (e_old, e_new) for comp in range(3)])
-    drives[...] = jnp.zeros_like(drives)
+def gather_drive(field_ref, placed, drives, first, high, low):
+    high[...], low[...] = stacked([(field_ref, comp) for comp in range(3)])
 
     def group(index, carry):
         lines = placed[pl.ds(TAKE * index, TAKE)]
         offsets = jnp.concatenate([lines[slot : slot + 1] for slot in range(TAKE)], axis=1)
         got = gather_lines(high[...], low[...], offsets, TAKE * CZ)
-        for field in range(6):
+        for comp in range(3):
             for slot in range(TAKE):
-                drives[TAKE * index + slot, field : field + 1] = got[field][
+                drives[first + comp, pl.ds(TAKE * index + slot, 1)] = got[comp][
                     :, slot * CZ : (slot + 1) * CZ
                 ]
         return carry
 
     lax.fori_loop(0, SLOTS // TAKE, group, 0)
+
+
+def first_drive_kernel(e_ref, placed, e_seen, h_seen, surf_ref, drives, sampled, high, low):
+    gather_drive(e_ref, placed, drives, 0, high, low)
+    sample_rows(e_seen, h_seen, surf_ref, sampled)
+
+
+def second_drive_kernel(e_ref, placed, before, drives, high, low):
+    drives[0:3] = before[...]
+    gather_drive(e_ref, placed, drives, 3, high, low)
 
 
 def sample_rows(e_ref, h_ref, surf_ref, sampled):
@@ -409,13 +418,25 @@
 
 
 FAR = 48
-LOAD = 64
-CELL = 16
+LOAD = 48
 
 
 def partner(step):
     index = lax.axis_index("gx")
     return (index >> 2) ^ step, (index & 3) ^ step
+
+
+def chunk(drives, owner_x):
+    return drives[:, pl.ds(pl.multiple_of(8 * owner_x, 8), 8)]
+
+
+def pick(tiles, pairs):
+    rows = row_index(8, CZ) >> 1
+    result = jnp.zeros((8, CZ), F32)
+    for tile, (taken, put) in zip(tiles, pairs):
+        moved = pltpu.roll(tile, (2 * put - 2 * taken + 8) & 7, 0)
+        result = jnp.where(rows == put, moved, result)
+    return result
 
 
 def fold_kernel(pieces, drives, total, *loads):
@@ -423,37 +444,34 @@
     for step in (1, 2, 3):
         load = loads[step - 1]
         load[0:FAR] = total[...]
-        load[FAR:] = drives[pl.ds(partner(step)[0], 1)][0]
+        load[FAR:] = chunk(drives, partner(step)[0]).reshape(LOAD, CZ)
 
 
 def relay_kernel(total_in, drives, one, two, three, total, kept, *loads):
-    arrived = (one, two, three)
     total[...] = (total_in[...] + one[0:FAR]) + (two[0:FAR] + three[0:FAR])
-    own = partner(0)[0]
+    held = [chunk(drives, partner(0)[0]).reshape(LOAD, CZ)]
+    held += [arrived[FAR:] for arrived in (one, two, three)]
     for step in range(4):
         target = partner(step)[1]
-        out, first = (kept, 0) if step == 0 else (loads[step - 1], FAR)
+        out, first = (loads[step - 1], FAR) if step else (kept, 0)
         if step:
             out[0:FAR] = total[...]
-        spot = pl.multiple_of(target * CELL, CELL)
-        for source in range(4):
-            if source == 0:
-                piece = drives[pl.ds(own, 1), pl.ds(spot, CELL)][0]
-            else:
-                piece = arrived[source - 1][pl.ds(FAR + spot, CELL)]
-            out[first + source * CELL : first + (source + 1) * CELL] = piece
+        for field in range(6):
+            tiles = [value[8 * field : 8 * field + 8] for value in held]
+            start = first + 8 * field
+            out[start : start + 8] = pick(tiles, [(target, source) for source in range(4)])
 
 
 def finish_kernel(total_in, kept, one, two, three, spread_out, back):
     total = (total_in[...] + one[0:FAR]) + (two[0:FAR] + three[0:FAR])
     for peer in range(8):
         spread_out[peer] = total
-    for step, arrived in enumerate((kept, one, two, three)):
-        first = FAR if step else 0
-        for source in range(4):
-            brick = partner(source)[0] * 4 + partner(step)[1]
-            start = first + source * CELL
-            back[pl.ds(brick, 1)] = arrived[start : start + CELL][None]
+    held = [kept[...]] + [arrived[FAR:] for arrived in (one, two, three)]
+    for source in range(4):
+        rows = pl.ds(pl.multiple_of(8 * partner(source)[0], 8), 8)
+        for field in range(6):
+            tiles = [value[8 * field : 8 * field + 8] for value in held]
+            back[field, rows] = pick(tiles, [(source, partner(step)[1]) for step in range(4)])
 
 
 def final_kernel(
@@ -536,7 +554,7 @@
     ground, lower, lasing, upper = [state_ref[6 + level] for level in range(4)]
     pump = pump_ref[...]
     for step in range(STEPS):
-        drive = [drives[:, 3 * step + c] for c in range(3)]
+        drive = [drives[3 * step + c] for c in range(3)]
         inversion = lasing - lower
         power = jnp.zeros_like(pump)
         for c in range(3):
@@ -645,10 +663,18 @@
         ),
         in_specs=[pl.BlockSpec(memory_space=pltpu.SMEM), hbm, vmem, vmem, vmem],
         scratch=[pltpu.SMEM((1, SLOTS), jnp.int32), pltpu.SemaphoreType.DMA],
+        moved=MIB // 4,
         name="phase",
     )
     *near, placed = lax.optimization_barrier((*near, placed))
-    h_one, *edge = call(magnetic_kernel, (dense,) + faces, (e_old, h_old, *near), name="magnetic")
+    h_one, *edge = call(
+        magnetic_kernel,
+        (dense,) + faces,
+        (e_old, h_old, *near),
+        flops=10**11,
+        moved=100 * MIB,
+        name="magnetic",
+    )
     edge = shifted(edge, up)
     spread_now = scattered(0, placed, fields, "scatter")
     e_one, *near, rates = call(
@@ -663,7 +689,14 @@
     h_two, *edge = call(magnetic_kernel, (dense,) + faces, (e_one, h_one, *near), name="magnetic2")
     edge = shifted(edge, up)
     e_seen, h_seen, h_two = lax.optimization_barrier((e_one, h_one, h_two))
-    early = call(sample_rows, shape(8, CZ), (e_seen, h_seen, surf), name="sample")
+    halves = [pltpu.VMEM((3 * HALF, WIDE), BF16)] * 2
+    before, early = call(
+        first_drive_kernel,
+        (shape(3, SLOTS, CZ), shape(8, CZ)),
+        (e_old, placed, e_seen, h_seen, surf),
+        scratch=halves,
+        name="drive",
+    )
     part = shape(12 * FREQ // 2, DIRS)
     e_two, keep, send = call(
         final_kernel,
@@ -676,12 +709,12 @@
     chip, e_seen = lax.optimization_barrier((chip, e_one))
     pieces = lax.all_to_all(chip.reshape(8, FAR, DIRS), "gy", 0, 0, tiled=True)
     drives = call(
-        drive_kernel,
-        shape(SLOTS, 8, CZ),
-        (e_old, e_seen, placed),
-        scratch=[pltpu.VMEM((6 * HALF, WIDE), BF16)] * 2,
-        name="drive",
-    ).reshape(4, LOAD, CZ)
+        second_drive_kernel,
+        shape(6, SLOTS, CZ),
+        (e_seen, placed, before),
+        scratch=halves,
+        name="drive2",
+    )
     load = shape(FAR + LOAD, CZ)
     total, *loads = call(
         fold_kernel, (shape(FAR, DIRS),) + (load,) * 3, (pieces, drives), name="fold"
@@ -707,14 +740,14 @@
     e_out, h_out = call(store_kernel, (dense, dense), (e_two, h_two), name="store")
     copies, back = call(
         finish_kernel,
-        (shape(8, FAR, DIRS), shape(SLOTS // 2, CELL, CZ)),
+        (shape(8, FAR, DIRS), shape(6, SLOTS, CZ)),
         (total, kept, *loads),
         name="finish",
     )
     state_out = call(
         atoms_kernel,
         shape(10, SLOTS, CZ),
-        (state, pumps, back.reshape(SLOTS, 8, CZ)),
+        (state, pumps, back),
         name="atoms",
     )
     copies, state_out, e_out, h_out = lax.optimization_barrier((copies, state_out, e_out, h_out))

time: 98 us -> 93 us (0.949)
  starting transfers between devices: 44.8 us -> 40.3 us
  waiting for transfers between devices: 21.4 us -> 19.8 us
    all_to_all x1, starting transfers between devices: 11 us -> 3.51 us  [local(): fields = lax.all_to_all(packed, 'gx', 0, 0, tiled=True)]
    ppermute x12, waiting for transfers between devices: 10.9 us -> 3.78 us  [shifted(): lax.ppermute(part, axis, perm)]
    all_to_all x1, waiting for transfers between devices: 0.01 us -> 4.23 us  [local(): fields = lax.all_to_all(packed, 'gx', 0, 0, tiled=True)]
    ppermute x12, starting transfers between devices: 16.6 us -> 20.3 us  [shifted(): lax.ppermute(part, axis, perm)]
    ppermute x3, waiting for transfers between devices: 5.24 us -> 3.61 us  [local(): lax.ppermute(value, 'gx', [(a * 4 + z, a * 4 + (z ^ k)) for a in range(4)...]
    ppermute x3, waiting for transfers between devices: 2.15 us -> 3.67 us  [local(): lax.ppermute(value, 'gx', [(a * 4 + z, (a ^ k) * 4 + z) for a in range(4)...]
    all_to_all x1, waiting for transfers between devices: 1.74 us -> 3.04 us  [local(): pieces = lax.all_to_all(chip.reshape(8, FAR, DIRS), 'gy', 0, 0, tiled=True)]
  transfers between devices with their start and end apart: 21 -> 21, of which waited for: 10 -> 9; matrix products, arithmetic and copies ran while one was open for 0% -> 0% of each run, Pallas kernels for 12% -> 14%
where the time goes in v6:
time: 93 us; the launch traced here: 92.6 us
  starting transfers between devices  40.3 us (43%)
  waiting for transfers between devices  19.8 us (21%)
  Pallas kernels  19.3 us (21%)
  blocking collectives  10.4 us (11%)
  between operations  1.48 us (2%)
  other arithmetic  1.4 us (2%)
    ppermute x12, starting transfers between devices, shifted(): lax.ppermute(part, axis, perm)  20.3 us
    pallas_call x15, Pallas kernels, call(): pl.pallas_call(kernel, out_shape=outs, in_specs=in_specs or [pl.BlockSpec...  19.3 us
    all_to_all x1, blocking collectives, local(): gathered = lax.all_to_all(copies, 'gy', 0, 0, tiled=True)  10.4 us
    ppermute x3, starting transfers between devices, local(): lax.ppermute(value, 'gx', [(a * 4 + z, a * 4 + (z ^ k)) for a in range(4)...  6.58 us
    all_to_all x1, starting transfers between devices, local(): pieces = lax.all_to_all(chip.reshape(8, FAR, DIRS), 'gy', 0, 0, tiled=True)  4.98 us
    ppermute x3, starting transfers between devices, local(): lax.ppermute(value, 'gx', [(a * 4 + z, (a ^ k) * 4 + z) for a in range(4)...  4.79 us
    all_to_all x1, waiting for transfers between devices, local(): fields = lax.all_to_all(packed, 'gx', 0, 0, tiled=True)  4.23 us
    ppermute x12, waiting for transfers between devices, shifted(): lax.ppermute(part, axis, perm)  3.78 us
  transfers between devices with their start and end apart: 21, of which 9 were waited for; matrix products, arithmetic and copies ran while one was open for 0% of the time, Pallas kernels for 14%

profile of v6, /device:TPU:8, one launch (start us, length us, event | category | flops | bytes accessed | tf_op | source)
XLA Modules:
  0.0 92.6 jit_solution(5191425523970531597)
XLA Ops:
  0.6 1.8 %prepare.1 = (f32[2,24,128]{2,1,0:T(8,128)S(1)}, f32[2,8,128]{2,1,0:T(8,128)S(1)}, f32[2,192,128]{2,1,0:T(8,128)S(1)}, f32[16,16,128]{2,1,0:T(8,128)}, f32[3,192...) custom-call(f32[3,192,128]{2,1,0:T(8,128)} %bitcast.22, ...), custom_call_target="tpu_custom_call" | custom-call | bytes 2097152 | tf_op jit(solution)/shard_map/prepare/pallas_call | solution.py:48
  2.6 8.6 %collective-permute-start = (f32[2,24,128]{2,1,0:T(8,128)S(1)}, f32[2,24,128]{2,1,0:T(8,128)S(1)}, u32[]{:S(2)}, u32[]{:S(2)}) collective-permute-start(f32[2,24,128]{2,1,0:T(8,128)S(1)} %get-tuple-element.68), channel_id=1, source_target_pairs={{16,0},{32,16},{48,32},{64,48},{80,64},{96,80},{112,96},{128,112},... | collective-permute-start | bytes 73736 | tf_op jit(solution)/shard_map/ppermute | solution.py:620
  11.6 3.5 %all-to-all-start = ((f32[16,16,128]{2,1,0:T(8,128)}), f32[16,16,128]{2,1,0:T(8,128)S(1)}, u32[]{:S(2)}, u32[]{:S(2)}) async-start(f32[16,16,128]{2,1,0:T(8,128)} %get-tuple-element.81), calls=%async_computation | async-start | bytes 262144 | tf_op jit(solution)/shard_map/all_to_all | solution.py:647
  15.8 1.5 %phase.1 = (s32[32,128]{1,0:T(8,128)S(1)}, s32[1,128]{1,0:T(1,128)S(1)}, f32[4,128,128]{2,1,0:T(8,128)S(1)}, f32[2,128,128]{2,1,0:T(8,128)S(1)}, f32[2,128,128]{2,1,0:T(8,128)S(1)}) custom-call(s32[1]{0:T(128)} %bitcast.20.count_ref, s32[1,32]{1,0:T(1,128)} %bitcast.29, s32[32,128]{1,0:T(8,128)} %bitcast.28, s32[1,128]{1,0:T(1,128)} %bitcast.30, ...), custom_call_target="tpu_custom_call" | custom-call | bytes 262144 | tf_op jit(solution)/shard_map/phase/pallas_call | solution.py:48
  17.6 2.8 %collective-permute-start.3 = (f32[2,24,128]{2,1,0:T(8,128)S(1)}, f32[2,24,128]{2,1,0:T(8,128)S(1)}, u32[]{:S(2)}, u32[]{:S(2)}) collective-permute-start(f32[2,24,128]{2,1,0:T(8,128)S(1)} %get-tuple-element.76), channel_id=1, source_target_pairs={{0,16},{16,32},{32,48},{48,64},{64,80},{80,96},{96,112},{112,128},... | collective-permute-start | bytes 73736 | tf_op jit(solution)/shard_map/ppermute | solution.py:620
  20.3 1.6 %collective-permute-start.4 = (f32[2,8,128]{2,1,0:T(8,128)S(1)}, f32[2,8,128]{2,1,0:T(8,128)S(1)}, u32[]{:S(2)}, u32[]{:S(2)}) collective-permute-start(f32[2,8,128]{2,1,0:T(8,128)S(1)} %get-tuple-element.77), channel_id=1, source_target_pairs={{0,2},{2,4},{4,6},{6,8},{8,10},{10,12},{12,14},{14,0},{1,3},{3,5},... | collective-permute-start | bytes 24584 | tf_op jit(solution)/shard_map/ppermute | solution.py:620
  21.9 4.2 %all-to-all-done.fields_ref = f32[16,16,128]{2,1,0:T(8,128)S(1)} async-done(((f32[16,16,128]{2,1,0:T(8,128)}), f32[16,16,128]{2,1,0:T(8,128)S(1)}, u32[]{:S(2)}, u32[]{:S(2)}) %all-to-all-start) | async-done | bytes 131104 | tf_op jit(solution)/shard_map/all_to_all | solution.py:647
  26.1 2.9 %scatter.1.dense = f32[4,192,128]{2,1,0:T(8,128)S(1)} custom-call(s32[32,128]{1,0:T(8,128)S(1)} %get-tuple-element.80.placed, f32[16,16,128]{2,1,0:T(8,128)S(1)} %all-to-all-done.fields_ref), custom_call_target="tpu_custom_call" | custom-call | bytes 2097152 | tf_op jit(solution)/shard_map/scatter/pallas_call | solution.py:48
  29.5 1.2 %collective-permute-start.6 = (f32[2,24,128]{2,1,0:T(8,128)S(1)}, f32[2,24,128]{2,1,0:T(8,128)S(1)}, u32[]{:S(2)}, u32[]{:S(2)}) collective-permute-start(f32[2,24,128]{2,1,0:T(8,128)S(1)} %get-tuple-element.83), channel_id=1, source_target_pairs={{16,0},{32,16},{48,32},{64,48},{80,64},{96,80},{112,96},{128,112},... | collective-permute-start | bytes 73736 | tf_op jit(solution)/shard_map/ppermute | solution.py:620
  30.7 3.5 %collective-permute-start.7 = (f32[2,8,128]{2,1,0:T(8,128)S(1)}, f32[2,8,128]{2,1,0:T(8,128)S(1)}, u32[]{:S(2)}, u32[]{:S(2)}) collective-permute-start(f32[2,8,128]{2,1,0:T(8,128)S(1)} %get-tuple-element.84), channel_id=1, source_target_pairs={{2,0},{4,2},{6,4},{8,6},{10,8},{12,10},{14,12},{0,14},{3,1},{5,3},... | collective-permute-start | bytes 24584 | tf_op jit(solution)/shard_map/ppermute | solution.py:620
  34.1 2.9 %scatter2.1.dense = f32[4,192,128]{2,1,0:T(8,128)S(1)} custom-call(s32[32,128]{1,0:T(8,128)S(1)} %get-tuple-element.80.placed, f32[16,16,128]{2,1,0:T(8,128)S(1)} %all-to-all-done.fields_ref), custom_call_target="tpu_custom_call" | custom-call | bytes 2097152 | tf_op jit(solution)/shard_map/scatter2/pallas_call | solution.py:48
  37.4 1.9 %collective-permute-start.9 = (f32[2,24,128]{2,1,0:T(8,128)S(1)}, f32[2,24,128]{2,1,0:T(8,128)S(1)}, u32[]{:S(2)}, u32[]{:S(2)}) collective-permute-start(f32[2,24,128]{2,1,0:T(8,128)S(1)} %get-tuple-element.91), channel_id=1, source_target_pairs={{0,16},{16,32},{32,48},{48,64},{64,80},{80,96},{96,112},{112,128},... | collective-permute-start | bytes 73736 | tf_op jit(solution)/shard_map/ppermute | solution.py:620
  39.2 2.5 %drive.1 = (f32[3,32,128]{2,1,0:T(8,128)S(1)}, f32[8,128]{1,0:T(8,128)S(1)}) custom-call(f32[3,192,128]{2,1,0:T(8,128)S(1)} %get-tuple-element.66.e_ref, s32[32,128]{1,0:T(8,128)S(1)} %get-tuple-element.80.placed, f32[3,192,128]{2,1,0:T(8,128)S(1)} %get-tuple-element.106.e_ref.e_seen, f32[3,192,128]{2,1,0:T(8,128)S(1)} %get-tuple-element.98.h_ref.h_seen, ...), custom_call_target="tpu_custom_call" | custom-call | bytes 2097152 | tf_op jit(solution)/shard_map/drive/pallas_call | solution.py:48
  41.8 1.1 %collective-permute-done.10.face_y = f32[2,8,128]{2,1,0:T(8,128)S(1)} collective-permute-done((f32[2,8,128]{2,1,0:T(8,128)S(1)}, f32[2,8,128]{2,1,0:T(8,128)S(1)}, u32[]{:S(2)}, u32[]{:S(2)}) %collective-permute-start.10) | collective-permute-done | bytes 8224 | tf_op jit(solution)/shard_map/ppermute | solution.py:620
  42.9 2.6 %collective-permute-done.9.face_x = f32[2,24,128]{2,1,0:T(8,128)S(1)} collective-permute-done((f32[2,24,128]{2,1,0:T(8,128)S(1)}, f32[2,24,128]{2,1,0:T(8,128)S(1)}, u32[]{:S(2)}, u32[]{:S(2)}) %collective-permute-start.9) | collective-permute-done | bytes 24608 | tf_op jit(solution)/shard_map/ppermute | solution.py:620
  45.5 3.2 %final.1 = (f32[3,192,128]{2,1,0:T(8,128)S(1)}, f32[384,128]{1,0:T(8,128)S(1)}, f32[384,128]{1,0:T(8,128)S(1)}) custom-call(f32[3,192,128]{2,1,0:T(8,128)S(1)} %get-tuple-element.106.e_ref.e_seen, f32[3,192,128]{2,1,0:T(8,128)S(1)} %get-tuple-element.90.h_ref, f32[2,24,128]{2,1,0:T(8,128)S(1)} %collective-permute-done.9.face_x, ...), custom_call_target="tpu_custom_call" | custom-call | bytes 2097152 | tf_op jit(solution)/shard_map/final/pallas_call | solution.py:48
  48.8 1.4 %collective-permute-done.12 = f32[384,128]{1,0:T(8,128)S(1)} collective-permute-done((f32[384,128]{1,0:T(8,128)S(1)}, f32[384,128]{1,0:T(8,128)S(1)}, u32[]{:S(2)}, u32[]{:S(2)}) %collective-permute-start.12) | collective-permute-done | bytes 196640 | tf_op jit(solution)/shard_map/ppermute | solution.py:708
  50.9 5.0 %all-to-all-start.1 = ((f32[8,48,128]{2,1,0:T(8,128)}), f32[8,48,128]{2,1,0:T(8,128)S(1)}, u32[]{:S(2)}, u32[]{:S(2)}) async-start(f32[8,48,128]{2,1,0:T(8,128)} %bitcast.10), calls=%async_computation.1 | async-start | bytes 393216 | tf_op jit(solution)/shard_map/all_to_all | solution.py:710
  55.9 2.2 %drive2.1.drives = f32[6,32,128]{2,1,0:T(8,128)S(1)} custom-call(f32[3,192,128]{2,1,0:T(8,128)S(1)} %get-tuple-element.106.e_ref.e_seen, s32[32,128]{1,0:T(8,128)S(1)} %get-tuple-element.80.placed, f32[3,32,128]{2,1,0:T(8,128)S(1)} %get-tuple-element.107.before), custom_call_target="tpu_custom_call" | custom-call | bytes 2097152 | tf_op jit(solution)/shard_map/drive2/pallas_call | solution.py:48
  58.1 3.0 %all-to-all-done.1.pieces = f32[8,48,128]{2,1,0:T(8,128)S(1)} async-done(((f32[8,48,128]{2,1,0:T(8,128)}), f32[8,48,128]{2,1,0:T(8,128)S(1)}, u32[]{:S(2)}, u32[]{:S(2)}) %all-to-all-start.1) | async-done | bytes 196640 | tf_op jit(solution)/shard_map/all_to_all | solution.py:710
  61.6 2.7 %collective-permute-start.14 = (f32[96,128]{1,0:T(8,128)S(1)}, f32[96,128]{1,0:T(8,128)S(1)}, u32[]{:S(2)}, u32[]{:S(2)}) collective-permute-start(f32[96,128]{1,0:T(8,128)S(1)} %get-tuple-element.110), channel_id=1, source_target_pairs={{0,128},{16,144},{32,160},{48,176},{64,192},{80,208},{96,224},{112... | collective-permute-start | bytes 147464 | tf_op jit(solution)/shard_map/ppermute | solution.py:723
  64.3 1.6 %collective-permute-start.15 = (f32[96,128]{1,0:T(8,128)S(1)}, f32[96,128]{1,0:T(8,128)S(1)}, u32[]{:S(2)}, u32[]{:S(2)}) collective-permute-start(f32[96,128]{1,0:T(8,128)S(1)} %get-tuple-element.111), channel_id=1, source_target_pairs={{0,192},{16,208},{32,224},{48,240},{64,128},{80,144},{96,160},{112... | collective-permute-start | bytes 147464 | tf_op jit(solution)/shard_map/ppermute | solution.py:723
  65.9 1.3 %collective-permute-done.14.two = f32[96,128]{1,0:T(8,128)S(1)} collective-permute-done((f32[96,128]{1,0:T(8,128)S(1)}, f32[96,128]{1,0:T(8,128)S(1)}, u32[]{:S(2)}, u32[]{:S(2)}) %collective-permute-start.14) | collective-permute-done | bytes 49184 | tf_op jit(solution)/shard_map/ppermute | solution.py:723
  67.3 2.3 %collective-permute-done.15.three = f32[96,128]{1,0:T(8,128)S(1)} collective-permute-done((f32[96,128]{1,0:T(8,128)S(1)}, f32[96,128]{1,0:T(8,128)S(1)}, u32[]{:S(2)}, u32[]{:S(2)}) %collective-permute-start.15) | collective-permute-done | bytes 49184 | tf_op jit(solution)/shard_map/ppermute | solution.py:723
  69.7 2.4 %collective-permute-start.16 = (f32[96,128]{1,0:T(8,128)S(1)}, f32[96,128]{1,0:T(8,128)S(1)}, u32[]{:S(2)}, u32[]{:S(2)}) collective-permute-start(f32[96,128]{1,0:T(8,128)S(1)} %get-tuple-element.114), channel_id=1, source_target_pairs={{0,16},{16,0},{32,48},{48,32},{64,80},{80,64},{96,112},{112,96},{1... | collective-permute-start | bytes 147464 | tf_op jit(solution)/shard_map/ppermute | solution.py:735
  72.1 2.3 %collective-permute-start.17 = (f32[96,128]{1,0:T(8,128)S(1)}, f32[96,128]{1,0:T(8,128)S(1)}, u32[]{:S(2)}, u32[]{:S(2)}) collective-permute-start(f32[96,128]{1,0:T(8,128)S(1)} %get-tuple-element.115), channel_id=1, source_target_pairs={{0,32},{16,48},{32,0},{48,16},{64,96},{80,112},{96,64},{112,80},{1... | collective-permute-start | bytes 147464 | tf_op jit(solution)/shard_map/ppermute | solution.py:735
  74.4 1.9 %collective-permute-start.18 = (f32[96,128]{1,0:T(8,128)S(1)}, f32[96,128]{1,0:T(8,128)S(1)}, u32[]{:S(2)}, u32[]{:S(2)}) collective-permute-start(f32[96,128]{1,0:T(8,128)S(1)} %get-tuple-element.116), channel_id=1, source_target_pairs={{0,48},{16,32},{32,16},{48,0},{64,112},{80,96},{96,80},{112,64},{1... | collective-permute-start | bytes 147464 | tf_op jit(solution)/shard_map/ppermute | solution.py:735
  76.2 0.8 store.1
  77.1 3.0 %collective-permute-done.17.two = f32[96,128]{1,0:T(8,128)S(1)} collective-permute-done((f32[96,128]{1,0:T(8,128)S(1)}, f32[96,128]{1,0:T(8,128)S(1)}, u32[]{:S(2)}, u32[]{:S(2)}) %collective-permute-start.17) | collective-permute-done | bytes 49184 | tf_op jit(solution)/shard_map/ppermute | solution.py:735
  80.8 0.7 atoms.1
  81.5 10.4 %all_to_all.15 = f32[8,48,128]{2,1,0:T(8,128)S(1)} all-to-all(f32[8,48,128]{2,1,0:T(8,128)S(1)} %get-tuple-element.127), channel_id=1, replica_groups=mesh['gx'=16,'gy'=8,'gz'=2] {'gy'}, dimensions={0} | all-to-all | bytes 393216 | tf_op jit(solution)/shard_map/all_to_all | solution.py:754
  91.9 0.7 add.7
  (30 shorter events, 3.3 us)
Async XLA Ops:
  2.5 14.8 %collective-permute-start.2 = (f32[2,192,128]{2,1,0:T(8,128)S(1)}, f32[2,192,128]{2,1,0:T(8,128)S(1)}, u32[]{:S(2)}, u32[]{:S(2)}) collective-permute-start(f32[2,192,128]{2,1,0:T(8,128)S(1)} %get-tuple-element.70), channel_id=1, source_target_pairs={{1,0},{0,1},{3,2},{2,3},{5,4},{4,5},{7,6},{6,7},{9,8},{8,9},{11,10... | collective-permute-start | bytes 589832 | tf_op jit(solution)/shard_map/ppermute | solution.py:620
  2.6 14.7 %collective-permute-start = (f32[2,24,128]{2,1,0:T(8,128)S(1)}, f32[2,24,128]{2,1,0:T(8,128)S(1)}, u32[]{:S(2)}, u32[]{:S(2)}) collective-permute-start(f32[2,24,128]{2,1,0:T(8,128)S(1)} %get-tuple-element.68), channel_id=1, source_target_pairs={{16,0},{32,16},{48,32},{64,48},{80,64},{96,80},{112,96},{128,112},... | collective-permute-start | bytes 73736 | tf_op jit(solution)/shard_map/ppermute | solution.py:620
  11.2 6.1 %collective-permute-start.1 = (f32[2,8,128]{2,1,0:T(8,128)S(1)}, f32[2,8,128]{2,1,0:T(8,128)S(1)}, u32[]{:S(2)}, u32[]{:S(2)}) collective-permute-start(f32[2,8,128]{2,1,0:T(8,128)S(1)} %get-tuple-element.69), channel_id=1, source_target_pairs={{2,0},{4,2},{6,4},{8,6},{10,8},{12,10},{14,12},{0,14},{3,1},{5,3},... | collective-permute-start | bytes 24584 | tf_op jit(solution)/shard_map/ppermute | solution.py:620
  11.6 14.5 %all-to-all-start = ((f32[16,16,128]{2,1,0:T(8,128)}), f32[16,16,128]{2,1,0:T(8,128)S(1)}, u32[]{:S(2)}, u32[]{:S(2)}) async-start(f32[16,16,128]{2,1,0:T(8,128)} %get-tuple-element.81), calls=%async_computation | async-start | bytes 262144 | tf_op jit(solution)/shard_map/all_to_all | solution.py:647
  17.5 11.7 %collective-permute-start.5 = (f32[2,192,128]{2,1,0:T(8,128)S(1)}, f32[2,192,128]{2,1,0:T(8,128)S(1)}, u32[]{:S(2)}, u32[]{:S(2)}) collective-permute-start(f32[2,192,128]{2,1,0:T(8,128)S(1)} %get-tuple-element.78), channel_id=1, source_target_pairs={{0,1},{1,0},{2,3},{3,2},{4,5},{5,4},{6,7},{7,6},{8,9},{9,8},{10,11... | collective-permute-start | bytes 589832 | tf_op jit(solution)/shard_map/ppermute | solution.py:620
  17.6 11.6 %collective-permute-start.3 = (f32[2,24,128]{2,1,0:T(8,128)S(1)}, f32[2,24,128]{2,1,0:T(8,128)S(1)}, u32[]{:S(2)}, u32[]{:S(2)}) collective-permute-start(f32[2,24,128]{2,1,0:T(8,128)S(1)} %get-tuple-element.76), channel_id=1, source_target_pairs={{0,16},{16,32},{32,48},{48,64},{64,80},{80,96},{96,112},{112,128},... | collective-permute-start | bytes 73736 | tf_op jit(solution)/shard_map/ppermute | solution.py:620
  20.3 8.8 %collective-permute-start.4 = (f32[2,8,128]{2,1,0:T(8,128)S(1)}, f32[2,8,128]{2,1,0:T(8,128)S(1)}, u32[]{:S(2)}, u32[]{:S(2)}) collective-permute-start(f32[2,8,128]{2,1,0:T(8,128)S(1)} %get-tuple-element.77), channel_id=1, source_target_pairs={{0,2},{2,4},{4,6},{6,8},{8,10},{10,12},{12,14},{14,0},{1,3},{3,5},... | collective-permute-start | bytes 24584 | tf_op jit(solution)/shard_map/ppermute | solution.py:620
  29.4 7.8 %collective-permute-start.8 = (f32[2,192,128]{2,1,0:T(8,128)S(1)}, f32[2,192,128]{2,1,0:T(8,128)S(1)}, u32[]{:S(2)}, u32[]{:S(2)}) collective-permute-start(f32[2,192,128]{2,1,0:T(8,128)S(1)} %get-tuple-element.85), channel_id=1, source_target_pairs={{1,0},{0,1},{3,2},{2,3},{5,4},{4,5},{7,6},{6,7},{9,8},{8,9},{11,10... | collective-permute-start | bytes 589832 | tf_op jit(solution)/shard_map/ppermute | solution.py:620
  29.5 7.6 %collective-permute-start.6 = (f32[2,24,128]{2,1,0:T(8,128)S(1)}, f32[2,24,128]{2,1,0:T(8,128)S(1)}, u32[]{:S(2)}, u32[]{:S(2)}) collective-permute-start(f32[2,24,128]{2,1,0:T(8,128)S(1)} %get-tuple-element.83), channel_id=1, source_target_pairs={{16,0},{32,16},{48,32},{64,48},{80,64},{96,80},{112,96},{128,112},... | collective-permute-start | bytes 73736 | tf_op jit(solution)/shard_map/ppermute | solution.py:620
  30.7 6.4 %collective-permute-start.7 = (f32[2,8,128]{2,1,0:T(8,128)S(1)}, f32[2,8,128]{2,1,0:T(8,128)S(1)}, u32[]{:S(2)}, u32[]{:S(2)}) collective-permute-start(f32[2,8,128]{2,1,0:T(8,128)S(1)} %get-tuple-element.84), channel_id=1, source_target_pairs={{2,0},{4,2},{6,4},{8,6},{10,8},{12,10},{14,12},{0,14},{3,1},{5,3},... | collective-permute-start | bytes 24584 | tf_op jit(solution)/shard_map/ppermute | solution.py:620
  37.3 8.2 %collective-permute-start.11 = (f32[2,192,128]{2,1,0:T(8,128)S(1)}, f32[2,192,128]{2,1,0:T(8,128)S(1)}, u32[]{:S(2)}, u32[]{:S(2)}) collective-permute-start(f32[2,192,128]{2,1,0:T(8,128)S(1)} %get-tuple-element.93), channel_id=1, source_target_pairs={{0,1},{1,0},{2,3},{3,2},{4,5},{5,4},{6,7},{7,6},{8,9},{9,8},{10,11... | collective-permute-start | bytes 589832 | tf_op jit(solution)/shard_map/ppermute | solution.py:620
  37.4 8.1 %collective-permute-start.9 = (f32[2,24,128]{2,1,0:T(8,128)S(1)}, f32[2,24,128]{2,1,0:T(8,128)S(1)}, u32[]{:S(2)}, u32[]{:S(2)}) collective-permute-start(f32[2,24,128]{2,1,0:T(8,128)S(1)} %get-tuple-element.91), channel_id=1, source_target_pairs={{0,16},{16,32},{32,48},{48,64},{64,80},{80,96},{96,112},{112,128},... | collective-permute-start | bytes 73736 | tf_op jit(solution)/shard_map/ppermute | solution.py:620
  39.2 3.7 %collective-permute-start.10 = (f32[2,8,128]{2,1,0:T(8,128)S(1)}, f32[2,8,128]{2,1,0:T(8,128)S(1)}, u32[]{:S(2)}, u32[]{:S(2)}) collective-permute-start(f32[2,8,128]{2,1,0:T(8,128)S(1)} %get-tuple-element.92), channel_id=1, source_target_pairs={{0,2},{2,4},{4,6},{6,8},{8,10},{10,12},{12,14},{14,0},{1,3},{3,5},... | collective-permute-start | bytes 24584 | tf_op jit(solution)/shard_map/ppermute | solution.py:620
  48.7 1.5 %collective-permute-start.12 = (f32[384,128]{1,0:T(8,128)S(1)}, f32[384,128]{1,0:T(8,128)S(1)}, u32[]{:S(2)}, u32[]{:S(2)}) collective-permute-start(f32[384,128]{1,0:T(8,128)S(1)} %get-tuple-element.104), channel_id=1, source_target_pairs={{1,0},{0,1},{3,2},{2,3},{5,4},{4,5},{7,6},{6,7},{9,8},{8,9},{11,10... | collective-permute-start | bytes 589832 | tf_op jit(solution)/shard_map/ppermute | solution.py:708
  50.9 10.2 %all-to-all-start.1 = ((f32[8,48,128]{2,1,0:T(8,128)}), f32[8,48,128]{2,1,0:T(8,128)S(1)}, u32[]{:S(2)}, u32[]{:S(2)}) async-start(f32[8,48,128]{2,1,0:T(8,128)} %bitcast.10), calls=%async_computation.1 | async-start | bytes 393216 | tf_op jit(solution)/shard_map/all_to_all | solution.py:710
  61.2 4.8 %collective-permute-start.13 = (f32[96,128]{1,0:T(8,128)S(1)}, f32[96,128]{1,0:T(8,128)S(1)}, u32[]{:S(2)}, u32[]{:S(2)}) collective-permute-start(f32[96,128]{1,0:T(8,128)S(1)} %get-tuple-element.109), channel_id=1, source_target_pairs={{0,64},{16,80},{32,96},{48,112},{64,0},{80,16},{96,32},{112,48},{1... | collective-permute-start | bytes 147464 | tf_op jit(solution)/shard_map/ppermute | solution.py:723
  61.6 5.7 %collective-permute-start.14 = (f32[96,128]{1,0:T(8,128)S(1)}, f32[96,128]{1,0:T(8,128)S(1)}, u32[]{:S(2)}, u32[]{:S(2)}) collective-permute-start(f32[96,128]{1,0:T(8,128)S(1)} %get-tuple-element.110), channel_id=1, source_target_pairs={{0,128},{16,144},{32,160},{48,176},{64,192},{80,208},{96,224},{112... | collective-permute-start | bytes 147464 | tf_op jit(solution)/shard_map/ppermute | solution.py:723
  64.3 5.3 %collective-permute-start.15 = (f32[96,128]{1,0:T(8,128)S(1)}, f32[96,128]{1,0:T(8,128)S(1)}, u32[]{:S(2)}, u32[]{:S(2)}) collective-permute-start(f32[96,128]{1,0:T(8,128)S(1)} %get-tuple-element.111), channel_id=1, source_target_pairs={{0,192},{16,208},{32,224},{48,240},{64,128},{80,144},{96,160},{112... | collective-permute-start | bytes 147464 | tf_op jit(solution)/shard_map/ppermute | solution.py:723
  69.7 7.4 %collective-permute-start.16 = (f32[96,128]{1,0:T(8,128)S(1)}, f32[96,128]{1,0:T(8,128)S(1)}, u32[]{:S(2)}, u32[]{:S(2)}) collective-permute-start(f32[96,128]{1,0:T(8,128)S(1)} %get-tuple-element.114), channel_id=1, source_target_pairs={{0,16},{16,0},{32,48},{48,32},{64,80},{80,64},{96,112},{112,96},{1... | collective-permute-start | bytes 147464 | tf_op jit(solution)/shard_map/ppermute | solution.py:735
  72.1 8.0 %collective-permute-start.17 = (f32[96,128]{1,0:T(8,128)S(1)}, f32[96,128]{1,0:T(8,128)S(1)}, u32[]{:S(2)}, u32[]{:S(2)}) collective-permute-start(f32[96,128]{1,0:T(8,128)S(1)} %get-tuple-element.115), channel_id=1, source_target_pairs={{0,32},{16,48},{32,0},{48,16},{64,96},{80,112},{96,64},{112,80},{1... | collective-permute-start | bytes 147464 | tf_op jit(solution)/shard_map/ppermute | solution.py:735
  74.4 6.3 %collective-permute-start.18 = (f32[96,128]{1,0:T(8,128)S(1)}, f32[96,128]{1,0:T(8,128)S(1)}, u32[]{:S(2)}, u32[]{:S(2)}) collective-permute-start(f32[96,128]{1,0:T(8,128)S(1)} %get-tuple-element.116), channel_id=1, source_target_pairs={{0,48},{16,32},{32,16},{48,0},{64,112},{80,96},{96,80},{112,64},{1... | collective-permute-start | bytes 147464 | tf_op jit(solution)/shard_map/ppermute | solution.py:735
  81.5 10.4 %copy-start = (f32[32,12,128]{2,0,1:T(8,128)S(1)}, f32[32,12,128]{2,0,1:T(8,128)}, u32[]{:S(2)}) copy-start(f32[32,12,128]{2,0,1:T(8,128)} %param.20) | copy-start | bytes 589828

commit v7 on v6

--- a/solution.py
+++ b/solution.py
@@ -137,34 +137,10 @@
     return kept
 
 
-def prepare_kernel(
-    e_hbm,
-    state_hbm,
-    h_hbm,
-    eps_hbm,
-    pump_hbm,
-    out_x,
-    out_y,
-    out_z,
-    packed,
-    e_out,
-    state,
-    h_out,
-    eps_out,
-    pump_out,
-    sems,
-):
+def prepare_kernel(e_hbm, state_hbm, out_x, out_y, out_z, packed, e_out, state, sems):
     copies = [
-        pltpu.make_async_copy(source, target, sems.at[place])
-        for place, (source, target) in enumerate(
-            (
-                (e_hbm, e_out),
-                (state_hbm, state),
-                (h_hbm, h_out),
-                (eps_hbm, eps_out),
-                (pump_hbm, pump_out),
-            )
-        )
+        pltpu.make_async_copy(e_hbm, e_out, sems.at[0]),
+        pltpu.make_async_copy(state_hbm, state, sems.at[1]),
     ]
     for copy in copies:
         copy.start()
@@ -179,8 +155,6 @@
     for field, value in enumerate(free + [lasing - lower] + polar + [lasing_free - lower_free]):
         for owner in range(SLOTS // 2):
             packed[owner, 2 * field : 2 * field + 2] = value[2 * owner : 2 * owner + 2]
-    for copy in copies[2:]:
-        copy.wait()
 
 
 def magnetic_kernel(e_ref, h_ref, face_x, face_y, face_z, h_out, out_x, out_y, out_z):
@@ -221,61 +195,37 @@
     return row_index(HALF, width) == (offsets >> 8)
 
 
-GROUP = 16
-
-
-def scatter_kernel(first, placed, fields_ref, dense, total, spots, columns):
-    def group(index, carry):
-        lines = placed[pl.ds(GROUP * index, GROUP)]
-        for slot in range(GROUP):
-            line = lines[slot : slot + 1]
-            hits = wide_hits(line, CZ)
-            tall = tall_hits(line, CZ).astype(F32).astype(BF16).reshape(6, 16, CZ)
-            values = fields_ref[
-                (GROUP // 2) * index + slot // 2, pl.ds(2 * first + slot % 2, 4, 2), :
-            ]
-            for place, part in enumerate(split_parts(values)):
-                across = (place * GROUP + slot) * CZ
-                columns[:, across : across + CZ] = hits
-                part = part.astype(F32)
-                for field in range(4):
-                    row = jnp.broadcast_to(part[field : field + 1], (16, CZ)).astype(BF16)
-                    spots[field * HALF : (field + 1) * HALF, across : across + CZ] = (
-                        tall * row[None]
-                    ).reshape(HALF, CZ)
-        got = lax.dot_general(
-            spots[...], columns[...], (((1,), (1,)), ((), ())), preferred_element_type=F32
-        )
-
-        @pl.when(index == 0)
-        def _():
-            total[...] = got
-
-        @pl.when(index > 0)
-        def _():
-            total[...] += got
-
-        return carry
-
-    lax.fori_loop(0, SLOTS // GROUP, group, 0)
+def scatter_kernel(first, placed, fields_ref, dense, spots, columns):
+    for slot in range(SLOTS):
+        line = placed[slot : slot + 1]
+        across = slice(slot * CZ, (slot + 1) * CZ)
+        columns[:, across] = wide_hits(line, CZ)
+        tall = tall_hits(line, CZ).astype(F32).astype(BF16).reshape(6, 16, CZ)
+        values = fields_ref[slot // 2, pl.ds(2 * first + slot % 2, 4, 2), :]
+        for place, part in enumerate(split_parts(values)):
+            part = part.astype(F32)
+            for field in range(4):
+                row = jnp.broadcast_to(part[field : field + 1], (16, CZ)).astype(BF16)
+                top = (4 * place + field) * HALF
+                spots[top : top + HALF, across] = (tall * row[None]).reshape(HALF, CZ)
+    total = lax.dot_general(
+        spots[...], columns[...], (((1,), (1,)), ((), ())), preferred_element_type=F32
+    )
+    total = total[: 4 * HALF] + total[4 * HALF :]
     for field in range(4):
         got = total[field * HALF : (field + 1) * HALF]
         dense[field, pl.ds(0, HALF, 2), :] = got[:, :CZ]
         dense[field, pl.ds(1, HALF, 2), :] = got[:, CZ:]
 
 
-def scattered(first, placed, fields, name):
-    return call(
-        functools.partial(scatter_kernel, first),
-        shape(4, ROWS, CZ),
-        (placed, fields),
-        scratch=[
-            pltpu.VMEM((4 * HALF, WIDE), F32),
-            pltpu.VMEM((4 * HALF, 2 * GROUP * CZ), BF16),
-            pltpu.VMEM((WIDE, 2 * GROUP * CZ), BF16),
-        ],
-        name=name,
-    )
+SCATTER = [pltpu.VMEM((8 * HALF, SLOTS * CZ), BF16), pltpu.VMEM((WIDE, SLOTS * CZ), BF16)]
+
+
+def scatter_sample_kernel(
+    placed, fields_ref, e_ref, h_ref, surf_ref, dense, sampled, spots, columns
+):
+    scatter_kernel(4, placed, fields_ref, dense, spots, columns)
+    sample_rows(e_ref, h_ref, surf_ref, sampled)
 
 
 def electric_kernel(
@@ -302,35 +252,36 @@
 
 
 def stacked(fields):
-    return split_parts(jnp.concatenate([paired(ref, comp) for ref, comp in fields], axis=0))
-
-
-def gather_lines(high, low, offsets, width):
+    return jnp.concatenate(
+        split_parts(jnp.concatenate([paired(ref, comp) for ref, comp in fields], axis=0)), axis=0
+    )
+
+
+def gather_lines(values, offsets, width):
     hits = wide_hits(offsets, width)
     tall = tall_hits(offsets, width)
-    picked = jnp.dot(high, hits, preferred_element_type=F32)
-    picked = picked + jnp.dot(low, hits, preferred_element_type=F32)
-    return [
-        jnp.sum(
-            jnp.where(tall, picked[field * HALF : (field + 1) * HALF], 0.0), axis=0, keepdims=True
-        )
-        for field in range(picked.shape[0] // HALF)
-    ]
-
-
-TAKE = 8
-
-
-def gather_drive(field_ref, placed, drives, first, high, low):
-    high[...], low[...] = stacked([(field_ref, comp) for comp in range(3)])
+    picked = jnp.dot(values, hits, preferred_element_type=F32)
+    lines = []
+    for field in range(6):
+        rows = slice(field * HALF, (field + 1) * HALF)
+        both = picked[rows] + picked[6 * HALF :][rows]
+        lines.append(jnp.sum(jnp.where(tall, both, 0.0), axis=0, keepdims=True))
+    return lines
+
+
+TAKE = 16
+
+
+def drive_kernel(e_old, e_new, placed, drives, values):
+    values[...] = stacked([(ref, comp) for ref in (e_old, e_new) for comp in range(3)])
 
     def group(index, carry):
         lines = placed[pl.ds(TAKE * index, TAKE)]
         offsets = jnp.concatenate([lines[slot : slot + 1] for slot in range(TAKE)], axis=1)
-        got = gather_lines(high[...], low[...], offsets, TAKE * CZ)
-        for comp in range(3):
+        got = gather_lines(values[...], offsets, TAKE * CZ)
+        for field in range(6):
             for slot in range(TAKE):
-                drives[first + comp, pl.ds(TAKE * index + slot, 1)] = got[comp][
+                drives[field, pl.ds(TAKE * index + slot, 1)] = got[field][
                     :, slot * CZ : (slot + 1) * CZ
                 ]
         return carry
@@ -338,19 +289,9 @@
     lax.fori_loop(0, SLOTS // TAKE, group, 0)
 
 
-def first_drive_kernel(e_ref, placed, e_seen, h_seen, surf_ref, drives, sampled, high, low):
-    gather_drive(e_ref, placed, drives, 0, high, low)
-    sample_rows(e_seen, h_seen, surf_ref, sampled)
-
-
-def second_drive_kernel(e_ref, placed, before, drives, high, low):
-    drives[0:3] = before[...]
-    gather_drive(e_ref, placed, drives, 3, high, low)
-
-
 def sample_rows(e_ref, h_ref, surf_ref, sampled):
-    high, low = stacked([(ref, comp) for ref in (e_ref, h_ref) for comp in range(3)])
-    got = gather_lines(high, low, surf_ref[...], CZ)
+    values = stacked([(ref, comp) for ref in (e_ref, h_ref) for comp in range(3)])
+    got = gather_lines(values, surf_ref[...], CZ)
     sampled[...] = jnp.zeros_like(sampled)
     for field in range(6):
         sampled[field : field + 1] = got[field]
@@ -366,16 +307,37 @@
     offsets_ref,
     surf_ref,
     units_ref,
+    h_hbm,
+    eps_hbm,
+    pump_hbm,
+    far_hbm,
     placed,
     surf_out,
     starts,
     turn,
     factors,
+    h_out,
+    eps_out,
+    pump_out,
+    far_out,
     owner_ref,
-    sem,
+    sems,
 ):
-    copy = pltpu.make_async_copy(owner_hbm, owner_ref, sem)
-    copy.start()
+    own = pl.ds(pl.multiple_of(FAR * lax.axis_index("gy"), 8), FAR)
+    copies = [
+        pltpu.make_async_copy(source, target, sems.at[place])
+        for place, (source, target) in enumerate(
+            (
+                (owner_hbm, owner_ref),
+                (h_hbm, h_out),
+                (eps_hbm, eps_out),
+                (pump_hbm, pump_out),
+                (far_hbm.at[own], far_out),
+            )
+        )
+    ]
+    for copy in copies:
+        copy.start()
     lanes = lax.broadcasted_iota(jnp.int32, (8, DIRS), 1)
     omega = freq_low + freq_pitch * (lanes & (FREQ - 1)).astype(F32)
     moment = omega * jnp.where(lanes < FREQ, time_step, 2.0 * time_step)
@@ -410,7 +372,8 @@
     turn[0], turn[1] = powers[1]
     starts[0], starts[1] = low_start
     starts[2], starts[3] = high_start
-    copy.wait()
+    for copy in copies:
+        copy.wait()
     count = count_ref[0]
     for slot in range(SLOTS):
         line = offsets_ref[slot : slot + 1]
@@ -462,8 +425,9 @@
             out[start : start + 8] = pick(tiles, [(target, source) for source in range(4)])
 
 
-def finish_kernel(total_in, kept, one, two, three, spread_out, back):
+def finish_kernel(total_in, kept, one, two, three, far_ref, spread_out, back):
     total = (total_in[...] + one[0:FAR]) + (two[0:FAR] + three[0:FAR])
+    total = far_ref[...] + total
     for peer in range(8):
         spread_out[peer] = total
     held = [kept[...]] + [arrived[FAR:] for arrived in (one, two, three)]
@@ -621,31 +585,20 @@
             for part, axis, perm in zip(parts, ("gx", "gy", "gz"), perms)
         ]
 
-    *near, packed, e_old, state, h_old, eps, pumps = call(
+    *near, packed, e_old, state = call(
         prepare_kernel,
-        faces
-        + (
-            shape(SLOTS // 2, 16, CZ),
-            dense,
-            shape(10, SLOTS, CZ),
-            dense,
-            shape(ROWS, CZ),
-            shape(SLOTS, CZ),
-        ),
+        faces + (shape(SLOTS // 2, 16, CZ), dense, shape(10, SLOTS, CZ)),
         stay(
             efield.reshape(3, ROWS, CZ),
             jnp.transpose(gain_state.reshape(SLOTS, 10, CZ), (1, 0, 2)),
-            hfield.reshape(3, ROWS, CZ),
-            inv_eps.reshape(ROWS, CZ),
-            pump.reshape(SLOTS, CZ),
         ),
-        in_specs=[hbm] * 5,
-        scratch=[pltpu.SemaphoreType.DMA((5,))],
+        in_specs=[hbm] * 2,
+        scratch=[pltpu.SemaphoreType.DMA((2,))],
         name="prepare",
     )
     near = shifted(near, down)
     fields = lax.all_to_all(packed, "gx", 0, 0, tiled=True)
-    placed, surf, starts, turn, factors = call(
+    placed, surf, starts, turn, factors, h_old, eps, pumps, far_part = call(
         phase_kernel,
         (
             shape(SLOTS, CZ, dtype=jnp.int32),
@@ -653,6 +606,10 @@
             shape(4, CZ, DIRS),
             shape(2, CZ, DIRS),
             shape(2, STEPS * FREQ, DIRS),
+            dense,
+            shape(ROWS, CZ),
+            shape(SLOTS, CZ),
+            shape(FAR, DIRS),
         ),
         [gain_count.reshape(1)]
         + stay(
@@ -660,13 +617,16 @@
             gain_offsets.reshape(SLOTS, CZ),
             surf_offsets.reshape(1, CZ),
             jnp.asarray(directions(DIRS)),
+            hfield.reshape(3, ROWS, CZ),
+            inv_eps.reshape(ROWS, CZ),
+            pump.reshape(SLOTS, CZ),
+            jnp.transpose(far_acc, (1, 0, 2)).reshape(8 * FAR, DIRS),
         ),
-        in_specs=[pl.BlockSpec(memory_space=pltpu.SMEM), hbm, vmem, vmem, vmem],
-        scratch=[pltpu.SMEM((1, SLOTS), jnp.int32), pltpu.SemaphoreType.DMA],
+        in_specs=[pl.BlockSpec(memory_space=pltpu.SMEM), hbm, vmem, vmem, vmem] + [hbm] * 4,
+        scratch=[pltpu.SMEM((1, SLOTS), jnp.int32), pltpu.SemaphoreType.DMA((5,))],
         moved=MIB // 4,
         name="phase",
     )
-    *near, placed = lax.optimization_barrier((*near, placed))
     h_one, *edge = call(
         magnetic_kernel,
         (dense,) + faces,
@@ -676,7 +636,13 @@
         name="magnetic",
     )
     edge = shifted(edge, up)
-    spread_now = scattered(0, placed, fields, "scatter")
+    spread_now = call(
+        functools.partial(scatter_kernel, 0),
+        shape(4, ROWS, CZ),
+        (placed, fields),
+        scratch=SCATTER,
+        name="scatter",
+    )
     e_one, *near, rates = call(
         electric_kernel,
         (dense,) + faces + (shape(4, ROWS, CZ),),
@@ -684,19 +650,25 @@
         name="electric",
     )
     near = shifted(near, down)
-    spread_next = scattered(4, placed, fields, "scatter2")
+    spread_next, early = call(
+        scatter_sample_kernel,
+        (shape(4, ROWS, CZ), shape(8, CZ)),
+        (placed, fields, e_one, h_one, surf),
+        scratch=SCATTER,
+        name="scatter2",
+    )
     *near, spread_next = lax.optimization_barrier((*near, spread_next))
     h_two, *edge = call(magnetic_kernel, (dense,) + faces, (e_one, h_one, *near), name="magnetic2")
     edge = shifted(edge, up)
-    e_seen, h_seen, h_two = lax.optimization_barrier((e_one, h_one, h_two))
-    halves = [pltpu.VMEM((3 * HALF, WIDE), BF16)] * 2
-    before, early = call(
-        first_drive_kernel,
-        (shape(3, SLOTS, CZ), shape(8, CZ)),
-        (e_old, placed, e_seen, h_seen, surf),
-        scratch=halves,
+    e_seen, h_two = lax.optimization_barrier((e_one, h_two))
+    drives = call(
+        drive_kernel,
+        shape(6, SLOTS, CZ),
+        (e_old, e_seen, placed),
+        scratch=[pltpu.VMEM((12 * HALF, WIDE), BF16)],
         name="drive",
     )
+    *edge, drives = lax.optimization_barrier((*edge, drives))
     part = shape(12 * FREQ // 2, DIRS)
     e_two, keep, send = call(
         final_kernel,
@@ -706,15 +678,7 @@
         name="final",
     )
     chip = keep + lax.ppermute(send, "gz", down[2])
-    chip, e_seen = lax.optimization_barrier((chip, e_one))
     pieces = lax.all_to_all(chip.reshape(8, FAR, DIRS), "gy", 0, 0, tiled=True)
-    drives = call(
-        second_drive_kernel,
-        shape(6, SLOTS, CZ),
-        (e_seen, placed, before),
-        scratch=halves,
-        name="drive2",
-    )
     load = shape(FAR + LOAD, CZ)
     total, *loads = call(
         fold_kernel, (shape(FAR, DIRS),) + (load,) * 3, (pieces, drives), name="fold"
@@ -741,7 +705,7 @@
     copies, back = call(
         finish_kernel,
         (shape(8, FAR, DIRS), shape(6, SLOTS, CZ)),
-        (total, kept, *loads),
+        (total, kept, *loads, far_part),
         name="finish",
     )
     state_out = call(
@@ -752,7 +716,7 @@
     )
     copies, state_out, e_out, h_out = lax.optimization_barrier((copies, state_out, e_out, h_out))
     gathered = lax.all_to_all(copies, "gy", 0, 0, tiled=True)
-    far_out = far_acc + jnp.transpose(gathered.reshape(12, FREQ // 2, DIRS), (1, 0, 2))
+    far_out = jnp.transpose(gathered.reshape(12, FREQ // 2, DIRS), (1, 0, 2))
     return (
         e_out.reshape(efield.shape),
         h_out.reshape(hfield.shape),

time: 93 us -> 91 us (0.978)
  blocking collectives: 10.4 us -> 20.8 us
  starting transfers between devices: 40.3 us -> 35.5 us
  waiting for transfers between devices: 19.8 us -> 15.3 us
  Pallas kernels: 19.3 us -> 16.9 us
  other arithmetic: 1.4 us -> 0.02 us
    all_to_all x0 -> x1, blocking collectives: none -> 10.5 us  [local(): pieces = lax.all_to_all(chip.reshape(8, FAR, DIRS), 'gy', 0, 0, tiled=True)]
    all_to_all x1 -> x0, starting transfers between devices: 4.98 us -> none  [local(): pieces = lax.all_to_all(chip.reshape(8, FAR, DIRS), 'gy', 0, 0, tiled=True)]
    all_to_all x1 -> x0, waiting for transfers between devices: 3.04 us -> none  [local(): pieces = lax.all_to_all(chip.reshape(8, FAR, DIRS), 'gy', 0, 0, tiled=True)]
    pallas_call x15 -> x14, Pallas kernels: 19.3 us -> 16.9 us  [call(): pl.pallas_call(kernel, out_shape=outs, in_specs=in_specs or [pl.BlockSpec...]
  transfers between devices with their start and end apart: 21 -> 20, of which waited for: 9 -> 8; matrix products, arithmetic and copies ran while one was open for 0% -> 0% of each run, Pallas kernels for 14% -> 12%
where the time goes in v7:
time: 91 us; the launch traced here: 90.6 us
  starting transfers between devices  35.5 us (39%)
  blocking collectives  20.8 us (23%)
  Pallas kernels  16.9 us (19%)
  waiting for transfers between devices  15.3 us (17%)
  between operations  1.48 us (2%)
    ppermute x12, starting transfers between devices, shifted(): lax.ppermute(part, axis, perm)  20.5 us
    pallas_call x14, Pallas kernels, call(): pl.pallas_call(kernel, out_shape=outs, in_specs=in_specs or [pl.BlockSpec...  16.9 us
    all_to_all x1, blocking collectives, local(): pieces = lax.all_to_all(chip.reshape(8, FAR, DIRS), 'gy', 0, 0, tiled=True)  10.5 us
    all_to_all x1, blocking collectives, local(): gathered = lax.all_to_all(copies, 'gy', 0, 0, tiled=True)  10.3 us
    ppermute x3, starting transfers between devices, local(): lax.ppermute(value, 'gx', [(a * 4 + z, a * 4 + (z ^ k)) for a in range(4)...  6.58 us
    ppermute x3, starting transfers between devices, local(): lax.ppermute(value, 'gx', [(a * 4 + z, (a ^ k) * 4 + z) for a in range(4)...  4.79 us
    all_to_all x1, waiting for transfers between devices, local(): fields = lax.all_to_all(packed, 'gx', 0, 0, tiled=True)  3.88 us
    ppermute x12, waiting for transfers between devices, shifted(): lax.ppermute(part, axis, perm)  3.56 us
  transfers between devices with their start and end apart: 20, of which 8 were waited for; matrix products, arithmetic and copies ran while one was open for 0% of the time, Pallas kernels for 12%

profile of v7, /device:TPU:8, one launch (start us, length us, event | category | flops | bytes accessed | tf_op | source)
XLA Modules:
  0.0 90.6 jit_solution(10118214350338967024)
XLA Ops:
  0.6 1.7 %prepare.1 = (f32[2,24,128]{2,1,0:T(8,128)S(1)}, f32[2,8,128]{2,1,0:T(8,128)S(1)}, f32[2,192,128]{2,1,0:T(8,128)S(1)}, f32[16,16,128]{2,1,0:T(8,128)}, f32[3,192...) custom-call(f32[3,192,128]{2,1,0:T(8,128)} %bitcast.26, f32[10,32,128]{2,1,0:T(8,128)} %bitcast.29), custom_call_target="tpu_custom_call" | custom-call | bytes 2097152 | tf_op jit(solution)/shard_map/prepare/pallas_call | solution.py:48
  2.4 8.6 %collective-permute-start = (f32[2,24,128]{2,1,0:T(8,128)S(1)}, f32[2,24,128]{2,1,0:T(8,128)S(1)}, u32[]{:S(2)}, u32[]{:S(2)}) collective-permute-start(f32[2,24,128]{2,1,0:T(8,128)S(1)} %get-tuple-element.66), channel_id=1, source_target_pairs={{16,0},{32,16},{48,32},{64,48},{80,64},{96,80},{112,96},{128,112},... | collective-permute-start | bytes 73736 | tf_op jit(solution)/shard_map/ppermute | solution.py:584
  11.0 0.4 collective-permute-start.1
  11.5 3.5 %all-to-all-start = ((f32[16,16,128]{2,1,0:T(8,128)}), f32[16,16,128]{2,1,0:T(8,128)S(1)}, u32[]{:S(2)}, u32[]{:S(2)}) async-start(f32[16,16,128]{2,1,0:T(8,128)} %get-tuple-element.75), calls=%async_computation | async-start | bytes 262144 | tf_op jit(solution)/shard_map/all_to_all | solution.py:600
  15.6 1.8 %phase.1 = (s32[32,128]{1,0:T(8,128)S(1)}, s32[1,128]{1,0:T(1,128)S(1)}, f32[4,128,128]{2,1,0:T(8,128)S(1)}, f32[2,128,128]{2,1,0:T(8,128)S(1)}, f32[2,128,128]{...) custom-call(s32[1]{0:T(128)} %bitcast.23.count_ref, ...), custom_call_target="tpu_custom_call" | custom-call | bytes 262144 | tf_op jit(solution)/shard_map/phase/pallas_call | solution.py:48
  17.8 2.8 %collective-permute-start.3 = (f32[2,24,128]{2,1,0:T(8,128)S(1)}, f32[2,24,128]{2,1,0:T(8,128)S(1)}, u32[]{:S(2)}, u32[]{:S(2)}) collective-permute-start(f32[2,24,128]{2,1,0:T(8,128)S(1)} %get-tuple-element.70), channel_id=1, source_target_pairs={{0,16},{16,32},{32,48},{48,64},{64,80},{80,96},{96,112},{112,128},... | collective-permute-start | bytes 73736 | tf_op jit(solution)/shard_map/ppermute | solution.py:584
  20.6 1.6 %collective-permute-start.4 = (f32[2,8,128]{2,1,0:T(8,128)S(1)}, f32[2,8,128]{2,1,0:T(8,128)S(1)}, u32[]{:S(2)}, u32[]{:S(2)}) collective-permute-start(f32[2,8,128]{2,1,0:T(8,128)S(1)} %get-tuple-element.71), channel_id=1, source_target_pairs={{0,2},{2,4},{4,6},{6,8},{8,10},{10,12},{12,14},{14,0},{1,3},{3,5},... | collective-permute-start | bytes 24584 | tf_op jit(solution)/shard_map/ppermute | solution.py:584
  22.1 3.9 %all-to-all-done.fields_ref = f32[16,16,128]{2,1,0:T(8,128)S(1)} async-done(((f32[16,16,128]{2,1,0:T(8,128)}), f32[16,16,128]{2,1,0:T(8,128)S(1)}, u32[]{:S(2)}, u32[]{:S(2)}) %all-to-all-start) | async-done | bytes 131104 | tf_op jit(solution)/shard_map/all_to_all | solution.py:600
  26.0 2.4 %scatter.1.dense = f32[4,192,128]{2,1,0:T(8,128)S(1)} custom-call(s32[32,128]{1,0:T(8,128)S(1)} %get-tuple-element.74.placed, f32[16,16,128]{2,1,0:T(8,128)S(1)} %all-to-all-done.fields_ref), custom_call_target="tpu_custom_call" | custom-call | bytes 2097152 | tf_op jit(solution)/shard_map/scatter/pallas_call | solution.py:48
  28.8 1.2 %collective-permute-start.6 = (f32[2,24,128]{2,1,0:T(8,128)S(1)}, f32[2,24,128]{2,1,0:T(8,128)S(1)}, u32[]{:S(2)}, u32[]{:S(2)}) collective-permute-start(f32[2,24,128]{2,1,0:T(8,128)S(1)} %get-tuple-element.77), channel_id=1, source_target_pairs={{16,0},{32,16},{48,32},{64,48},{80,64},{96,80},{112,96},{128,112},... | collective-permute-start | bytes 73736 | tf_op jit(solution)/shard_map/ppermute | solution.py:584
  30.0 3.8 %collective-permute-start.7 = (f32[2,8,128]{2,1,0:T(8,128)S(1)}, f32[2,8,128]{2,1,0:T(8,128)S(1)}, u32[]{:S(2)}, u32[]{:S(2)}) collective-permute-start(f32[2,8,128]{2,1,0:T(8,128)S(1)} %get-tuple-element.78), channel_id=1, source_target_pairs={{2,0},{4,2},{6,4},{8,6},{10,8},{12,10},{14,12},{0,14},{3,1},{5,3},... | collective-permute-start | bytes 24584 | tf_op jit(solution)/shard_map/ppermute | solution.py:584
  33.7 2.6 %scatter2.1 = (f32[4,192,128]{2,1,0:T(8,128)S(1)}, f32[8,128]{1,0:T(8,128)S(1)}) custom-call(s32[32,128]{1,0:T(8,128)S(1)} %get-tuple-element.74.placed, f32[16,16,128]{2,1,0:T(8,128)S(1)} %all-to-all-done.fields_ref, f32[3,192,128]{2,1,0:T(8,128)S(1)} %get-tuple-element.90.e_ref.e_new, f32[3,192,128]{2,1,0:T(8,128)S(1)} %get-tuple-element.69.h_ref, ...), custom_call_target="tpu_custom_call" | custom-call | bytes 2097152 | tf_op jit(solution)/shard_map/scatter2/pallas_call | solution.py:48
  36.8 1.6 %collective-permute-start.9 = (f32[2,24,128]{2,1,0:T(8,128)S(1)}, f32[2,24,128]{2,1,0:T(8,128)S(1)}, u32[]{:S(2)}, u32[]{:S(2)}) collective-permute-start(f32[2,24,128]{2,1,0:T(8,128)S(1)} %get-tuple-element.87), channel_id=1, source_target_pairs={{0,16},{16,32},{32,48},{48,64},{64,80},{80,96},{96,112},{112,128},... | collective-permute-start | bytes 73736 | tf_op jit(solution)/shard_map/ppermute | solution.py:584
  38.4 3.0 %drive.1.drives = f32[6,32,128]{2,1,0:T(8,128)S(1)} custom-call(f32[3,192,128]{2,1,0:T(8,128)S(1)} %get-tuple-element.64.e_ref.e_old, f32[3,192,128]{2,1,0:T(8,128)S(1)} %get-tuple-element.90.e_ref.e_new, s32[32,128]{1,0:T(8,128)S(1)} %get-tuple-element.74.placed), custom_call_target="tpu_custom_call" | custom-call | bytes 2097152 | tf_op jit(solution)/shard_map/drive/pallas_call | solution.py:48
  41.4 0.7 collective-permute-done.10.face_y
  42.0 2.9 %collective-permute-done.9.face_x = f32[2,24,128]{2,1,0:T(8,128)S(1)} collective-permute-done((f32[2,24,128]{2,1,0:T(8,128)S(1)}, f32[2,24,128]{2,1,0:T(8,128)S(1)}, u32[]{:S(2)}, u32[]{:S(2)}) %collective-permute-start.9) | collective-permute-done | bytes 24608 | tf_op jit(solution)/shard_map/ppermute | solution.py:584
  44.9 3.2 %final.1 = (f32[3,192,128]{2,1,0:T(8,128)S(1)}, f32[384,128]{1,0:T(8,128)S(1)}, f32[384,128]{1,0:T(8,128)S(1)}) custom-call(f32[3,192,128]{2,1,0:T(8,128)S(1)} %get-tuple-element.90.e_ref.e_new, f32[3,192,128]{2,1,0:T(8,128)S(1)} %get-tuple-element.86.h_ref, f32[2,24,128]{2,1,0:T(8,128)S(1)} %collective-permute-done.9.face_x, ...), custom_call_target="tpu_custom_call" | custom-call | bytes 2097152 | tf_op jit(solution)/shard_map/final/pallas_call | solution.py:48
  48.2 1.4 %collective-permute-done.12 = f32[384,128]{1,0:T(8,128)S(1)} collective-permute-done((f32[384,128]{1,0:T(8,128)S(1)}, f32[384,128]{1,0:T(8,128)S(1)}, u32[]{:S(2)}, u32[]{:S(2)}) %collective-permute-start.12) | collective-permute-done | bytes 196640 | tf_op jit(solution)/shard_map/ppermute | solution.py:680
  49.6 10.5 %all_to_all.15.pieces = f32[8,48,128]{2,1,0:T(8,128)S(1)} all-to-all(f32[8,48,128]{2,1,0:T(8,128)S(1)} %bitcast.25), channel_id=1, replica_groups=mesh['gx'=16,'gy'=8,'gz'=2] {'gy'}, dimensions={0} | all-to-all | bytes 393216 | tf_op jit(solution)/shard_map/all_to_all | solution.py:681
  60.4 2.7 %collective-permute-start.14 = (f32[96,128]{1,0:T(8,128)S(1)}, f32[96,128]{1,0:T(8,128)S(1)}, u32[]{:S(2)}, u32[]{:S(2)}) collective-permute-start(f32[96,128]{1,0:T(8,128)S(1)} %get-tuple-element.105), channel_id=1, source_target_pairs={{0,128},{16,144},{32,160},{48,176},{64,192},{80,208},{96,224},{112... | collective-permute-start | bytes 147464 | tf_op jit(solution)/shard_map/ppermute | solution.py:687
  63.1 1.9 %collective-permute-start.15 = (f32[96,128]{1,0:T(8,128)S(1)}, f32[96,128]{1,0:T(8,128)S(1)}, u32[]{:S(2)}, u32[]{:S(2)}) collective-permute-start(f32[96,128]{1,0:T(8,128)S(1)} %get-tuple-element.106), channel_id=1, source_target_pairs={{0,192},{16,208},{32,224},{48,240},{64,128},{80,144},{96,160},{112... | collective-permute-start | bytes 147464 | tf_op jit(solution)/shard_map/ppermute | solution.py:687
  65.0 1.1 %collective-permute-done.14.two = f32[96,128]{1,0:T(8,128)S(1)} collective-permute-done((f32[96,128]{1,0:T(8,128)S(1)}, f32[96,128]{1,0:T(8,128)S(1)}, u32[]{:S(2)}, u32[]{:S(2)}) %collective-permute-start.14) | collective-permute-done | bytes 49184 | tf_op jit(solution)/shard_map/ppermute | solution.py:687
  66.1 2.3 %collective-permute-done.15.three = f32[96,128]{1,0:T(8,128)S(1)} collective-permute-done((f32[96,128]{1,0:T(8,128)S(1)}, f32[96,128]{1,0:T(8,128)S(1)}, u32[]{:S(2)}, u32[]{:S(2)}) %collective-permute-start.15) | collective-permute-done | bytes 49184 | tf_op jit(solution)/shard_map/ppermute | solution.py:687
  68.4 1.9 %collective-permute-start.16 = (f32[96,128]{1,0:T(8,128)S(1)}, f32[96,128]{1,0:T(8,128)S(1)}, u32[]{:S(2)}, u32[]{:S(2)}) collective-permute-start(f32[96,128]{1,0:T(8,128)S(1)} %get-tuple-element.109), channel_id=1, source_target_pairs={{0,16},{16,0},{32,48},{48,32},{64,80},{80,64},{96,112},{112,96},{1... | collective-permute-start | bytes 147464 | tf_op jit(solution)/shard_map/ppermute | solution.py:699
  70.3 2.2 %collective-permute-start.17 = (f32[96,128]{1,0:T(8,128)S(1)}, f32[96,128]{1,0:T(8,128)S(1)}, u32[]{:S(2)}, u32[]{:S(2)}) collective-permute-start(f32[96,128]{1,0:T(8,128)S(1)} %get-tuple-element.110), channel_id=1, source_target_pairs={{0,32},{16,48},{32,0},{48,16},{64,96},{80,112},{96,64},{112,80},{1... | collective-permute-start | bytes 147464 | tf_op jit(solution)/shard_map/ppermute | solution.py:699
  72.5 2.5 %collective-permute-start.18 = (f32[96,128]{1,0:T(8,128)S(1)}, f32[96,128]{1,0:T(8,128)S(1)}, u32[]{:S(2)}, u32[]{:S(2)}) collective-permute-start(f32[96,128]{1,0:T(8,128)S(1)} %get-tuple-element.111), channel_id=1, source_target_pairs={{0,48},{16,32},{32,16},{48,0},{64,112},{80,96},{96,80},{112,64},{1... | collective-permute-start | bytes 147464 | tf_op jit(solution)/shard_map/ppermute | solution.py:699
  75.0 0.8 store.1
  75.9 2.5 %collective-permute-done.17.two = f32[96,128]{1,0:T(8,128)S(1)} collective-permute-done((f32[96,128]{1,0:T(8,128)S(1)}, f32[96,128]{1,0:T(8,128)S(1)}, u32[]{:S(2)}, u32[]{:S(2)}) %collective-permute-start.17) | collective-permute-done | bytes 49184 | tf_op jit(solution)/shard_map/ppermute | solution.py:699
  78.4 0.5 collective-permute-done.18.three
  79.0 0.7 atoms.1
  79.7 10.3 %all_to_all.16 = f32[8,48,128]{2,1,0:T(8,128)S(1)} all-to-all(f32[8,48,128]{2,1,0:T(8,128)S(1)} %get-tuple-element.123), channel_id=1, replica_groups=mesh['gx'=16,'gy'=8,'gz'=2] {'gy'}, dimensions={0} | all-to-all | bytes 393216 | tf_op jit(solution)/shard_map/all_to_all | solution.py:718
  90.0 0.7 copy.17
  (26 shorter events, 1.5 us)
Async XLA Ops:
  2.3 15.1 %collective-permute-start.2 = (f32[2,192,128]{2,1,0:T(8,128)S(1)}, f32[2,192,128]{2,1,0:T(8,128)S(1)}, u32[]{:S(2)}, u32[]{:S(2)}) collective-permute-start(f32[2,192,128]{2,1,0:T(8,128)S(1)} %get-tuple-element.68), channel_id=1, source_target_pairs={{1,0},{0,1},{3,2},{2,3},{5,4},{4,5},{7,6},{6,7},{9,8},{8,9},{11,10... | collective-permute-start | bytes 589832 | tf_op jit(solution)/shard_map/ppermute | solution.py:584
  2.4 15.0 %collective-permute-start = (f32[2,24,128]{2,1,0:T(8,128)S(1)}, f32[2,24,128]{2,1,0:T(8,128)S(1)}, u32[]{:S(2)}, u32[]{:S(2)}) collective-permute-start(f32[2,24,128]{2,1,0:T(8,128)S(1)} %get-tuple-element.66), channel_id=1, source_target_pairs={{16,0},{32,16},{48,32},{64,48},{80,64},{96,80},{112,96},{128,112},... | collective-permute-start | bytes 73736 | tf_op jit(solution)/shard_map/ppermute | solution.py:584
  11.0 6.5 %collective-permute-start.1 = (f32[2,8,128]{2,1,0:T(8,128)S(1)}, f32[2,8,128]{2,1,0:T(8,128)S(1)}, u32[]{:S(2)}, u32[]{:S(2)}) collective-permute-start(f32[2,8,128]{2,1,0:T(8,128)S(1)} %get-tuple-element.67), channel_id=1, source_target_pairs={{2,0},{4,2},{6,4},{8,6},{10,8},{12,10},{14,12},{0,14},{3,1},{5,3},... | collective-permute-start | bytes 24584 | tf_op jit(solution)/shard_map/ppermute | solution.py:584
  11.5 14.5 %all-to-all-start = ((f32[16,16,128]{2,1,0:T(8,128)}), f32[16,16,128]{2,1,0:T(8,128)S(1)}, u32[]{:S(2)}, u32[]{:S(2)}) async-start(f32[16,16,128]{2,1,0:T(8,128)} %get-tuple-element.75), calls=%async_computation | async-start | bytes 262144 | tf_op jit(solution)/shard_map/all_to_all | solution.py:600
  17.7 10.8 %collective-permute-start.5 = (f32[2,192,128]{2,1,0:T(8,128)S(1)}, f32[2,192,128]{2,1,0:T(8,128)S(1)}, u32[]{:S(2)}, u32[]{:S(2)}) collective-permute-start(f32[2,192,128]{2,1,0:T(8,128)S(1)} %get-tuple-element.72), channel_id=1, source_target_pairs={{0,1},{1,0},{2,3},{3,2},{4,5},{5,4},{6,7},{7,6},{8,9},{9,8},{10,11... | collective-permute-start | bytes 589832 | tf_op jit(solution)/shard_map/ppermute | solution.py:584
  17.8 10.6 %collective-permute-start.3 = (f32[2,24,128]{2,1,0:T(8,128)S(1)}, f32[2,24,128]{2,1,0:T(8,128)S(1)}, u32[]{:S(2)}, u32[]{:S(2)}) collective-permute-start(f32[2,24,128]{2,1,0:T(8,128)S(1)} %get-tuple-element.70), channel_id=1, source_target_pairs={{0,16},{16,32},{32,48},{48,64},{64,80},{80,96},{96,112},{112,128},... | collective-permute-start | bytes 73736 | tf_op jit(solution)/shard_map/ppermute | solution.py:584
  20.6 7.8 %collective-permute-start.4 = (f32[2,8,128]{2,1,0:T(8,128)S(1)}, f32[2,8,128]{2,1,0:T(8,128)S(1)}, u32[]{:S(2)}, u32[]{:S(2)}) collective-permute-start(f32[2,8,128]{2,1,0:T(8,128)S(1)} %get-tuple-element.71), channel_id=1, source_target_pairs={{0,2},{2,4},{4,6},{6,8},{8,10},{10,12},{12,14},{14,0},{1,3},{3,5},... | collective-permute-start | bytes 24584 | tf_op jit(solution)/shard_map/ppermute | solution.py:584
  28.7 7.7 %collective-permute-start.8 = (f32[2,192,128]{2,1,0:T(8,128)S(1)}, f32[2,192,128]{2,1,0:T(8,128)S(1)}, u32[]{:S(2)}, u32[]{:S(2)}) collective-permute-start(f32[2,192,128]{2,1,0:T(8,128)S(1)} %get-tuple-element.79), channel_id=1, source_target_pairs={{1,0},{0,1},{3,2},{2,3},{5,4},{4,5},{7,6},{6,7},{9,8},{8,9},{11,10... | collective-permute-start | bytes 589832 | tf_op jit(solution)/shard_map/ppermute | solution.py:584
  28.8 7.6 %collective-permute-start.6 = (f32[2,24,128]{2,1,0:T(8,128)S(1)}, f32[2,24,128]{2,1,0:T(8,128)S(1)}, u32[]{:S(2)}, u32[]{:S(2)}) collective-permute-start(f32[2,24,128]{2,1,0:T(8,128)S(1)} %get-tuple-element.77), channel_id=1, source_target_pairs={{16,0},{32,16},{48,32},{64,48},{80,64},{96,80},{112,96},{128,112},... | collective-permute-start | bytes 73736 | tf_op jit(solution)/shard_map/ppermute | solution.py:584
  30.0 6.3 %collective-permute-start.7 = (f32[2,8,128]{2,1,0:T(8,128)S(1)}, f32[2,8,128]{2,1,0:T(8,128)S(1)}, u32[]{:S(2)}, u32[]{:S(2)}) collective-permute-start(f32[2,8,128]{2,1,0:T(8,128)S(1)} %get-tuple-element.78), channel_id=1, source_target_pairs={{2,0},{4,2},{6,4},{8,6},{10,8},{12,10},{14,12},{0,14},{3,1},{5,3},... | collective-permute-start | bytes 24584 | tf_op jit(solution)/shard_map/ppermute | solution.py:584
  36.5 8.4 %collective-permute-start.11 = (f32[2,192,128]{2,1,0:T(8,128)S(1)}, f32[2,192,128]{2,1,0:T(8,128)S(1)}, u32[]{:S(2)}, u32[]{:S(2)}) collective-permute-start(f32[2,192,128]{2,1,0:T(8,128)S(1)} %get-tuple-element.89), channel_id=1, source_target_pairs={{0,1},{1,0},{2,3},{3,2},{4,5},{5,4},{6,7},{7,6},{8,9},{9,8},{10,11... | collective-permute-start | bytes 589832 | tf_op jit(solution)/shard_map/ppermute | solution.py:584
  36.8 8.1 %collective-permute-start.9 = (f32[2,24,128]{2,1,0:T(8,128)S(1)}, f32[2,24,128]{2,1,0:T(8,128)S(1)}, u32[]{:S(2)}, u32[]{:S(2)}) collective-permute-start(f32[2,24,128]{2,1,0:T(8,128)S(1)} %get-tuple-element.87), channel_id=1, source_target_pairs={{0,16},{16,32},{32,48},{48,64},{64,80},{80,96},{96,112},{112,128},... | collective-permute-start | bytes 73736 | tf_op jit(solution)/shard_map/ppermute | solution.py:584
  38.4 3.7 %collective-permute-start.10 = (f32[2,8,128]{2,1,0:T(8,128)S(1)}, f32[2,8,128]{2,1,0:T(8,128)S(1)}, u32[]{:S(2)}, u32[]{:S(2)}) collective-permute-start(f32[2,8,128]{2,1,0:T(8,128)S(1)} %get-tuple-element.88), channel_id=1, source_target_pairs={{0,2},{2,4},{4,6},{6,8},{8,10},{10,12},{12,14},{14,0},{1,3},{3,5},... | collective-permute-start | bytes 24584 | tf_op jit(solution)/shard_map/ppermute | solution.py:584
  48.1 1.5 %collective-permute-start.12 = (f32[384,128]{1,0:T(8,128)S(1)}, f32[384,128]{1,0:T(8,128)S(1)}, u32[]{:S(2)}, u32[]{:S(2)}) collective-permute-start(f32[384,128]{1,0:T(8,128)S(1)} %get-tuple-element.101), channel_id=1, source_target_pairs={{1,0},{0,1},{3,2},{2,3},{5,4},{4,5},{7,6},{6,7},{9,8},{8,9},{11,10... | collective-permute-start | bytes 589832 | tf_op jit(solution)/shard_map/ppermute | solution.py:680
  60.2 4.8 %collective-permute-start.13 = (f32[96,128]{1,0:T(8,128)S(1)}, f32[96,128]{1,0:T(8,128)S(1)}, u32[]{:S(2)}, u32[]{:S(2)}) collective-permute-start(f32[96,128]{1,0:T(8,128)S(1)} %get-tuple-element.104), channel_id=1, source_target_pairs={{0,64},{16,80},{32,96},{48,112},{64,0},{80,16},{96,32},{112,48},{1... | collective-permute-start | bytes 147464 | tf_op jit(solution)/shard_map/ppermute | solution.py:687
  60.4 5.7 %collective-permute-start.14 = (f32[96,128]{1,0:T(8,128)S(1)}, f32[96,128]{1,0:T(8,128)S(1)}, u32[]{:S(2)}, u32[]{:S(2)}) collective-permute-start(f32[96,128]{1,0:T(8,128)S(1)} %get-tuple-element.105), channel_id=1, source_target_pairs={{0,128},{16,144},{32,160},{48,176},{64,192},{80,208},{96,224},{112... | collective-permute-start | bytes 147464 | tf_op jit(solution)/shard_map/ppermute | solution.py:687
  63.1 5.3 %collective-permute-start.15 = (f32[96,128]{1,0:T(8,128)S(1)}, f32[96,128]{1,0:T(8,128)S(1)}, u32[]{:S(2)}, u32[]{:S(2)}) collective-permute-start(f32[96,128]{1,0:T(8,128)S(1)} %get-tuple-element.106), channel_id=1, source_target_pairs={{0,192},{16,208},{32,224},{48,240},{64,128},{80,144},{96,160},{112... | collective-permute-start | bytes 147464 | tf_op jit(solution)/shard_map/ppermute | solution.py:687
  68.4 7.4 %collective-permute-start.16 = (f32[96,128]{1,0:T(8,128)S(1)}, f32[96,128]{1,0:T(8,128)S(1)}, u32[]{:S(2)}, u32[]{:S(2)}) collective-permute-start(f32[96,128]{1,0:T(8,128)S(1)} %get-tuple-element.109), channel_id=1, source_target_pairs={{0,16},{16,0},{32,48},{48,32},{64,80},{80,64},{96,112},{112,96},{1... | collective-permute-start | bytes 147464 | tf_op jit(solution)/shard_map/ppermute | solution.py:699
  70.3 8.1 %collective-permute-start.17 = (f32[96,128]{1,0:T(8,128)S(1)}, f32[96,128]{1,0:T(8,128)S(1)}, u32[]{:S(2)}, u32[]{:S(2)}) collective-permute-start(f32[96,128]{1,0:T(8,128)S(1)} %get-tuple-element.110), channel_id=1, source_target_pairs={{0,32},{16,48},{32,0},{48,16},{64,96},{80,112},{96,64},{112,80},{1... | collective-permute-start | bytes 147464 | tf_op jit(solution)/shard_map/ppermute | solution.py:699
  72.5 6.4 %collective-permute-start.18 = (f32[96,128]{1,0:T(8,128)S(1)}, f32[96,128]{1,0:T(8,128)S(1)}, u32[]{:S(2)}, u32[]{:S(2)}) collective-permute-start(f32[96,128]{1,0:T(8,128)S(1)} %get-tuple-element.111), channel_id=1, source_target_pairs={{0,48},{16,32},{32,16},{48,0},{64,112},{80,96},{96,80},{112,64},{1... | collective-permute-start | bytes 147464 | tf_op jit(solution)/shard_map/ppermute | solution.py:699

commit v8 on v7

--- a/solution.py
+++ b/solution.py
@@ -1,4 +1,3 @@
-import functools
 import math
 
 import jax
@@ -139,14 +138,12 @@
 
 def prepare_kernel(e_hbm, state_hbm, out_x, out_y, out_z, packed, e_out, state, sems):
     copies = [
-        pltpu.make_async_copy(e_hbm, e_out, sems.at[0]),
-        pltpu.make_async_copy(state_hbm, state, sems.at[1]),
+        pltpu.make_async_copy(state_hbm, state, sems.at[0]),
+        pltpu.make_async_copy(e_hbm, e_out, sems.at[1]),
     ]
     for copy in copies:
         copy.start()
     copies[0].wait()
-    first_layers(e_out, out_x, out_y, out_z)
-    copies[1].wait()
     lower, lasing, upper = state[7], state[8], state[9]
     lasing_free = lasing + time_step * (upper / upper_life - lasing / lasing_life)
     lower_free = lower + time_step * (lasing / lasing_life - lower / lower_life)
@@ -155,6 +152,8 @@
     for field, value in enumerate(free + [lasing - lower] + polar + [lasing_free - lower_free]):
         for owner in range(SLOTS // 2):
             packed[owner, 2 * field : 2 * field + 2] = value[2 * owner : 2 * owner + 2]
+    copies[1].wait()
+    first_layers(e_out, out_x, out_y, out_z)
 
 
 def magnetic_kernel(e_ref, h_ref, face_x, face_y, face_z, h_out, out_x, out_y, out_z):
@@ -195,19 +194,17 @@
     return row_index(HALF, width) == (offsets >> 8)
 
 
-def scatter_kernel(first, placed, fields_ref, dense, spots, columns):
+def place_fields(first, fields_ref, dense, tall, spots, columns):
     for slot in range(SLOTS):
-        line = placed[slot : slot + 1]
         across = slice(slot * CZ, (slot + 1) * CZ)
-        columns[:, across] = wide_hits(line, CZ)
-        tall = tall_hits(line, CZ).astype(F32).astype(BF16).reshape(6, 16, CZ)
+        hits = tall[:, across].reshape(6, 16, CZ)
         values = fields_ref[slot // 2, pl.ds(2 * first + slot % 2, 4, 2), :]
         for place, part in enumerate(split_parts(values)):
             part = part.astype(F32)
             for field in range(4):
                 row = jnp.broadcast_to(part[field : field + 1], (16, CZ)).astype(BF16)
                 top = (4 * place + field) * HALF
-                spots[top : top + HALF, across] = (tall * row[None]).reshape(HALF, CZ)
+                spots[top : top + HALF, across] = (hits * row[None]).reshape(HALF, CZ)
     total = lax.dot_general(
         spots[...], columns[...], (((1,), (1,)), ((), ())), preferred_element_type=F32
     )
@@ -218,13 +215,19 @@
         dense[field, pl.ds(1, HALF, 2), :] = got[:, CZ:]
 
 
-SCATTER = [pltpu.VMEM((8 * HALF, SLOTS * CZ), BF16), pltpu.VMEM((WIDE, SLOTS * CZ), BF16)]
+def scatter_kernel(placed, fields_ref, dense, tall, columns, spots):
+    for slot in range(SLOTS):
+        line = placed[slot : slot + 1]
+        across = slice(slot * CZ, (slot + 1) * CZ)
+        columns[:, across] = wide_hits(line, CZ)
+        tall[:, across] = tall_hits(line, CZ).astype(F32).astype(BF16)
+    place_fields(0, fields_ref, dense, tall, spots, columns)
 
 
 def scatter_sample_kernel(
-    placed, fields_ref, e_ref, h_ref, surf_ref, dense, sampled, spots, columns
+    fields_ref, tall, columns, e_ref, h_ref, surf_ref, dense, sampled, spots
 ):
-    scatter_kernel(4, placed, fields_ref, dense, spots, columns)
+    place_fields(4, fields_ref, dense, tall, spots, columns)
     sample_rows(e_ref, h_ref, surf_ref, sampled)
 
 
@@ -257,8 +260,7 @@
     )
 
 
-def gather_lines(values, offsets, width):
-    hits = wide_hits(offsets, width)
+def gather_lines(values, hits, offsets, width):
     tall = tall_hits(offsets, width)
     picked = jnp.dot(values, hits, preferred_element_type=F32)
     lines = []
@@ -272,26 +274,23 @@
 TAKE = 16
 
 
-def drive_kernel(e_old, e_new, placed, drives, values):
+def drive_kernel(e_old, e_new, placed, columns, drives, values):
     values[...] = stacked([(ref, comp) for ref in (e_old, e_new) for comp in range(3)])
-
-    def group(index, carry):
-        lines = placed[pl.ds(TAKE * index, TAKE)]
-        offsets = jnp.concatenate([lines[slot : slot + 1] for slot in range(TAKE)], axis=1)
-        got = gather_lines(values[...], offsets, TAKE * CZ)
+    for group in range(0, SLOTS, TAKE):
+        offsets = jnp.concatenate([placed[group + n : group + n + 1] for n in range(TAKE)], axis=1)
+        hits = columns[:, group * CZ : (group + TAKE) * CZ]
+        got = gather_lines(values[...], hits, offsets, TAKE * CZ)
         for field in range(6):
             for slot in range(TAKE):
-                drives[field, pl.ds(TAKE * index + slot, 1)] = got[field][
+                drives[field, group + slot : group + slot + 1] = got[field][
                     :, slot * CZ : (slot + 1) * CZ
                 ]
-        return carry
-
-    lax.fori_loop(0, SLOTS // TAKE, group, 0)
 
 
 def sample_rows(e_ref, h_ref, surf_ref, sampled):
     values = stacked([(ref, comp) for ref in (e_ref, h_ref) for comp in range(3)])
-    got = gather_lines(values, surf_ref[...], CZ)
+    offsets = surf_ref[...]
+    got = gather_lines(values, wide_hits(offsets, CZ), offsets, CZ)
     sampled[...] = jnp.zeros_like(sampled)
     for field in range(6):
         sampled[field : field + 1] = got[field]
@@ -304,9 +303,9 @@
 def phase_kernel(
     count_ref,
     owner_hbm,
-    offsets_ref,
-    surf_ref,
-    units_ref,
+    offsets_hbm,
+    surf_hbm,
+    units_hbm,
     h_hbm,
     eps_hbm,
     pump_hbm,
@@ -321,6 +320,8 @@
     pump_out,
     far_out,
     owner_ref,
+    offsets_ref,
+    units_ref,
     sems,
 ):
     own = pl.ds(pl.multiple_of(FAR * lax.axis_index("gy"), 8), FAR)
@@ -328,7 +329,10 @@
         pltpu.make_async_copy(source, target, sems.at[place])
         for place, (source, target) in enumerate(
             (
+                (surf_hbm, surf_out),
+                (units_hbm, units_ref),
                 (owner_hbm, owner_ref),
+                (offsets_hbm, offsets_ref),
                 (h_hbm, h_out),
                 (eps_hbm, eps_out),
                 (pump_hbm, pump_out),
@@ -343,8 +347,9 @@
     moment = omega * jnp.where(lanes < FREQ, time_step, 2.0 * time_step)
     for place, value in enumerate((jnp.cos(moment), jnp.sin(moment))):
         factors[place] = jnp.transpose(jnp.broadcast_to(value[0:1], (DIRS, DIRS)))
-    cells = surf_ref[...]
-    surf_out[...] = cells
+    copies[0].wait()
+    copies[1].wait()
+    cells = surf_out[...]
     rows = cells >> 7
     layer = (rows * 2731) >> 16
     cell_x = lax.axis_index("gx") * CX + layer
@@ -372,7 +377,7 @@
     turn[0], turn[1] = powers[1]
     starts[0], starts[1] = low_start
     starts[2], starts[3] = high_start
-    for copy in copies:
+    for copy in copies[2:]:
         copy.wait()
     count = count_ref[0]
     for slot in range(SLOTS):
@@ -622,8 +627,13 @@
             pump.reshape(SLOTS, CZ),
             jnp.transpose(far_acc, (1, 0, 2)).reshape(8 * FAR, DIRS),
         ),
-        in_specs=[pl.BlockSpec(memory_space=pltpu.SMEM), hbm, vmem, vmem, vmem] + [hbm] * 4,
-        scratch=[pltpu.SMEM((1, SLOTS), jnp.int32), pltpu.SemaphoreType.DMA((5,))],
+        in_specs=[pl.BlockSpec(memory_space=pltpu.SMEM)] + [hbm] * 8,
+        scratch=[
+            pltpu.SMEM((1, SLOTS), jnp.int32),
+            pltpu.VMEM((SLOTS, CZ), jnp.int32),
+            pltpu.VMEM((8, DIRS), F32),
+            pltpu.SemaphoreType.DMA((8,)),
+        ],
         moved=MIB // 4,
         name="phase",
     )
@@ -636,11 +646,16 @@
         name="magnetic",
     )
     edge = shifted(edge, up)
-    spread_now = call(
-        functools.partial(scatter_kernel, 0),
-        shape(4, ROWS, CZ),
+    spots = pltpu.VMEM((8 * HALF, SLOTS * CZ), BF16)
+    spread_now, tall, columns = call(
+        scatter_kernel,
+        (
+            shape(4, ROWS, CZ),
+            shape(HALF, SLOTS * CZ, dtype=BF16),
+            shape(WIDE, SLOTS * CZ, dtype=BF16),
+        ),
         (placed, fields),
-        scratch=SCATTER,
+        scratch=[spots],
         name="scatter",
     )
     e_one, *near, rates = call(
@@ -653,8 +668,8 @@
     spread_next, early = call(
         scatter_sample_kernel,
         (shape(4, ROWS, CZ), shape(8, CZ)),
-        (placed, fields, e_one, h_one, surf),
-        scratch=SCATTER,
+        (fields, tall, columns, e_one, h_one, surf),
+        scratch=[spots],
         name="scatter2",
     )
     *near, spread_next = lax.optimization_barrier((*near, spread_next))
@@ -664,7 +679,7 @@
     drives = call(
         drive_kernel,
         shape(6, SLOTS, CZ),
-        (e_old, e_seen, placed),
+        (e_old, e_seen, placed, columns),
         scratch=[pltpu.VMEM((12 * HALF, WIDE), BF16)],
         name="drive",
     )

time: 91 us -> 90.4 us (level)
  Pallas kernels: 16.9 us -> 15.6 us
  waiting for transfers between devices: 15.3 us -> 16.5 us
    pallas_call x14, Pallas kernels: 16.9 us -> 15.6 us  [call(): pl.pallas_call(kernel, out_shape=outs, in_specs=in_specs or [pl.BlockSpec...]
  transfers between devices with their start and end apart: 20 -> 20, of which waited for: 8 -> 8; matrix products, arithmetic and copies ran while one was open for 0% -> 0% of each run, Pallas kernels for 12% -> 10%
where the time goes in v8:
time: 90.4 us; the launch traced here: 90.1 us
  starting transfers between devices  35.5 us (39%)
  blocking collectives  20.4 us (23%)
  waiting for transfers between devices  16.5 us (18%)
  Pallas kernels  15.6 us (17%)
  between operations  1.47 us (2%)
    ppermute x12, starting transfers between devices, shifted(): lax.ppermute(part, axis, perm)  20.5 us
    pallas_call x14, Pallas kernels, call(): pl.pallas_call(kernel, out_shape=outs, in_specs=in_specs or [pl.BlockSpec...  15.6 us
    all_to_all x1, blocking collectives, local(): pieces = lax.all_to_all(chip.reshape(8, FAR, DIRS), 'gy', 0, 0, tiled=True)  10.4 us
    all_to_all x1, blocking collectives, local(): gathered = lax.all_to_all(copies, 'gy', 0, 0, tiled=True)  10 us
    ppermute x3, starting transfers between devices, local(): lax.ppermute(value, 'gx', [(a * 4 + z, a * 4 + (z ^ k)) for a in range(4)...  6.58 us
    ppermute x3, starting transfers between devices, local(): lax.ppermute(value, 'gx', [(a * 4 + z, (a ^ k) * 4 + z) for a in range(4)...  4.79 us
    all_to_all x1, waiting for transfers between devices, local(): fields = lax.all_to_all(packed, 'gx', 0, 0, tiled=True)  4.54 us
    ppermute x3, waiting for transfers between devices, local(): lax.ppermute(value, 'gx', [(a * 4 + z, (a ^ k) * 4 + z) for a in range(4)...  3.59 us
  transfers between devices with their start and end apart: 20, of which 8 were waited for; matrix products, arithmetic and copies ran while one was open for 0% of the time, Pallas kernels for 10%

profile of v8, /device:TPU:8, one launch (start us, length us, event | category | flops | bytes accessed | tf_op | source)
XLA Modules:
  0.0 90.1 jit_solution(4918063486858095615)
XLA Ops:
  0.6 1.7 %prepare.1 = (f32[2,24,128]{2,1,0:T(8,128)S(1)}, f32[2,8,128]{2,1,0:T(8,128)S(1)}, f32[2,192,128]{2,1,0:T(8,128)S(1)}, f32[16,16,128]{2,1,0:T(8,128)}, f32[3,192...) custom-call(f32[3,192,128]{2,1,0:T(8,128)} %bitcast.26, f32[10,32,128]{2,1,0:T(8,128)} %bitcast.29), custom_call_target="tpu_custom_call" | custom-call | bytes 2097152 | tf_op jit(solution)/shard_map/prepare/pallas_call | solution.py:47
  2.5 8.6 %collective-permute-start = (f32[2,24,128]{2,1,0:T(8,128)S(1)}, f32[2,24,128]{2,1,0:T(8,128)S(1)}, u32[]{:S(2)}, u32[]{:S(2)}) collective-permute-start(f32[2,24,128]{2,1,0:T(8,128)S(1)} %get-tuple-element.69), channel_id=1, source_target_pairs={{16,0},{32,16},{48,32},{64,48},{80,64},{96,80},{112,96},{128,112},... | collective-permute-start | bytes 73736 | tf_op jit(solution)/shard_map/ppermute | solution.py:589
  11.0 0.4 collective-permute-start.1
  11.5 3.5 %all-to-all-start = ((f32[16,16,128]{2,1,0:T(8,128)}), f32[16,16,128]{2,1,0:T(8,128)S(1)}, u32[]{:S(2)}, u32[]{:S(2)}) async-start(f32[16,16,128]{2,1,0:T(8,128)} %get-tuple-element.78), calls=%async_computation | async-start | bytes 262144 | tf_op jit(solution)/shard_map/all_to_all | solution.py:605
  15.7 1.2 %phase.1 = (s32[32,128]{1,0:T(8,128)S(1)}, s32[1,128]{1,0:T(1,128)S(1)}, f32[4,128,128]{2,1,0:T(8,128)S(1)}, f32[2,128,128]{2,1,0:T(8,128)S(1)}, f32[2,128,128]{...) custom-call(s32[1]{0:T(128)} %bitcast.23.count_ref, ...), custom_call_target="tpu_custom_call" | custom-call | bytes 262144 | tf_op jit(solution)/shard_map/phase/pallas_call | solution.py:47
  17.1 2.8 %collective-permute-start.3 = (f32[2,24,128]{2,1,0:T(8,128)S(1)}, f32[2,24,128]{2,1,0:T(8,128)S(1)}, u32[]{:S(2)}, u32[]{:S(2)}) collective-permute-start(f32[2,24,128]{2,1,0:T(8,128)S(1)} %get-tuple-element.73), channel_id=1, source_target_pairs={{0,16},{16,32},{32,48},{48,64},{64,80},{80,96},{96,112},{112,128},... | collective-permute-start | bytes 73736 | tf_op jit(solution)/shard_map/ppermute | solution.py:589
  19.9 1.6 %collective-permute-start.4 = (f32[2,8,128]{2,1,0:T(8,128)S(1)}, f32[2,8,128]{2,1,0:T(8,128)S(1)}, u32[]{:S(2)}, u32[]{:S(2)}) collective-permute-start(f32[2,8,128]{2,1,0:T(8,128)S(1)} %get-tuple-element.74), channel_id=1, source_target_pairs={{0,2},{2,4},{4,6},{6,8},{8,10},{10,12},{12,14},{14,0},{1,3},{3,5},... | collective-permute-start | bytes 24584 | tf_op jit(solution)/shard_map/ppermute | solution.py:589
  21.5 4.5 %all-to-all-done.fields_ref = f32[16,16,128]{2,1,0:T(8,128)S(1)} async-done(((f32[16,16,128]{2,1,0:T(8,128)}), f32[16,16,128]{2,1,0:T(8,128)S(1)}, u32[]{:S(2)}, u32[]{:S(2)}) %all-to-all-start) | async-done | bytes 131104 | tf_op jit(solution)/shard_map/all_to_all | solution.py:605
  26.0 2.5 %scatter.1 = (f32[4,192,128]{2,1,0:T(8,128)S(1)}, bf16[96,4096]{1,0:T(8,128)(2,1)S(1)}, bf16[256,4096]{1,0:T(8,128)(2,1)S(1)}) custom-call(s32[32,128]{1,0:T(8,128)S(1)} %get-tuple-element.77.placed, f32[16,16,128]{2,1,0:T(8,128)S(1)} %all-to-all-done.fields_ref), custom_call_target="tpu_custom_call" | custom-call | bytes 2097152 | tf_op jit(solution)/shard_map/scatter/pallas_call | solution.py:47
  28.9 1.2 %collective-permute-start.6 = (f32[2,24,128]{2,1,0:T(8,128)S(1)}, f32[2,24,128]{2,1,0:T(8,128)S(1)}, u32[]{:S(2)}, u32[]{:S(2)}) collective-permute-start(f32[2,24,128]{2,1,0:T(8,128)S(1)} %get-tuple-element.81), channel_id=1, source_target_pairs={{16,0},{32,16},{48,32},{64,48},{80,64},{96,80},{112,96},{128,112},... | collective-permute-start | bytes 73736 | tf_op jit(solution)/shard_map/ppermute | solution.py:589
  30.1 3.5 %collective-permute-start.7 = (f32[2,8,128]{2,1,0:T(8,128)S(1)}, f32[2,8,128]{2,1,0:T(8,128)S(1)}, u32[]{:S(2)}, u32[]{:S(2)}) collective-permute-start(f32[2,8,128]{2,1,0:T(8,128)S(1)} %get-tuple-element.82), channel_id=1, source_target_pairs={{2,0},{4,2},{6,4},{8,6},{10,8},{12,10},{14,12},{0,14},{3,1},{5,3},... | collective-permute-start | bytes 24584 | tf_op jit(solution)/shard_map/ppermute | solution.py:589
  33.6 2.1 %scatter2.1 = (f32[4,192,128]{2,1,0:T(8,128)S(1)}, f32[8,128]{1,0:T(8,128)S(1)}) custom-call(f32[16,16,128]{2,1,0:T(8,128)S(1)} %all-to-all-done.fields_ref, bf16[96,4096]{1,0:T(8,128)(2,1)S(1)} %get-tuple-element.84.tall, bf16[256,4096]{1,0:T(8,128)(2,1)S(1)} %get-tuple-element.85.columns, f32[3,192,128]{2,1,0:T(8,128)S(1)} %get-tuple-element.96.e_ref.e_new, ...), custom_call_target="tpu_custom_call" | custom-call | bytes 2097152 | tf_op jit(solution)/shard_map/scatter2/pallas_call | solution.py:47
  36.1 1.9 %collective-permute-start.9 = (f32[2,24,128]{2,1,0:T(8,128)S(1)}, f32[2,24,128]{2,1,0:T(8,128)S(1)}, u32[]{:S(2)}, u32[]{:S(2)}) collective-permute-start(f32[2,24,128]{2,1,0:T(8,128)S(1)} %get-tuple-element.93), channel_id=1, source_target_pairs={{0,16},{16,32},{32,48},{48,64},{64,80},{80,96},{96,112},{112,128},... | collective-permute-start | bytes 73736 | tf_op jit(solution)/shard_map/ppermute | solution.py:589
  38.0 2.7 %drive.1.drives = f32[6,32,128]{2,1,0:T(8,128)S(1)} custom-call(f32[3,192,128]{2,1,0:T(8,128)S(1)} %get-tuple-element.67.e_ref.e_old, f32[3,192,128]{2,1,0:T(8,128)S(1)} %get-tuple-element.96.e_ref.e_new, s32[32,128]{1,0:T(8,128)S(1)} %get-tuple-element.77.placed, bf16[256,4096]{1,0:T(8,128)(2,1)S(1)} %get-tuple-element.85.columns), custom_call_target="tpu_custom_call" | custom-call | bytes 2097152 | tf_op jit(solution)/shard_map/drive/pallas_call | solution.py:47
  40.7 0.9 collective-permute-done.10.face_y
  41.6 2.6 %collective-permute-done.9.face_x = f32[2,24,128]{2,1,0:T(8,128)S(1)} collective-permute-done((f32[2,24,128]{2,1,0:T(8,128)S(1)}, f32[2,24,128]{2,1,0:T(8,128)S(1)}, u32[]{:S(2)}, u32[]{:S(2)}) %collective-permute-start.9) | collective-permute-done | bytes 24608 | tf_op jit(solution)/shard_map/ppermute | solution.py:589
  44.2 3.2 %final.1 = (f32[3,192,128]{2,1,0:T(8,128)S(1)}, f32[384,128]{1,0:T(8,128)S(1)}, f32[384,128]{1,0:T(8,128)S(1)}) custom-call(f32[3,192,128]{2,1,0:T(8,128)S(1)} %get-tuple-element.96.e_ref.e_new, f32[3,192,128]{2,1,0:T(8,128)S(1)} %get-tuple-element.92.h_ref, f32[2,24,128]{2,1,0:T(8,128)S(1)} %collective-permute-done.9.face_x, ...), custom_call_target="tpu_custom_call" | custom-call | bytes 2097152 | tf_op jit(solution)/shard_map/final/pallas_call | solution.py:47
  47.5 1.4 %collective-permute-done.12 = f32[384,128]{1,0:T(8,128)S(1)} collective-permute-done((f32[384,128]{1,0:T(8,128)S(1)}, f32[384,128]{1,0:T(8,128)S(1)}, u32[]{:S(2)}, u32[]{:S(2)}) %collective-permute-start.12) | collective-permute-done | bytes 196640 | tf_op jit(solution)/shard_map/ppermute | solution.py:695
  49.0 10.4 %all_to_all.15.pieces = f32[8,48,128]{2,1,0:T(8,128)S(1)} all-to-all(f32[8,48,128]{2,1,0:T(8,128)S(1)} %bitcast.25), channel_id=1, replica_groups=mesh['gx'=16,'gy'=8,'gz'=2] {'gy'}, dimensions={0} | all-to-all | bytes 393216 | tf_op jit(solution)/shard_map/all_to_all | solution.py:696
  59.7 2.7 %collective-permute-start.14 = (f32[96,128]{1,0:T(8,128)S(1)}, f32[96,128]{1,0:T(8,128)S(1)}, u32[]{:S(2)}, u32[]{:S(2)}) collective-permute-start(f32[96,128]{1,0:T(8,128)S(1)} %get-tuple-element.111), channel_id=1, source_target_pairs={{0,128},{16,144},{32,160},{48,176},{64,192},{80,208},{96,224},{112... | collective-permute-start | bytes 147464 | tf_op jit(solution)/shard_map/ppermute | solution.py:702
  62.4 1.7 %collective-permute-start.15 = (f32[96,128]{1,0:T(8,128)S(1)}, f32[96,128]{1,0:T(8,128)S(1)}, u32[]{:S(2)}, u32[]{:S(2)}) collective-permute-start(f32[96,128]{1,0:T(8,128)S(1)} %get-tuple-element.112), channel_id=1, source_target_pairs={{0,192},{16,208},{32,224},{48,240},{64,128},{80,144},{96,160},{112... | collective-permute-start | bytes 147464 | tf_op jit(solution)/shard_map/ppermute | solution.py:702
  64.2 1.3 %collective-permute-done.14.two = f32[96,128]{1,0:T(8,128)S(1)} collective-permute-done((f32[96,128]{1,0:T(8,128)S(1)}, f32[96,128]{1,0:T(8,128)S(1)}, u32[]{:S(2)}, u32[]{:S(2)}) %collective-permute-start.14) | collective-permute-done | bytes 49184 | tf_op jit(solution)/shard_map/ppermute | solution.py:702
  65.4 2.3 %collective-permute-done.15.three = f32[96,128]{1,0:T(8,128)S(1)} collective-permute-done((f32[96,128]{1,0:T(8,128)S(1)}, f32[96,128]{1,0:T(8,128)S(1)}, u32[]{:S(2)}, u32[]{:S(2)}) %collective-permute-start.15) | collective-permute-done | bytes 49184 | tf_op jit(solution)/shard_map/ppermute | solution.py:702
  67.8 1.8 %collective-permute-start.16 = (f32[96,128]{1,0:T(8,128)S(1)}, f32[96,128]{1,0:T(8,128)S(1)}, u32[]{:S(2)}, u32[]{:S(2)}) collective-permute-start(f32[96,128]{1,0:T(8,128)S(1)} %get-tuple-element.115), channel_id=1, source_target_pairs={{0,16},{16,0},{32,48},{48,32},{64,80},{80,64},{96,112},{112,96},{1... | collective-permute-start | bytes 147464 | tf_op jit(solution)/shard_map/ppermute | solution.py:714
  69.6 2.9 %collective-permute-start.17 = (f32[96,128]{1,0:T(8,128)S(1)}, f32[96,128]{1,0:T(8,128)S(1)}, u32[]{:S(2)}, u32[]{:S(2)}) collective-permute-start(f32[96,128]{1,0:T(8,128)S(1)} %get-tuple-element.116), channel_id=1, source_target_pairs={{0,32},{16,48},{32,0},{48,16},{64,96},{80,112},{96,64},{112,80},{1... | collective-permute-start | bytes 147464 | tf_op jit(solution)/shard_map/ppermute | solution.py:714
  72.4 1.9 %collective-permute-start.18 = (f32[96,128]{1,0:T(8,128)S(1)}, f32[96,128]{1,0:T(8,128)S(1)}, u32[]{:S(2)}, u32[]{:S(2)}) collective-permute-start(f32[96,128]{1,0:T(8,128)S(1)} %get-tuple-element.117), channel_id=1, source_target_pairs={{0,48},{16,32},{32,16},{48,0},{64,112},{80,96},{96,80},{112,64},{1... | collective-permute-start | bytes 147464 | tf_op jit(solution)/shard_map/ppermute | solution.py:714
  74.4 0.8 store.1
  75.2 2.6 %collective-permute-done.17.two = f32[96,128]{1,0:T(8,128)S(1)} collective-permute-done((f32[96,128]{1,0:T(8,128)S(1)}, f32[96,128]{1,0:T(8,128)S(1)}, u32[]{:S(2)}, u32[]{:S(2)}) %collective-permute-start.17) | collective-permute-done | bytes 49184 | tf_op jit(solution)/shard_map/ppermute | solution.py:714
  77.8 0.8 collective-permute-done.18.three
  78.7 0.7 atoms.1
  79.4 10.0 %all_to_all.16 = f32[8,48,128]{2,1,0:T(8,128)S(1)} all-to-all(f32[8,48,128]{2,1,0:T(8,128)S(1)} %get-tuple-element.129), channel_id=1, replica_groups=mesh['gx'=16,'gy'=8,'gz'=2] {'gy'}, dimensions={0} | all-to-all | bytes 393216 | tf_op jit(solution)/shard_map/all_to_all | solution.py:733
  89.4 0.7 copy.17
  (26 shorter events, 1.7 us)
Async XLA Ops:
  2.4 14.5 %collective-permute-start.2 = (f32[2,192,128]{2,1,0:T(8,128)S(1)}, f32[2,192,128]{2,1,0:T(8,128)S(1)}, u32[]{:S(2)}, u32[]{:S(2)}) collective-permute-start(f32[2,192,128]{2,1,0:T(8,128)S(1)} %get-tuple-element.71), channel_id=1, source_target_pairs={{1,0},{0,1},{3,2},{2,3},{5,4},{4,5},{7,6},{6,7},{9,8},{8,9},{11,10... | collective-permute-start | bytes 589832 | tf_op jit(solution)/shard_map/ppermute | solution.py:589
  2.5 14.4 %collective-permute-start = (f32[2,24,128]{2,1,0:T(8,128)S(1)}, f32[2,24,128]{2,1,0:T(8,128)S(1)}, u32[]{:S(2)}, u32[]{:S(2)}) collective-permute-start(f32[2,24,128]{2,1,0:T(8,128)S(1)} %get-tuple-element.69), channel_id=1, source_target_pairs={{16,0},{32,16},{48,32},{64,48},{80,64},{96,80},{112,96},{128,112},... | collective-permute-start | bytes 73736 | tf_op jit(solution)/shard_map/ppermute | solution.py:589
  11.0 5.8 %collective-permute-start.1 = (f32[2,8,128]{2,1,0:T(8,128)S(1)}, f32[2,8,128]{2,1,0:T(8,128)S(1)}, u32[]{:S(2)}, u32[]{:S(2)}) collective-permute-start(f32[2,8,128]{2,1,0:T(8,128)S(1)} %get-tuple-element.70), channel_id=1, source_target_pairs={{2,0},{4,2},{6,4},{8,6},{10,8},{12,10},{14,12},{0,14},{3,1},{5,3},... | collective-permute-start | bytes 24584 | tf_op jit(solution)/shard_map/ppermute | solution.py:589
  11.5 14.5 %all-to-all-start = ((f32[16,16,128]{2,1,0:T(8,128)}), f32[16,16,128]{2,1,0:T(8,128)S(1)}, u32[]{:S(2)}, u32[]{:S(2)}) async-start(f32[16,16,128]{2,1,0:T(8,128)} %get-tuple-element.78), calls=%async_computation | async-start | bytes 262144 | tf_op jit(solution)/shard_map/all_to_all | solution.py:605
  17.0 11.5 %collective-permute-start.5 = (f32[2,192,128]{2,1,0:T(8,128)S(1)}, f32[2,192,128]{2,1,0:T(8,128)S(1)}, u32[]{:S(2)}, u32[]{:S(2)}) collective-permute-start(f32[2,192,128]{2,1,0:T(8,128)S(1)} %get-tuple-element.75), channel_id=1, source_target_pairs={{0,1},{1,0},{2,3},{3,2},{4,5},{5,4},{6,7},{7,6},{8,9},{9,8},{10,11... | collective-permute-start | bytes 589832 | tf_op jit(solution)/shard_map/ppermute | solution.py:589
  17.1 11.4 %collective-permute-start.3 = (f32[2,24,128]{2,1,0:T(8,128)S(1)}, f32[2,24,128]{2,1,0:T(8,128)S(1)}, u32[]{:S(2)}, u32[]{:S(2)}) collective-permute-start(f32[2,24,128]{2,1,0:T(8,128)S(1)} %get-tuple-element.73), channel_id=1, source_target_pairs={{0,16},{16,32},{32,48},{48,64},{64,80},{80,96},{96,112},{112,128},... | collective-permute-start | bytes 73736 | tf_op jit(solution)/shard_map/ppermute | solution.py:589
  19.9 8.6 %collective-permute-start.4 = (f32[2,8,128]{2,1,0:T(8,128)S(1)}, f32[2,8,128]{2,1,0:T(8,128)S(1)}, u32[]{:S(2)}, u32[]{:S(2)}) collective-permute-start(f32[2,8,128]{2,1,0:T(8,128)S(1)} %get-tuple-element.74), channel_id=1, source_target_pairs={{0,2},{2,4},{4,6},{6,8},{8,10},{10,12},{12,14},{14,0},{1,3},{3,5},... | collective-permute-start | bytes 24584 | tf_op jit(solution)/shard_map/ppermute | solution.py:589
  28.8 6.9 %collective-permute-start.8 = (f32[2,192,128]{2,1,0:T(8,128)S(1)}, f32[2,192,128]{2,1,0:T(8,128)S(1)}, u32[]{:S(2)}, u32[]{:S(2)}) collective-permute-start(f32[2,192,128]{2,1,0:T(8,128)S(1)} %get-tuple-element.83), channel_id=1, source_target_pairs={{1,0},{0,1},{3,2},{2,3},{5,4},{4,5},{7,6},{6,7},{9,8},{8,9},{11,10... | collective-permute-start | bytes 589832 | tf_op jit(solution)/shard_map/ppermute | solution.py:589
  28.9 6.8 %collective-permute-start.6 = (f32[2,24,128]{2,1,0:T(8,128)S(1)}, f32[2,24,128]{2,1,0:T(8,128)S(1)}, u32[]{:S(2)}, u32[]{:S(2)}) collective-permute-start(f32[2,24,128]{2,1,0:T(8,128)S(1)} %get-tuple-element.81), channel_id=1, source_target_pairs={{16,0},{32,16},{48,32},{64,48},{80,64},{96,80},{112,96},{128,112},... | collective-permute-start | bytes 73736 | tf_op jit(solution)/shard_map/ppermute | solution.py:589
  30.1 5.6 %collective-permute-start.7 = (f32[2,8,128]{2,1,0:T(8,128)S(1)}, f32[2,8,128]{2,1,0:T(8,128)S(1)}, u32[]{:S(2)}, u32[]{:S(2)}) collective-permute-start(f32[2,8,128]{2,1,0:T(8,128)S(1)} %get-tuple-element.82), channel_id=1, source_target_pairs={{2,0},{4,2},{6,4},{8,6},{10,8},{12,10},{14,12},{0,14},{3,1},{5,3},... | collective-permute-start | bytes 24584 | tf_op jit(solution)/shard_map/ppermute | solution.py:589
  35.8 8.4 %collective-permute-start.11 = (f32[2,192,128]{2,1,0:T(8,128)S(1)}, f32[2,192,128]{2,1,0:T(8,128)S(1)}, u32[]{:S(2)}, u32[]{:S(2)}) collective-permute-start(f32[2,192,128]{2,1,0:T(8,128)S(1)} %get-tuple-element.95), channel_id=1, source_target_pairs={{0,1},{1,0},{2,3},{3,2},{4,5},{5,4},{6,7},{7,6},{8,9},{9,8},{10,11... | collective-permute-start | bytes 589832 | tf_op jit(solution)/shard_map/ppermute | solution.py:589
  36.1 8.1 %collective-permute-start.9 = (f32[2,24,128]{2,1,0:T(8,128)S(1)}, f32[2,24,128]{2,1,0:T(8,128)S(1)}, u32[]{:S(2)}, u32[]{:S(2)}) collective-permute-start(f32[2,24,128]{2,1,0:T(8,128)S(1)} %get-tuple-element.93), channel_id=1, source_target_pairs={{0,16},{16,32},{32,48},{48,64},{64,80},{80,96},{96,112},{112,128},... | collective-permute-start | bytes 73736 | tf_op jit(solution)/shard_map/ppermute | solution.py:589
  38.0 3.7 %collective-permute-start.10 = (f32[2,8,128]{2,1,0:T(8,128)S(1)}, f32[2,8,128]{2,1,0:T(8,128)S(1)}, u32[]{:S(2)}, u32[]{:S(2)}) collective-permute-start(f32[2,8,128]{2,1,0:T(8,128)S(1)} %get-tuple-element.94), channel_id=1, source_target_pairs={{0,2},{2,4},{4,6},{6,8},{8,10},{10,12},{12,14},{14,0},{1,3},{3,5},... | collective-permute-start | bytes 24584 | tf_op jit(solution)/shard_map/ppermute | solution.py:589
  47.4 1.5 %collective-permute-start.12 = (f32[384,128]{1,0:T(8,128)S(1)}, f32[384,128]{1,0:T(8,128)S(1)}, u32[]{:S(2)}, u32[]{:S(2)}) collective-permute-start(f32[384,128]{1,0:T(8,128)S(1)} %get-tuple-element.107), channel_id=1, source_target_pairs={{1,0},{0,1},{3,2},{2,3},{5,4},{4,5},{7,6},{6,7},{9,8},{8,9},{11,10... | collective-permute-start | bytes 589832 | tf_op jit(solution)/shard_map/ppermute | solution.py:695
  59.4 4.8 %collective-permute-start.13 = (f32[96,128]{1,0:T(8,128)S(1)}, f32[96,128]{1,0:T(8,128)S(1)}, u32[]{:S(2)}, u32[]{:S(2)}) collective-permute-start(f32[96,128]{1,0:T(8,128)S(1)} %get-tuple-element.110), channel_id=1, source_target_pairs={{0,64},{16,80},{32,96},{48,112},{64,0},{80,16},{96,32},{112,48},{1... | collective-permute-start | bytes 147464 | tf_op jit(solution)/shard_map/ppermute | solution.py:702
  59.7 5.7 %collective-permute-start.14 = (f32[96,128]{1,0:T(8,128)S(1)}, f32[96,128]{1,0:T(8,128)S(1)}, u32[]{:S(2)}, u32[]{:S(2)}) collective-permute-start(f32[96,128]{1,0:T(8,128)S(1)} %get-tuple-element.111), channel_id=1, source_target_pairs={{0,128},{16,144},{32,160},{48,176},{64,192},{80,208},{96,224},{112... | collective-permute-start | bytes 147464 | tf_op jit(solution)/shard_map/ppermute | solution.py:702
  62.4 5.3 %collective-permute-start.15 = (f32[96,128]{1,0:T(8,128)S(1)}, f32[96,128]{1,0:T(8,128)S(1)}, u32[]{:S(2)}, u32[]{:S(2)}) collective-permute-start(f32[96,128]{1,0:T(8,128)S(1)} %get-tuple-element.112), channel_id=1, source_target_pairs={{0,192},{16,208},{32,224},{48,240},{64,128},{80,144},{96,160},{112... | collective-permute-start | bytes 147464 | tf_op jit(solution)/shard_map/ppermute | solution.py:702
  67.8 7.4 %collective-permute-start.16 = (f32[96,128]{1,0:T(8,128)S(1)}, f32[96,128]{1,0:T(8,128)S(1)}, u32[]{:S(2)}, u32[]{:S(2)}) collective-permute-start(f32[96,128]{1,0:T(8,128)S(1)} %get-tuple-element.115), channel_id=1, source_target_pairs={{0,16},{16,0},{32,48},{48,32},{64,80},{80,64},{96,112},{112,96},{1... | collective-permute-start | bytes 147464 | tf_op jit(solution)/shard_map/ppermute | solution.py:714
  69.6 8.2 %collective-permute-start.17 = (f32[96,128]{1,0:T(8,128)S(1)}, f32[96,128]{1,0:T(8,128)S(1)}, u32[]{:S(2)}, u32[]{:S(2)}) collective-permute-start(f32[96,128]{1,0:T(8,128)S(1)} %get-tuple-element.116), channel_id=1, source_target_pairs={{0,32},{16,48},{32,0},{48,16},{64,96},{80,112},{96,64},{112,80},{1... | collective-permute-start | bytes 147464 | tf_op jit(solution)/shard_map/ppermute | solution.py:714
  72.4 6.2 %collective-permute-start.18 = (f32[96,128]{1,0:T(8,128)S(1)}, f32[96,128]{1,0:T(8,128)S(1)}, u32[]{:S(2)}, u32[]{:S(2)}) collective-permute-start(f32[96,128]{1,0:T(8,128)S(1)} %get-tuple-element.117), channel_id=1, source_target_pairs={{0,48},{16,32},{32,16},{48,0},{64,112},{80,96},{96,80},{112,64},{1... | collective-permute-start | bytes 147464 | tf_op jit(solution)/shard_map/ppermute | solution.py:714

commit v9 on v8

--- a/solution.py
+++ b/solution.py
@@ -412,13 +412,14 @@
     for step in (1, 2, 3):
         load = loads[step - 1]
         load[0:FAR] = total[...]
-        load[FAR:] = chunk(drives, partner(step)[0]).reshape(LOAD, CZ)
+        load[FAR : FAR + LOAD] = chunk(drives, partner(step)[0]).reshape(LOAD, CZ)
+    loads[1][FAR + LOAD :] = jnp.zeros((8, CZ), F32)
 
 
 def relay_kernel(total_in, drives, one, two, three, total, kept, *loads):
     total[...] = (total_in[...] + one[0:FAR]) + (two[0:FAR] + three[0:FAR])
     held = [chunk(drives, partner(0)[0]).reshape(LOAD, CZ)]
-    held += [arrived[FAR:] for arrived in (one, two, three)]
+    held += [arrived[FAR : FAR + LOAD] for arrived in (one, two, three)]
     for step in range(4):
         target = partner(step)[1]
         out, first = (loads[step - 1], FAR) if step else (kept, 0)
@@ -428,6 +429,7 @@
             tiles = [value[8 * field : 8 * field + 8] for value in held]
             start = first + 8 * field
             out[start : start + 8] = pick(tiles, [(target, source) for source in range(4)])
+    loads[1][FAR + LOAD :] = jnp.zeros((8, CZ), F32)
 
 
 def finish_kernel(total_in, kept, one, two, three, far_ref, spread_out, back):
@@ -435,7 +437,7 @@
     total = far_ref[...] + total
     for peer in range(8):
         spread_out[peer] = total
-    held = [kept[...]] + [arrived[FAR:] for arrived in (one, two, three)]
+    held = [kept[...]] + [arrived[FAR : FAR + LOAD] for arrived in (one, two, three)]
     for source in range(4):
         rows = pl.ds(pl.multiple_of(8 * partner(source)[0], 8), 8)
         for field in range(6):
@@ -694,33 +696,33 @@
     )
     chip = keep + lax.ppermute(send, "gz", down[2])
     pieces = lax.all_to_all(chip.reshape(8, FAR, DIRS), "gy", 0, 0, tiled=True)
-    load = shape(FAR + LOAD, CZ)
-    total, *loads = call(
-        fold_kernel, (shape(FAR, DIRS),) + (load,) * 3, (pieces, drives), name="fold"
-    )
-    loads = [
+    loads = tuple(shape(FAR + LOAD + 8 * (step == 2), CZ) for step in (1, 2, 3))
+    total, *sent = call(
+        fold_kernel, (shape(FAR, DIRS),) + loads, (pieces, drives), name="fold"
+    )
+    got = [
         lax.ppermute(
             value, "gx", [(a * 4 + z, (a ^ k) * 4 + z) for a in range(4) for z in range(4)]
         )
-        for k, value in enumerate(loads, 1)
+        for k, value in enumerate(sent, 1)
     ]
-    total, kept, *loads = call(
+    total, kept, *sent = call(
         relay_kernel,
-        (shape(FAR, DIRS), shape(LOAD, CZ)) + (load,) * 3,
-        (total, drives, *loads),
+        (shape(FAR, DIRS), shape(LOAD, CZ)) + loads,
+        (total, drives, *got),
         name="relay",
     )
-    loads = [
+    got = [
         lax.ppermute(
             value, "gx", [(a * 4 + z, a * 4 + (z ^ k)) for a in range(4) for z in range(4)]
         )
-        for k, value in enumerate(loads, 1)
+        for k, value in enumerate(sent, 1)
     ]
     e_out, h_out = call(store_kernel, (dense, dense), (e_two, h_two), name="store")
     copies, back = call(
         finish_kernel,
         (shape(8, FAR, DIRS), shape(6, SLOTS, CZ)),
-        (total, kept, *loads, far_part),
+        (total, kept, *got, far_part),
         name="finish",
     )
     state_out = call(

time: 90.4 us -> 89.8 us (level)
  transfers between devices with their start and end apart: 20 -> 20, of which waited for: 8 -> 8; matrix products, arithmetic and copies ran while one was open for 0% -> 0% of each run, Pallas kernels for 10% -> 11%
where the time goes in v9:
time: 89.8 us; the launch traced here: 89.5 us
  starting transfers between devices  34.9 us (39%)
  blocking collectives  20.2 us (22%)
  waiting for transfers between devices  16.6 us (18%)
  Pallas kernels  15.6 us (17%)
  between operations  1.48 us (2%)
    ppermute x12, starting transfers between devices, shifted(): lax.ppermute(part, axis, perm)  20.5 us
    pallas_call x14, Pallas kernels, call(): pl.pallas_call(kernel, out_shape=outs, in_specs=in_specs or [pl.BlockSpec...  15.6 us
    all_to_all x1, blocking collectives, local(): pieces = lax.all_to_all(chip.reshape(8, FAR, DIRS), 'gy', 0, 0, tiled=True)  10.4 us
    all_to_all x1, blocking collectives, local(): gathered = lax.all_to_all(copies, 'gy', 0, 0, tiled=True)  9.86 us
    ppermute x3, starting transfers between devices, local(): lax.ppermute(value, 'gx', [(a * 4 + z, a * 4 + (z ^ k)) for a in range(4)...  6.58 us
    all_to_all x1, waiting for transfers between devices, local(): fields = lax.all_to_all(packed, 'gx', 0, 0, tiled=True)  4.54 us
    ppermute x3, starting transfers between devices, local(): lax.ppermute(value, 'gx', [(a * 4 + z, (a ^ k) * 4 + z) for a in range(4)...  4.18 us
    ppermute x3, waiting for transfers between devices, local(): lax.ppermute(value, 'gx', [(a * 4 + z, (a ^ k) * 4 + z) for a in range(4)...  3.59 us
  transfers between devices with their start and end apart: 20, of which 8 were waited for; matrix products, arithmetic and copies ran while one was open for 0% of the time, Pallas kernels for 11%

profile of v9, /device:TPU:8, one launch (start us, length us, event | category | flops | bytes accessed | tf_op | source)
XLA Modules:
  0.0 89.5 jit_solution(12943970253004373281)
XLA Ops:
  0.6 1.7 %prepare.1 = (f32[2,24,128]{2,1,0:T(8,128)S(1)}, f32[2,8,128]{2,1,0:T(8,128)S(1)}, f32[2,192,128]{2,1,0:T(8,128)S(1)}, f32[16,16,128]{2,1,0:T(8,128)}, f32[3,192...) custom-call(f32[3,192,128]{2,1,0:T(8,128)} %bitcast.26, f32[10,32,128]{2,1,0:T(8,128)} %bitcast.29), custom_call_target="tpu_custom_call" | custom-call | bytes 2097152 | tf_op jit(solution)/shard_map/prepare/pallas_call | solution.py:47
  2.5 8.6 %collective-permute-start = (f32[2,24,128]{2,1,0:T(8,128)S(1)}, f32[2,24,128]{2,1,0:T(8,128)S(1)}, u32[]{:S(2)}, u32[]{:S(2)}) collective-permute-start(f32[2,24,128]{2,1,0:T(8,128)S(1)} %get-tuple-element.69), channel_id=1, source_target_pairs={{16,0},{32,16},{48,32},{64,48},{80,64},{96,80},{112,96},{128,112},... | collective-permute-start | bytes 73736 | tf_op jit(solution)/shard_map/ppermute | solution.py:591
  11.5 3.5 %all-to-all-start = ((f32[16,16,128]{2,1,0:T(8,128)}), f32[16,16,128]{2,1,0:T(8,128)S(1)}, u32[]{:S(2)}, u32[]{:S(2)}) async-start(f32[16,16,128]{2,1,0:T(8,128)} %get-tuple-element.78), calls=%async_computation | async-start | bytes 262144 | tf_op jit(solution)/shard_map/all_to_all | solution.py:607
  15.7 1.2 %phase.1 = (s32[32,128]{1,0:T(8,128)S(1)}, s32[1,128]{1,0:T(1,128)S(1)}, f32[4,128,128]{2,1,0:T(8,128)S(1)}, f32[2,128,128]{2,1,0:T(8,128)S(1)}, f32[2,128,128]{...) custom-call(s32[1]{0:T(128)} %bitcast.23.count_ref, ...), custom_call_target="tpu_custom_call" | custom-call | bytes 262144 | tf_op jit(solution)/shard_map/phase/pallas_call | solution.py:47
  17.1 2.8 %collective-permute-start.3 = (f32[2,24,128]{2,1,0:T(8,128)S(1)}, f32[2,24,128]{2,1,0:T(8,128)S(1)}, u32[]{:S(2)}, u32[]{:S(2)}) collective-permute-start(f32[2,24,128]{2,1,0:T(8,128)S(1)} %get-tuple-element.73), channel_id=1, source_target_pairs={{0,16},{16,32},{32,48},{48,64},{64,80},{80,96},{96,112},{112,128},... | collective-permute-start | bytes 73736 | tf_op jit(solution)/shard_map/ppermute | solution.py:591
  19.9 1.6 %collective-permute-start.4 = (f32[2,8,128]{2,1,0:T(8,128)S(1)}, f32[2,8,128]{2,1,0:T(8,128)S(1)}, u32[]{:S(2)}, u32[]{:S(2)}) collective-permute-start(f32[2,8,128]{2,1,0:T(8,128)S(1)} %get-tuple-element.74), channel_id=1, source_target_pairs={{0,2},{2,4},{4,6},{6,8},{8,10},{10,12},{12,14},{14,0},{1,3},{3,5},... | collective-permute-start | bytes 24584 | tf_op jit(solution)/shard_map/ppermute | solution.py:591
  21.5 4.5 %all-to-all-done.fields_ref = f32[16,16,128]{2,1,0:T(8,128)S(1)} async-done(((f32[16,16,128]{2,1,0:T(8,128)}), f32[16,16,128]{2,1,0:T(8,128)S(1)}, u32[]{:S(2)}, u32[]{:S(2)}) %all-to-all-start) | async-done | bytes 131104 | tf_op jit(solution)/shard_map/all_to_all | solution.py:607
  26.0 2.5 %scatter.1 = (f32[4,192,128]{2,1,0:T(8,128)S(1)}, bf16[96,4096]{1,0:T(8,128)(2,1)S(1)}, bf16[256,4096]{1,0:T(8,128)(2,1)S(1)}) custom-call(s32[32,128]{1,0:T(8,128)S(1)} %get-tuple-element.77.placed, f32[16,16,128]{2,1,0:T(8,128)S(1)} %all-to-all-done.fields_ref), custom_call_target="tpu_custom_call" | custom-call | bytes 2097152 | tf_op jit(solution)/shard_map/scatter/pallas_call | solution.py:47
  28.9 1.2 %collective-permute-start.6 = (f32[2,24,128]{2,1,0:T(8,128)S(1)}, f32[2,24,128]{2,1,0:T(8,128)S(1)}, u32[]{:S(2)}, u32[]{:S(2)}) collective-permute-start(f32[2,24,128]{2,1,0:T(8,128)S(1)} %get-tuple-element.81), channel_id=1, source_target_pairs={{16,0},{32,16},{48,32},{64,48},{80,64},{96,80},{112,96},{128,112},... | collective-permute-start | bytes 73736 | tf_op jit(solution)/shard_map/ppermute | solution.py:591
  30.1 3.5 %collective-permute-start.7 = (f32[2,8,128]{2,1,0:T(8,128)S(1)}, f32[2,8,128]{2,1,0:T(8,128)S(1)}, u32[]{:S(2)}, u32[]{:S(2)}) collective-permute-start(f32[2,8,128]{2,1,0:T(8,128)S(1)} %get-tuple-element.82), channel_id=1, source_target_pairs={{2,0},{4,2},{6,4},{8,6},{10,8},{12,10},{14,12},{0,14},{3,1},{5,3},... | collective-permute-start | bytes 24584 | tf_op jit(solution)/shard_map/ppermute | solution.py:591
  33.6 2.1 %scatter2.1 = (f32[4,192,128]{2,1,0:T(8,128)S(1)}, f32[8,128]{1,0:T(8,128)S(1)}) custom-call(f32[16,16,128]{2,1,0:T(8,128)S(1)} %all-to-all-done.fields_ref, bf16[96,4096]{1,0:T(8,128)(2,1)S(1)} %get-tuple-element.84.tall, bf16[256,4096]{1,0:T(8,128)(2,1)S(1)} %get-tuple-element.85.columns, f32[3,192,128]{2,1,0:T(8,128)S(1)} %get-tuple-element.96.e_ref.e_new, ...), custom_call_target="tpu_custom_call" | custom-call | bytes 2097152 | tf_op jit(solution)/shard_map/scatter2/pallas_call | solution.py:47
  36.1 1.9 %collective-permute-start.9 = (f32[2,24,128]{2,1,0:T(8,128)S(1)}, f32[2,24,128]{2,1,0:T(8,128)S(1)}, u32[]{:S(2)}, u32[]{:S(2)}) collective-permute-start(f32[2,24,128]{2,1,0:T(8,128)S(1)} %get-tuple-element.93), channel_id=1, source_target_pairs={{0,16},{16,32},{32,48},{48,64},{64,80},{80,96},{96,112},{112,128},... | collective-permute-start | bytes 73736 | tf_op jit(solution)/shard_map/ppermute | solution.py:591
  38.0 2.7 %drive.1.drives = f32[6,32,128]{2,1,0:T(8,128)S(1)} custom-call(f32[3,192,128]{2,1,0:T(8,128)S(1)} %get-tuple-element.67.e_ref.e_old, f32[3,192,128]{2,1,0:T(8,128)S(1)} %get-tuple-element.96.e_ref.e_new, s32[32,128]{1,0:T(8,128)S(1)} %get-tuple-element.77.placed, bf16[256,4096]{1,0:T(8,128)(2,1)S(1)} %get-tuple-element.85.columns), custom_call_target="tpu_custom_call" | custom-call | bytes 2097152 | tf_op jit(solution)/shard_map/drive/pallas_call | solution.py:47
  40.7 0.9 collective-permute-done.10.face_y
  41.6 2.6 %collective-permute-done.9.face_x = f32[2,24,128]{2,1,0:T(8,128)S(1)} collective-permute-done((f32[2,24,128]{2,1,0:T(8,128)S(1)}, f32[2,24,128]{2,1,0:T(8,128)S(1)}, u32[]{:S(2)}, u32[]{:S(2)}) %collective-permute-start.9) | collective-permute-done | bytes 24608 | tf_op jit(solution)/shard_map/ppermute | solution.py:591
  44.2 3.2 %final.1 = (f32[3,192,128]{2,1,0:T(8,128)S(1)}, f32[384,128]{1,0:T(8,128)S(1)}, f32[384,128]{1,0:T(8,128)S(1)}) custom-call(f32[3,192,128]{2,1,0:T(8,128)S(1)} %get-tuple-element.96.e_ref.e_new, f32[3,192,128]{2,1,0:T(8,128)S(1)} %get-tuple-element.92.h_ref, f32[2,24,128]{2,1,0:T(8,128)S(1)} %collective-permute-done.9.face_x, ...), custom_call_target="tpu_custom_call" | custom-call | bytes 2097152 | tf_op jit(solution)/shard_map/final/pallas_call | solution.py:47
  47.5 1.4 %collective-permute-done.12 = f32[384,128]{1,0:T(8,128)S(1)} collective-permute-done((f32[384,128]{1,0:T(8,128)S(1)}, f32[384,128]{1,0:T(8,128)S(1)}, u32[]{:S(2)}, u32[]{:S(2)}) %collective-permute-start.12) | collective-permute-done | bytes 196640 | tf_op jit(solution)/shard_map/ppermute | solution.py:697
  49.0 10.4 %all_to_all.15.pieces = f32[8,48,128]{2,1,0:T(8,128)S(1)} all-to-all(f32[8,48,128]{2,1,0:T(8,128)S(1)} %bitcast.25), channel_id=1, replica_groups=mesh['gx'=16,'gy'=8,'gz'=2] {'gy'}, dimensions={0} | all-to-all | bytes 393216 | tf_op jit(solution)/shard_map/all_to_all | solution.py:698
  59.4 1.9 %collective-permute-start.14 = (f32[104,128]{1,0:T(8,128)S(1)}, f32[104,128]{1,0:T(8,128)S(1)}, u32[]{:S(2)}, u32[]{:S(2)}) collective-permute-start(f32[104,128]{1,0:T(8,128)S(1)} %get-tuple-element.111), channel_id=1, source_target_pairs={{0,128},{16,144},{32,160},{48,176},{64,192},{80,208},{96,224},{112... | collective-permute-start | bytes 159752 | tf_op jit(solution)/shard_map/ppermute | solution.py:704
  61.2 0.6 collective-permute-start.13
  61.8 1.7 %collective-permute-start.15 = (f32[96,128]{1,0:T(8,128)S(1)}, f32[96,128]{1,0:T(8,128)S(1)}, u32[]{:S(2)}, u32[]{:S(2)}) collective-permute-start(f32[96,128]{1,0:T(8,128)S(1)} %get-tuple-element.112), channel_id=1, source_target_pairs={{0,192},{16,208},{32,224},{48,240},{64,128},{80,144},{96,160},{112... | collective-permute-start | bytes 147464 | tf_op jit(solution)/shard_map/ppermute | solution.py:704
  63.5 1.8 %collective-permute-done.13.one = f32[96,128]{1,0:T(8,128)S(1)} collective-permute-done((f32[96,128]{1,0:T(8,128)S(1)}, f32[96,128]{1,0:T(8,128)S(1)}, u32[]{:S(2)}, u32[]{:S(2)}) %collective-permute-start.13) | collective-permute-done | bytes 49184 | tf_op jit(solution)/shard_map/ppermute | solution.py:704
  65.3 1.8 %collective-permute-done.15.three = f32[96,128]{1,0:T(8,128)S(1)} collective-permute-done((f32[96,128]{1,0:T(8,128)S(1)}, f32[96,128]{1,0:T(8,128)S(1)}, u32[]{:S(2)}, u32[]{:S(2)}) %collective-permute-start.15) | collective-permute-done | bytes 49184 | tf_op jit(solution)/shard_map/ppermute | solution.py:704
  67.2 3.0 %collective-permute-start.17 = (f32[104,128]{1,0:T(8,128)S(1)}, f32[104,128]{1,0:T(8,128)S(1)}, u32[]{:S(2)}, u32[]{:S(2)}) collective-permute-start(f32[104,128]{1,0:T(8,128)S(1)} %get-tuple-element.116), channel_id=1, source_target_pairs={{0,32},{16,48},{32,0},{48,16},{64,96},{80,112},{96,64},{112,80},{1... | collective-permute-start | bytes 159752 | tf_op jit(solution)/shard_map/ppermute | solution.py:716
  70.2 1.7 %collective-permute-start.16 = (f32[96,128]{1,0:T(8,128)S(1)}, f32[96,128]{1,0:T(8,128)S(1)}, u32[]{:S(2)}, u32[]{:S(2)}) collective-permute-start(f32[96,128]{1,0:T(8,128)S(1)} %get-tuple-element.115), channel_id=1, source_target_pairs={{0,16},{16,0},{32,48},{48,32},{64,80},{80,64},{96,112},{112,96},{1... | collective-permute-start | bytes 147464 | tf_op jit(solution)/shard_map/ppermute | solution.py:716
  71.8 1.9 %collective-permute-start.18 = (f32[96,128]{1,0:T(8,128)S(1)}, f32[96,128]{1,0:T(8,128)S(1)}, u32[]{:S(2)}, u32[]{:S(2)}) collective-permute-start(f32[96,128]{1,0:T(8,128)S(1)} %get-tuple-element.117), channel_id=1, source_target_pairs={{0,48},{16,32},{32,16},{48,0},{64,112},{80,96},{96,80},{112,64},{1... | collective-permute-start | bytes 147464 | tf_op jit(solution)/shard_map/ppermute | solution.py:716
  73.8 0.8 store.1
  74.6 2.0 %collective-permute-done.16.one = f32[96,128]{1,0:T(8,128)S(1)} collective-permute-done((f32[96,128]{1,0:T(8,128)S(1)}, f32[96,128]{1,0:T(8,128)S(1)}, u32[]{:S(2)}, u32[]{:S(2)}) %collective-permute-start.16) | collective-permute-done | bytes 49184 | tf_op jit(solution)/shard_map/ppermute | solution.py:716
  76.6 1.5 %collective-permute-done.18.three = f32[96,128]{1,0:T(8,128)S(1)} collective-permute-done((f32[96,128]{1,0:T(8,128)S(1)}, f32[96,128]{1,0:T(8,128)S(1)}, u32[]{:S(2)}, u32[]{:S(2)}) %collective-permute-start.18) | collective-permute-done | bytes 49184 | tf_op jit(solution)/shard_map/ppermute | solution.py:716
  78.2 0.7 atoms.1
  78.9 9.9 %all_to_all.16 = f32[8,48,128]{2,1,0:T(8,128)S(1)} all-to-all(f32[8,48,128]{2,1,0:T(8,128)S(1)} %get-tuple-element.129), channel_id=1, replica_groups=mesh['gx'=16,'gy'=8,'gz'=2] {'gy'}, dimensions={0} | all-to-all | bytes 393216 | tf_op jit(solution)/shard_map/all_to_all | solution.py:735
  88.8 0.7 copy.17
  (26 shorter events, 1.8 us)
Async XLA Ops:
  2.4 14.5 %collective-permute-start.2 = (f32[2,192,128]{2,1,0:T(8,128)S(1)}, f32[2,192,128]{2,1,0:T(8,128)S(1)}, u32[]{:S(2)}, u32[]{:S(2)}) collective-permute-start(f32[2,192,128]{2,1,0:T(8,128)S(1)} %get-tuple-element.71), channel_id=1, source_target_pairs={{1,0},{0,1},{3,2},{2,3},{5,4},{4,5},{7,6},{6,7},{9,8},{8,9},{11,10... | collective-permute-start | bytes 589832 | tf_op jit(solution)/shard_map/ppermute | solution.py:591
  2.5 14.4 %collective-permute-start = (f32[2,24,128]{2,1,0:T(8,128)S(1)}, f32[2,24,128]{2,1,0:T(8,128)S(1)}, u32[]{:S(2)}, u32[]{:S(2)}) collective-permute-start(f32[2,24,128]{2,1,0:T(8,128)S(1)} %get-tuple-element.69), channel_id=1, source_target_pairs={{16,0},{32,16},{48,32},{64,48},{80,64},{96,80},{112,96},{128,112},... | collective-permute-start | bytes 73736 | tf_op jit(solution)/shard_map/ppermute | solution.py:591
  11.0 5.8 %collective-permute-start.1 = (f32[2,8,128]{2,1,0:T(8,128)S(1)}, f32[2,8,128]{2,1,0:T(8,128)S(1)}, u32[]{:S(2)}, u32[]{:S(2)}) collective-permute-start(f32[2,8,128]{2,1,0:T(8,128)S(1)} %get-tuple-element.70), channel_id=1, source_target_pairs={{2,0},{4,2},{6,4},{8,6},{10,8},{12,10},{14,12},{0,14},{3,1},{5,3},... | collective-permute-start | bytes 24584 | tf_op jit(solution)/shard_map/ppermute | solution.py:591
  11.5 14.5 %all-to-all-start = ((f32[16,16,128]{2,1,0:T(8,128)}), f32[16,16,128]{2,1,0:T(8,128)S(1)}, u32[]{:S(2)}, u32[]{:S(2)}) async-start(f32[16,16,128]{2,1,0:T(8,128)} %get-tuple-element.78), calls=%async_computation | async-start | bytes 262144 | tf_op jit(solution)/shard_map/all_to_all | solution.py:607
  17.0 11.5 %collective-permute-start.5 = (f32[2,192,128]{2,1,0:T(8,128)S(1)}, f32[2,192,128]{2,1,0:T(8,128)S(1)}, u32[]{:S(2)}, u32[]{:S(2)}) collective-permute-start(f32[2,192,128]{2,1,0:T(8,128)S(1)} %get-tuple-element.75), channel_id=1, source_target_pairs={{0,1},{1,0},{2,3},{3,2},{4,5},{5,4},{6,7},{7,6},{8,9},{9,8},{10,11... | collective-permute-start | bytes 589832 | tf_op jit(solution)/shard_map/ppermute | solution.py:591
  17.1 11.4 %collective-permute-start.3 = (f32[2,24,128]{2,1,0:T(8,128)S(1)}, f32[2,24,128]{2,1,0:T(8,128)S(1)}, u32[]{:S(2)}, u32[]{:S(2)}) collective-permute-start(f32[2,24,128]{2,1,0:T(8,128)S(1)} %get-tuple-element.73), channel_id=1, source_target_pairs={{0,16},{16,32},{32,48},{48,64},{64,80},{80,96},{96,112},{112,128},... | collective-permute-start | bytes 73736 | tf_op jit(solution)/shard_map/ppermute | solution.py:591
  19.9 8.6 %collective-permute-start.4 = (f32[2,8,128]{2,1,0:T(8,128)S(1)}, f32[2,8,128]{2,1,0:T(8,128)S(1)}, u32[]{:S(2)}, u32[]{:S(2)}) collective-permute-start(f32[2,8,128]{2,1,0:T(8,128)S(1)} %get-tuple-element.74), channel_id=1, source_target_pairs={{0,2},{2,4},{4,6},{6,8},{8,10},{10,12},{12,14},{14,0},{1,3},{3,5},... | collective-permute-start | bytes 24584 | tf_op jit(solution)/shard_map/ppermute | solution.py:591
  28.8 6.9 %collective-permute-start.8 = (f32[2,192,128]{2,1,0:T(8,128)S(1)}, f32[2,192,128]{2,1,0:T(8,128)S(1)}, u32[]{:S(2)}, u32[]{:S(2)}) collective-permute-start(f32[2,192,128]{2,1,0:T(8,128)S(1)} %get-tuple-element.83), channel_id=1, source_target_pairs={{1,0},{0,1},{3,2},{2,3},{5,4},{4,5},{7,6},{6,7},{9,8},{8,9},{11,10... | collective-permute-start | bytes 589832 | tf_op jit(solution)/shard_map/ppermute | solution.py:591
  28.9 6.8 %collective-permute-start.6 = (f32[2,24,128]{2,1,0:T(8,128)S(1)}, f32[2,24,128]{2,1,0:T(8,128)S(1)}, u32[]{:S(2)}, u32[]{:S(2)}) collective-permute-start(f32[2,24,128]{2,1,0:T(8,128)S(1)} %get-tuple-element.81), channel_id=1, source_target_pairs={{16,0},{32,16},{48,32},{64,48},{80,64},{96,80},{112,96},{128,112},... | collective-permute-start | bytes 73736 | tf_op jit(solution)/shard_map/ppermute | solution.py:591
  30.1 5.6 %collective-permute-start.7 = (f32[2,8,128]{2,1,0:T(8,128)S(1)}, f32[2,8,128]{2,1,0:T(8,128)S(1)}, u32[]{:S(2)}, u32[]{:S(2)}) collective-permute-start(f32[2,8,128]{2,1,0:T(8,128)S(1)} %get-tuple-element.82), channel_id=1, source_target_pairs={{2,0},{4,2},{6,4},{8,6},{10,8},{12,10},{14,12},{0,14},{3,1},{5,3},... | collective-permute-start | bytes 24584 | tf_op jit(solution)/shard_map/ppermute | solution.py:591
  35.8 8.4 %collective-permute-start.11 = (f32[2,192,128]{2,1,0:T(8,128)S(1)}, f32[2,192,128]{2,1,0:T(8,128)S(1)}, u32[]{:S(2)}, u32[]{:S(2)}) collective-permute-start(f32[2,192,128]{2,1,0:T(8,128)S(1)} %get-tuple-element.95), channel_id=1, source_target_pairs={{0,1},{1,0},{2,3},{3,2},{4,5},{5,4},{6,7},{7,6},{8,9},{9,8},{10,11... | collective-permute-start | bytes 589832 | tf_op jit(solution)/shard_map/ppermute | solution.py:591
  36.1 8.1 %collective-permute-start.9 = (f32[2,24,128]{2,1,0:T(8,128)S(1)}, f32[2,24,128]{2,1,0:T(8,128)S(1)}, u32[]{:S(2)}, u32[]{:S(2)}) collective-permute-start(f32[2,24,128]{2,1,0:T(8,128)S(1)} %get-tuple-element.93), channel_id=1, source_target_pairs={{0,16},{16,32},{32,48},{48,64},{64,80},{80,96},{96,112},{112,128},... | collective-permute-start | bytes 73736 | tf_op jit(solution)/shard_map/ppermute | solution.py:591
  38.0 3.7 %collective-permute-start.10 = (f32[2,8,128]{2,1,0:T(8,128)S(1)}, f32[2,8,128]{2,1,0:T(8,128)S(1)}, u32[]{:S(2)}, u32[]{:S(2)}) collective-permute-start(f32[2,8,128]{2,1,0:T(8,128)S(1)} %get-tuple-element.94), channel_id=1, source_target_pairs={{0,2},{2,4},{4,6},{6,8},{8,10},{10,12},{12,14},{14,0},{1,3},{3,5},... | collective-permute-start | bytes 24584 | tf_op jit(solution)/shard_map/ppermute | solution.py:591
  47.4 1.5 %collective-permute-start.12 = (f32[384,128]{1,0:T(8,128)S(1)}, f32[384,128]{1,0:T(8,128)S(1)}, u32[]{:S(2)}, u32[]{:S(2)}) collective-permute-start(f32[384,128]{1,0:T(8,128)S(1)} %get-tuple-element.107), channel_id=1, source_target_pairs={{1,0},{0,1},{3,2},{2,3},{5,4},{4,5},{7,6},{6,7},{9,8},{8,9},{11,10... | collective-permute-start | bytes 589832 | tf_op jit(solution)/shard_map/ppermute | solution.py:697
  59.4 7.8 %collective-permute-start.14 = (f32[104,128]{1,0:T(8,128)S(1)}, f32[104,128]{1,0:T(8,128)S(1)}, u32[]{:S(2)}, u32[]{:S(2)}) collective-permute-start(f32[104,128]{1,0:T(8,128)S(1)} %get-tuple-element.111), channel_id=1, source_target_pairs={{0,128},{16,144},{32,160},{48,176},{64,192},{80,208},{96,224},{112... | collective-permute-start | bytes 159752 | tf_op jit(solution)/shard_map/ppermute | solution.py:704
  61.2 4.1 %collective-permute-start.13 = (f32[96,128]{1,0:T(8,128)S(1)}, f32[96,128]{1,0:T(8,128)S(1)}, u32[]{:S(2)}, u32[]{:S(2)}) collective-permute-start(f32[96,128]{1,0:T(8,128)S(1)} %get-tuple-element.110), channel_id=1, source_target_pairs={{0,64},{16,80},{32,96},{48,112},{64,0},{80,16},{96,32},{112,48},{1... | collective-permute-start | bytes 147464 | tf_op jit(solution)/shard_map/ppermute | solution.py:704
  61.8 5.3 %collective-permute-start.15 = (f32[96,128]{1,0:T(8,128)S(1)}, f32[96,128]{1,0:T(8,128)S(1)}, u32[]{:S(2)}, u32[]{:S(2)}) collective-permute-start(f32[96,128]{1,0:T(8,128)S(1)} %get-tuple-element.112), channel_id=1, source_target_pairs={{0,192},{16,208},{32,224},{48,240},{64,128},{80,144},{96,160},{112... | collective-permute-start | bytes 147464 | tf_op jit(solution)/shard_map/ppermute | solution.py:704
  67.2 10.9 %collective-permute-start.17 = (f32[104,128]{1,0:T(8,128)S(1)}, f32[104,128]{1,0:T(8,128)S(1)}, u32[]{:S(2)}, u32[]{:S(2)}) collective-permute-start(f32[104,128]{1,0:T(8,128)S(1)} %get-tuple-element.116), channel_id=1, source_target_pairs={{0,32},{16,48},{32,0},{48,16},{64,96},{80,112},{96,64},{112,80},{1... | collective-permute-start | bytes 159752 | tf_op jit(solution)/shard_map/ppermute | solution.py:716
  70.2 6.5 %collective-permute-start.16 = (f32[96,128]{1,0:T(8,128)S(1)}, f32[96,128]{1,0:T(8,128)S(1)}, u32[]{:S(2)}, u32[]{:S(2)}) collective-permute-start(f32[96,128]{1,0:T(8,128)S(1)} %get-tuple-element.115), channel_id=1, source_target_pairs={{0,16},{16,0},{32,48},{48,32},{64,80},{80,64},{96,112},{112,96},{1... | collective-permute-start | bytes 147464 | tf_op jit(solution)/shard_map/ppermute | solution.py:716
  71.8 6.3 %collective-permute-start.18 = (f32[96,128]{1,0:T(8,128)S(1)}, f32[96,128]{1,0:T(8,128)S(1)}, u32[]{:S(2)}, u32[]{:S(2)}) collective-permute-start(f32[96,128]{1,0:T(8,128)S(1)} %get-tuple-element.117), channel_id=1, source_target_pairs={{0,48},{16,32},{32,16},{48,0},{64,112},{80,96},{96,80},{112,64},{1... | collective-permute-start | bytes 147464 | tf_op jit(solution)/shard_map/ppermute | solution.py:716

commit v10 on v9

--- a/solution.py
+++ b/solution.py
@@ -460,7 +460,7 @@
     turn,
     factors,
     e_out,
-    keep_out,
+    left_out,
     send_out,
     late,
     now,
@@ -483,40 +483,48 @@
         ],
         axis=0,
     )
-    own = lax.axis_index("gz")
-    for side, out in ((1, send_out), (0, keep_out)):
-        target = lax.rem(own + side, 2)
-        now[0] = starts[2 * target]
-        now[1] = starts[2 * target + 1]
-        for freq in range(FREQ // 2):
-            here = (now[0], now[1])
-            re_high, re_low = split_parts(here[0])
-            im_high, im_low = split_parts(here[1])
-            right = jnp.concatenate(
-                [
-                    jnp.concatenate([re_high, im_high], axis=1),
-                    jnp.concatenate([re_low, im_low], axis=1),
-                ],
-                axis=0,
-            )
+    left_out[...] = left
+    far_half(1, left, starts, turn, factors, send_out, now)
+
+
+def keep_kernel(left, starts, turn, factors, keep_out, now):
+    far_half(0, left[...], starts, turn, factors, keep_out, now)
+
+
+def far_half(side, left, starts, turn, factors, out, now):
+    target = lax.rem(lax.axis_index("gz") + side, 2)
+    now[0] = starts[2 * target]
+    now[1] = starts[2 * target + 1]
+    for freq in range(FREQ // 2):
+        here = (now[0], now[1])
+        re_high, re_low = split_parts(here[0])
+        im_high, im_low = split_parts(here[1])
+        right = jnp.concatenate(
+            [
+                jnp.concatenate([re_high, im_high], axis=1),
+                jnp.concatenate([re_low, im_low], axis=1),
+            ],
+            axis=0,
+        )
+        if freq < FREQ // 2 - 1:
             now[0], now[1] = times(here, (turn[0], turn[1]))
-            both = jnp.dot(left, right, preferred_element_type=F32)
-            both = both[0:16] + both[16:32]
-            real = jnp.zeros((8, DIRS), F32)
-            imag = jnp.zeros((8, DIRS), F32)
-            for step in range(STEPS):
-                row = pl.ds(step * FREQ + target * (FREQ // 2) + freq, 1)
-                cosine = factors[0, row]
-                sine = factors[1, row]
-                upper = both[8 * step : 8 * step + 8, 0:DIRS]
-                under = both[8 * step : 8 * step + 8, DIRS:]
-                real = real + (cosine * upper + sine * under)
-                imag = imag + (cosine * under - sine * upper)
-            for comp in range(6):
-                row = comp * (FREQ // 2) + freq
-                out[row : row + 1] = real[comp : comp + 1]
-                row = (comp + 6) * (FREQ // 2) + freq
-                out[row : row + 1] = imag[comp : comp + 1]
+        both = jnp.dot(left, right, preferred_element_type=F32)
+        both = both[0:16] + both[16:32]
+        real = jnp.zeros((8, DIRS), F32)
+        imag = jnp.zeros((8, DIRS), F32)
+        for step in range(STEPS):
+            row = pl.ds(step * FREQ + target * (FREQ // 2) + freq, 1)
+            cosine = factors[0, row]
+            sine = factors[1, row]
+            upper = both[8 * step : 8 * step + 8, 0:DIRS]
+            under = both[8 * step : 8 * step + 8, DIRS:]
+            real = real + (cosine * upper + sine * under)
+            imag = imag + (cosine * under - sine * upper)
+        for comp in range(6):
+            row = comp * (FREQ // 2) + freq
+            out[row : row + 1] = real[comp : comp + 1]
+            row = (comp + 6) * (FREQ // 2) + freq
+            out[row : row + 1] = imag[comp : comp + 1]
 
 
 def atoms_kernel(state_ref, pump_ref, drives, out):
@@ -687,14 +695,19 @@
     )
     *edge, drives = lax.optimization_barrier((*edge, drives))
     part = shape(12 * FREQ // 2, DIRS)
-    e_two, keep, send = call(
+    hold = pltpu.VMEM((2, CZ, DIRS), F32)
+    e_two, left, send = call(
         final_kernel,
-        (dense, part, part),
+        (dense, shape(32, 2 * CZ, dtype=BF16), part),
         (e_one, h_two, *edge, eps, rates, spread_next, surf, early, starts, turn, factors),
-        scratch=[pltpu.VMEM((8, CZ), F32), pltpu.VMEM((2, CZ, DIRS), F32)],
+        scratch=[pltpu.VMEM((8, CZ), F32), hold],
         name="final",
     )
-    chip = keep + lax.ppermute(send, "gz", down[2])
+    send = lax.ppermute(send, "gz", down[2])
+    keep = call(
+        keep_kernel, part, (left, starts, turn, factors), scratch=[hold], flops=10**10, name="keep"
+    )
+    chip = keep + send
     pieces = lax.all_to_all(chip.reshape(8, FAR, DIRS), "gy", 0, 0, tiled=True)
     loads = tuple(shape(FAR + LOAD + 8 * (step == 2), CZ) for step in (1, 2, 3))
     total, *sent = call(

time: 89.8 us -> 88.6 us (0.987)
  waiting for transfers between devices: 16.6 us -> 15.5 us
    ppermute x1, waiting for transfers between devices: 1.43 us -> 0.27 us  [local(): send = lax.ppermute(send, 'gz', down[2])]
    pallas_call x14 -> x15, Pallas kernels: 15.6 us -> 15.5 us  [call(): pl.pallas_call(kernel, out_shape=outs, in_specs=in_specs or [pl.BlockSpec...]
  transfers between devices with their start and end apart: 20 -> 20, of which waited for: 8 -> 8; matrix products, arithmetic and copies ran while one was open for 0% -> 0% of each run, Pallas kernels for 11% -> 12%
where the time goes in v10:
time: 88.6 us; the launch traced here: 88.4 us
  starting transfers between devices  34.9 us (39%)
  blocking collectives  20.3 us (23%)
  Pallas kernels  15.5 us (17%)
  waiting for transfers between devices  15.5 us (17%)
  between operations  1.49 us (2%)
    ppermute x12, starting transfers between devices, shifted(): lax.ppermute(part, axis, perm)  20.5 us
    pallas_call x15, Pallas kernels, call(): pl.pallas_call(kernel, out_shape=outs, in_specs=in_specs or [pl.BlockSpec...  15.5 us
    all_to_all x1, blocking collectives, local(): pieces = lax.all_to_all(chip.reshape(8, FAR, DIRS), 'gy', 0, 0, tiled=True)  10.4 us
    all_to_all x1, blocking collectives, local(): gathered = lax.all_to_all(copies, 'gy', 0, 0, tiled=True)  9.86 us
    ppermute x3, starting transfers between devices, local(): lax.ppermute(value, 'gx', [(a * 4 + z, a * 4 + (z ^ k)) for a in range(4)...  6.58 us
    all_to_all x1, waiting for transfers between devices, local(): fields = lax.all_to_all(packed, 'gx', 0, 0, tiled=True)  4.54 us
    ppermute x3, starting transfers between devices, local(): lax.ppermute(value, 'gx', [(a * 4 + z, (a ^ k) * 4 + z) for a in range(4)...  4.18 us
    ppermute x3, waiting for transfers between devices, local(): lax.ppermute(value, 'gx', [(a * 4 + z, (a ^ k) * 4 + z) for a in range(4)...  3.65 us
  transfers between devices with their start and end apart: 20, of which 8 were waited for; matrix products, arithmetic and copies ran while one was open for 0% of the time, Pallas kernels for 12%

profile of v10, /device:TPU:8, one launch (start us, length us, event | category | flops | bytes accessed | tf_op | source)
XLA Modules:
  0.0 88.4 jit_solution(12121592108455107615)
XLA Ops:
  0.6 1.7 %prepare.1 = (f32[2,24,128]{2,1,0:T(8,128)S(1)}, f32[2,8,128]{2,1,0:T(8,128)S(1)}, f32[2,192,128]{2,1,0:T(8,128)S(1)}, f32[16,16,128]{2,1,0:T(8,128)}, f32[3,192...) custom-call(f32[3,192,128]{2,1,0:T(8,128)} %bitcast.26, f32[10,32,128]{2,1,0:T(8,128)} %bitcast.29), custom_call_target="tpu_custom_call" | custom-call | bytes 2097152 | tf_op jit(solution)/shard_map/prepare/pallas_call | solution.py:47
  2.5 8.6 %collective-permute-start = (f32[2,24,128]{2,1,0:T(8,128)S(1)}, f32[2,24,128]{2,1,0:T(8,128)S(1)}, u32[]{:S(2)}, u32[]{:S(2)}) collective-permute-start(f32[2,24,128]{2,1,0:T(8,128)S(1)} %get-tuple-element.69), channel_id=1, source_target_pairs={{16,0},{32,16},{48,32},{64,48},{80,64},{96,80},{112,96},{128,112},... | collective-permute-start | bytes 73736 | tf_op jit(solution)/shard_map/ppermute | solution.py:599
  11.5 3.5 %all-to-all-start = ((f32[16,16,128]{2,1,0:T(8,128)}), f32[16,16,128]{2,1,0:T(8,128)S(1)}, u32[]{:S(2)}, u32[]{:S(2)}) async-start(f32[16,16,128]{2,1,0:T(8,128)} %get-tuple-element.78), calls=%async_computation | async-start | bytes 262144 | tf_op jit(solution)/shard_map/all_to_all | solution.py:615
  15.7 1.2 %phase.1 = (s32[32,128]{1,0:T(8,128)S(1)}, s32[1,128]{1,0:T(1,128)S(1)}, f32[4,128,128]{2,1,0:T(8,128)S(1)}, f32[2,128,128]{2,1,0:T(8,128)S(1)}, f32[2,128,128]{...) custom-call(s32[1]{0:T(128)} %bitcast.23.count_ref, ...), custom_call_target="tpu_custom_call" | custom-call | bytes 262144 | tf_op jit(solution)/shard_map/phase/pallas_call | solution.py:47
  17.1 2.8 %collective-permute-start.3 = (f32[2,24,128]{2,1,0:T(8,128)S(1)}, f32[2,24,128]{2,1,0:T(8,128)S(1)}, u32[]{:S(2)}, u32[]{:S(2)}) collective-permute-start(f32[2,24,128]{2,1,0:T(8,128)S(1)} %get-tuple-element.73), channel_id=1, source_target_pairs={{0,16},{16,32},{32,48},{48,64},{64,80},{80,96},{96,112},{112,128},... | collective-permute-start | bytes 73736 | tf_op jit(solution)/shard_map/ppermute | solution.py:599
  19.9 1.6 %collective-permute-start.4 = (f32[2,8,128]{2,1,0:T(8,128)S(1)}, f32[2,8,128]{2,1,0:T(8,128)S(1)}, u32[]{:S(2)}, u32[]{:S(2)}) collective-permute-start(f32[2,8,128]{2,1,0:T(8,128)S(1)} %get-tuple-element.74), channel_id=1, source_target_pairs={{0,2},{2,4},{4,6},{6,8},{8,10},{10,12},{12,14},{14,0},{1,3},{3,5},... | collective-permute-start | bytes 24584 | tf_op jit(solution)/shard_map/ppermute | solution.py:599
  21.5 4.5 %all-to-all-done.fields_ref = f32[16,16,128]{2,1,0:T(8,128)S(1)} async-done(((f32[16,16,128]{2,1,0:T(8,128)}), f32[16,16,128]{2,1,0:T(8,128)S(1)}, u32[]{:S(2)}, u32[]{:S(2)}) %all-to-all-start) | async-done | bytes 131104 | tf_op jit(solution)/shard_map/all_to_all | solution.py:615
  26.0 2.5 %scatter.1 = (f32[4,192,128]{2,1,0:T(8,128)S(1)}, bf16[96,4096]{1,0:T(8,128)(2,1)S(1)}, bf16[256,4096]{1,0:T(8,128)(2,1)S(1)}) custom-call(s32[32,128]{1,0:T(8,128)S(1)} %get-tuple-element.77.placed, f32[16,16,128]{2,1,0:T(8,128)S(1)} %all-to-all-done.fields_ref), custom_call_target="tpu_custom_call" | custom-call | bytes 2097152 | tf_op jit(solution)/shard_map/scatter/pallas_call | solution.py:47
  28.9 1.2 %collective-permute-start.6 = (f32[2,24,128]{2,1,0:T(8,128)S(1)}, f32[2,24,128]{2,1,0:T(8,128)S(1)}, u32[]{:S(2)}, u32[]{:S(2)}) collective-permute-start(f32[2,24,128]{2,1,0:T(8,128)S(1)} %get-tuple-element.81), channel_id=1, source_target_pairs={{16,0},{32,16},{48,32},{64,48},{80,64},{96,80},{112,96},{128,112},... | collective-permute-start | bytes 73736 | tf_op jit(solution)/shard_map/ppermute | solution.py:599
  30.1 3.5 %collective-permute-start.7 = (f32[2,8,128]{2,1,0:T(8,128)S(1)}, f32[2,8,128]{2,1,0:T(8,128)S(1)}, u32[]{:S(2)}, u32[]{:S(2)}) collective-permute-start(f32[2,8,128]{2,1,0:T(8,128)S(1)} %get-tuple-element.82), channel_id=1, source_target_pairs={{2,0},{4,2},{6,4},{8,6},{10,8},{12,10},{14,12},{0,14},{3,1},{5,3},... | collective-permute-start | bytes 24584 | tf_op jit(solution)/shard_map/ppermute | solution.py:599
  33.5 2.1 %scatter2.1 = (f32[4,192,128]{2,1,0:T(8,128)S(1)}, f32[8,128]{1,0:T(8,128)S(1)}) custom-call(f32[16,16,128]{2,1,0:T(8,128)S(1)} %all-to-all-done.fields_ref, bf16[96,4096]{1,0:T(8,128)(2,1)S(1)} %get-tuple-element.84.tall, bf16[256,4096]{1,0:T(8,128)(2,1)S(1)} %get-tuple-element.85.columns, f32[3,192,128]{2,1,0:T(8,128)S(1)} %get-tuple-element.96.e_ref.e_new, ...), custom_call_target="tpu_custom_call" | custom-call | bytes 2097152 | tf_op jit(solution)/shard_map/scatter2/pallas_call | solution.py:47
  36.1 1.9 %collective-permute-start.9 = (f32[2,24,128]{2,1,0:T(8,128)S(1)}, f32[2,24,128]{2,1,0:T(8,128)S(1)}, u32[]{:S(2)}, u32[]{:S(2)}) collective-permute-start(f32[2,24,128]{2,1,0:T(8,128)S(1)} %get-tuple-element.93), channel_id=1, source_target_pairs={{0,16},{16,32},{32,48},{48,64},{64,80},{80,96},{96,112},{112,128},... | collective-permute-start | bytes 73736 | tf_op jit(solution)/shard_map/ppermute | solution.py:599
  38.0 2.7 %drive.1.drives = f32[6,32,128]{2,1,0:T(8,128)S(1)} custom-call(f32[3,192,128]{2,1,0:T(8,128)S(1)} %get-tuple-element.67.e_ref.e_old, f32[3,192,128]{2,1,0:T(8,128)S(1)} %get-tuple-element.96.e_ref.e_new, s32[32,128]{1,0:T(8,128)S(1)} %get-tuple-element.77.placed, bf16[256,4096]{1,0:T(8,128)(2,1)S(1)} %get-tuple-element.85.columns), custom_call_target="tpu_custom_call" | custom-call | bytes 2097152 | tf_op jit(solution)/shard_map/drive/pallas_call | solution.py:47
  40.7 0.9 %collective-permute-done.10.face_y = f32[2,8,128]{2,1,0:T(8,128)S(1)} collective-permute-done((f32[2,8,128]{2,1,0:T(8,128)S(1)}, f32[2,8,128]{2,1,0:T(8,128)S(1)}, u32[]{:S(2)}, u32[]{:S(2)}) %collective-permute-start.10) | collective-permute-done | bytes 8224 | tf_op jit(solution)/shard_map/ppermute | solution.py:599
  41.6 2.6 %collective-permute-done.9.face_x = f32[2,24,128]{2,1,0:T(8,128)S(1)} collective-permute-done((f32[2,24,128]{2,1,0:T(8,128)S(1)}, f32[2,24,128]{2,1,0:T(8,128)S(1)}, u32[]{:S(2)}, u32[]{:S(2)}) %collective-permute-start.9) | collective-permute-done | bytes 24608 | tf_op jit(solution)/shard_map/ppermute | solution.py:599
  44.2 2.0 %final.1 = (f32[3,192,128]{2,1,0:T(8,128)S(1)}, bf16[32,256]{1,0:T(8,128)(2,1)S(1)}, f32[384,128]{1,0:T(8,128)S(1)}) custom-call(f32[3,192,128]{2,1,0:T(8,128)S(1)} %get-tuple-element.96.e_ref.e_new, f32[3,192,128]{2,1,0:T(8,128)S(1)} %get-tuple-element.92.h_ref, f32[2,24,128]{2,1,0:T(8,128)S(1)} %collective-permute-done.9.face_x, ...), custom_call_target="tpu_custom_call" | custom-call | bytes 2097152 | tf_op jit(solution)/shard_map/final/pallas_call | solution.py:47
  46.3 1.1 %keep.1 = f32[384,128]{1,0:T(8,128)S(1)} custom-call(bf16[32,256]{1,0:T(8,128)(2,1)S(1)} %get-tuple-element.106.left, f32[4,128,128]{2,1,0:T(8,128)S(1)} %get-tuple-element.103.starts, f32[2,128,128]{2,1,0:T(8,128)S(1)} %get-tuple-element.104.turn, f32[2,128,128]{2,1,0:T(8,128)S(1)} %get-tuple-element.105.factors), custom_call_target="tpu_custom_call" | custom-call | flops 10000000000 | bytes 2097152 | tf_op jit(solution)/shard_map/keep/pallas_call | solution.py:47
  47.7 10.4 %all_to_all.15.pieces = f32[8,48,128]{2,1,0:T(8,128)S(1)} all-to-all(f32[8,48,128]{2,1,0:T(8,128)S(1)} %bitcast.25), channel_id=1, replica_groups=mesh['gx'=16,'gy'=8,'gz'=2] {'gy'}, dimensions={0} | all-to-all | bytes 393216 | tf_op jit(solution)/shard_map/all_to_all | solution.py:711
  58.2 1.9 %collective-permute-start.14 = (f32[104,128]{1,0:T(8,128)S(1)}, f32[104,128]{1,0:T(8,128)S(1)}, u32[]{:S(2)}, u32[]{:S(2)}) collective-permute-start(f32[104,128]{1,0:T(8,128)S(1)} %get-tuple-element.111), channel_id=1, source_target_pairs={{0,128},{16,144},{32,160},{48,176},{64,192},{80,208},{96,224},{112... | collective-permute-start | bytes 159752 | tf_op jit(solution)/shard_map/ppermute | solution.py:717
  60.1 0.6 collective-permute-start.13
  60.7 1.7 %collective-permute-start.15 = (f32[96,128]{1,0:T(8,128)S(1)}, f32[96,128]{1,0:T(8,128)S(1)}, u32[]{:S(2)}, u32[]{:S(2)}) collective-permute-start(f32[96,128]{1,0:T(8,128)S(1)} %get-tuple-element.112), channel_id=1, source_target_pairs={{0,192},{16,208},{32,224},{48,240},{64,128},{80,144},{96,160},{112... | collective-permute-start | bytes 147464 | tf_op jit(solution)/shard_map/ppermute | solution.py:717
  62.4 1.8 %collective-permute-done.13.one = f32[96,128]{1,0:T(8,128)S(1)} collective-permute-done((f32[96,128]{1,0:T(8,128)S(1)}, f32[96,128]{1,0:T(8,128)S(1)}, u32[]{:S(2)}, u32[]{:S(2)}) %collective-permute-start.13) | collective-permute-done | bytes 49184 | tf_op jit(solution)/shard_map/ppermute | solution.py:717
  64.2 1.8 %collective-permute-done.15.three = f32[96,128]{1,0:T(8,128)S(1)} collective-permute-done((f32[96,128]{1,0:T(8,128)S(1)}, f32[96,128]{1,0:T(8,128)S(1)}, u32[]{:S(2)}, u32[]{:S(2)}) %collective-permute-start.15) | collective-permute-done | bytes 49184 | tf_op jit(solution)/shard_map/ppermute | solution.py:717
  66.1 2.9 %collective-permute-start.17 = (f32[104,128]{1,0:T(8,128)S(1)}, f32[104,128]{1,0:T(8,128)S(1)}, u32[]{:S(2)}, u32[]{:S(2)}) collective-permute-start(f32[104,128]{1,0:T(8,128)S(1)} %get-tuple-element.116), channel_id=1, source_target_pairs={{0,32},{16,48},{32,0},{48,16},{64,96},{80,112},{96,64},{112,80},{1... | collective-permute-start | bytes 159752 | tf_op jit(solution)/shard_map/ppermute | solution.py:729
  69.0 1.7 %collective-permute-start.16 = (f32[96,128]{1,0:T(8,128)S(1)}, f32[96,128]{1,0:T(8,128)S(1)}, u32[]{:S(2)}, u32[]{:S(2)}) collective-permute-start(f32[96,128]{1,0:T(8,128)S(1)} %get-tuple-element.115), channel_id=1, source_target_pairs={{0,16},{16,0},{32,48},{48,32},{64,80},{80,64},{96,112},{112,96},{1... | collective-permute-start | bytes 147464 | tf_op jit(solution)/shard_map/ppermute | solution.py:729
  70.7 1.9 %collective-permute-start.18 = (f32[96,128]{1,0:T(8,128)S(1)}, f32[96,128]{1,0:T(8,128)S(1)}, u32[]{:S(2)}, u32[]{:S(2)}) collective-permute-start(f32[96,128]{1,0:T(8,128)S(1)} %get-tuple-element.117), channel_id=1, source_target_pairs={{0,48},{16,32},{32,16},{48,0},{64,112},{80,96},{96,80},{112,64},{1... | collective-permute-start | bytes 147464 | tf_op jit(solution)/shard_map/ppermute | solution.py:729
  72.7 0.8 store.1
  73.5 2.0 %collective-permute-done.16.one = f32[96,128]{1,0:T(8,128)S(1)} collective-permute-done((f32[96,128]{1,0:T(8,128)S(1)}, f32[96,128]{1,0:T(8,128)S(1)}, u32[]{:S(2)}, u32[]{:S(2)}) %collective-permute-start.16) | collective-permute-done | bytes 49184 | tf_op jit(solution)/shard_map/ppermute | solution.py:729
  75.5 1.5 %collective-permute-done.18.three = f32[96,128]{1,0:T(8,128)S(1)} collective-permute-done((f32[96,128]{1,0:T(8,128)S(1)}, f32[96,128]{1,0:T(8,128)S(1)}, u32[]{:S(2)}, u32[]{:S(2)}) %collective-permute-start.18) | collective-permute-done | bytes 49184 | tf_op jit(solution)/shard_map/ppermute | solution.py:729
  77.1 0.7 atoms.1
  77.8 9.9 %all_to_all.16 = f32[8,48,128]{2,1,0:T(8,128)S(1)} all-to-all(f32[8,48,128]{2,1,0:T(8,128)S(1)} %get-tuple-element.129), channel_id=1, replica_groups=mesh['gx'=16,'gy'=8,'gz'=2] {'gy'}, dimensions={0} | all-to-all | bytes 393216 | tf_op jit(solution)/shard_map/all_to_all | solution.py:748
  87.7 0.7 copy.17
  (27 shorter events, 2.1 us)
Async XLA Ops:
  2.4 14.5 %collective-permute-start.2 = (f32[2,192,128]{2,1,0:T(8,128)S(1)}, f32[2,192,128]{2,1,0:T(8,128)S(1)}, u32[]{:S(2)}, u32[]{:S(2)}) collective-permute-start(f32[2,192,128]{2,1,0:T(8,128)S(1)} %get-tuple-element.71), channel_id=1, source_target_pairs={{1,0},{0,1},{3,2},{2,3},{5,4},{4,5},{7,6},{6,7},{9,8},{8,9},{11,10... | collective-permute-start | bytes 589832 | tf_op jit(solution)/shard_map/ppermute | solution.py:599
  2.5 14.4 %collective-permute-start = (f32[2,24,128]{2,1,0:T(8,128)S(1)}, f32[2,24,128]{2,1,0:T(8,128)S(1)}, u32[]{:S(2)}, u32[]{:S(2)}) collective-permute-start(f32[2,24,128]{2,1,0:T(8,128)S(1)} %get-tuple-element.69), channel_id=1, source_target_pairs={{16,0},{32,16},{48,32},{64,48},{80,64},{96,80},{112,96},{128,112},... | collective-permute-start | bytes 73736 | tf_op jit(solution)/shard_map/ppermute | solution.py:599
  11.0 5.8 %collective-permute-start.1 = (f32[2,8,128]{2,1,0:T(8,128)S(1)}, f32[2,8,128]{2,1,0:T(8,128)S(1)}, u32[]{:S(2)}, u32[]{:S(2)}) collective-permute-start(f32[2,8,128]{2,1,0:T(8,128)S(1)} %get-tuple-element.70), channel_id=1, source_target_pairs={{2,0},{4,2},{6,4},{8,6},{10,8},{12,10},{14,12},{0,14},{3,1},{5,3},... | collective-permute-start | bytes 24584 | tf_op jit(solution)/shard_map/ppermute | solution.py:599
  11.5 14.5 %all-to-all-start = ((f32[16,16,128]{2,1,0:T(8,128)}), f32[16,16,128]{2,1,0:T(8,128)S(1)}, u32[]{:S(2)}, u32[]{:S(2)}) async-start(f32[16,16,128]{2,1,0:T(8,128)} %get-tuple-element.78), calls=%async_computation | async-start | bytes 262144 | tf_op jit(solution)/shard_map/all_to_all | solution.py:615
  17.0 11.5 %collective-permute-start.5 = (f32[2,192,128]{2,1,0:T(8,128)S(1)}, f32[2,192,128]{2,1,0:T(8,128)S(1)}, u32[]{:S(2)}, u32[]{:S(2)}) collective-permute-start(f32[2,192,128]{2,1,0:T(8,128)S(1)} %get-tuple-element.75), channel_id=1, source_target_pairs={{0,1},{1,0},{2,3},{3,2},{4,5},{5,4},{6,7},{7,6},{8,9},{9,8},{10,11... | collective-permute-start | bytes 589832 | tf_op jit(solution)/shard_map/ppermute | solution.py:599
  17.1 11.4 %collective-permute-start.3 = (f32[2,24,128]{2,1,0:T(8,128)S(1)}, f32[2,24,128]{2,1,0:T(8,128)S(1)}, u32[]{:S(2)}, u32[]{:S(2)}) collective-permute-start(f32[2,24,128]{2,1,0:T(8,128)S(1)} %get-tuple-element.73), channel_id=1, source_target_pairs={{0,16},{16,32},{32,48},{48,64},{64,80},{80,96},{96,112},{112,128},... | collective-permute-start | bytes 73736 | tf_op jit(solution)/shard_map/ppermute | solution.py:599
  19.9 8.6 %collective-permute-start.4 = (f32[2,8,128]{2,1,0:T(8,128)S(1)}, f32[2,8,128]{2,1,0:T(8,128)S(1)}, u32[]{:S(2)}, u32[]{:S(2)}) collective-permute-start(f32[2,8,128]{2,1,0:T(8,128)S(1)} %get-tuple-element.74), channel_id=1, source_target_pairs={{0,2},{2,4},{4,6},{6,8},{8,10},{10,12},{12,14},{14,0},{1,3},{3,5},... | collective-permute-start | bytes 24584 | tf_op jit(solution)/shard_map/ppermute | solution.py:599
  28.8 6.9 %collective-permute-start.8 = (f32[2,192,128]{2,1,0:T(8,128)S(1)}, f32[2,192,128]{2,1,0:T(8,128)S(1)}, u32[]{:S(2)}, u32[]{:S(2)}) collective-permute-start(f32[2,192,128]{2,1,0:T(8,128)S(1)} %get-tuple-element.83), channel_id=1, source_target_pairs={{1,0},{0,1},{3,2},{2,3},{5,4},{4,5},{7,6},{6,7},{9,8},{8,9},{11,10... | collective-permute-start | bytes 589832 | tf_op jit(solution)/shard_map/ppermute | solution.py:599
  28.9 6.8 %collective-permute-start.6 = (f32[2,24,128]{2,1,0:T(8,128)S(1)}, f32[2,24,128]{2,1,0:T(8,128)S(1)}, u32[]{:S(2)}, u32[]{:S(2)}) collective-permute-start(f32[2,24,128]{2,1,0:T(8,128)S(1)} %get-tuple-element.81), channel_id=1, source_target_pairs={{16,0},{32,16},{48,32},{64,48},{80,64},{96,80},{112,96},{128,112},... | collective-permute-start | bytes 73736 | tf_op jit(solution)/shard_map/ppermute | solution.py:599
  30.1 5.5 %collective-permute-start.7 = (f32[2,8,128]{2,1,0:T(8,128)S(1)}, f32[2,8,128]{2,1,0:T(8,128)S(1)}, u32[]{:S(2)}, u32[]{:S(2)}) collective-permute-start(f32[2,8,128]{2,1,0:T(8,128)S(1)} %get-tuple-element.82), channel_id=1, source_target_pairs={{2,0},{4,2},{6,4},{8,6},{10,8},{12,10},{14,12},{0,14},{3,1},{5,3},... | collective-permute-start | bytes 24584 | tf_op jit(solution)/shard_map/ppermute | solution.py:599
  35.8 8.4 %collective-permute-start.11 = (f32[2,192,128]{2,1,0:T(8,128)S(1)}, f32[2,192,128]{2,1,0:T(8,128)S(1)}, u32[]{:S(2)}, u32[]{:S(2)}) collective-permute-start(f32[2,192,128]{2,1,0:T(8,128)S(1)} %get-tuple-element.95), channel_id=1, source_target_pairs={{0,1},{1,0},{2,3},{3,2},{4,5},{5,4},{6,7},{7,6},{8,9},{9,8},{10,11... | collective-permute-start | bytes 589832 | tf_op jit(solution)/shard_map/ppermute | solution.py:599
  36.1 8.1 %collective-permute-start.9 = (f32[2,24,128]{2,1,0:T(8,128)S(1)}, f32[2,24,128]{2,1,0:T(8,128)S(1)}, u32[]{:S(2)}, u32[]{:S(2)}) collective-permute-start(f32[2,24,128]{2,1,0:T(8,128)S(1)} %get-tuple-element.93), channel_id=1, source_target_pairs={{0,16},{16,32},{32,48},{48,64},{64,80},{80,96},{96,112},{112,128},... | collective-permute-start | bytes 73736 | tf_op jit(solution)/shard_map/ppermute | solution.py:599
  37.9 3.7 %collective-permute-start.10 = (f32[2,8,128]{2,1,0:T(8,128)S(1)}, f32[2,8,128]{2,1,0:T(8,128)S(1)}, u32[]{:S(2)}, u32[]{:S(2)}) collective-permute-start(f32[2,8,128]{2,1,0:T(8,128)S(1)} %get-tuple-element.94), channel_id=1, source_target_pairs={{0,2},{2,4},{4,6},{6,8},{8,10},{10,12},{12,14},{14,0},{1,3},{3,5},... | collective-permute-start | bytes 24584 | tf_op jit(solution)/shard_map/ppermute | solution.py:599
  46.2 1.5 %collective-permute-start.12 = (f32[384,128]{1,0:T(8,128)S(1)}, f32[384,128]{1,0:T(8,128)S(1)}, u32[]{:S(2)}, u32[]{:S(2)}) collective-permute-start(f32[384,128]{1,0:T(8,128)S(1)} %get-tuple-element.107), channel_id=1, source_target_pairs={{1,0},{0,1},{3,2},{2,3},{5,4},{4,5},{7,6},{6,7},{9,8},{8,9},{11,10... | collective-permute-start | bytes 589832 | tf_op jit(solution)/shard_map/ppermute | solution.py:706
  58.2 7.8 %collective-permute-start.14 = (f32[104,128]{1,0:T(8,128)S(1)}, f32[104,128]{1,0:T(8,128)S(1)}, u32[]{:S(2)}, u32[]{:S(2)}) collective-permute-start(f32[104,128]{1,0:T(8,128)S(1)} %get-tuple-element.111), channel_id=1, source_target_pairs={{0,128},{16,144},{32,160},{48,176},{64,192},{80,208},{96,224},{112... | collective-permute-start | bytes 159752 | tf_op jit(solution)/shard_map/ppermute | solution.py:717
  60.1 4.1 %collective-permute-start.13 = (f32[96,128]{1,0:T(8,128)S(1)}, f32[96,128]{1,0:T(8,128)S(1)}, u32[]{:S(2)}, u32[]{:S(2)}) collective-permute-start(f32[96,128]{1,0:T(8,128)S(1)} %get-tuple-element.110), channel_id=1, source_target_pairs={{0,64},{16,80},{32,96},{48,112},{64,0},{80,16},{96,32},{112,48},{1... | collective-permute-start | bytes 147464 | tf_op jit(solution)/shard_map/ppermute | solution.py:717
  60.7 5.3 %collective-permute-start.15 = (f32[96,128]{1,0:T(8,128)S(1)}, f32[96,128]{1,0:T(8,128)S(1)}, u32[]{:S(2)}, u32[]{:S(2)}) collective-permute-start(f32[96,128]{1,0:T(8,128)S(1)} %get-tuple-element.112), channel_id=1, source_target_pairs={{0,192},{16,208},{32,224},{48,240},{64,128},{80,144},{96,160},{112... | collective-permute-start | bytes 147464 | tf_op jit(solution)/shard_map/ppermute | solution.py:717
  66.1 11.0 %collective-permute-start.17 = (f32[104,128]{1,0:T(8,128)S(1)}, f32[104,128]{1,0:T(8,128)S(1)}, u32[]{:S(2)}, u32[]{:S(2)}) collective-permute-start(f32[104,128]{1,0:T(8,128)S(1)} %get-tuple-element.116), channel_id=1, source_target_pairs={{0,32},{16,48},{32,0},{48,16},{64,96},{80,112},{96,64},{112,80},{1... | collective-permute-start | bytes 159752 | tf_op jit(solution)/shard_map/ppermute | solution.py:729
  69.0 6.5 %collective-permute-start.16 = (f32[96,128]{1,0:T(8,128)S(1)}, f32[96,128]{1,0:T(8,128)S(1)}, u32[]{:S(2)}, u32[]{:S(2)}) collective-permute-start(f32[96,128]{1,0:T(8,128)S(1)} %get-tuple-element.115), channel_id=1, source_target_pairs={{0,16},{16,0},{32,48},{48,32},{64,80},{80,64},{96,112},{112,96},{1... | collective-permute-start | bytes 147464 | tf_op jit(solution)/shard_map/ppermute | solution.py:729
  70.7 6.3 %collective-permute-start.18 = (f32[96,128]{1,0:T(8,128)S(1)}, f32[96,128]{1,0:T(8,128)S(1)}, u32[]{:S(2)}, u32[]{:S(2)}) collective-permute-start(f32[96,128]{1,0:T(8,128)S(1)} %get-tuple-element.117), channel_id=1, source_target_pairs={{0,48},{16,32},{32,16},{48,0},{64,112},{80,96},{96,80},{112,64},{1... | collective-permute-start | bytes 147464 | tf_op jit(solution)/shard_map/ppermute | solution.py:729

commit v11 on v10

--- a/solution.py
+++ b/solution.py
@@ -136,14 +136,19 @@
     return kept
 
 
-def prepare_kernel(e_hbm, state_hbm, out_x, out_y, out_z, packed, e_out, state, sems):
+def prepare_kernel(e_hbm, state_hbm, out_x, out_y, out_z, e_out, state, sems):
     copies = [
-        pltpu.make_async_copy(state_hbm, state, sems.at[0]),
-        pltpu.make_async_copy(e_hbm, e_out, sems.at[1]),
+        pltpu.make_async_copy(e_hbm, e_out, sems.at[0]),
+        pltpu.make_async_copy(state_hbm, state, sems.at[1]),
     ]
     for copy in copies:
         copy.start()
     copies[0].wait()
+    first_layers(e_out, out_x, out_y, out_z)
+    copies[1].wait()
+
+
+def pack_kernel(state, packed):
     lower, lasing, upper = state[7], state[8], state[9]
     lasing_free = lasing + time_step * (upper / upper_life - lasing / lasing_life)
     lower_free = lower + time_step * (lasing / lasing_life - lower / lower_life)
@@ -152,8 +157,6 @@
     for field, value in enumerate(free + [lasing - lower] + polar + [lasing_free - lower_free]):
         for owner in range(SLOTS // 2):
             packed[owner, 2 * field : 2 * field + 2] = value[2 * owner : 2 * owner + 2]
-    copies[1].wait()
-    first_layers(e_out, out_x, out_y, out_z)
 
 
 def magnetic_kernel(e_ref, h_ref, face_x, face_y, face_z, h_out, out_x, out_y, out_z):
@@ -527,7 +530,8 @@
             out[row : row + 1] = imag[comp : comp + 1]
 
 
-def atoms_kernel(state_ref, pump_ref, drives, out):
+def atoms_kernel(state_ref, pump_ref, drives, far_ref, out, far_out):
+    far_out[...] = far_ref[...]
     polar = [state_ref[c] for c in range(3)]
     rate = [state_ref[3 + c] for c in range(3)]
     ground, lower, lasing, upper = [state_ref[6 + level] for level in range(4)]
@@ -600,9 +604,9 @@
             for part, axis, perm in zip(parts, ("gx", "gy", "gz"), perms)
         ]
 
-    *near, packed, e_old, state = call(
+    *near, e_old, state = call(
         prepare_kernel,
-        faces + (shape(SLOTS // 2, 16, CZ), dense, shape(10, SLOTS, CZ)),
+        faces + (dense, shape(10, SLOTS, CZ)),
         stay(
             efield.reshape(3, ROWS, CZ),
             jnp.transpose(gain_state.reshape(SLOTS, 10, CZ), (1, 0, 2)),
@@ -612,6 +616,7 @@
         name="prepare",
     )
     near = shifted(near, down)
+    packed = call(pack_kernel, shape(SLOTS // 2, 16, CZ), (state,), name="pack")
     fields = lax.all_to_all(packed, "gx", 0, 0, tiled=True)
     placed, surf, starts, turn, factors, h_old, eps, pumps, far_part = call(
         phase_kernel,
@@ -738,15 +743,16 @@
         (total, kept, *got, far_part),
         name="finish",
     )
-    state_out = call(
+    copies, e_out, h_out = lax.optimization_barrier((copies, e_out, h_out))
+    gathered = lax.all_to_all(copies, "gy", 0, 0, tiled=True)
+    back, gathered = lax.optimization_barrier((back, gathered))
+    state_out, far_out = call(
         atoms_kernel,
-        shape(10, SLOTS, CZ),
-        (state, pumps, back),
+        (shape(10, SLOTS, CZ), shape(8, FAR, DIRS)),
+        (state, pumps, back, gathered),
         name="atoms",
     )
-    copies, state_out, e_out, h_out = lax.optimization_barrier((copies, state_out, e_out, h_out))
-    gathered = lax.all_to_all(copies, "gy", 0, 0, tiled=True)
-    far_out = jnp.transpose(gathered.reshape(12, FREQ // 2, DIRS), (1, 0, 2))
+    far_out = jnp.transpose(far_out.reshape(12, FREQ // 2, DIRS), (1, 0, 2))
     return (
         e_out.reshape(efield.shape),
         h_out.reshape(hfield.shape),

time: 88.6 us -> 88 us (level)
    pallas_call x15 -> x16, Pallas kernels: 15.5 us -> 15.5 us  [call(): pl.pallas_call(kernel, out_shape=outs, in_specs=in_specs or [pl.BlockSpec...]
  transfers between devices with their start and end apart: 20 -> 20, of which waited for: 8 -> 8; matrix products, arithmetic and copies ran while one was open for 0% -> 0% of each run, Pallas kernels for 12% -> 13%
where the time goes in v11:
time: 88 us; the launch traced here: 87.7 us
  starting transfers between devices  34.9 us (40%)
  blocking collectives  20.3 us (23%)
  Pallas kernels  15.5 us (18%)
  waiting for transfers between devices  15.5 us (18%)
  between operations  1.49 us (2%)
    ppermute x12, starting transfers between devices, shifted(): lax.ppermute(part, axis, perm)  20.5 us
    pallas_call x16, Pallas kernels, call(): pl.pallas_call(kernel, out_shape=outs, in_specs=in_specs or [pl.BlockSpec...  15.5 us
    all_to_all x1, blocking collectives, local(): pieces = lax.all_to_all(chip.reshape(8, FAR, DIRS), 'gy', 0, 0, tiled=True)  10.4 us
    all_to_all x1, blocking collectives, local(): gathered = lax.all_to_all(copies, 'gy', 0, 0, tiled=True)  9.87 us
    ppermute x3, starting transfers between devices, local(): lax.ppermute(value, 'gx', [(a * 4 + z, a * 4 + (z ^ k)) for a in range(4)...  6.58 us
    all_to_all x1, waiting for transfers between devices, local(): fields = lax.all_to_all(packed, 'gx', 0, 0, tiled=True)  4.54 us
    ppermute x3, starting transfers between devices, local(): lax.ppermute(value, 'gx', [(a * 4 + z, (a ^ k) * 4 + z) for a in range(4)...  4.18 us
    ppermute x3, waiting for transfers between devices, local(): lax.ppermute(value, 'gx', [(a * 4 + z, (a ^ k) * 4 + z) for a in range(4)...  3.65 us
  transfers between devices with their start and end apart: 20, of which 8 were waited for; matrix products, arithmetic and copies ran while one was open for 0% of the time, Pallas kernels for 13%

profile of v11, /device:TPU:8, one launch (start us, length us, event | category | flops | bytes accessed | tf_op | source)
XLA Modules:
  0.0 87.7 jit_solution(6121183462516461307)
XLA Ops:
  0.6 1.0 %prepare.1 = (f32[2,24,128]{2,1,0:T(8,128)S(1)}, f32[2,8,128]{2,1,0:T(8,128)S(1)}, f32[2,192,128]{2,1,0:T(8,128)S(1)}, f32[3,192,128]{2,1,0:T(8,128)S(1)}, f32[10,32,128]{2,1,0:T(8,128)S(1)}) custom-call(f32[3,192,128]{2,1,0:T(8,128)} %bitcast.25, f32[10,32,128]{2,1,0:T(8,128)} %bitcast.28), custom_call_target="tpu_custom_call" | custom-call | bytes 2097152 | tf_op jit(solution)/shard_map/prepare/pallas_call | solution.py:47
  1.8 8.6 %collective-permute-start = (f32[2,24,128]{2,1,0:T(8,128)S(1)}, f32[2,24,128]{2,1,0:T(8,128)S(1)}, u32[]{:S(2)}, u32[]{:S(2)}) collective-permute-start(f32[2,24,128]{2,1,0:T(8,128)S(1)} %get-tuple-element.71), channel_id=1, source_target_pairs={{16,0},{32,16},{48,32},{64,48},{80,64},{96,80},{112,96},{128,112},... | collective-permute-start | bytes 73736 | tf_op jit(solution)/shard_map/ppermute | solution.py:603
  10.8 0.7 pack.1
  11.5 3.5 %all-to-all-start = ((f32[16,16,128]{2,1,0:T(8,128)}), f32[16,16,128]{2,1,0:T(8,128)S(1)}, u32[]{:S(2)}, u32[]{:S(2)}) async-start(f32[16,16,128]{2,1,0:T(8,128)} %pack.1), calls=%async_computation | async-start | bytes 262144 | tf_op jit(solution)/shard_map/all_to_all | solution.py:620
  15.6 1.2 %phase.1 = (s32[32,128]{1,0:T(8,128)S(1)}, s32[1,128]{1,0:T(1,128)S(1)}, f32[4,128,128]{2,1,0:T(8,128)S(1)}, f32[2,128,128]{2,1,0:T(8,128)S(1)}, f32[2,128,128]{...) custom-call(s32[1]{0:T(128)} %bitcast.23.count_ref, ...), custom_call_target="tpu_custom_call" | custom-call | bytes 262144 | tf_op jit(solution)/shard_map/phase/pallas_call | solution.py:47
  17.1 2.8 %collective-permute-start.3 = (f32[2,24,128]{2,1,0:T(8,128)S(1)}, f32[2,24,128]{2,1,0:T(8,128)S(1)}, u32[]{:S(2)}, u32[]{:S(2)}) collective-permute-start(f32[2,24,128]{2,1,0:T(8,128)S(1)} %get-tuple-element.75), channel_id=1, source_target_pairs={{0,16},{16,32},{32,48},{48,64},{64,80},{80,96},{96,112},{112,128},... | collective-permute-start | bytes 73736 | tf_op jit(solution)/shard_map/ppermute | solution.py:603
  19.9 1.6 %collective-permute-start.4 = (f32[2,8,128]{2,1,0:T(8,128)S(1)}, f32[2,8,128]{2,1,0:T(8,128)S(1)}, u32[]{:S(2)}, u32[]{:S(2)}) collective-permute-start(f32[2,8,128]{2,1,0:T(8,128)S(1)} %get-tuple-element.76), channel_id=1, source_target_pairs={{0,2},{2,4},{4,6},{6,8},{8,10},{10,12},{12,14},{14,0},{1,3},{3,5},... | collective-permute-start | bytes 24584 | tf_op jit(solution)/shard_map/ppermute | solution.py:603
  21.5 4.5 %all-to-all-done.fields_ref = f32[16,16,128]{2,1,0:T(8,128)S(1)} async-done(((f32[16,16,128]{2,1,0:T(8,128)}), f32[16,16,128]{2,1,0:T(8,128)S(1)}, u32[]{:S(2)}, u32[]{:S(2)}) %all-to-all-start) | async-done | bytes 131104 | tf_op jit(solution)/shard_map/all_to_all | solution.py:620
  26.0 2.5 %scatter.1 = (f32[4,192,128]{2,1,0:T(8,128)S(1)}, bf16[96,4096]{1,0:T(8,128)(2,1)S(1)}, bf16[256,4096]{1,0:T(8,128)(2,1)S(1)}) custom-call(s32[32,128]{1,0:T(8,128)S(1)} %get-tuple-element.79.placed, f32[16,16,128]{2,1,0:T(8,128)S(1)} %all-to-all-done.fields_ref), custom_call_target="tpu_custom_call" | custom-call | bytes 2097152 | tf_op jit(solution)/shard_map/scatter/pallas_call | solution.py:47
  28.8 1.2 %collective-permute-start.6 = (f32[2,24,128]{2,1,0:T(8,128)S(1)}, f32[2,24,128]{2,1,0:T(8,128)S(1)}, u32[]{:S(2)}, u32[]{:S(2)}) collective-permute-start(f32[2,24,128]{2,1,0:T(8,128)S(1)} %get-tuple-element.83), channel_id=1, source_target_pairs={{16,0},{32,16},{48,32},{64,48},{80,64},{96,80},{112,96},{128,112},... | collective-permute-start | bytes 73736 | tf_op jit(solution)/shard_map/ppermute | solution.py:603
  30.1 3.5 %collective-permute-start.7 = (f32[2,8,128]{2,1,0:T(8,128)S(1)}, f32[2,8,128]{2,1,0:T(8,128)S(1)}, u32[]{:S(2)}, u32[]{:S(2)}) collective-permute-start(f32[2,8,128]{2,1,0:T(8,128)S(1)} %get-tuple-element.84), channel_id=1, source_target_pairs={{2,0},{4,2},{6,4},{8,6},{10,8},{12,10},{14,12},{0,14},{3,1},{5,3},... | collective-permute-start | bytes 24584 | tf_op jit(solution)/shard_map/ppermute | solution.py:603
  33.5 2.1 %scatter2.1 = (f32[4,192,128]{2,1,0:T(8,128)S(1)}, f32[8,128]{1,0:T(8,128)S(1)}) custom-call(f32[16,16,128]{2,1,0:T(8,128)S(1)} %all-to-all-done.fields_ref, bf16[96,4096]{1,0:T(8,128)(2,1)S(1)} %get-tuple-element.86.tall, bf16[256,4096]{1,0:T(8,128)(2,1)S(1)} %get-tuple-element.87.columns, f32[3,192,128]{2,1,0:T(8,128)S(1)} %get-tuple-element.98.e_ref.e_new, ...), custom_call_target="tpu_custom_call" | custom-call | bytes 2097152 | tf_op jit(solution)/shard_map/scatter2/pallas_call | solution.py:47
  36.1 1.9 %collective-permute-start.9 = (f32[2,24,128]{2,1,0:T(8,128)S(1)}, f32[2,24,128]{2,1,0:T(8,128)S(1)}, u32[]{:S(2)}, u32[]{:S(2)}) collective-permute-start(f32[2,24,128]{2,1,0:T(8,128)S(1)} %get-tuple-element.95), channel_id=1, source_target_pairs={{0,16},{16,32},{32,48},{48,64},{64,80},{80,96},{96,112},{112,128},... | collective-permute-start | bytes 73736 | tf_op jit(solution)/shard_map/ppermute | solution.py:603
  37.9 2.7 %drive.1.drives = f32[6,32,128]{2,1,0:T(8,128)S(1)} custom-call(f32[3,192,128]{2,1,0:T(8,128)S(1)} %get-tuple-element.69.e_ref.e_old, f32[3,192,128]{2,1,0:T(8,128)S(1)} %get-tuple-element.98.e_ref.e_new, s32[32,128]{1,0:T(8,128)S(1)} %get-tuple-element.79.placed, bf16[256,4096]{1,0:T(8,128)(2,1)S(1)} %get-tuple-element.87.columns), custom_call_target="tpu_custom_call" | custom-call | bytes 2097152 | tf_op jit(solution)/shard_map/drive/pallas_call | solution.py:47
  40.7 0.9 %collective-permute-done.10.face_y = f32[2,8,128]{2,1,0:T(8,128)S(1)} collective-permute-done((f32[2,8,128]{2,1,0:T(8,128)S(1)}, f32[2,8,128]{2,1,0:T(8,128)S(1)}, u32[]{:S(2)}, u32[]{:S(2)}) %collective-permute-start.10) | collective-permute-done | bytes 8224 | tf_op jit(solution)/shard_map/ppermute | solution.py:603
  41.6 2.6 %collective-permute-done.9.face_x = f32[2,24,128]{2,1,0:T(8,128)S(1)} collective-permute-done((f32[2,24,128]{2,1,0:T(8,128)S(1)}, f32[2,24,128]{2,1,0:T(8,128)S(1)}, u32[]{:S(2)}, u32[]{:S(2)}) %collective-permute-start.9) | collective-permute-done | bytes 24608 | tf_op jit(solution)/shard_map/ppermute | solution.py:603
  44.2 2.0 %final.1 = (f32[3,192,128]{2,1,0:T(8,128)S(1)}, bf16[32,256]{1,0:T(8,128)(2,1)S(1)}, f32[384,128]{1,0:T(8,128)S(1)}) custom-call(f32[3,192,128]{2,1,0:T(8,128)S(1)} %get-tuple-element.98.e_ref.e_new, f32[3,192,128]{2,1,0:T(8,128)S(1)} %get-tuple-element.94.h_ref, f32[2,24,128]{2,1,0:T(8,128)S(1)} %collective-permute-done.9.face_x, ...), custom_call_target="tpu_custom_call" | custom-call | bytes 2097152 | tf_op jit(solution)/shard_map/final/pallas_call | solution.py:47
  46.3 1.2 %keep.1 = f32[384,128]{1,0:T(8,128)S(1)} custom-call(bf16[32,256]{1,0:T(8,128)(2,1)S(1)} %get-tuple-element.108.left, f32[4,128,128]{2,1,0:T(8,128)S(1)} %get-tuple-element.105.starts, f32[2,128,128]{2,1,0:T(8,128)S(1)} %get-tuple-element.106.turn, f32[2,128,128]{2,1,0:T(8,128)S(1)} %get-tuple-element.107.factors), custom_call_target="tpu_custom_call" | custom-call | flops 10000000000 | bytes 2097152 | tf_op jit(solution)/shard_map/keep/pallas_call | solution.py:47
  47.7 10.4 %all_to_all.15.pieces = f32[8,48,128]{2,1,0:T(8,128)S(1)} all-to-all(f32[8,48,128]{2,1,0:T(8,128)S(1)} %bitcast.24), channel_id=1, replica_groups=mesh['gx'=16,'gy'=8,'gz'=2] {'gy'}, dimensions={0} | all-to-all | bytes 393216 | tf_op jit(solution)/shard_map/all_to_all | solution.py:716
  58.2 1.9 %collective-permute-start.14 = (f32[104,128]{1,0:T(8,128)S(1)}, f32[104,128]{1,0:T(8,128)S(1)}, u32[]{:S(2)}, u32[]{:S(2)}) collective-permute-start(f32[104,128]{1,0:T(8,128)S(1)} %get-tuple-element.113), channel_id=1, source_target_pairs={{0,128},{16,144},{32,160},{48,176},{64,192},{80,208},{96,224},{112... | collective-permute-start | bytes 159752 | tf_op jit(solution)/shard_map/ppermute | solution.py:722
  60.1 0.6 collective-permute-start.13
  60.7 1.6 %collective-permute-start.15 = (f32[96,128]{1,0:T(8,128)S(1)}, f32[96,128]{1,0:T(8,128)S(1)}, u32[]{:S(2)}, u32[]{:S(2)}) collective-permute-start(f32[96,128]{1,0:T(8,128)S(1)} %get-tuple-element.114), channel_id=1, source_target_pairs={{0,192},{16,208},{32,224},{48,240},{64,128},{80,144},{96,160},{112... | collective-permute-start | bytes 147464 | tf_op jit(solution)/shard_map/ppermute | solution.py:722
  62.4 1.8 %collective-permute-done.13.one = f32[96,128]{1,0:T(8,128)S(1)} collective-permute-done((f32[96,128]{1,0:T(8,128)S(1)}, f32[96,128]{1,0:T(8,128)S(1)}, u32[]{:S(2)}, u32[]{:S(2)}) %collective-permute-start.13) | collective-permute-done | bytes 49184 | tf_op jit(solution)/shard_map/ppermute | solution.py:722
  64.2 1.8 %collective-permute-done.15.three = f32[96,128]{1,0:T(8,128)S(1)} collective-permute-done((f32[96,128]{1,0:T(8,128)S(1)}, f32[96,128]{1,0:T(8,128)S(1)}, u32[]{:S(2)}, u32[]{:S(2)}) %collective-permute-start.15) | collective-permute-done | bytes 49184 | tf_op jit(solution)/shard_map/ppermute | solution.py:722
  66.1 2.9 %collective-permute-start.17 = (f32[104,128]{1,0:T(8,128)S(1)}, f32[104,128]{1,0:T(8,128)S(1)}, u32[]{:S(2)}, u32[]{:S(2)}) collective-permute-start(f32[104,128]{1,0:T(8,128)S(1)} %get-tuple-element.118), channel_id=1, source_target_pairs={{0,32},{16,48},{32,0},{48,16},{64,96},{80,112},{96,64},{112,80},{1... | collective-permute-start | bytes 159752 | tf_op jit(solution)/shard_map/ppermute | solution.py:734
  69.0 1.7 %collective-permute-start.16 = (f32[96,128]{1,0:T(8,128)S(1)}, f32[96,128]{1,0:T(8,128)S(1)}, u32[]{:S(2)}, u32[]{:S(2)}) collective-permute-start(f32[96,128]{1,0:T(8,128)S(1)} %get-tuple-element.117), channel_id=1, source_target_pairs={{0,16},{16,0},{32,48},{48,32},{64,80},{80,64},{96,112},{112,96},{1... | collective-permute-start | bytes 147464 | tf_op jit(solution)/shard_map/ppermute | solution.py:734
  70.7 1.9 %collective-permute-start.18 = (f32[96,128]{1,0:T(8,128)S(1)}, f32[96,128]{1,0:T(8,128)S(1)}, u32[]{:S(2)}, u32[]{:S(2)}) collective-permute-start(f32[96,128]{1,0:T(8,128)S(1)} %get-tuple-element.119), channel_id=1, source_target_pairs={{0,48},{16,32},{32,16},{48,0},{64,112},{80,96},{96,80},{112,64},{1... | collective-permute-start | bytes 147464 | tf_op jit(solution)/shard_map/ppermute | solution.py:734
  72.7 0.8 store.1
  73.5 2.0 %collective-permute-done.16.one = f32[96,128]{1,0:T(8,128)S(1)} collective-permute-done((f32[96,128]{1,0:T(8,128)S(1)}, f32[96,128]{1,0:T(8,128)S(1)}, u32[]{:S(2)}, u32[]{:S(2)}) %collective-permute-start.16) | collective-permute-done | bytes 49184 | tf_op jit(solution)/shard_map/ppermute | solution.py:734
  75.5 1.5 %collective-permute-done.18.three = f32[96,128]{1,0:T(8,128)S(1)} collective-permute-done((f32[96,128]{1,0:T(8,128)S(1)}, f32[96,128]{1,0:T(8,128)S(1)}, u32[]{:S(2)}, u32[]{:S(2)}) %collective-permute-start.18) | collective-permute-done | bytes 49184 | tf_op jit(solution)/shard_map/ppermute | solution.py:734
  77.1 9.9 %all_to_all.16.far_ref = f32[8,48,128]{2,1,0:T(8,128)S(1)} all-to-all(f32[8,48,128]{2,1,0:T(8,128)S(1)} %get-tuple-element.129), channel_id=1, replica_groups=mesh['gx'=16,'gy'=8,'gz'=2] {'gy'}, dimensions={0} | all-to-all | bytes 393216 | tf_op jit(solution)/shard_map/all_to_all | solution.py:747
  87.0 0.8 atoms.1
  (27 shorter events, 2.1 us)
Async XLA Ops:
  1.7 15.2 %collective-permute-start.2 = (f32[2,192,128]{2,1,0:T(8,128)S(1)}, f32[2,192,128]{2,1,0:T(8,128)S(1)}, u32[]{:S(2)}, u32[]{:S(2)}) collective-permute-start(f32[2,192,128]{2,1,0:T(8,128)S(1)} %get-tuple-element.73), channel_id=1, source_target_pairs={{1,0},{0,1},{3,2},{2,3},{5,4},{4,5},{7,6},{6,7},{9,8},{8,9},{11,10... | collective-permute-start | bytes 589832 | tf_op jit(solution)/shard_map/ppermute | solution.py:603
  1.8 15.1 %collective-permute-start = (f32[2,24,128]{2,1,0:T(8,128)S(1)}, f32[2,24,128]{2,1,0:T(8,128)S(1)}, u32[]{:S(2)}, u32[]{:S(2)}) collective-permute-start(f32[2,24,128]{2,1,0:T(8,128)S(1)} %get-tuple-element.71), channel_id=1, source_target_pairs={{16,0},{32,16},{48,32},{64,48},{80,64},{96,80},{112,96},{128,112},... | collective-permute-start | bytes 73736 | tf_op jit(solution)/shard_map/ppermute | solution.py:603
  10.3 6.5 %collective-permute-start.1 = (f32[2,8,128]{2,1,0:T(8,128)S(1)}, f32[2,8,128]{2,1,0:T(8,128)S(1)}, u32[]{:S(2)}, u32[]{:S(2)}) collective-permute-start(f32[2,8,128]{2,1,0:T(8,128)S(1)} %get-tuple-element.72), channel_id=1, source_target_pairs={{2,0},{4,2},{6,4},{8,6},{10,8},{12,10},{14,12},{0,14},{3,1},{5,3},... | collective-permute-start | bytes 24584 | tf_op jit(solution)/shard_map/ppermute | solution.py:603
  11.5 14.5 %all-to-all-start = ((f32[16,16,128]{2,1,0:T(8,128)}), f32[16,16,128]{2,1,0:T(8,128)S(1)}, u32[]{:S(2)}, u32[]{:S(2)}) async-start(f32[16,16,128]{2,1,0:T(8,128)} %pack.1), calls=%async_computation | async-start | bytes 262144 | tf_op jit(solution)/shard_map/all_to_all | solution.py:620
  17.0 11.5 %collective-permute-start.5 = (f32[2,192,128]{2,1,0:T(8,128)S(1)}, f32[2,192,128]{2,1,0:T(8,128)S(1)}, u32[]{:S(2)}, u32[]{:S(2)}) collective-permute-start(f32[2,192,128]{2,1,0:T(8,128)S(1)} %get-tuple-element.77), channel_id=1, source_target_pairs={{0,1},{1,0},{2,3},{3,2},{4,5},{5,4},{6,7},{7,6},{8,9},{9,8},{10,11... | collective-permute-start | bytes 589832 | tf_op jit(solution)/shard_map/ppermute | solution.py:603
  17.1 11.4 %collective-permute-start.3 = (f32[2,24,128]{2,1,0:T(8,128)S(1)}, f32[2,24,128]{2,1,0:T(8,128)S(1)}, u32[]{:S(2)}, u32[]{:S(2)}) collective-permute-start(f32[2,24,128]{2,1,0:T(8,128)S(1)} %get-tuple-element.75), channel_id=1, source_target_pairs={{0,16},{16,32},{32,48},{48,64},{64,80},{80,96},{96,112},{112,128},... | collective-permute-start | bytes 73736 | tf_op jit(solution)/shard_map/ppermute | solution.py:603
  19.9 8.6 %collective-permute-start.4 = (f32[2,8,128]{2,1,0:T(8,128)S(1)}, f32[2,8,128]{2,1,0:T(8,128)S(1)}, u32[]{:S(2)}, u32[]{:S(2)}) collective-permute-start(f32[2,8,128]{2,1,0:T(8,128)S(1)} %get-tuple-element.76), channel_id=1, source_target_pairs={{0,2},{2,4},{4,6},{6,8},{8,10},{10,12},{12,14},{14,0},{1,3},{3,5},... | collective-permute-start | bytes 24584 | tf_op jit(solution)/shard_map/ppermute | solution.py:603
  28.7 6.9 %collective-permute-start.8 = (f32[2,192,128]{2,1,0:T(8,128)S(1)}, f32[2,192,128]{2,1,0:T(8,128)S(1)}, u32[]{:S(2)}, u32[]{:S(2)}) collective-permute-start(f32[2,192,128]{2,1,0:T(8,128)S(1)} %get-tuple-element.85), channel_id=1, source_target_pairs={{1,0},{0,1},{3,2},{2,3},{5,4},{4,5},{7,6},{6,7},{9,8},{8,9},{11,10... | collective-permute-start | bytes 589832 | tf_op jit(solution)/shard_map/ppermute | solution.py:603
  28.8 6.8 %collective-permute-start.6 = (f32[2,24,128]{2,1,0:T(8,128)S(1)}, f32[2,24,128]{2,1,0:T(8,128)S(1)}, u32[]{:S(2)}, u32[]{:S(2)}) collective-permute-start(f32[2,24,128]{2,1,0:T(8,128)S(1)} %get-tuple-element.83), channel_id=1, source_target_pairs={{16,0},{32,16},{48,32},{64,48},{80,64},{96,80},{112,96},{128,112},... | collective-permute-start | bytes 73736 | tf_op jit(solution)/shard_map/ppermute | solution.py:603
  30.1 5.5 %collective-permute-start.7 = (f32[2,8,128]{2,1,0:T(8,128)S(1)}, f32[2,8,128]{2,1,0:T(8,128)S(1)}, u32[]{:S(2)}, u32[]{:S(2)}) collective-permute-start(f32[2,8,128]{2,1,0:T(8,128)S(1)} %get-tuple-element.84), channel_id=1, source_target_pairs={{2,0},{4,2},{6,4},{8,6},{10,8},{12,10},{14,12},{0,14},{3,1},{5,3},... | collective-permute-start | bytes 24584 | tf_op jit(solution)/shard_map/ppermute | solution.py:603
  35.8 8.4 %collective-permute-start.11 = (f32[2,192,128]{2,1,0:T(8,128)S(1)}, f32[2,192,128]{2,1,0:T(8,128)S(1)}, u32[]{:S(2)}, u32[]{:S(2)}) collective-permute-start(f32[2,192,128]{2,1,0:T(8,128)S(1)} %get-tuple-element.97), channel_id=1, source_target_pairs={{0,1},{1,0},{2,3},{3,2},{4,5},{5,4},{6,7},{7,6},{8,9},{9,8},{10,11... | collective-permute-start | bytes 589832 | tf_op jit(solution)/shard_map/ppermute | solution.py:603
  36.1 8.1 %collective-permute-start.9 = (f32[2,24,128]{2,1,0:T(8,128)S(1)}, f32[2,24,128]{2,1,0:T(8,128)S(1)}, u32[]{:S(2)}, u32[]{:S(2)}) collective-permute-start(f32[2,24,128]{2,1,0:T(8,128)S(1)} %get-tuple-element.95), channel_id=1, source_target_pairs={{0,16},{16,32},{32,48},{48,64},{64,80},{80,96},{96,112},{112,128},... | collective-permute-start | bytes 73736 | tf_op jit(solution)/shard_map/ppermute | solution.py:603
  37.9 3.7 %collective-permute-start.10 = (f32[2,8,128]{2,1,0:T(8,128)S(1)}, f32[2,8,128]{2,1,0:T(8,128)S(1)}, u32[]{:S(2)}, u32[]{:S(2)}) collective-permute-start(f32[2,8,128]{2,1,0:T(8,128)S(1)} %get-tuple-element.96), channel_id=1, source_target_pairs={{0,2},{2,4},{4,6},{6,8},{8,10},{10,12},{12,14},{14,0},{1,3},{3,5},... | collective-permute-start | bytes 24584 | tf_op jit(solution)/shard_map/ppermute | solution.py:603
  46.2 1.5 %collective-permute-start.12 = (f32[384,128]{1,0:T(8,128)S(1)}, f32[384,128]{1,0:T(8,128)S(1)}, u32[]{:S(2)}, u32[]{:S(2)}) collective-permute-start(f32[384,128]{1,0:T(8,128)S(1)} %get-tuple-element.109), channel_id=1, source_target_pairs={{1,0},{0,1},{3,2},{2,3},{5,4},{4,5},{7,6},{6,7},{9,8},{8,9},{11,10... | collective-permute-start | bytes 589832 | tf_op jit(solution)/shard_map/ppermute | solution.py:711
  58.2 7.8 %collective-permute-start.14 = (f32[104,128]{1,0:T(8,128)S(1)}, f32[104,128]{1,0:T(8,128)S(1)}, u32[]{:S(2)}, u32[]{:S(2)}) collective-permute-start(f32[104,128]{1,0:T(8,128)S(1)} %get-tuple-element.113), channel_id=1, source_target_pairs={{0,128},{16,144},{32,160},{48,176},{64,192},{80,208},{96,224},{112... | collective-permute-start | bytes 159752 | tf_op jit(solution)/shard_map/ppermute | solution.py:722
  60.1 4.1 %collective-permute-start.13 = (f32[96,128]{1,0:T(8,128)S(1)}, f32[96,128]{1,0:T(8,128)S(1)}, u32[]{:S(2)}, u32[]{:S(2)}) collective-permute-start(f32[96,128]{1,0:T(8,128)S(1)} %get-tuple-element.112), channel_id=1, source_target_pairs={{0,64},{16,80},{32,96},{48,112},{64,0},{80,16},{96,32},{112,48},{1... | collective-permute-start | bytes 147464 | tf_op jit(solution)/shard_map/ppermute | solution.py:722
  60.7 5.3 %collective-permute-start.15 = (f32[96,128]{1,0:T(8,128)S(1)}, f32[96,128]{1,0:T(8,128)S(1)}, u32[]{:S(2)}, u32[]{:S(2)}) collective-permute-start(f32[96,128]{1,0:T(8,128)S(1)} %get-tuple-element.114), channel_id=1, source_target_pairs={{0,192},{16,208},{32,224},{48,240},{64,128},{80,144},{96,160},{112... | collective-permute-start | bytes 147464 | tf_op jit(solution)/shard_map/ppermute | solution.py:722
  66.1 11.0 %collective-permute-start.17 = (f32[104,128]{1,0:T(8,128)S(1)}, f32[104,128]{1,0:T(8,128)S(1)}, u32[]{:S(2)}, u32[]{:S(2)}) collective-permute-start(f32[104,128]{1,0:T(8,128)S(1)} %get-tuple-element.118), channel_id=1, source_target_pairs={{0,32},{16,48},{32,0},{48,16},{64,96},{80,112},{96,64},{112,80},{1... | collective-permute-start | bytes 159752 | tf_op jit(solution)/shard_map/ppermute | solution.py:734
  69.0 6.5 %collective-permute-start.16 = (f32[96,128]{1,0:T(8,128)S(1)}, f32[96,128]{1,0:T(8,128)S(1)}, u32[]{:S(2)}, u32[]{:S(2)}) collective-permute-start(f32[96,128]{1,0:T(8,128)S(1)} %get-tuple-element.117), channel_id=1, source_target_pairs={{0,16},{16,0},{32,48},{48,32},{64,80},{80,64},{96,112},{112,96},{1... | collective-permute-start | bytes 147464 | tf_op jit(solution)/shard_map/ppermute | solution.py:734
  70.7 6.3 %collective-permute-start.18 = (f32[96,128]{1,0:T(8,128)S(1)}, f32[96,128]{1,0:T(8,128)S(1)}, u32[]{:S(2)}, u32[]{:S(2)}) collective-permute-start(f32[96,128]{1,0:T(8,128)S(1)} %get-tuple-element.119), channel_id=1, source_target_pairs={{0,48},{16,32},{32,16},{48,0},{64,112},{80,96},{96,80},{112,64},{1... | collective-permute-start | bytes 147464 | tf_op jit(solution)/shard_map/ppermute | solution.py:734

commit v12 on v11

--- a/solution.py
+++ b/solution.py
@@ -218,18 +218,30 @@
         dense[field, pl.ds(1, HALF, 2), :] = got[:, CZ:]
 
 
-def scatter_kernel(placed, fields_ref, dense, tall, columns, spots):
+def scatter_kernel(placed, columns, fields_ref, dense, tall, spots):
     for slot in range(SLOTS):
         line = placed[slot : slot + 1]
         across = slice(slot * CZ, (slot + 1) * CZ)
-        columns[:, across] = wide_hits(line, CZ)
         tall[:, across] = tall_hits(line, CZ).astype(F32).astype(BF16)
     place_fields(0, fields_ref, dense, tall, spots, columns)
 
 
 def scatter_sample_kernel(
-    fields_ref, tall, columns, e_ref, h_ref, surf_ref, dense, sampled, spots
+    fields_ref,
+    tall,
+    columns,
+    e_ref,
+    h_ref,
+    surf_ref,
+    units_ref,
+    dense,
+    sampled,
+    starts,
+    turn,
+    factors,
+    spots,
 ):
+    phase_tables(surf_ref, units_ref, starts, turn, factors)
     place_fields(4, fields_ref, dense, tall, spots, columns)
     sample_rows(e_ref, h_ref, surf_ref, sampled)
 
@@ -303,56 +315,13 @@
     return (left[0] * right[0] - left[1] * right[1], left[1] * right[0] + left[0] * right[1])
 
 
-def phase_kernel(
-    count_ref,
-    owner_hbm,
-    offsets_hbm,
-    surf_hbm,
-    units_hbm,
-    h_hbm,
-    eps_hbm,
-    pump_hbm,
-    far_hbm,
-    placed,
-    surf_out,
-    starts,
-    turn,
-    factors,
-    h_out,
-    eps_out,
-    pump_out,
-    far_out,
-    owner_ref,
-    offsets_ref,
-    units_ref,
-    sems,
-):
-    own = pl.ds(pl.multiple_of(FAR * lax.axis_index("gy"), 8), FAR)
-    copies = [
-        pltpu.make_async_copy(source, target, sems.at[place])
-        for place, (source, target) in enumerate(
-            (
-                (surf_hbm, surf_out),
-                (units_hbm, units_ref),
-                (owner_hbm, owner_ref),
-                (offsets_hbm, offsets_ref),
-                (h_hbm, h_out),
-                (eps_hbm, eps_out),
-                (pump_hbm, pump_out),
-                (far_hbm.at[own], far_out),
-            )
-        )
-    ]
-    for copy in copies:
-        copy.start()
+def phase_tables(surf_ref, units_ref, starts, turn, factors):
     lanes = lax.broadcasted_iota(jnp.int32, (8, DIRS), 1)
     omega = freq_low + freq_pitch * (lanes & (FREQ - 1)).astype(F32)
     moment = omega * jnp.where(lanes < FREQ, time_step, 2.0 * time_step)
     for place, value in enumerate((jnp.cos(moment), jnp.sin(moment))):
         factors[place] = jnp.transpose(jnp.broadcast_to(value[0:1], (DIRS, DIRS)))
-    copies[0].wait()
-    copies[1].wait()
-    cells = surf_out[...]
+    cells = surf_ref[...]
     rows = cells >> 7
     layer = (rows * 2731) >> 16
     cell_x = lax.axis_index("gx") * CX + layer
@@ -380,12 +349,53 @@
     turn[0], turn[1] = powers[1]
     starts[0], starts[1] = low_start
     starts[2], starts[3] = high_start
-    for copy in copies[2:]:
+
+
+def phase_kernel(
+    count_ref,
+    owner_hbm,
+    offsets_hbm,
+    surf_hbm,
+    h_hbm,
+    eps_hbm,
+    pump_hbm,
+    far_hbm,
+    placed,
+    columns,
+    surf_out,
+    h_out,
+    eps_out,
+    pump_out,
+    far_out,
+    owner_ref,
+    offsets_ref,
+    sems,
+):
+    own = pl.ds(pl.multiple_of(FAR * lax.axis_index("gy"), 8), FAR)
+    copies = [
+        pltpu.make_async_copy(source, target, sems.at[place])
+        for place, (source, target) in enumerate(
+            (
+                (surf_hbm, surf_out),
+                (owner_hbm, owner_ref),
+                (offsets_hbm, offsets_ref),
+                (h_hbm, h_out),
+                (eps_hbm, eps_out),
+                (pump_hbm, pump_out),
+                (far_hbm.at[own], far_out),
+            )
+        )
+    ]
+    for copy in copies:
+        copy.start()
+    for copy in copies:
         copy.wait()
     count = count_ref[0]
     for slot in range(SLOTS):
         line = offsets_ref[slot : slot + 1]
         placed[pl.ds(owner_ref[0, slot], 1)] = jnp.where(slot < count, line, -1)
+    for slot in range(SLOTS):
+        columns[:, slot * CZ : (slot + 1) * CZ] = wide_hits(placed[slot : slot + 1], CZ)
 
 
 FAR = 48
@@ -618,14 +628,12 @@
     near = shifted(near, down)
     packed = call(pack_kernel, shape(SLOTS // 2, 16, CZ), (state,), name="pack")
     fields = lax.all_to_all(packed, "gx", 0, 0, tiled=True)
-    placed, surf, starts, turn, factors, h_old, eps, pumps, far_part = call(
+    placed, columns, surf, h_old, eps, pumps, far_part = call(
         phase_kernel,
         (
             shape(SLOTS, CZ, dtype=jnp.int32),
+            shape(WIDE, SLOTS * CZ, dtype=BF16),
             shape(1, CZ, dtype=jnp.int32),
-            shape(4, CZ, DIRS),
-            shape(2, CZ, DIRS),
-            shape(2, STEPS * FREQ, DIRS),
             dense,
             shape(ROWS, CZ),
             shape(SLOTS, CZ),
@@ -636,18 +644,16 @@
             block_owner.reshape(1, SLOTS),
             gain_offsets.reshape(SLOTS, CZ),
             surf_offsets.reshape(1, CZ),
-            jnp.asarray(directions(DIRS)),
             hfield.reshape(3, ROWS, CZ),
             inv_eps.reshape(ROWS, CZ),
             pump.reshape(SLOTS, CZ),
             jnp.transpose(far_acc, (1, 0, 2)).reshape(8 * FAR, DIRS),
         ),
-        in_specs=[pl.BlockSpec(memory_space=pltpu.SMEM)] + [hbm] * 8,
+        in_specs=[pl.BlockSpec(memory_space=pltpu.SMEM)] + [hbm] * 7,
         scratch=[
             pltpu.SMEM((1, SLOTS), jnp.int32),
             pltpu.VMEM((SLOTS, CZ), jnp.int32),
-            pltpu.VMEM((8, DIRS), F32),
-            pltpu.SemaphoreType.DMA((8,)),
+            pltpu.SemaphoreType.DMA((7,)),
         ],
         moved=MIB // 4,
         name="phase",
@@ -662,14 +668,10 @@
     )
     edge = shifted(edge, up)
     spots = pltpu.VMEM((8 * HALF, SLOTS * CZ), BF16)
-    spread_now, tall, columns = call(
+    spread_now, tall = call(
         scatter_kernel,
-        (
-            shape(4, ROWS, CZ),
-            shape(HALF, SLOTS * CZ, dtype=BF16),
-            shape(WIDE, SLOTS * CZ, dtype=BF16),
-        ),
-        (placed, fields),
+        (shape(4, ROWS, CZ), shape(HALF, SLOTS * CZ, dtype=BF16)),
+        (placed, columns, fields),
         scratch=[spots],
         name="scatter",
     )
@@ -680,10 +682,16 @@
         name="electric",
     )
     near = shifted(near, down)
-    spread_next, early = call(
+    spread_next, early, starts, turn, factors = call(
         scatter_sample_kernel,
-        (shape(4, ROWS, CZ), shape(8, CZ)),
-        (fields, tall, columns, e_one, h_one, surf),
+        (
+            shape(4, ROWS, CZ),
+            shape(8, CZ),
+            shape(4, CZ, DIRS),
+            shape(2, CZ, DIRS),
+            shape(2, STEPS * FREQ, DIRS),
+        ),
+        [fields, tall, columns, e_one, h_one, surf] + stay(jnp.asarray(directions(DIRS))),
         scratch=[spots],
         name="scatter2",
     )

time: 88 us -> 88.9 us (1.010)
  Pallas kernels: 15.5 us -> 17.6 us
    pallas_call x16, Pallas kernels: 15.5 us -> 17.6 us  [call(): pl.pallas_call(kernel, out_shape=outs, in_specs=in_specs or [pl.BlockSpec...]
    all_to_all x1, waiting for transfers between devices: 4.54 us -> 3.14 us  [local(): fields = lax.all_to_all(packed, 'gx', 0, 0, tiled=True)]
    ppermute x12, waiting for transfers between devices: 3.53 us -> 4.79 us  [shifted(): lax.ppermute(part, axis, perm)]
  transfers between devices with their start and end apart: 20 -> 20, of which waited for: 8 -> 8; matrix products, arithmetic and copies ran while one was open for 0% -> 0% of each run, Pallas kernels for 13% -> 15%
where the time goes in v12:
time: 88.9 us; the launch traced here: 88.5 us
  starting transfers between devices  34.7 us (39%)
  blocking collectives  19.8 us (22%)
  Pallas kernels  17.6 us (20%)
  waiting for transfers between devices  14.9 us (17%)
  between operations  1.47 us (2%)
    ppermute x12, starting transfers between devices, shifted(): lax.ppermute(part, axis, perm)  20.3 us
    pallas_call x16, Pallas kernels, call(): pl.pallas_call(kernel, out_shape=outs, in_specs=in_specs or [pl.BlockSpec...  17.6 us
    all_to_all x1, blocking collectives, local(): pieces = lax.all_to_all(chip.reshape(8, FAR, DIRS), 'gy', 0, 0, tiled=True)  10.1 us
    all_to_all x1, blocking collectives, local(): gathered = lax.all_to_all(copies, 'gy', 0, 0, tiled=True)  9.71 us
    ppermute x3, starting transfers between devices, local(): lax.ppermute(value, 'gx', [(a * 4 + z, a * 4 + (z ^ k)) for a in range(4)...  6.58 us
    ppermute x12, waiting for transfers between devices, shifted(): lax.ppermute(part, axis, perm)  4.79 us
    ppermute x3, starting transfers between devices, local(): lax.ppermute(value, 'gx', [(a * 4 + z, (a ^ k) * 4 + z) for a in range(4)...  4.18 us
    ppermute x3, waiting for transfers between devices, local(): lax.ppermute(value, 'gx', [(a * 4 + z, (a ^ k) * 4 + z) for a in range(4)...  3.72 us
  transfers between devices with their start and end apart: 20, of which 8 were waited for; matrix products, arithmetic and copies ran while one was open for 0% of the time, Pallas kernels for 15%

profile of v12, /device:TPU:8, one launch (start us, length us, event | category | flops | bytes accessed | tf_op | source)
XLA Modules:
  0.0 88.5 jit_solution(16525578666955660224)
XLA Ops:
  0.6 1.0 %prepare.1 = (f32[2,24,128]{2,1,0:T(8,128)S(1)}, f32[2,8,128]{2,1,0:T(8,128)S(1)}, f32[2,192,128]{2,1,0:T(8,128)S(1)}, f32[3,192,128]{2,1,0:T(8,128)S(1)}, f32[10,32,128]{2,1,0:T(8,128)S(1)}) custom-call(f32[3,192,128]{2,1,0:T(8,128)} %bitcast.25, f32[10,32,128]{2,1,0:T(8,128)} %bitcast.28), custom_call_target="tpu_custom_call" | custom-call | bytes 2097152 | tf_op jit(solution)/shard_map/prepare/pallas_call | solution.py:47
  1.8 8.6 %collective-permute-start = (f32[2,24,128]{2,1,0:T(8,128)S(1)}, f32[2,24,128]{2,1,0:T(8,128)S(1)}, u32[]{:S(2)}, u32[]{:S(2)}) collective-permute-start(f32[2,24,128]{2,1,0:T(8,128)S(1)} %get-tuple-element.71), channel_id=1, source_target_pairs={{16,0},{32,16},{48,32},{64,48},{80,64},{96,80},{112,96},{128,112},... | collective-permute-start | bytes 73736 | tf_op jit(solution)/shard_map/ppermute | solution.py:613
  10.8 0.7 pack.1
  11.5 3.5 %all-to-all-start = ((f32[16,16,128]{2,1,0:T(8,128)}), f32[16,16,128]{2,1,0:T(8,128)S(1)}, u32[]{:S(2)}, u32[]{:S(2)}) async-start(f32[16,16,128]{2,1,0:T(8,128)} %pack.1), calls=%async_computation | async-start | bytes 262144 | tf_op jit(solution)/shard_map/all_to_all | solution.py:630
  15.6 2.1 %phase.1 = (s32[32,128]{1,0:T(8,128)S(1)}, bf16[256,4096]{1,0:T(8,128)(2,1)S(1)}, s32[1,128]{1,0:T(1,128)S(1)}, f32[3,192,128]{2,1,0:T(8,128)S(1)}, f32[192,128]...) custom-call(s32[1]{0:T(128)} %bitcast.23.count_ref, s32[1,32]{1,0:T(1,128)} %bitcast.32, ...), custom_call_target="tpu_custom_call" | custom-call | bytes 262144 | tf_op jit(solution)/shard_map/phase/pallas_call | solution.py:47
  17.7 0.8 magnetic.1
  18.6 2.7 %collective-permute-start.3 = (f32[2,24,128]{2,1,0:T(8,128)S(1)}, f32[2,24,128]{2,1,0:T(8,128)S(1)}, u32[]{:S(2)}, u32[]{:S(2)}) collective-permute-start(f32[2,24,128]{2,1,0:T(8,128)S(1)} %get-tuple-element.75), channel_id=1, source_target_pairs={{0,16},{16,32},{32,48},{48,64},{64,80},{80,96},{96,112},{112,128},... | collective-permute-start | bytes 73736 | tf_op jit(solution)/shard_map/ppermute | solution.py:613
  21.3 1.6 %collective-permute-start.4 = (f32[2,8,128]{2,1,0:T(8,128)S(1)}, f32[2,8,128]{2,1,0:T(8,128)S(1)}, u32[]{:S(2)}, u32[]{:S(2)}) collective-permute-start(f32[2,8,128]{2,1,0:T(8,128)S(1)} %get-tuple-element.76), channel_id=1, source_target_pairs={{0,2},{2,4},{4,6},{6,8},{8,10},{10,12},{12,14},{14,0},{1,3},{3,5},... | collective-permute-start | bytes 24584 | tf_op jit(solution)/shard_map/ppermute | solution.py:613
  22.9 3.1 %all-to-all-done.fields_ref = f32[16,16,128]{2,1,0:T(8,128)S(1)} async-done(((f32[16,16,128]{2,1,0:T(8,128)}), f32[16,16,128]{2,1,0:T(8,128)S(1)}, u32[]{:S(2)}, u32[]{:S(2)}) %all-to-all-start) | async-done | bytes 131104 | tf_op jit(solution)/shard_map/all_to_all | solution.py:630
  26.0 2.2 %scatter.1 = (f32[4,192,128]{2,1,0:T(8,128)S(1)}, bf16[96,4096]{1,0:T(8,128)(2,1)S(1)}) custom-call(s32[32,128]{1,0:T(8,128)S(1)} %get-tuple-element.79.placed, bf16[256,4096]{1,0:T(8,128)(2,1)S(1)} %get-tuple-element.80.columns, f32[16,16,128]{2,1,0:T(8,128)S(1)} %all-to-all-done.fields_ref), custom_call_target="tpu_custom_call" | custom-call | bytes 2097152 | tf_op jit(solution)/shard_map/scatter/pallas_call | solution.py:47
  28.6 1.8 %collective-permute-start.6 = (f32[2,24,128]{2,1,0:T(8,128)S(1)}, f32[2,24,128]{2,1,0:T(8,128)S(1)}, u32[]{:S(2)}, u32[]{:S(2)}) collective-permute-start(f32[2,24,128]{2,1,0:T(8,128)S(1)} %get-tuple-element.84), channel_id=1, source_target_pairs={{16,0},{32,16},{48,32},{64,48},{80,64},{96,80},{112,96},{128,112},... | collective-permute-start | bytes 73736 | tf_op jit(solution)/shard_map/ppermute | solution.py:613
  30.4 4.2 %collective-permute-start.7 = (f32[2,8,128]{2,1,0:T(8,128)S(1)}, f32[2,8,128]{2,1,0:T(8,128)S(1)}, u32[]{:S(2)}, u32[]{:S(2)}) collective-permute-start(f32[2,8,128]{2,1,0:T(8,128)S(1)} %get-tuple-element.85), channel_id=1, source_target_pairs={{2,0},{4,2},{6,4},{8,6},{10,8},{12,10},{14,12},{0,14},{3,1},{5,3},... | collective-permute-start | bytes 24584 | tf_op jit(solution)/shard_map/ppermute | solution.py:613
  34.5 2.8 %scatter2.1 = (f32[4,192,128]{2,1,0:T(8,128)S(1)}, f32[8,128]{1,0:T(8,128)S(1)}, f32[4,128,128]{2,1,0:T(8,128)S(1)}, f32[2,128,128]{2,1,0:T(8,128)S(1)}, f32[2,128,128]{2,1,0:T(8,128)S(1)}) custom-call(f32[16,16,128]{2,1,0:T(8,128)S(1)} %all-to-all-done.fields_ref, bf16[96,4096]{1,0:T(8,128)(2,1)S(1)} %get-tuple-element.87.tall, ...), custom_call_target="tpu_custom_call" | custom-call | bytes 2097152 | tf_op jit(solution)/shard_map/scatter2/pallas_call | solution.py:47
  37.8 0.6 collective-permute-start.9
  38.4 2.7 %drive.1.drives = f32[6,32,128]{2,1,0:T(8,128)S(1)} custom-call(f32[3,192,128]{2,1,0:T(8,128)S(1)} %get-tuple-element.69.e_ref.e_old, f32[3,192,128]{2,1,0:T(8,128)S(1)} %get-tuple-element.98.e_ref.e_new, s32[32,128]{1,0:T(8,128)S(1)} %get-tuple-element.79.placed, bf16[256,4096]{1,0:T(8,128)(2,1)S(1)} %get-tuple-element.80.columns), custom_call_target="tpu_custom_call" | custom-call | bytes 2097152 | tf_op jit(solution)/shard_map/drive/pallas_call | solution.py:47
  41.2 1.6 %collective-permute-done.10.face_y = f32[2,8,128]{2,1,0:T(8,128)S(1)} collective-permute-done((f32[2,8,128]{2,1,0:T(8,128)S(1)}, f32[2,8,128]{2,1,0:T(8,128)S(1)}, u32[]{:S(2)}, u32[]{:S(2)}) %collective-permute-start.10) | collective-permute-done | bytes 8224 | tf_op jit(solution)/shard_map/ppermute | solution.py:613
  42.8 3.1 %collective-permute-done.9.face_x = f32[2,24,128]{2,1,0:T(8,128)S(1)} collective-permute-done((f32[2,24,128]{2,1,0:T(8,128)S(1)}, f32[2,24,128]{2,1,0:T(8,128)S(1)}, u32[]{:S(2)}, u32[]{:S(2)}) %collective-permute-start.9) | collective-permute-done | bytes 24608 | tf_op jit(solution)/shard_map/ppermute | solution.py:613
  45.9 2.0 %final.1 = (f32[3,192,128]{2,1,0:T(8,128)S(1)}, bf16[32,256]{1,0:T(8,128)(2,1)S(1)}, f32[384,128]{1,0:T(8,128)S(1)}) custom-call(f32[3,192,128]{2,1,0:T(8,128)S(1)} %get-tuple-element.98.e_ref.e_new, f32[3,192,128]{2,1,0:T(8,128)S(1)} %get-tuple-element.94.h_ref, f32[2,24,128]{2,1,0:T(8,128)S(1)} %collective-permute-done.9.face_x, ...), custom_call_target="tpu_custom_call" | custom-call | bytes 2097152 | tf_op jit(solution)/shard_map/final/pallas_call | solution.py:47
  48.1 1.2 %keep.1 = f32[384,128]{1,0:T(8,128)S(1)} custom-call(bf16[32,256]{1,0:T(8,128)(2,1)S(1)} %get-tuple-element.108.left, f32[4,128,128]{2,1,0:T(8,128)S(1)} %get-tuple-element.105.starts, f32[2,128,128]{2,1,0:T(8,128)S(1)} %get-tuple-element.106.turn, f32[2,128,128]{2,1,0:T(8,128)S(1)} %get-tuple-element.107.factors), custom_call_target="tpu_custom_call" | custom-call | flops 10000000000 | bytes 2097152 | tf_op jit(solution)/shard_map/keep/pallas_call | solution.py:47
  49.5 10.1 %all_to_all.15.pieces = f32[8,48,128]{2,1,0:T(8,128)S(1)} all-to-all(f32[8,48,128]{2,1,0:T(8,128)S(1)} %bitcast.24), channel_id=1, replica_groups=mesh['gx'=16,'gy'=8,'gz'=2] {'gy'}, dimensions={0} | all-to-all | bytes 393216 | tf_op jit(solution)/shard_map/all_to_all | solution.py:724
  59.6 2.0 %collective-permute-start.14 = (f32[104,128]{1,0:T(8,128)S(1)}, f32[104,128]{1,0:T(8,128)S(1)}, u32[]{:S(2)}, u32[]{:S(2)}) collective-permute-start(f32[104,128]{1,0:T(8,128)S(1)} %get-tuple-element.113), channel_id=1, source_target_pairs={{0,128},{16,144},{32,160},{48,176},{64,192},{80,208},{96,224},{112... | collective-permute-start | bytes 159752 | tf_op jit(solution)/shard_map/ppermute | solution.py:730
  61.6 0.6 collective-permute-start.13
  62.2 1.6 %collective-permute-start.15 = (f32[96,128]{1,0:T(8,128)S(1)}, f32[96,128]{1,0:T(8,128)S(1)}, u32[]{:S(2)}, u32[]{:S(2)}) collective-permute-start(f32[96,128]{1,0:T(8,128)S(1)} %get-tuple-element.114), channel_id=1, source_target_pairs={{0,192},{16,208},{32,224},{48,240},{64,128},{80,144},{96,160},{112... | collective-permute-start | bytes 147464 | tf_op jit(solution)/shard_map/ppermute | solution.py:730
  63.8 1.9 %collective-permute-done.13.one = f32[96,128]{1,0:T(8,128)S(1)} collective-permute-done((f32[96,128]{1,0:T(8,128)S(1)}, f32[96,128]{1,0:T(8,128)S(1)}, u32[]{:S(2)}, u32[]{:S(2)}) %collective-permute-start.13) | collective-permute-done | bytes 49184 | tf_op jit(solution)/shard_map/ppermute | solution.py:730
  65.7 1.8 %collective-permute-done.15.three = f32[96,128]{1,0:T(8,128)S(1)} collective-permute-done((f32[96,128]{1,0:T(8,128)S(1)}, f32[96,128]{1,0:T(8,128)S(1)}, u32[]{:S(2)}, u32[]{:S(2)}) %collective-permute-start.15) | collective-permute-done | bytes 49184 | tf_op jit(solution)/shard_map/ppermute | solution.py:730
  67.6 2.7 %collective-permute-start.17 = (f32[104,128]{1,0:T(8,128)S(1)}, f32[104,128]{1,0:T(8,128)S(1)}, u32[]{:S(2)}, u32[]{:S(2)}) collective-permute-start(f32[104,128]{1,0:T(8,128)S(1)} %get-tuple-element.118), channel_id=1, source_target_pairs={{0,32},{16,48},{32,0},{48,16},{64,96},{80,112},{96,64},{112,80},{1... | collective-permute-start | bytes 159752 | tf_op jit(solution)/shard_map/ppermute | solution.py:742
  70.2 1.4 %collective-permute-start.16 = (f32[96,128]{1,0:T(8,128)S(1)}, f32[96,128]{1,0:T(8,128)S(1)}, u32[]{:S(2)}, u32[]{:S(2)}) collective-permute-start(f32[96,128]{1,0:T(8,128)S(1)} %get-tuple-element.117), channel_id=1, source_target_pairs={{0,16},{16,0},{32,48},{48,32},{64,80},{80,64},{96,112},{112,96},{1... | collective-permute-start | bytes 147464 | tf_op jit(solution)/shard_map/ppermute | solution.py:742
  71.6 2.6 %collective-permute-start.18 = (f32[96,128]{1,0:T(8,128)S(1)}, f32[96,128]{1,0:T(8,128)S(1)}, u32[]{:S(2)}, u32[]{:S(2)}) collective-permute-start(f32[96,128]{1,0:T(8,128)S(1)} %get-tuple-element.119), channel_id=1, source_target_pairs={{0,48},{16,32},{32,16},{48,0},{64,112},{80,96},{96,80},{112,64},{1... | collective-permute-start | bytes 147464 | tf_op jit(solution)/shard_map/ppermute | solution.py:742
  74.2 0.8 store.1
  75.2 2.8 %collective-permute-done.18.three = f32[96,128]{1,0:T(8,128)S(1)} collective-permute-done((f32[96,128]{1,0:T(8,128)S(1)}, f32[96,128]{1,0:T(8,128)S(1)}, u32[]{:S(2)}, u32[]{:S(2)}) %collective-permute-start.18) | collective-permute-done | bytes 49184 | tf_op jit(solution)/shard_map/ppermute | solution.py:742
  78.1 9.7 %all_to_all.16.far_ref = f32[8,48,128]{2,1,0:T(8,128)S(1)} all-to-all(f32[8,48,128]{2,1,0:T(8,128)S(1)} %get-tuple-element.129), channel_id=1, replica_groups=mesh['gx'=16,'gy'=8,'gz'=2] {'gy'}, dimensions={0} | all-to-all | bytes 393216 | tf_op jit(solution)/shard_map/all_to_all | solution.py:755
  87.8 0.8 atoms.1
  (27 shorter events, 2.1 us)
Async XLA Ops:
  1.7 16.1 %collective-permute-start.2 = (f32[2,192,128]{2,1,0:T(8,128)S(1)}, f32[2,192,128]{2,1,0:T(8,128)S(1)}, u32[]{:S(2)}, u32[]{:S(2)}) collective-permute-start(f32[2,192,128]{2,1,0:T(8,128)S(1)} %get-tuple-element.73), channel_id=1, source_target_pairs={{1,0},{0,1},{3,2},{2,3},{5,4},{4,5},{7,6},{6,7},{9,8},{8,9},{11,10... | collective-permute-start | bytes 589832 | tf_op jit(solution)/shard_map/ppermute | solution.py:613
  1.8 16.0 %collective-permute-start = (f32[2,24,128]{2,1,0:T(8,128)S(1)}, f32[2,24,128]{2,1,0:T(8,128)S(1)}, u32[]{:S(2)}, u32[]{:S(2)}) collective-permute-start(f32[2,24,128]{2,1,0:T(8,128)S(1)} %get-tuple-element.71), channel_id=1, source_target_pairs={{16,0},{32,16},{48,32},{64,48},{80,64},{96,80},{112,96},{128,112},... | collective-permute-start | bytes 73736 | tf_op jit(solution)/shard_map/ppermute | solution.py:613
  10.3 7.4 %collective-permute-start.1 = (f32[2,8,128]{2,1,0:T(8,128)S(1)}, f32[2,8,128]{2,1,0:T(8,128)S(1)}, u32[]{:S(2)}, u32[]{:S(2)}) collective-permute-start(f32[2,8,128]{2,1,0:T(8,128)S(1)} %get-tuple-element.72), channel_id=1, source_target_pairs={{2,0},{4,2},{6,4},{8,6},{10,8},{12,10},{14,12},{0,14},{3,1},{5,3},... | collective-permute-start | bytes 24584 | tf_op jit(solution)/shard_map/ppermute | solution.py:613
  11.5 14.5 %all-to-all-start = ((f32[16,16,128]{2,1,0:T(8,128)}), f32[16,16,128]{2,1,0:T(8,128)S(1)}, u32[]{:S(2)}, u32[]{:S(2)}) async-start(f32[16,16,128]{2,1,0:T(8,128)} %pack.1), calls=%async_computation | async-start | bytes 262144 | tf_op jit(solution)/shard_map/all_to_all | solution.py:630
  18.6 9.7 %collective-permute-start.5 = (f32[2,192,128]{2,1,0:T(8,128)}, f32[2,192,128]{2,1,0:T(8,128)S(1)}, u32[]{:S(2)}, u32[]{:S(2)}) collective-permute-start(f32[2,192,128]{2,1,0:T(8,128)} %get-tuple-element.77), channel_id=1, source_target_pairs={{0,1},{1,0},{2,3},{3,2},{4,5},{5,4},{6,7},{7,6},{8,9},{9,8},{10,11... | collective-permute-start | bytes 589832 | tf_op jit(solution)/shard_map/ppermute | solution.py:613
  18.6 9.7 %collective-permute-start.3 = (f32[2,24,128]{2,1,0:T(8,128)S(1)}, f32[2,24,128]{2,1,0:T(8,128)S(1)}, u32[]{:S(2)}, u32[]{:S(2)}) collective-permute-start(f32[2,24,128]{2,1,0:T(8,128)S(1)} %get-tuple-element.75), channel_id=1, source_target_pairs={{0,16},{16,32},{32,48},{48,64},{64,80},{80,96},{96,112},{112,128},... | collective-permute-start | bytes 73736 | tf_op jit(solution)/shard_map/ppermute | solution.py:613
  21.3 6.9 %collective-permute-start.4 = (f32[2,8,128]{2,1,0:T(8,128)S(1)}, f32[2,8,128]{2,1,0:T(8,128)S(1)}, u32[]{:S(2)}, u32[]{:S(2)}) collective-permute-start(f32[2,8,128]{2,1,0:T(8,128)S(1)} %get-tuple-element.76), channel_id=1, source_target_pairs={{0,2},{2,4},{4,6},{6,8},{8,10},{10,12},{12,14},{14,0},{1,3},{3,5},... | collective-permute-start | bytes 24584 | tf_op jit(solution)/shard_map/ppermute | solution.py:613
  28.5 8.8 %collective-permute-start.8 = (f32[2,192,128]{2,1,0:T(8,128)S(1)}, f32[2,192,128]{2,1,0:T(8,128)S(1)}, u32[]{:S(2)}, u32[]{:S(2)}) collective-permute-start(f32[2,192,128]{2,1,0:T(8,128)S(1)} %get-tuple-element.86), channel_id=1, source_target_pairs={{1,0},{0,1},{3,2},{2,3},{5,4},{4,5},{7,6},{6,7},{9,8},{8,9},{11,10... | collective-permute-start | bytes 589832 | tf_op jit(solution)/shard_map/ppermute | solution.py:613
  28.6 8.7 %collective-permute-start.6 = (f32[2,24,128]{2,1,0:T(8,128)S(1)}, f32[2,24,128]{2,1,0:T(8,128)S(1)}, u32[]{:S(2)}, u32[]{:S(2)}) collective-permute-start(f32[2,24,128]{2,1,0:T(8,128)S(1)} %get-tuple-element.84), channel_id=1, source_target_pairs={{16,0},{32,16},{48,32},{64,48},{80,64},{96,80},{112,96},{128,112},... | collective-permute-start | bytes 73736 | tf_op jit(solution)/shard_map/ppermute | solution.py:613
  30.4 7.0 %collective-permute-start.7 = (f32[2,8,128]{2,1,0:T(8,128)S(1)}, f32[2,8,128]{2,1,0:T(8,128)S(1)}, u32[]{:S(2)}, u32[]{:S(2)}) collective-permute-start(f32[2,8,128]{2,1,0:T(8,128)S(1)} %get-tuple-element.85), channel_id=1, source_target_pairs={{2,0},{4,2},{6,4},{8,6},{10,8},{12,10},{14,12},{0,14},{3,1},{5,3},... | collective-permute-start | bytes 24584 | tf_op jit(solution)/shard_map/ppermute | solution.py:613
  37.5 8.4 %collective-permute-start.11 = (f32[2,192,128]{2,1,0:T(8,128)S(1)}, f32[2,192,128]{2,1,0:T(8,128)S(1)}, u32[]{:S(2)}, u32[]{:S(2)}) collective-permute-start(f32[2,192,128]{2,1,0:T(8,128)S(1)} %get-tuple-element.97), channel_id=1, source_target_pairs={{0,1},{1,0},{2,3},{3,2},{4,5},{5,4},{6,7},{7,6},{8,9},{9,8},{10,11... | collective-permute-start | bytes 589832 | tf_op jit(solution)/shard_map/ppermute | solution.py:613
  37.8 8.1 %collective-permute-start.9 = (f32[2,24,128]{2,1,0:T(8,128)S(1)}, f32[2,24,128]{2,1,0:T(8,128)S(1)}, u32[]{:S(2)}, u32[]{:S(2)}) collective-permute-start(f32[2,24,128]{2,1,0:T(8,128)S(1)} %get-tuple-element.95), channel_id=1, source_target_pairs={{0,16},{16,32},{32,48},{48,64},{64,80},{80,96},{96,112},{112,128},... | collective-permute-start | bytes 73736 | tf_op jit(solution)/shard_map/ppermute | solution.py:613
  38.4 4.4 %collective-permute-start.10 = (f32[2,8,128]{2,1,0:T(8,128)S(1)}, f32[2,8,128]{2,1,0:T(8,128)S(1)}, u32[]{:S(2)}, u32[]{:S(2)}) collective-permute-start(f32[2,8,128]{2,1,0:T(8,128)S(1)} %get-tuple-element.96), channel_id=1, source_target_pairs={{0,2},{2,4},{4,6},{6,8},{8,10},{10,12},{12,14},{14,0},{1,3},{3,5},... | collective-permute-start | bytes 24584 | tf_op jit(solution)/shard_map/ppermute | solution.py:613
  48.0 1.5 %collective-permute-start.12 = (f32[384,128]{1,0:T(8,128)S(1)}, f32[384,128]{1,0:T(8,128)S(1)}, u32[]{:S(2)}, u32[]{:S(2)}) collective-permute-start(f32[384,128]{1,0:T(8,128)S(1)} %get-tuple-element.109), channel_id=1, source_target_pairs={{1,0},{0,1},{3,2},{2,3},{5,4},{4,5},{7,6},{6,7},{9,8},{8,9},{11,10... | collective-permute-start | bytes 589832 | tf_op jit(solution)/shard_map/ppermute | solution.py:719
  59.6 7.9 %collective-permute-start.14 = (f32[104,128]{1,0:T(8,128)S(1)}, f32[104,128]{1,0:T(8,128)S(1)}, u32[]{:S(2)}, u32[]{:S(2)}) collective-permute-start(f32[104,128]{1,0:T(8,128)S(1)} %get-tuple-element.113), channel_id=1, source_target_pairs={{0,128},{16,144},{32,160},{48,176},{64,192},{80,208},{96,224},{112... | collective-permute-start | bytes 159752 | tf_op jit(solution)/shard_map/ppermute | solution.py:730
  61.6 4.1 %collective-permute-start.13 = (f32[96,128]{1,0:T(8,128)S(1)}, f32[96,128]{1,0:T(8,128)S(1)}, u32[]{:S(2)}, u32[]{:S(2)}) collective-permute-start(f32[96,128]{1,0:T(8,128)S(1)} %get-tuple-element.112), channel_id=1, source_target_pairs={{0,64},{16,80},{32,96},{48,112},{64,0},{80,16},{96,32},{112,48},{1... | collective-permute-start | bytes 147464 | tf_op jit(solution)/shard_map/ppermute | solution.py:730
  62.2 5.3 %collective-permute-start.15 = (f32[96,128]{1,0:T(8,128)S(1)}, f32[96,128]{1,0:T(8,128)S(1)}, u32[]{:S(2)}, u32[]{:S(2)}) collective-permute-start(f32[96,128]{1,0:T(8,128)S(1)} %get-tuple-element.114), channel_id=1, source_target_pairs={{0,192},{16,208},{32,224},{48,240},{64,128},{80,144},{96,160},{112... | collective-permute-start | bytes 147464 | tf_op jit(solution)/shard_map/ppermute | solution.py:730
  67.6 10.4 %collective-permute-start.17 = (f32[104,128]{1,0:T(8,128)S(1)}, f32[104,128]{1,0:T(8,128)S(1)}, u32[]{:S(2)}, u32[]{:S(2)}) collective-permute-start(f32[104,128]{1,0:T(8,128)S(1)} %get-tuple-element.118), channel_id=1, source_target_pairs={{0,32},{16,48},{32,0},{48,16},{64,96},{80,112},{96,64},{112,80},{1... | collective-permute-start | bytes 159752 | tf_op jit(solution)/shard_map/ppermute | solution.py:742
  70.2 5.0 %collective-permute-start.16 = (f32[96,128]{1,0:T(8,128)S(1)}, f32[96,128]{1,0:T(8,128)S(1)}, u32[]{:S(2)}, u32[]{:S(2)}) collective-permute-start(f32[96,128]{1,0:T(8,128)S(1)} %get-tuple-element.117), channel_id=1, source_target_pairs={{0,16},{16,0},{32,48},{48,32},{64,80},{80,64},{96,112},{112,96},{1... | collective-permute-start | bytes 147464 | tf_op jit(solution)/shard_map/ppermute | solution.py:742
  71.6 6.4 %collective-permute-start.18 = (f32[96,128]{1,0:T(8,128)S(1)}, f32[96,128]{1,0:T(8,128)S(1)}, u32[]{:S(2)}, u32[]{:S(2)}) collective-permute-start(f32[96,128]{1,0:T(8,128)S(1)} %get-tuple-element.119), channel_id=1, source_target_pairs={{0,48},{16,32},{32,16},{48,0},{64,112},{80,96},{96,80},{112,64},{1... | collective-permute-start | bytes 147464 | tf_op jit(solution)/shard_map/ppermute | solution.py:742

commit v13 on v11

--- a/solution.py
+++ b/solution.py
@@ -267,9 +267,10 @@
     tall = tall_hits(offsets, width)
     picked = jnp.dot(values, hits, preferred_element_type=F32)
     lines = []
-    for field in range(6):
+    fields = values.shape[0] // (2 * HALF)
+    for field in range(fields):
         rows = slice(field * HALF, (field + 1) * HALF)
-        both = picked[rows] + picked[6 * HALF :][rows]
+        both = picked[rows] + picked[fields * HALF :][rows]
         lines.append(jnp.sum(jnp.where(tall, both, 0.0), axis=0, keepdims=True))
     return lines
 
@@ -277,7 +278,11 @@
 TAKE = 16
 
 
-def drive_kernel(e_old, e_new, placed, columns, drives, values):
+def drive_kernel(
+    e_old, e_new, placed, columns, h_ref, surf_ref, drives, seen, values
+):
+    seen[...] = jnp.zeros_like(seen)
+    sample_field(h_ref, surf_ref, seen, 3)
     values[...] = stacked([(ref, comp) for ref in (e_old, e_new) for comp in range(3)])
     for group in range(0, SLOTS, TAKE):
         offsets = jnp.concatenate([placed[group + n : group + n + 1] for n in range(TAKE)], axis=1)
@@ -288,6 +293,14 @@
                 drives[field, group + slot : group + slot + 1] = got[field][
                     :, slot * CZ : (slot + 1) * CZ
                 ]
+
+
+def sample_field(ref, surf_ref, sampled, first):
+    offsets = surf_ref[...]
+    values = stacked([(ref, comp) for comp in range(3)])
+    got = gather_lines(values, wide_hits(offsets, CZ), offsets, CZ)
+    for comp in range(3):
+        sampled[first + comp : first + comp + 1] = got[comp]
 
 
 def sample_rows(e_ref, h_ref, surf_ref, sampled):
@@ -459,6 +472,7 @@
     dense,
     surf_ref,
     early_ref,
+    seen,
     starts,
     turn,
     factors,
@@ -476,7 +490,8 @@
         polar = dense[comp] + time_step * rates[comp]
         rate = keep_rate * rates[comp] - spring * polar + gain_push * later * field
         e_out[comp] = field + scaled * (curls[comp] - rate)
-    sample_rows(e_out, h_ref, surf_ref, late)
+    late[...] = seen[...]
+    sample_field(e_out, surf_ref, late, 0)
     scale = 1.0 / math.sqrt(STEPS * CZ * 256)
     high, low = split_parts(scale * jnp.concatenate([early_ref[...], late[...]], axis=0))
     left = jnp.concatenate(
@@ -691,10 +706,10 @@
     h_two, *edge = call(magnetic_kernel, (dense,) + faces, (e_one, h_one, *near), name="magnetic2")
     edge = shifted(edge, up)
     e_seen, h_two = lax.optimization_barrier((e_one, h_two))
-    drives = call(
+    drives, seen = call(
         drive_kernel,
-        shape(6, SLOTS, CZ),
-        (e_old, e_seen, placed, columns),
+        (shape(6, SLOTS, CZ), shape(8, CZ)),
+        (e_old, e_seen, placed, columns, h_two, surf),
         scratch=[pltpu.VMEM((12 * HALF, WIDE), BF16)],
         name="drive",
     )
@@ -704,7 +719,7 @@
     e_two, left, send = call(
         final_kernel,
         (dense, shape(32, 2 * CZ, dtype=BF16), part),
-        (e_one, h_two, *edge, eps, rates, spread_next, surf, early, starts, turn, factors),
+        (e_one, h_two, *edge, eps, rates, spread_next, surf, early, seen, starts, turn, factors),
         scratch=[pltpu.VMEM((8, CZ), F32), hold],
         name="final",
     )

time: 88 us -> 87.9 us (level)
  no operation moved by 1% of the time
where the time goes in v13:
time: 87.9 us; the launch traced here: 87.6 us
  starting transfers between devices  34.8 us (40%)
  blocking collectives  20.3 us (23%)
  Pallas kernels  15.5 us (18%)
  waiting for transfers between devices  15.4 us (18%)
  between operations  1.48 us (2%)
    ppermute x12, starting transfers between devices, shifted(): lax.ppermute(part, axis, perm)  20.5 us
    pallas_call x16, Pallas kernels, call(): pl.pallas_call(kernel, out_shape=outs, in_specs=in_specs or [pl.BlockSpec...  15.5 us
    all_to_all x1, blocking collectives, local(): pieces = lax.all_to_all(chip.reshape(8, FAR, DIRS), 'gy', 0, 0, tiled=True)  10.4 us
    all_to_all x1, blocking collectives, local(): gathered = lax.all_to_all(copies, 'gy', 0, 0, tiled=True)  9.87 us
    ppermute x3, starting transfers between devices, local(): lax.ppermute(value, 'gx', [(a * 4 + z, a * 4 + (z ^ k)) for a in range(4)...  6.58 us
    all_to_all x1, waiting for transfers between devices, local(): fields = lax.all_to_all(packed, 'gx', 0, 0, tiled=True)  4.54 us
    ppermute x3, starting transfers between devices, local(): lax.ppermute(value, 'gx', [(a * 4 + z, (a ^ k) * 4 + z) for a in range(4)...  4.18 us
    ppermute x3, waiting for transfers between devices, local(): lax.ppermute(value, 'gx', [(a * 4 + z, a * 4 + (z ^ k)) for a in range(4)...  3.62 us
  transfers between devices with their start and end apart: 20, of which 8 were waited for; matrix products, arithmetic and copies ran while one was open for 0% of the time, Pallas kernels for 13%

profile of v13, /device:TPU:8, one launch (start us, length us, event | category | flops | bytes accessed | tf_op | source)
XLA Modules:
  0.0 87.6 jit_solution(15425629774889596330)
XLA Ops:
  0.6 1.0 %prepare.1 = (f32[2,24,128]{2,1,0:T(8,128)S(1)}, f32[2,8,128]{2,1,0:T(8,128)S(1)}, f32[2,192,128]{2,1,0:T(8,128)S(1)}, f32[3,192,128]{2,1,0:T(8,128)S(1)}, f32[10,32,128]{2,1,0:T(8,128)S(1)}) custom-call(f32[3,192,128]{2,1,0:T(8,128)} %bitcast.25, f32[10,32,128]{2,1,0:T(8,128)} %bitcast.28), custom_call_target="tpu_custom_call" | custom-call | bytes 2097152 | tf_op jit(solution)/shard_map/prepare/pallas_call | solution.py:47
  1.8 8.6 %collective-permute-start = (f32[2,24,128]{2,1,0:T(8,128)S(1)}, f32[2,24,128]{2,1,0:T(8,128)S(1)}, u32[]{:S(2)}, u32[]{:S(2)}) collective-permute-start(f32[2,24,128]{2,1,0:T(8,128)S(1)} %get-tuple-element.73), channel_id=1, source_target_pairs={{16,0},{32,16},{48,32},{64,48},{80,64},{96,80},{112,96},{128,112},... | collective-permute-start | bytes 73736 | tf_op jit(solution)/shard_map/ppermute | solution.py:618
  10.8 0.7 pack.1
  11.5 3.5 %all-to-all-start = ((f32[16,16,128]{2,1,0:T(8,128)}), f32[16,16,128]{2,1,0:T(8,128)S(1)}, u32[]{:S(2)}, u32[]{:S(2)}) async-start(f32[16,16,128]{2,1,0:T(8,128)} %pack.1), calls=%async_computation | async-start | bytes 262144 | tf_op jit(solution)/shard_map/all_to_all | solution.py:635
  15.6 1.2 %phase.1 = (s32[32,128]{1,0:T(8,128)S(1)}, s32[1,128]{1,0:T(1,128)S(1)}, f32[4,128,128]{2,1,0:T(8,128)S(1)}, f32[2,128,128]{2,1,0:T(8,128)S(1)}, f32[2,128,128]{...) custom-call(s32[1]{0:T(128)} %bitcast.23.count_ref, ...), custom_call_target="tpu_custom_call" | custom-call | bytes 262144 | tf_op jit(solution)/shard_map/phase/pallas_call | solution.py:47
  17.1 2.8 %collective-permute-start.3 = (f32[2,24,128]{2,1,0:T(8,128)S(1)}, f32[2,24,128]{2,1,0:T(8,128)S(1)}, u32[]{:S(2)}, u32[]{:S(2)}) collective-permute-start(f32[2,24,128]{2,1,0:T(8,128)S(1)} %get-tuple-element.77), channel_id=1, source_target_pairs={{0,16},{16,32},{32,48},{48,64},{64,80},{80,96},{96,112},{112,128},... | collective-permute-start | bytes 73736 | tf_op jit(solution)/shard_map/ppermute | solution.py:618
  19.9 1.6 %collective-permute-start.4 = (f32[2,8,128]{2,1,0:T(8,128)S(1)}, f32[2,8,128]{2,1,0:T(8,128)S(1)}, u32[]{:S(2)}, u32[]{:S(2)}) collective-permute-start(f32[2,8,128]{2,1,0:T(8,128)S(1)} %get-tuple-element.78), channel_id=1, source_target_pairs={{0,2},{2,4},{4,6},{6,8},{8,10},{10,12},{12,14},{14,0},{1,3},{3,5},... | collective-permute-start | bytes 24584 | tf_op jit(solution)/shard_map/ppermute | solution.py:618
  21.5 4.5 %all-to-all-done.fields_ref = f32[16,16,128]{2,1,0:T(8,128)S(1)} async-done(((f32[16,16,128]{2,1,0:T(8,128)}), f32[16,16,128]{2,1,0:T(8,128)S(1)}, u32[]{:S(2)}, u32[]{:S(2)}) %all-to-all-start) | async-done | bytes 131104 | tf_op jit(solution)/shard_map/all_to_all | solution.py:635
  26.0 2.6 %scatter.1 = (f32[4,192,128]{2,1,0:T(8,128)S(1)}, bf16[96,4096]{1,0:T(8,128)(2,1)S(1)}, bf16[256,4096]{1,0:T(8,128)(2,1)S(1)}) custom-call(s32[32,128]{1,0:T(8,128)S(1)} %get-tuple-element.81.placed, f32[16,16,128]{2,1,0:T(8,128)S(1)} %all-to-all-done.fields_ref), custom_call_target="tpu_custom_call" | custom-call | bytes 2097152 | tf_op jit(solution)/shard_map/scatter/pallas_call | solution.py:47
  29.0 1.2 %collective-permute-start.6 = (f32[2,24,128]{2,1,0:T(8,128)S(1)}, f32[2,24,128]{2,1,0:T(8,128)S(1)}, u32[]{:S(2)}, u32[]{:S(2)}) collective-permute-start(f32[2,24,128]{2,1,0:T(8,128)S(1)} %get-tuple-element.85), channel_id=1, source_target_pairs={{16,0},{32,16},{48,32},{64,48},{80,64},{96,80},{112,96},{128,112},... | collective-permute-start | bytes 73736 | tf_op jit(solution)/shard_map/ppermute | solution.py:618
  30.2 3.5 %collective-permute-start.7 = (f32[2,8,128]{2,1,0:T(8,128)S(1)}, f32[2,8,128]{2,1,0:T(8,128)S(1)}, u32[]{:S(2)}, u32[]{:S(2)}) collective-permute-start(f32[2,8,128]{2,1,0:T(8,128)S(1)} %get-tuple-element.86), channel_id=1, source_target_pairs={{2,0},{4,2},{6,4},{8,6},{10,8},{12,10},{14,12},{0,14},{3,1},{5,3},... | collective-permute-start | bytes 24584 | tf_op jit(solution)/shard_map/ppermute | solution.py:618
  33.6 2.1 %scatter2.1 = (f32[4,192,128]{2,1,0:T(8,128)S(1)}, f32[8,128]{1,0:T(8,128)S(1)}) custom-call(f32[16,16,128]{2,1,0:T(8,128)S(1)} %all-to-all-done.fields_ref, bf16[96,4096]{1,0:T(8,128)(2,1)S(1)} %get-tuple-element.88.tall, bf16[256,4096]{1,0:T(8,128)(2,1)S(1)} %get-tuple-element.89.columns, f32[3,192,128]{2,1,0:T(8,128)S(1)} %get-tuple-element.100.e_ref.e_new, ...), custom_call_target="tpu_custom_call" | custom-call | bytes 2097152 | tf_op jit(solution)/shard_map/scatter2/pallas_call | solution.py:47
  36.2 1.9 %collective-permute-start.9 = (f32[2,24,128]{2,1,0:T(8,128)S(1)}, f32[2,24,128]{2,1,0:T(8,128)S(1)}, u32[]{:S(2)}, u32[]{:S(2)}) collective-permute-start(f32[2,24,128]{2,1,0:T(8,128)S(1)} %get-tuple-element.97), channel_id=1, source_target_pairs={{0,16},{16,32},{32,48},{48,64},{64,80},{80,96},{96,112},{112,128},... | collective-permute-start | bytes 73736 | tf_op jit(solution)/shard_map/ppermute | solution.py:618
  38.1 2.9 %drive.1 = (f32[6,32,128]{2,1,0:T(8,128)S(1)}, f32[8,128]{1,0:T(8,128)S(1)}) custom-call(f32[3,192,128]{2,1,0:T(8,128)S(1)} %get-tuple-element.71.e_ref.e_old, f32[3,192,128]{2,1,0:T(8,128)S(1)} %get-tuple-element.100.e_ref.e_new, s32[32,128]{1,0:T(8,128)S(1)} %get-tuple-element.81.placed, bf16[256,4096]{1,0:T(8,128)(2,1)S(1)} %get-tuple-element.89.columns, ...), custom_call_target="tpu_custom_call" | custom-call | bytes 2097152 | tf_op jit(solution)/shard_map/drive/pallas_call | solution.py:47
  40.9 0.8 collective-permute-done.10.face_y
  41.7 2.6 %collective-permute-done.9.face_x = f32[2,24,128]{2,1,0:T(8,128)S(1)} collective-permute-done((f32[2,24,128]{2,1,0:T(8,128)S(1)}, f32[2,24,128]{2,1,0:T(8,128)S(1)}, u32[]{:S(2)}, u32[]{:S(2)}) %collective-permute-start.9) | collective-permute-done | bytes 24608 | tf_op jit(solution)/shard_map/ppermute | solution.py:618
  44.3 1.7 %final.1 = (f32[3,192,128]{2,1,0:T(8,128)S(1)}, bf16[32,256]{1,0:T(8,128)(2,1)S(1)}, f32[384,128]{1,0:T(8,128)S(1)}) custom-call(f32[3,192,128]{2,1,0:T(8,128)S(1)} %get-tuple-element.100.e_ref.e_new, f32[3,192,128]{2,1,0:T(8,128)S(1)} %get-tuple-element.96.h_ref, f32[2,24,128]{2,1,0:T(8,128)S(1)} %collective-permute-done.9.face_x, ...), custom_call_target="tpu_custom_call" | custom-call | bytes 2097152 | tf_op jit(solution)/shard_map/final/pallas_call | solution.py:47
  46.2 1.1 %keep.1 = f32[384,128]{1,0:T(8,128)S(1)} custom-call(bf16[32,256]{1,0:T(8,128)(2,1)S(1)} %get-tuple-element.112.left, f32[4,128,128]{2,1,0:T(8,128)S(1)} %get-tuple-element.109.starts, f32[2,128,128]{2,1,0:T(8,128)S(1)} %get-tuple-element.110.turn, f32[2,128,128]{2,1,0:T(8,128)S(1)} %get-tuple-element.111.factors), custom_call_target="tpu_custom_call" | custom-call | flops 10000000000 | bytes 2097152 | tf_op jit(solution)/shard_map/keep/pallas_call | solution.py:47
  47.6 10.4 %all_to_all.15.pieces = f32[8,48,128]{2,1,0:T(8,128)S(1)} all-to-all(f32[8,48,128]{2,1,0:T(8,128)S(1)} %bitcast.24), channel_id=1, replica_groups=mesh['gx'=16,'gy'=8,'gz'=2] {'gy'}, dimensions={0} | all-to-all | bytes 393216 | tf_op jit(solution)/shard_map/all_to_all | solution.py:731
  58.1 1.8 %collective-permute-start.14 = (f32[104,128]{1,0:T(8,128)S(1)}, f32[104,128]{1,0:T(8,128)S(1)}, u32[]{:S(2)}, u32[]{:S(2)}) collective-permute-start(f32[104,128]{1,0:T(8,128)S(1)} %get-tuple-element.117), channel_id=1, source_target_pairs={{0,128},{16,144},{32,160},{48,176},{64,192},{80,208},{96,224},{112... | collective-permute-start | bytes 159752 | tf_op jit(solution)/shard_map/ppermute | solution.py:737
  59.9 0.6 collective-permute-start.13
  60.5 1.8 %collective-permute-start.15 = (f32[96,128]{1,0:T(8,128)S(1)}, f32[96,128]{1,0:T(8,128)S(1)}, u32[]{:S(2)}, u32[]{:S(2)}) collective-permute-start(f32[96,128]{1,0:T(8,128)S(1)} %get-tuple-element.118), channel_id=1, source_target_pairs={{0,192},{16,208},{32,224},{48,240},{64,128},{80,144},{96,160},{112... | collective-permute-start | bytes 147464 | tf_op jit(solution)/shard_map/ppermute | solution.py:737
  62.2 1.7 %collective-permute-done.13.one = f32[96,128]{1,0:T(8,128)S(1)} collective-permute-done((f32[96,128]{1,0:T(8,128)S(1)}, f32[96,128]{1,0:T(8,128)S(1)}, u32[]{:S(2)}, u32[]{:S(2)}) %collective-permute-start.13) | collective-permute-done | bytes 49184 | tf_op jit(solution)/shard_map/ppermute | solution.py:737
  64.0 1.8 %collective-permute-done.15.three = f32[96,128]{1,0:T(8,128)S(1)} collective-permute-done((f32[96,128]{1,0:T(8,128)S(1)}, f32[96,128]{1,0:T(8,128)S(1)}, u32[]{:S(2)}, u32[]{:S(2)}) %collective-permute-start.15) | collective-permute-done | bytes 49184 | tf_op jit(solution)/shard_map/ppermute | solution.py:737
  65.8 3.0 %collective-permute-start.17 = (f32[104,128]{1,0:T(8,128)S(1)}, f32[104,128]{1,0:T(8,128)S(1)}, u32[]{:S(2)}, u32[]{:S(2)}) collective-permute-start(f32[104,128]{1,0:T(8,128)S(1)} %get-tuple-element.122), channel_id=1, source_target_pairs={{0,32},{16,48},{32,0},{48,16},{64,96},{80,112},{96,64},{112,80},{1... | collective-permute-start | bytes 159752 | tf_op jit(solution)/shard_map/ppermute | solution.py:749
  68.9 1.7 %collective-permute-start.16 = (f32[96,128]{1,0:T(8,128)S(1)}, f32[96,128]{1,0:T(8,128)S(1)}, u32[]{:S(2)}, u32[]{:S(2)}) collective-permute-start(f32[96,128]{1,0:T(8,128)S(1)} %get-tuple-element.121), channel_id=1, source_target_pairs={{0,16},{16,0},{32,48},{48,32},{64,80},{80,64},{96,112},{112,96},{1... | collective-permute-start | bytes 147464 | tf_op jit(solution)/shard_map/ppermute | solution.py:749
  70.6 1.8 %collective-permute-start.18 = (f32[96,128]{1,0:T(8,128)S(1)}, f32[96,128]{1,0:T(8,128)S(1)}, u32[]{:S(2)}, u32[]{:S(2)}) collective-permute-start(f32[96,128]{1,0:T(8,128)S(1)} %get-tuple-element.123), channel_id=1, source_target_pairs={{0,48},{16,32},{32,16},{48,0},{64,112},{80,96},{96,80},{112,64},{1... | collective-permute-start | bytes 147464 | tf_op jit(solution)/shard_map/ppermute | solution.py:749
  72.4 0.8 store.1
  73.3 2.2 %collective-permute-done.16.one = f32[96,128]{1,0:T(8,128)S(1)} collective-permute-done((f32[96,128]{1,0:T(8,128)S(1)}, f32[96,128]{1,0:T(8,128)S(1)}, u32[]{:S(2)}, u32[]{:S(2)}) %collective-permute-start.16) | collective-permute-done | bytes 49184 | tf_op jit(solution)/shard_map/ppermute | solution.py:749
  75.5 1.4 %collective-permute-done.18.three = f32[96,128]{1,0:T(8,128)S(1)} collective-permute-done((f32[96,128]{1,0:T(8,128)S(1)}, f32[96,128]{1,0:T(8,128)S(1)}, u32[]{:S(2)}, u32[]{:S(2)}) %collective-permute-start.18) | collective-permute-done | bytes 49184 | tf_op jit(solution)/shard_map/ppermute | solution.py:749
  77.0 9.9 %all_to_all.16.far_ref = f32[8,48,128]{2,1,0:T(8,128)S(1)} all-to-all(f32[8,48,128]{2,1,0:T(8,128)S(1)} %get-tuple-element.133), channel_id=1, replica_groups=mesh['gx'=16,'gy'=8,'gz'=2] {'gy'}, dimensions={0} | all-to-all | bytes 393216 | tf_op jit(solution)/shard_map/all_to_all | solution.py:762
  86.8 0.8 atoms.1
  (27 shorter events, 2.1 us)
Async XLA Ops:
  1.7 15.2 %collective-permute-start.2 = (f32[2,192,128]{2,1,0:T(8,128)S(1)}, f32[2,192,128]{2,1,0:T(8,128)S(1)}, u32[]{:S(2)}, u32[]{:S(2)}) collective-permute-start(f32[2,192,128]{2,1,0:T(8,128)S(1)} %get-tuple-element.75), channel_id=1, source_target_pairs={{1,0},{0,1},{3,2},{2,3},{5,4},{4,5},{7,6},{6,7},{9,8},{8,9},{11,10... | collective-permute-start | bytes 589832 | tf_op jit(solution)/shard_map/ppermute | solution.py:618
  1.8 15.1 %collective-permute-start = (f32[2,24,128]{2,1,0:T(8,128)S(1)}, f32[2,24,128]{2,1,0:T(8,128)S(1)}, u32[]{:S(2)}, u32[]{:S(2)}) collective-permute-start(f32[2,24,128]{2,1,0:T(8,128)S(1)} %get-tuple-element.73), channel_id=1, source_target_pairs={{16,0},{32,16},{48,32},{64,48},{80,64},{96,80},{112,96},{128,112},... | collective-permute-start | bytes 73736 | tf_op jit(solution)/shard_map/ppermute | solution.py:618
  10.3 6.5 %collective-permute-start.1 = (f32[2,8,128]{2,1,0:T(8,128)S(1)}, f32[2,8,128]{2,1,0:T(8,128)S(1)}, u32[]{:S(2)}, u32[]{:S(2)}) collective-permute-start(f32[2,8,128]{2,1,0:T(8,128)S(1)} %get-tuple-element.74), channel_id=1, source_target_pairs={{2,0},{4,2},{6,4},{8,6},{10,8},{12,10},{14,12},{0,14},{3,1},{5,3},... | collective-permute-start | bytes 24584 | tf_op jit(solution)/shard_map/ppermute | solution.py:618
  11.5 14.5 %all-to-all-start = ((f32[16,16,128]{2,1,0:T(8,128)}), f32[16,16,128]{2,1,0:T(8,128)S(1)}, u32[]{:S(2)}, u32[]{:S(2)}) async-start(f32[16,16,128]{2,1,0:T(8,128)} %pack.1), calls=%async_computation | async-start | bytes 262144 | tf_op jit(solution)/shard_map/all_to_all | solution.py:635
  17.0 11.6 %collective-permute-start.5 = (f32[2,192,128]{2,1,0:T(8,128)S(1)}, f32[2,192,128]{2,1,0:T(8,128)S(1)}, u32[]{:S(2)}, u32[]{:S(2)}) collective-permute-start(f32[2,192,128]{2,1,0:T(8,128)S(1)} %get-tuple-element.79), channel_id=1, source_target_pairs={{0,1},{1,0},{2,3},{3,2},{4,5},{5,4},{6,7},{7,6},{8,9},{9,8},{10,11... | collective-permute-start | bytes 589832 | tf_op jit(solution)/shard_map/ppermute | solution.py:618
  17.1 11.5 %collective-permute-start.3 = (f32[2,24,128]{2,1,0:T(8,128)S(1)}, f32[2,24,128]{2,1,0:T(8,128)S(1)}, u32[]{:S(2)}, u32[]{:S(2)}) collective-permute-start(f32[2,24,128]{2,1,0:T(8,128)S(1)} %get-tuple-element.77), channel_id=1, source_target_pairs={{0,16},{16,32},{32,48},{48,64},{64,80},{80,96},{96,112},{112,128},... | collective-permute-start | bytes 73736 | tf_op jit(solution)/shard_map/ppermute | solution.py:618
  19.9 8.7 %collective-permute-start.4 = (f32[2,8,128]{2,1,0:T(8,128)S(1)}, f32[2,8,128]{2,1,0:T(8,128)S(1)}, u32[]{:S(2)}, u32[]{:S(2)}) collective-permute-start(f32[2,8,128]{2,1,0:T(8,128)S(1)} %get-tuple-element.78), channel_id=1, source_target_pairs={{0,2},{2,4},{4,6},{6,8},{8,10},{10,12},{12,14},{14,0},{1,3},{3,5},... | collective-permute-start | bytes 24584 | tf_op jit(solution)/shard_map/ppermute | solution.py:618
  28.9 6.9 %collective-permute-start.8 = (f32[2,192,128]{2,1,0:T(8,128)S(1)}, f32[2,192,128]{2,1,0:T(8,128)S(1)}, u32[]{:S(2)}, u32[]{:S(2)}) collective-permute-start(f32[2,192,128]{2,1,0:T(8,128)S(1)} %get-tuple-element.87), channel_id=1, source_target_pairs={{1,0},{0,1},{3,2},{2,3},{5,4},{4,5},{7,6},{6,7},{9,8},{8,9},{11,10... | collective-permute-start | bytes 589832 | tf_op jit(solution)/shard_map/ppermute | solution.py:618
  29.0 6.8 %collective-permute-start.6 = (f32[2,24,128]{2,1,0:T(8,128)S(1)}, f32[2,24,128]{2,1,0:T(8,128)S(1)}, u32[]{:S(2)}, u32[]{:S(2)}) collective-permute-start(f32[2,24,128]{2,1,0:T(8,128)S(1)} %get-tuple-element.85), channel_id=1, source_target_pairs={{16,0},{32,16},{48,32},{64,48},{80,64},{96,80},{112,96},{128,112},... | collective-permute-start | bytes 73736 | tf_op jit(solution)/shard_map/ppermute | solution.py:618
  30.2 5.5 %collective-permute-start.7 = (f32[2,8,128]{2,1,0:T(8,128)S(1)}, f32[2,8,128]{2,1,0:T(8,128)S(1)}, u32[]{:S(2)}, u32[]{:S(2)}) collective-permute-start(f32[2,8,128]{2,1,0:T(8,128)S(1)} %get-tuple-element.86), channel_id=1, source_target_pairs={{2,0},{4,2},{6,4},{8,6},{10,8},{12,10},{14,12},{0,14},{3,1},{5,3},... | collective-permute-start | bytes 24584 | tf_op jit(solution)/shard_map/ppermute | solution.py:618
  35.9 8.4 %collective-permute-start.11 = (f32[2,192,128]{2,1,0:T(8,128)S(1)}, f32[2,192,128]{2,1,0:T(8,128)S(1)}, u32[]{:S(2)}, u32[]{:S(2)}) collective-permute-start(f32[2,192,128]{2,1,0:T(8,128)S(1)} %get-tuple-element.99), channel_id=1, source_target_pairs={{0,1},{1,0},{2,3},{3,2},{4,5},{5,4},{6,7},{7,6},{8,9},{9,8},{10,11... | collective-permute-start | bytes 589832 | tf_op jit(solution)/shard_map/ppermute | solution.py:618
  36.2 8.1 %collective-permute-start.9 = (f32[2,24,128]{2,1,0:T(8,128)S(1)}, f32[2,24,128]{2,1,0:T(8,128)S(1)}, u32[]{:S(2)}, u32[]{:S(2)}) collective-permute-start(f32[2,24,128]{2,1,0:T(8,128)S(1)} %get-tuple-element.97), channel_id=1, source_target_pairs={{0,16},{16,32},{32,48},{48,64},{64,80},{80,96},{96,112},{112,128},... | collective-permute-start | bytes 73736 | tf_op jit(solution)/shard_map/ppermute | solution.py:618
  38.1 3.7 %collective-permute-start.10 = (f32[2,8,128]{2,1,0:T(8,128)S(1)}, f32[2,8,128]{2,1,0:T(8,128)S(1)}, u32[]{:S(2)}, u32[]{:S(2)}) collective-permute-start(f32[2,8,128]{2,1,0:T(8,128)S(1)} %get-tuple-element.98), channel_id=1, source_target_pairs={{0,2},{2,4},{4,6},{6,8},{8,10},{10,12},{12,14},{14,0},{1,3},{3,5},... | collective-permute-start | bytes 24584 | tf_op jit(solution)/shard_map/ppermute | solution.py:618
  46.1 1.5 %collective-permute-start.12 = (f32[384,128]{1,0:T(8,128)S(1)}, f32[384,128]{1,0:T(8,128)S(1)}, u32[]{:S(2)}, u32[]{:S(2)}) collective-permute-start(f32[384,128]{1,0:T(8,128)S(1)} %get-tuple-element.113), channel_id=1, source_target_pairs={{1,0},{0,1},{3,2},{2,3},{5,4},{4,5},{7,6},{6,7},{9,8},{8,9},{11,10... | collective-permute-start | bytes 589832 | tf_op jit(solution)/shard_map/ppermute | solution.py:726
  58.1 7.7 %collective-permute-start.14 = (f32[104,128]{1,0:T(8,128)S(1)}, f32[104,128]{1,0:T(8,128)S(1)}, u32[]{:S(2)}, u32[]{:S(2)}) collective-permute-start(f32[104,128]{1,0:T(8,128)S(1)} %get-tuple-element.117), channel_id=1, source_target_pairs={{0,128},{16,144},{32,160},{48,176},{64,192},{80,208},{96,224},{112... | collective-permute-start | bytes 159752 | tf_op jit(solution)/shard_map/ppermute | solution.py:737
  59.9 4.1 %collective-permute-start.13 = (f32[96,128]{1,0:T(8,128)S(1)}, f32[96,128]{1,0:T(8,128)S(1)}, u32[]{:S(2)}, u32[]{:S(2)}) collective-permute-start(f32[96,128]{1,0:T(8,128)S(1)} %get-tuple-element.116), channel_id=1, source_target_pairs={{0,64},{16,80},{32,96},{48,112},{64,0},{80,16},{96,32},{112,48},{1... | collective-permute-start | bytes 147464 | tf_op jit(solution)/shard_map/ppermute | solution.py:737
  60.5 5.3 %collective-permute-start.15 = (f32[96,128]{1,0:T(8,128)S(1)}, f32[96,128]{1,0:T(8,128)S(1)}, u32[]{:S(2)}, u32[]{:S(2)}) collective-permute-start(f32[96,128]{1,0:T(8,128)S(1)} %get-tuple-element.118), channel_id=1, source_target_pairs={{0,192},{16,208},{32,224},{48,240},{64,128},{80,144},{96,160},{112... | collective-permute-start | bytes 147464 | tf_op jit(solution)/shard_map/ppermute | solution.py:737
  65.8 11.1 %collective-permute-start.17 = (f32[104,128]{1,0:T(8,128)S(1)}, f32[104,128]{1,0:T(8,128)S(1)}, u32[]{:S(2)}, u32[]{:S(2)}) collective-permute-start(f32[104,128]{1,0:T(8,128)S(1)} %get-tuple-element.122), channel_id=1, source_target_pairs={{0,32},{16,48},{32,0},{48,16},{64,96},{80,112},{96,64},{112,80},{1... | collective-permute-start | bytes 159752 | tf_op jit(solution)/shard_map/ppermute | solution.py:749
  68.9 6.6 %collective-permute-start.16 = (f32[96,128]{1,0:T(8,128)S(1)}, f32[96,128]{1,0:T(8,128)S(1)}, u32[]{:S(2)}, u32[]{:S(2)}) collective-permute-start(f32[96,128]{1,0:T(8,128)S(1)} %get-tuple-element.121), channel_id=1, source_target_pairs={{0,16},{16,0},{32,48},{48,32},{64,80},{80,64},{96,112},{112,96},{1... | collective-permute-start | bytes 147464 | tf_op jit(solution)/shard_map/ppermute | solution.py:749
  70.6 6.3 %collective-permute-start.18 = (f32[96,128]{1,0:T(8,128)S(1)}, f32[96,128]{1,0:T(8,128)S(1)}, u32[]{:S(2)}, u32[]{:S(2)}) collective-permute-start(f32[96,128]{1,0:T(8,128)S(1)} %get-tuple-element.123), channel_id=1, source_target_pairs={{0,48},{16,32},{32,16},{48,0},{64,112},{80,96},{96,80},{112,64},{1... | collective-permute-start | bytes 147464 | tf_op jit(solution)/shard_map/ppermute | solution.py:749
